TPU v7x, 32 devices: a whole 2x2x4 slice. The times are simulated.
32 devices in a mesh: row: 4 (over y, x), col: 8 (over z, core).
Axes of the slice: x: 2, y: 2, z: 4, core: 2. Of those that a mesh axis runs over, the one named last changes fastest.
Arguments:
- alignment_left: bfloat16 [512, 16384], P(('row', 'col')), may hold values from -6 to 6
- alignment_right: bfloat16 [512, 16384], P('row', 'col'), may hold values from -6 to 6
- pair_features: bfloat16 [512, 512, 128], P('row', 'col'), may hold values from -6 to 6
- output_weight: bfloat16 [1024, 128], replicated, may hold values from -4 to 4
- output_bias: float32 [128], replicated, may hold values from -4 to 4
- norm_scale_gain: float32 [128], replicated, may hold values from 0.1 to 1.9
- projection_weight: bfloat16 [128, 512], replicated, may hold values from -0.5 to 0.5
- gate_offset_bias: float32 [128], replicated, may hold values from -4 to 4
Outputs:
- new_pair: bfloat16 [512, 512, 128], P('row', 'col')
- projections: bfloat16 [512, 512, 512], P('row', 'col')
All inputs are finite; a program needn't handle non-finite values.
Results may differ from a plain program's by a relative error of at most 0.0058.
Values may be sent and summed in bfloat16 or wider, within the bound.
No kernel may reach another device: no remote copies, remote signals or barrier semaphores. Data moves between devices by JAX's collectives and lax.ppermute only.
A program may use at most 192 MiB of HBM per device.

v0:
```python
import jax
import jax.numpy as jnp
from jax import lax
from jax.sharding import PartitionSpec as P

CHANNEL_WIDTH = 32


norm_eps = 1e-05


def project(values, norm_scale_gain, projection_weight, gate_offset_bias):
    widened = values.astype(jnp.float32)
    average = jnp.mean(widened, axis=-1, keepdims=True)
    centred = widened - average
    variance = jnp.mean(centred * centred, axis=-1, keepdims=True)
    normed = (centred * lax.rsqrt(variance + norm_eps) * norm_scale_gain).astype(jnp.bfloat16)
    projected = jnp.dot(normed, projection_weight, preferred_element_type=jnp.float32)
    quarter = projection_weight.shape[1] // 4
    head_part = projected[..., : 3 * quarter]
    gate_part = jax.nn.sigmoid(projected[..., 3 * quarter :] + gate_offset_bias)
    return jnp.concatenate([head_part, gate_part], axis=-1).astype(jnp.bfloat16)


def shards(
    alignment_left,
    alignment_right,
    pair_features,
    output_weight,
    output_bias,
    norm_scale_gain,
    projection_weight,
    gate_offset_bias,
):
    col_count = lax.axis_size("col")
    tile_rows, tile_cols, channels = pair_features.shape
    right_complete = lax.all_gather(alignment_right, "row", axis=0, tiled=True)
    alignment_depth = right_complete.shape[0]
    alignment_portion = lax.all_gather(alignment_left, "col", axis=0, tiled=True)
    residue_total = alignment_portion.shape[0]
    shaped = alignment_portion.reshape(residue_total, CHANNEL_WIDTH, alignment_depth)
    channel_products = lax.dot_general(
        shaped, right_complete, (((2,), (0,)), ((), ())), preferred_element_type=jnp.float32
    )
    outer_product_average = (channel_products / alignment_depth).astype(jnp.bfloat16)
    outer_product_average = outer_product_average.reshape(
        residue_total, CHANNEL_WIDTH, tile_cols, CHANNEL_WIDTH
    ).transpose(0, 2, 1, 3)
    outer_product_average = outer_product_average.reshape(
        residue_total * tile_cols, CHANNEL_WIDTH * CHANNEL_WIDTH
    )
    update = (
        jnp.dot(outer_product_average, output_weight, preferred_element_type=jnp.float32)
        + output_bias
    )
    fresh = pair_features.astype(jnp.float32).reshape(residue_total * tile_cols, channels) + update
    new_pair = fresh.astype(jnp.bfloat16).reshape(residue_total, tile_cols, channels)
    group_width = projection_weight.shape[1] // col_count
    residues = tile_cols * col_count
    projected = project(new_pair, norm_scale_gain, projection_weight, gate_offset_bias)
    across = lax.all_to_all(
        projected.reshape(tile_rows, tile_cols, col_count, group_width),
        "col",
        split_axis=2,
        concat_axis=1,
        tiled=True,
    )
    down_moved = lax.all_to_all(
        across.reshape(tile_rows, residues, group_width),
        "row",
        split_axis=1,
        concat_axis=0,
        tiled=True,
    )
    result = down_moved.transpose(1, 2, 0)
    return (new_pair, result)


def solution(mesh):
    placed = (
        P(("row", "col"), None),
        P("row", "col"),
        P("row", "col", None),
        P(),
        P(),
        P(),
        P(),
        P(),
    )
    return jax.shard_map(
        shards,
        mesh=mesh,
        in_specs=placed,
        out_specs=(P("row", "col", None), P("row", "col", None)),
        check_vma=False,
    )
```

profile of v0, /device:TPU:0, one launch (start us, length us, event | category | flops | bytes accessed | tf_op | source)
XLA Modules:
  0.0 594.6 jit_solution(1181712126200764461)
XLA Ops:
  7.2 0.0 copy-start
  7.2 0.0 all-gather.3.cloned.1.call-start
  7.2 0.7 all-gather.3.cloned.1.call-update
  7.9 0.0 all-gather.5.cloned.1.call-start
  8.0 0.7 all-gather.5.cloned.1.call-update
  8.7 50.8 %all-gather.3.cloned.1.call-done = bf16[128,16384]{1,0:T(8,128)(2,1)} async-done(((bf16[16,16384]{1,0:T(8,128)(2,1)}), bf16[128,16384]{1,0:T(8,128)(2,1)}) %all-gather.3.cloned.1.call-update) | async-done | bytes 4194320 | tf_op jit(solution)/shard_map/all_gather | solution.py:39
  59.5 6.4 %copy.27 = bf16[128,16384]{0,1:T(8,128)(2,1)} copy(bf16[128,16384]{1,0:T(8,128)(2,1)} %all-gather.3.cloned.1.call-done) | data formatting | bytes 8388608 | tf_op jit(solution)/shard_map/all_gather | solution.py:39
  65.9 29.6 %all-gather.5.cloned.1.call-done = bf16[512,2048]{1,0:T(8,128)(2,1)} async-done(((bf16[128,2048]{1,0:T(8,128)(2,1)}), bf16[512,2048]{1,0:T(8,128)(2,1)}) %all-gather.5.cloned.1.call-update) | async-done | bytes 2097168 | tf_op jit(solution)/shard_map/all_gather | solution.py:37
  95.4 14.9 %multiply_convert_fusion = bf16[128,32,2048]{2,0,1:T(8,128)(2,1)} fusion(bf16[128,32,512]{0,2,1:T(8,128)(2,1)} %bitcast.39, bf16[512,2048]{1,0:T(8,128)(2,1)} %all-gather.5.cloned.1.call-done), kind=kOutput, calls=%fused_computation | convolution fusion | flops 8606711808 | bytes 23068672 | tf_op jit(solution)/shard_map/dot_general | solution.py:42
  110.3 22.5 %copy.29 = bf16[128,32,2048]{0,2,1:T(8,128)(2,1)} copy(bf16[128,32,2048]{2,0,1:T(8,128)(2,1)} %multiply_convert_fusion) | data formatting | bytes 33554432 | tf_op jit(solution)/shard_map/convert_element_type | solution.py:45
  132.8 34.1 %copy.30 = bf16[128,64,32,32]{1,0,3,2:T(8,128)(2,1)} copy(bf16[128,64,32,32]{0,3,1,2:T(8,128)(2,1)} %bitcast.32) | data formatting | bytes 33554432 | tf_op jit(solution)/shard_map/transpose | solution.py:48
  166.9 0.0 copy-start.6
  166.9 44.0 %reshape.65 = bf16[8192,1024]{0,1:T(8,128)(2,1)} reshape(bf16[128,64,32,32]{1,0,3,2:T(8,128)(2,1)} %copy.30) | data formatting | bytes 33554432 | tf_op jit(solution)/shard_map/reshape | solution.py:49
  211.0 0.0 copy-done
  211.0 0.0 copy-done.6
  211.0 0.0 copy-start.4
  211.0 11.9 %convert_reduce_fusion = (f32[8192]{0:T(1024)S(1)}, bf16[8192,128]{1,0:T(8,128)(2,1)S(1)}) fusion(f32[128]{0:T(128)S(1)} %copy-done.6, bf16[8192,1024]{0,1:T(8,128)(2,1)} %reshape.65, bf16[1024,128]{1,0:T(8,128)(2,1)S(1)} %copy-done, bf16[8192,128]{1,0:T(8,128)(2,1)} %bitcast.40), kind=kOutput, calls=%fused_computation.7 | convolution fusion | flops 2153766912 | bytes 21266944 | tf_op jit(solution)/shard_map/dot_general | solution.py:53
  222.9 0.0 copy-start.2
  222.9 0.0 copy-start.3
  223.0 0.1 div.20
  223.0 2.3 fusion.3
  225.4 0.1 rsqrt.12
  225.5 0.0 copy-done.4
  225.5 3.8 multiply_convert_fusion.1
  229.3 0.0 copy-done.2
  229.3 0.0 copy-done.3
  229.3 8.1 %fusion.10 = f32[128,64,512]{2,0,1:T(8,128)} fusion(bf16[128,64,128]{2,1,0:T(8,128)(2,1)S(1)} %multiply_convert_fusion.1, bf16[128,512]{1,0:T(8,128)(2,1)S(1)} %copy-done.3), kind=kOutput, calls=%fused_computation.18 | convolution fusion | flops 1073741824 | bytes 19005440 | tf_op jit(solution)/shard_map/dot_general | solution.py:18
  237.4 0.0 copy-start.5
  237.4 5.6 slice.23
  243.1 0.0 copy-done.5
  243.1 4.6 fusion.8
  247.7 6.2 %pad_maximum_fusion = bf16[128,64,512]{2,0,1:T(8,128)(2,1)} fusion(bf16[128,64,128]{2,0,1:T(8,128)(2,1)} %fusion.8, bf16[128,64,384]{2,0,1:T(8,128)(2,1)S(1)} %slice.23), kind=kLoop, calls=%fused_computation.5 | loop fusion | flops 16777216 | bytes 16777216 | tf_op jit(solution)/shard_map/concatenate | solution.py:22
  253.9 12.0 %copy.32 = bf16[128,64,512]{0,2,1:T(8,128)(2,1)} copy(bf16[128,64,512]{2,0,1:T(8,128)(2,1)} %pad_maximum_fusion) | data formatting | bytes 16777216 | tf_op jit(solution)/shard_map/concatenate | solution.py:22
  265.9 9.7 %copy.33 = bf16[128,64,8,64]{0,3,1,2:T(8,128)(2,1)} copy(bf16[128,64,8,64]{0,3,2,1:T(8,128)(2,1)} %bitcast.33) | data formatting | bytes 16777216 | tf_op jit(solution)/shard_map/convert_element_type | solution.py:22
  275.6 188.7 %all_to_all.33 = bf16[128,64,8,64]{0,3,1,2:T(8,128)(2,1)S(1)} all-to-all(bf16[128,64,8,64]{0,3,1,2:T(8,128)(2,1)} %copy.33), channel_id=1, replica_groups=mesh['row'=4,'col'=8] {'col'}, dimensions={2} | all-to-all | bytes 16777216 | tf_op jit(solution)/shard_map/all_to_all | solution.py:61
  464.3 96.5 %all_to_all.34 = bf16[128,512,64]{0,2,1:T(8,128)(2,1)} all-to-all(bf16[128,512,64]{0,2,1:T(8,128)(2,1)S(1)} %bitcast.34), channel_id=1, replica_groups=mesh['row'=4,'col'=8] {'row'}, dimensions={1} | all-to-all | bytes 16777216 | tf_op jit(solution)/shard_map/all_to_all | solution.py:68
  560.8 13.6 %copy.34 = bf16[4,128,128,64]{2,3,1,0:T(8,128)(2,1)} copy(bf16[4,128,128,64]{1,3,2,0:T(8,128)(2,1)} %bitcast.35) | data formatting | bytes 16777216 | tf_op jit(solution)/shard_map/all_to_all | solution.py:68
  574.3 0.0 copy-start.1
  574.3 13.5 %copy.35 = bf16[128,64,512]{2,1,0:T(8,128)(2,1)} copy(bf16[128,64,512]{0,1,2:T(8,128)(2,1)} %bitcast.36) | data formatting | bytes 16777216
  587.8 0.0 copy-done.1
  (2 shorter events, 0.0 us)
Async XLA Ops:
  7.2 203.8 %copy-start = (bf16[1024,128]{1,0:T(8,128)(2,1)S(1)}, bf16[1024,128]{1,0:T(8,128)(2,1)}, u32[]{:S(2)}) copy-start(bf16[1024,128]{1,0:T(8,128)(2,1)} %param.11) | copy-start | bytes 786436
  7.2 52.3 %all-gather.3.cloned.1.call-start = ((), (), s32[]{:S(2)}) async-start(), calls=%async_computation.2 | async-start | bytes 4718592 | tf_op jit(solution)/shard_map/all_gather | solution.py:39
  7.9 87.5 %all-gather.5.cloned.1.call-start = ((), (), s32[]{:S(2)}) async-start(), calls=%async_computation.3 | async-start | bytes 2621440 | tf_op jit(solution)/shard_map/all_gather | solution.py:37
  166.9 44.0 %copy-start.6 = (f32[128]{0:T(128)S(1)}, f32[128]{0:T(128)}, u32[]{:S(2)}) copy-start(f32[128]{0:T(128)} %param.12) | copy-start | bytes 1540
  211.0 14.5 %copy-start.4 = (f32[128]{0:T(128)S(1)}, f32[128]{0:T(128)}, u32[]{:S(2)}) copy-start(f32[128]{0:T(128)} %param.13) | copy-start | bytes 1540
  222.9 6.4 %copy-start.2 = (bf16[8192,128]{1,0:T(8,128)(2,1)}, bf16[8192,128]{1,0:T(8,128)(2,1)S(1)}, u32[]{:S(2)}) copy-start(bf16[8192,128]{1,0:T(8,128)(2,1)S(1)} %get-tuple-element.7) | copy-start | bytes 6291460
  222.9 6.4 %copy-start.3 = (bf16[128,512]{1,0:T(8,128)(2,1)S(1)}, bf16[128,512]{1,0:T(8,128)(2,1)}, u32[]{:S(2)}) copy-start(bf16[128,512]{1,0:T(8,128)(2,1)} %param.14) | copy-start | bytes 393220
  237.4 5.6 copy-start.5
  574.3 13.5 %copy-start.1 = (bf16[1024,128]{1,0:T(8,128)(2,1)S(1)}, bf16[1024,128]{1,0:T(8,128)(2,1)}, u32[]{:S(2)}) copy-start(bf16[1024,128]{1,0:T(8,128)(2,1)} %param.11) | copy-start | bytes 786436
Sparse Core Ops, SparseCore 0:
  9.6 49.8 all-gather.2
  61.3 34.0 all-gather.4
where the time goes:
time: 598 us; the launch traced here: 595 us
  blocking collectives  285 us (48%)
  local copies, waits for them, and re-layouts  162 us (27%)
  waiting for transfers between devices  81.8 us (14%)
  matrix products  35 us (6%)
  other arithmetic  16.9 us (3%)
  between operations  14.1 us (2%)
    all_to_all x1, blocking collectives, shards(): lax.all_to_all(projected.reshape(tile_rows, tile_cols, col_count, group_w...  189 us
    all_to_all x1, blocking collectives, shards(): lax.all_to_all(across.reshape(tile_rows, residues, group_width), 'row', s...  96.5 us
    all_gather x1, waiting for transfers between devices, shards(): lax.all_gather(alignment_left, 'col', axis=0, tiled=True)  50.8 us
    reshape x1, local copies, waits for them, and re-layouts, shards(): outer_product_average.reshape(residue_total * tile_cols, CHANNEL_WIDTH *...  44 us
    transpose x1, local copies, waits for them, and re-layouts, shards(): outer_product_average = outer_product_average.reshape(residue_total, CHAN...  34.1 us
    all_gather x1, waiting for transfers between devices, shards(): right_complete = lax.all_gather(alignment_right, 'row', axis=0, tiled=True)  29.6 us
    convert_element_type x1, local copies, waits for them, and re-layouts, shards(): (channel_products / alignment_depth).astype(jnp.bfloat16)  22.5 us
    dot_general x1, matrix products, shards(): lax.dot_general(shaped, right_complete, (((2,), (0,)), ((), ())), preferr...  14.9 us
  transfers between devices with their start and end apart: 2, of which 2 were waited for; matrix products, arithmetic and copies ran while one was open for 1% of the time, Pallas kernels for 0%

commit v1 on v0

v1 whole, which is shorter than its diff:
```python
import functools

import jax
import jax.numpy as jnp
from jax import lax
from jax.experimental import pallas as pl
from jax.experimental.pallas import tpu as pltpu
from jax.sharding import PartitionSpec as P

CHANNEL_WIDTH = 32
CORES = 2
STEP = 16
VMEM_LIMIT = 50 * 1024 * 1024

norm_eps = 1e-05

NT = (((1,), (1,)), ((), ()))


def update_kernel(
    parts,
    part,
    where_ref,
    left_ref,
    *refs,
):
    rights = refs[:parts]
    pair_ref, weight_ref, bias_ref, gain_ref = refs[parts : parts + 4]
    new_ref, normed_ref, right_all, right_turned, outer, rows, sems = refs[-7:]
    tile_rows = pair_ref.shape[0]
    share = rights[0].shape[0]
    depth = share * parts
    width = STEP * CHANNEL_WIDTH
    mine = where_ref[0]
    copies = []
    for d in range(parts):
        source = rights[d].at[:, pl.ds(part * width, width)]
        place = pl.multiple_of((mine ^ d) * share, share)
        copy = pltpu.make_async_copy(source, right_all.at[pl.ds(place, share), :], sems.at[d])
        copy.start()
        copies.append(copy)
    rows[...] = pair_ref[...].astype(jnp.float32).reshape(tile_rows * STEP, -1)
    for copy in copies:
        copy.wait()
    right_turned[...] = right_all[...].T
    for c1 in range(0, CHANNEL_WIDTH, 2):
        both = jnp.concatenate(
            [left_ref[:, c * depth : (c + 1) * depth] for c in (c1, c1 + 1)], axis=0
        )
        product = lax.dot_general(right_turned[...], both, NT, preferred_element_type=jnp.float32)
        outer[:, c1 * tile_rows : (c1 + 2) * tile_rows] = (product * (1.0 / depth)).astype(jnp.bfloat16)
    for j in range(0, STEP, 2):
        columns = [
            jnp.concatenate(
                [
                    outer[
                        jj * CHANNEL_WIDTH : (jj + 1) * CHANNEL_WIDTH,
                        c1 * tile_rows : (c1 + 1) * tile_rows,
                    ]
                    for c1 in range(CHANNEL_WIDTH)
                ],
                axis=0,
            )
            for jj in (j, j + 1)
        ]
        update = jnp.dot(
            weight_ref[...], jnp.concatenate(columns, axis=1), preferred_element_type=jnp.float32
        )
        for jj in (j, j + 1):
            mine_update = update[:, (jj - j) * tile_rows : (jj - j + 1) * tile_rows] + bias_ref[...]
            place = pl.ds(jj, tile_rows, stride=STEP)
            fresh = rows[place, :].T + mine_update
            widened = fresh.astype(jnp.bfloat16).astype(jnp.float32)
            rows[place, :] = widened.T
            centred = widened - jnp.mean(widened, axis=0, keepdims=True)
            variance = jnp.mean(centred * centred, axis=0, keepdims=True)
            normed_ref[jj] = (centred * lax.rsqrt(variance + norm_eps) * gain_ref[...]).astype(jnp.bfloat16)
    new_ref[...] = rows[...].reshape(tile_rows, STEP, -1).astype(jnp.bfloat16)


def update_call(where, left, rights, pair, weight, bias, gain, earlier, part):
    tile_rows, tile_cols, channels = pair.shape
    parts = len(rights)
    depth = rights[0].shape[0] * parts
    width = STEP * CHANNEL_WIDTH
    whole = pl.BlockSpec(memory_space=pltpu.VMEM)
    far = pl.BlockSpec(memory_space=pl.ANY)
    block = pl.BlockSpec((tile_rows, STEP, channels), lambda g: (0, part, 0))
    args = [where, left, *rights, pair, weight, bias, gain]
    specs = [
        pl.BlockSpec(memory_space=pltpu.SMEM),
        whole,
        *[far] * parts,
        block,
        whole,
        whole,
        whole,
    ]
    aliases = {}
    if earlier is not None:
        aliases = {len(args): 0}
        args.append(earlier)
        specs.append(far)
    flops = 2 * width * CHANNEL_WIDTH * tile_rows * depth + 2 * STEP * tile_rows * CHANNEL_WIDTH**2 * channels
    return pl.pallas_call(
        functools.partial(update_kernel, parts, part),
        grid=(1,),
        in_specs=specs,
        out_specs=(block, pl.BlockSpec((STEP, channels, tile_rows), lambda g: (0, 0, 0))),
        out_shape=(
            jax.ShapeDtypeStruct(pair.shape, jnp.bfloat16),
            jax.ShapeDtypeStruct((STEP, channels, tile_rows), jnp.bfloat16),
        ),
        scratch_shapes=[
            pltpu.VMEM((depth, width), jnp.bfloat16),
            pltpu.VMEM((width, depth), jnp.bfloat16),
            pltpu.VMEM((width, CHANNEL_WIDTH * tile_rows), jnp.bfloat16),
            pltpu.VMEM((tile_rows * STEP, channels), jnp.float32),
            pltpu.SemaphoreType.DMA((parts,)),
        ],
        input_output_aliases=aliases,
        compiler_params=pltpu.CompilerParams(vmem_limit_bytes=VMEM_LIMIT),
        cost_estimate=pl.CostEstimate(flops=flops, bytes_accessed=8 * 2**20, transcendentals=0),
        name="update",
    )(*args)


def project_kernel(line, parts, where_ref, weight_ref, offset_ref, gate_ref, *refs):
    tiles = refs[: 2 * line - 1]
    outs = refs[2 * line - 1 : 2 * line - 1 + CORES * parts]
    held, sems = refs[-2:]
    mine, place = where_ref[0], where_ref[1]
    group = weight_ref.shape[0] // CORES
    lanes = held.shape[-1]

    def fetch(d):
        distance = (mine ^ d) - place
        for index in range(2 * line - 1):
            @pl.when(distance == index - (line - 1))
            def _():
                pltpu.make_async_copy(tiles[index], held.at[d % 2], sems.at[d % 2]).start()

    fetch(0)
    for d in range(parts):
        if d + 1 < parts:
            fetch(d + 1)
        pltpu.make_async_copy(tiles[0], held.at[d % 2], sems.at[d % 2]).wait()
        for j in range(0, STEP, 2):
            both = jnp.concatenate([held[d % 2, j], held[d % 2, j + 1]], axis=1)
            raw = jnp.dot(weight_ref[...], both, preferred_element_type=jnp.float32)
            gated = 1.0 / (1.0 + jnp.exp(-(raw + offset_ref[...])))
            result = jnp.where(gate_ref[...] > 0.0, gated, raw).astype(jnp.bfloat16)
            for e in range(CORES):
                for jj in range(2):
                    outs[d * CORES + e][j + jj] = result[
                        e * group : (e + 1) * group, jj * lanes : (jj + 1) * lanes
                    ]


def project_call(where, weight, offset, gate, tiles, parts):
    line = (len(tiles) + 1) // 2
    channels, lanes = tiles[0].shape[1:]
    group = weight.shape[0] // CORES
    whole = pl.BlockSpec(memory_space=pltpu.VMEM)
    far = pl.BlockSpec(memory_space=pl.ANY)
    shape = jax.ShapeDtypeStruct((STEP, group, lanes), jnp.bfloat16)
    return pl.pallas_call(
        functools.partial(project_kernel, line, parts),
        in_specs=[pl.BlockSpec(memory_space=pltpu.SMEM), whole, whole, whole, *[far] * len(tiles)],
        out_specs=[whole] * (CORES * parts),
        out_shape=[shape] * (CORES * parts),
        scratch_shapes=[
            pltpu.VMEM((2, STEP, channels, lanes), jnp.bfloat16),
            pltpu.SemaphoreType.DMA((2,)),
        ],
        compiler_params=pltpu.CompilerParams(vmem_limit_bytes=VMEM_LIMIT),
        cost_estimate=pl.CostEstimate(
            flops=2 * parts * STEP * channels * lanes * weight.shape[0],
            bytes_accessed=4 * 2**20,
            transcendentals=0,
        ),
        name="project",
    )(where, weight, offset, gate, *tiles)


def place_kernel(parts, part, tile_cols, where_ref, *refs):
    pieces = refs[: CORES * parts]
    out_ref, sems = refs[-2:]
    mine, core = where_ref[0], where_ref[2]
    step, group, lanes = pieces[0].shape
    copies = []
    for d in range(parts):
        for e in range(CORES):
            row = pl.multiple_of((core ^ e) * tile_cols + part * STEP, STEP)
            column = pl.multiple_of((mine ^ d) * lanes, lanes)
            copy = pltpu.make_async_copy(
                pieces[d * CORES + e],
                out_ref.at[pl.ds(row, step), :, pl.ds(column, lanes)],
                sems.at[d * CORES + e],
            )
            copy.start()
            copies.append(copy)
    for copy in copies:
        copy.wait()


def place_call(where, pieces, earlier, part, parts, tile_cols):
    step, group, lanes = pieces[0].shape
    far = pl.BlockSpec(memory_space=pl.ANY)
    args = [where, *pieces]
    aliases = {}
    if earlier is not None:
        aliases = {len(args): 0}
        args.append(earlier)
    return pl.pallas_call(
        functools.partial(place_kernel, parts, part, tile_cols),
        in_specs=[pl.BlockSpec(memory_space=pltpu.SMEM), *[far] * (len(args) - 1)],
        out_specs=far,
        out_shape=jax.ShapeDtypeStruct((CORES * tile_cols, group, parts * lanes), jnp.bfloat16),
        scratch_shapes=[pltpu.SemaphoreType.DMA((CORES * parts,))],
        input_output_aliases=aliases,
        cost_estimate=pl.CostEstimate(flops=0, bytes_accessed=4 * 2**20, transcendentals=0),
        name="place",
    )(*args)


def shards(
    alignment_left,
    alignment_right,
    pair_features,
    output_weight,
    output_bias,
    norm_scale_gain,
    projection_weight,
    gate_offset_bias,
):
    parts, cols = lax.axis_size("row"), lax.axis_size("col")
    line = cols // CORES
    assert line == parts
    tile_rows, tile_cols, channels = pair_features.shape
    row, col = lax.axis_index("row"), lax.axis_index("col")
    where = jnp.stack([row, col // CORES, col % CORES]).astype(jnp.int32)

    rights = [alignment_right]
    for d in range(1, parts):
        rights.append(lax.ppermute(alignment_right, "row", [(a, a ^ d) for a in range(parts)]))
    left = lax.all_gather(alignment_left, "col", axis=0, tiled=True)

    weight = output_weight.T
    bias = output_bias.reshape(channels, 1)
    gain = norm_scale_gain.reshape(channels, 1)

    total = projection_weight.shape[1]
    group = total // cols
    gate_start = total - gate_offset_bias.shape[0]
    turned = projection_weight.T
    offsets = jnp.concatenate([jnp.zeros((gate_start,), jnp.float32), gate_offset_bias]).reshape(total, 1)
    gates = (jnp.arange(total) >= gate_start).astype(jnp.float32).reshape(total, 1)

    def chosen(array):
        return jnp.concatenate(
            [lax.dynamic_slice_in_dim(array, (col ^ e) * group, group, 0) for e in range(CORES)], axis=0
        )

    my_weight, my_offsets, my_gates = chosen(turned), chosen(offsets), chosen(gates)

    new_pair, result = None, None
    for part in range(tile_cols // STEP):
        new_pair, normed = update_call(
            where, left, rights, pair_features, weight, bias, gain, new_pair, part
        )
        tiles = {0: normed}
        for s in range(1, line):
            up = [(z * CORES + k, (z + 1) * CORES + k) for z in range(s - 1, line - 1) for k in range(CORES)]
            down = [(cols - 1 - a, cols - 1 - b) for a, b in up]
            tiles[-s] = lax.ppermute(tiles[-(s - 1)], "col", up)
            tiles[s] = lax.ppermute(tiles[s - 1], "col", down)
        pieces = project_call(
            where,
            my_weight,
            my_offsets,
            my_gates,
            [tiles[o] for o in range(-(line - 1), line)],
            parts,
        )
        moved = []
        for d in range(parts):
            for e in range(CORES):
                piece = pieces[d * CORES + e]
                if d or e:
                    pairs = [
                        (a * cols + c, (a ^ d) * cols + (c ^ e)) for a in range(parts) for c in range(cols)
                    ]
                    piece = lax.ppermute(piece, ("row", "col"), pairs)
                moved.append(piece)
        result = place_call(where, moved, result, part, parts, tile_cols)
    return (new_pair, result)


def solution(mesh):
    placed = (
        P(("row", "col"), None),
        P("row", "col"),
        P("row", "col", None),
        P(),
        P(),
        P(),
        P(),
        P(),
    )
    return jax.shard_map(
        shards,
        mesh=mesh,
        in_specs=placed,
        out_specs=(P("row", "col", None), P("row", "col", None)),
        check_vma=False,
    )
```

time: 598 us -> 583 us (0.975)
  Pallas kernels: 0 us -> 308 us
  blocking collectives: 285 us -> 0 us
  local copies, waits for them, and re-layouts: 162 us -> 10.4 us
  waiting for transfers between devices: 81.8 us -> 177 us
  starting transfers between devices: 0.08 us -> 71.7 us
  matrix products: 35 us -> 0 us
  other arithmetic: 16.9 us -> 0.23 us
    pallas_call x0 -> x12, Pallas kernels: none -> 308 us  [the longest x4 261 us: place_call(): pl.pallas_call(functools.partial(place_kernel, parts, part, tile_cols), i...]
    all_to_all x2 -> x0, blocking collectives: 285 us -> none  [the longest x1 189 us: shards(): lax.all_to_all(projected.reshape(tile_rows, tile_cols, col_count, group_w...]
    ppermute x0 -> x55, waiting for transfers between devices: none -> 153 us  [the longest x12 86.6 us: shards(): tiles[s] = lax.ppermute(tiles[s - 1], 'col', down)]
    ppermute x0 -> x55, starting transfers between devices: none -> 71.6 us  [the longest x28 29.1 us: shards(): piece = lax.ppermute(piece, ('row', 'col'), pairs)]
    all_gather x2 -> x1, waiting for transfers between devices: 80.4 us -> 24 us  [shards(): left = lax.all_gather(alignment_left, 'col', axis=0, tiled=True)]
    reshape x1 -> x2, local copies, waits for them, and re-layouts: 44 us -> 1.52 us  [the longest x1 0.76 us: shards(): bias = output_bias.reshape(channels, 1)]
    dot_general x3 -> x0, matrix products: 35 us -> none  [the longest x1 14.9 us: shards(): lax.dot_general(shaped, right_complete, (((2,), (0,)), ((), ())), preferr...]
    transpose x1 -> x0, local copies, waits for them, and re-layouts: 34.1 us -> none  [shards(): outer_product_average = outer_product_average.reshape(residue_total, CHAN...]
  transfers between devices with their start and end apart: 2 -> 56, of which waited for: 2 -> 21; matrix products, arithmetic and copies ran while one was open for 1% -> 1% of each run, Pallas kernels for 0% -> 37%
where the time goes in v1:
time: 583 us; the launch traced here: 582 us
  Pallas kernels  308 us (53%)
  waiting for transfers between devices  177 us (30%)
  starting transfers between devices  71.7 us (12%)
  between operations  14.8 us (3%)
  local copies, waits for them, and re-layouts  10.4 us (2%)
    pallas_call x4, Pallas kernels, place_call(): pl.pallas_call(functools.partial(place_kernel, parts, part, tile_cols), i...  261 us
    ppermute x12, waiting for transfers between devices, shards(): tiles[s] = lax.ppermute(tiles[s - 1], 'col', down)  86.6 us
    ppermute x28, waiting for transfers between devices, shards(): piece = lax.ppermute(piece, ('row', 'col'), pairs)  45.7 us
    ppermute x28, starting transfers between devices, shards(): piece = lax.ppermute(piece, ('row', 'col'), pairs)  29.1 us
    pallas_call x4, Pallas kernels, update_call(): pl.pallas_call(functools.partial(update_kernel, parts, part), grid=(1,),...  28.9 us
    all_gather x1, waiting for transfers between devices, shards(): left = lax.all_gather(alignment_left, 'col', axis=0, tiled=True)  24 us
    ppermute x12, starting transfers between devices, shards(): tiles[-s] = lax.ppermute(tiles[-(s - 1)], 'col', up)  22.3 us
    ppermute x3, waiting for transfers between devices, shards(): lax.ppermute(alignment_right, 'row', [(a, a ^ d) for a in range(parts)])  20.3 us
  transfers between devices with their start and end apart: 56, of which 21 were waited for; matrix products, arithmetic and copies ran while one was open for 1% of the time, Pallas kernels for 37%

profile of v1, /device:TPU:0, one launch (start us, length us, event | category | flops | bytes accessed | tf_op | source)
XLA Modules:
  0.0 582.1 jit_solution(6073541857873313974)
XLA Ops:
  7.9 4.0 collective-permute-start.2
  15.2 9.7 %collective-permute-done.2.refs_3_ = bf16[128,2048]{1,0:T(8,128)(2,1)S(1)} collective-permute-done((bf16[128,2048]{1,0:T(8,128)(2,1)}, bf16[128,2048]{1,0:T(8,128)(2,1)S(1)}, u32[]{:S(2)}, u32[]{:S(2)}) %collective-permute-start.2) | collective-permute-done | bytes 524320 | tf_op jit(solution)/shard_map/ppermute | solution.py:246
  24.9 10.4 %collective-permute-done.1.refs_2_ = bf16[128,2048]{1,0:T(8,128)(2,1)S(1)} collective-permute-done((bf16[128,2048]{1,0:T(8,128)(2,1)}, bf16[128,2048]{1,0:T(8,128)(2,1)S(1)}, u32[]{:S(2)}, u32[]{:S(2)}) %collective-permute-start.1) | collective-permute-done | bytes 524320 | tf_op jit(solution)/shard_map/ppermute | solution.py:246
  35.5 24.0 %all-gather.2.cloned.1.call-done.left_ref = bf16[128,16384]{1,0:T(8,128)(2,1)} async-done(((bf16[16,16384]{1,0:T(8,128)(2,1)}), bf16[128,16384]{1,0:T(8,128)(2,1)}) %all-gather.2.cloned.1.call-update) | async-done | bytes 4194320 | tf_op jit(solution)/shard_map/all_gather | solution.py:247
  60.5 7.0 %update.4 = (bf16[128,64,128]{2,1,0:T(8,128)(2,1)}, bf16[16,128,128]{2,1,0:T(8,128)(2,1)S(1)}) custom-call(s32[3]{0:T(128)S(1)} %pad_add_fusion.where_ref, bf16[128,16384]{1,0:T(8,128)(2,1)} %all-gather.2.cloned.1.call-done.left_ref, bf16[128,2048]{1,0:T(8,128)(2,1)S(1)} %copy-done, bf16[128,2048]{1,0:T(8,128)(2,1)S(1)} %collective-permute-done.refs_1_, ...), custom_call_target="tpu_custom_call" | custom-call | flops 2684354560 | bytes 8388608 | tf_op jit(solution)/shard_map/update/pallas_call | solution.py:105
  67.5 7.2 %update.5 = (bf16[128,64,128]{2,1,0:T(8,128)(2,1)}, bf16[16,128,128]{2,1,0:T(8,128)(2,1)S(1)}) custom-call(s32[3]{0:T(128)S(1)} %pad_add_fusion.where_ref, bf16[128,16384]{1,0:T(8,128)(2,1)} %all-gather.2.cloned.1.call-done.left_ref, bf16[128,2048]{1,0:T(8,128)(2,1)S(1)} %copy-done, ...), custom_call_target="tpu_custom_call", output_to_operand_aliasing={{0}: (10, {})} | custom-call | flops 2684354560 | bytes 8388608 | tf_op jit(solution)/shard_map/update/pallas_call | solution.py:105
  74.8 7.2 %update.6 = (bf16[128,64,128]{2,1,0:T(8,128)(2,1)}, bf16[16,128,128]{2,1,0:T(8,128)(2,1)S(1)}) custom-call(s32[3]{0:T(128)S(1)} %pad_add_fusion.where_ref, bf16[128,16384]{1,0:T(8,128)(2,1)} %all-gather.2.cloned.1.call-done.left_ref, bf16[128,2048]{1,0:T(8,128)(2,1)S(1)} %copy-done, ...), custom_call_target="tpu_custom_call", output_to_operand_aliasing={{0}: (10, {})} | custom-call | flops 2684354560 | bytes 8388608 | tf_op jit(solution)/shard_map/update/pallas_call | solution.py:105
  82.0 7.4 %update.7 = (bf16[128,64,128]{2,1,0:T(8,128)(2,1)}, bf16[16,128,128]{2,1,0:T(8,128)(2,1)S(1)}) custom-call(s32[3]{0:T(128)S(1)} %pad_add_fusion.where_ref, bf16[128,16384]{1,0:T(8,128)(2,1)} %all-gather.2.cloned.1.call-done.left_ref, bf16[128,2048]{1,0:T(8,128)(2,1)S(1)} %copy-done, ...), custom_call_target="tpu_custom_call", output_to_operand_aliasing={{0}: (10, {})} | custom-call | flops 2684354560 | bytes 8388608 | tf_op jit(solution)/shard_map/update/pallas_call | solution.py:105
  90.8 4.6 collective-permute-start.3
  96.7 4.6 collective-permute-start.16
  102.6 3.6 collective-permute-done.6.refs_4_
  106.1 1.9 collective-permute-start.29
  109.3 8.0 %collective-permute-done.19.refs_4_ = bf16[16,128,128]{2,1,0:T(8,128)(2,1)S(1)} collective-permute-done((bf16[16,128,128]{2,1,0:T(8,128)(2,1)S(1)}, bf16[16,128,128]{2,1,0:T(8,128)(2,1)S(1)}, u32[]{:S(2)}, u32[]{:S(2)}) %collective-permute-start.19) | collective-permute-done | bytes 524320 | tf_op jit(solution)/shard_map/ppermute | solution.py:277
  117.4 1.9 collective-permute-start.42
  120.6 8.0 %collective-permute-done.32.refs_4_ = bf16[16,128,128]{2,1,0:T(8,128)(2,1)S(1)} collective-permute-done((bf16[16,128,128]{2,1,0:T(8,128)(2,1)S(1)}, bf16[16,128,128]{2,1,0:T(8,128)(2,1)S(1)}, u32[]{:S(2)}, u32[]{:S(2)}) %collective-permute-start.32) | collective-permute-done | bytes 524320 | tf_op jit(solution)/shard_map/ppermute | solution.py:277
  132.1 7.8 %collective-permute-done.45.refs_4_ = bf16[16,128,128]{2,1,0:T(8,128)(2,1)} collective-permute-done((bf16[16,128,128]{2,1,0:T(8,128)(2,1)S(1)}, bf16[16,128,128]{2,1,0:T(8,128)(2,1)}, u32[]{:S(2)}, u32[]{:S(2)}) %collective-permute-start.45) | collective-permute-done | bytes 524320 | tf_op jit(solution)/shard_map/ppermute | solution.py:277
  142.9 8.3 %collective-permute-done.7.refs_5_ = bf16[16,128,128]{2,1,0:T(8,128)(2,1)} collective-permute-done((bf16[16,128,128]{2,1,0:T(8,128)(2,1)S(1)}, bf16[16,128,128]{2,1,0:T(8,128)(2,1)}, u32[]{:S(2)}, u32[]{:S(2)}) %collective-permute-start.7) | collective-permute-done | bytes 524320 | tf_op jit(solution)/shard_map/ppermute | solution.py:277
  153.2 9.2 %collective-permute-done.20.refs_5_ = bf16[16,128,128]{2,1,0:T(8,128)(2,1)} collective-permute-done((bf16[16,128,128]{2,1,0:T(8,128)(2,1)S(1)}, bf16[16,128,128]{2,1,0:T(8,128)(2,1)}, u32[]{:S(2)}, u32[]{:S(2)}) %collective-permute-start.20) | collective-permute-done | bytes 524320 | tf_op jit(solution)/shard_map/ppermute | solution.py:277
  164.4 9.1 %collective-permute-done.33.refs_5_ = bf16[16,128,128]{2,1,0:T(8,128)(2,1)S(1)} collective-permute-done((bf16[16,128,128]{2,1,0:T(8,128)(2,1)S(1)}, bf16[16,128,128]{2,1,0:T(8,128)(2,1)S(1)}, u32[]{:S(2)}, u32[]{:S(2)}) %collective-permute-start.33) | collective-permute-done | bytes 524320 | tf_op jit(solution)/shard_map/ppermute | solution.py:277
  173.5 1.5 collective-permute-start.5
  176.5 8.4 %collective-permute-done.46.refs_5_ = bf16[16,128,128]{2,1,0:T(8,128)(2,1)} collective-permute-done((bf16[16,128,128]{2,1,0:T(8,128)(2,1)}, bf16[16,128,128]{2,1,0:T(8,128)(2,1)}, u32[]{:S(2)}, u32[]{:S(2)}) %collective-permute-start.46) | collective-permute-done | bytes 524320 | tf_op jit(solution)/shard_map/ppermute | solution.py:277
  187.6 8.5 %collective-permute-done.8.refs_6_ = bf16[16,128,128]{2,1,0:T(8,128)(2,1)} collective-permute-done((bf16[16,128,128]{2,1,0:T(8,128)(2,1)}, bf16[16,128,128]{2,1,0:T(8,128)(2,1)}, u32[]{:S(2)}, u32[]{:S(2)}) %collective-permute-start.8) | collective-permute-done | bytes 524320 | tf_op jit(solution)/shard_map/ppermute | solution.py:277
  196.1 1.5 collective-permute-start.31
  199.4 7.9 %collective-permute-done.21.refs_6_ = bf16[16,128,128]{2,1,0:T(8,128)(2,1)} collective-permute-done((bf16[16,128,128]{2,1,0:T(8,128)(2,1)}, bf16[16,128,128]{2,1,0:T(8,128)(2,1)}, u32[]{:S(2)}, u32[]{:S(2)}) %collective-permute-start.21) | collective-permute-done | bytes 524320 | tf_op jit(solution)/shard_map/ppermute | solution.py:277
  210.0 4.8 project.4
  215.6 4.1 project.5
  219.8 1.5 collective-permute-start.10
  221.5 7.6 %collective-permute-done.47.refs_6_ = bf16[16,128,128]{2,1,0:T(8,128)(2,1)} collective-permute-done((bf16[16,128,128]{2,1,0:T(8,128)(2,1)}, bf16[16,128,128]{2,1,0:T(8,128)(2,1)}, u32[]{:S(2)}, u32[]{:S(2)}) %collective-permute-start.47) | collective-permute-done | bytes 524320 | tf_op jit(solution)/shard_map/ppermute | solution.py:277
  230.6 1.5 collective-permute-start.25
  233.3 2.4 collective-permute-start.27
  235.7 4.4 project.6
  240.3 2.7 collective-permute-done.24.refs_3_
  245.6 10.3 %collective-permute-done.26.refs_5_ = bf16[16,64,128]{2,1,0:T(8,128)(2,1)S(1)} collective-permute-done((bf16[16,64,128]{2,1,0:T(8,128)(2,1)S(1)}, bf16[16,64,128]{2,1,0:T(8,128)(2,1)S(1)}, u32[]{:S(2)}, u32[]{:S(2)}) %collective-permute-start.26) | collective-permute-done | bytes 262176 | tf_op jit(solution)/shard_map/ppermute | solution.py:294
  256.4 2.0 collective-permute-start.38
  258.4 4.1 project.7
  263.7 1.7 collective-permute-start.40
  267.8 14.8 %collective-permute-done.39.refs_5_ = bf16[16,64,128]{2,1,0:T(8,128)(2,1)S(1)} collective-permute-done((bf16[16,64,128]{2,1,0:T(8,128)(2,1)S(1)}, bf16[16,64,128]{2,1,0:T(8,128)(2,1)S(1)}, u32[]{:S(2)}, u32[]{:S(2)}) %collective-permute-start.39) | collective-permute-done | bytes 262176 | tf_op jit(solution)/shard_map/ppermute | solution.py:294
  282.6 1.5 collective-permute-start.50
  286.9 1.7 collective-permute-start.54
  288.5 2.3 collective-permute-done.50.refs_3_
  290.8 2.2 collective-permute-start.11
  293.0 11.5 %collective-permute-done.51.refs_4_ = bf16[16,64,128]{2,1,0:T(8,128)(2,1)S(1)} collective-permute-done((bf16[16,64,128]{2,1,0:T(8,128)(2,1)S(1)}, bf16[16,64,128]{2,1,0:T(8,128)(2,1)S(1)}, u32[]{:S(2)}, u32[]{:S(2)}) %collective-permute-start.51) | collective-permute-done | bytes 262176 | tf_op jit(solution)/shard_map/ppermute | solution.py:294
  305.1 4.1 collective-permute-done.52.refs_5_
  310.1 1.8 collective-permute-start.14
  312.6 65.4 %place.4.refs_8_ = bf16[128,64,512]{2,1,0:T(8,128)(2,1)} custom-call(s32[3]{0:T(128)} %copy-done.13, bf16[16,64,128]{2,1,0:T(8,128)(2,1)} %copy-done.12, bf16[16,64,128]{2,1,0:T(8,128)(2,1)} %copy-done.39, bf16[16,64,128]{2,1,0:T(8,128)(2,1)} %copy-done.40, bf16[16,64,128]{2,1,0:T(8,128)(2,1)} %copy-done.41, bf16[16,64,128]{2,1,0:T(8,128)(2,1)} %copy-done.42, ...), custom_call_target="tpu_custom_call" | custom-call | bytes 4194304 | tf_op jit(solution)/shard_map/place/pallas_call | solution.py:215
  378.0 65.4 %place.5.refs_8_ = bf16[128,64,512]{2,1,0:T(8,128)(2,1)} custom-call(s32[3]{0:T(128)} %copy-done.13, bf16[16,64,128]{2,1,0:T(8,128)(2,1)} %copy-done.11, bf16[16,64,128]{2,1,0:T(8,128)(2,1)} %copy-done.27, bf16[16,64,128]{2,1,0:T(8,128)(2,1)} %copy-done.28, bf16[16,64,128]{2,1,0:T(8,128)(2,1)} %copy-done.29, ...), custom_call_target="tpu_custom_call", output_to_operand_aliasing={{}: (9, {})} | custom-call | bytes 4194304 | tf_op jit(solution)/shard_map/place/pallas_call | solution.py:215
  443.4 65.4 %place.6.refs_8_ = bf16[128,64,512]{2,1,0:T(8,128)(2,1)} custom-call(s32[3]{0:T(128)} %copy-done.13, bf16[16,64,128]{2,1,0:T(8,128)(2,1)} %copy-done.10, bf16[16,64,128]{2,1,0:T(8,128)(2,1)} %copy-done.20, bf16[16,64,128]{2,1,0:T(8,128)(2,1)} %copy-done.21, bf16[16,64,128]{2,1,0:T(8,128)(2,1)} %copy-done.22, ...), custom_call_target="tpu_custom_call", output_to_operand_aliasing={{}: (9, {})} | custom-call | bytes 4194304 | tf_op jit(solution)/shard_map/place/pallas_call | solution.py:215
  509.9 65.4 %place.7 = bf16[128,64,512]{2,1,0:T(8,128)(2,1)} custom-call(s32[3]{0:T(128)} %copy-done.13, bf16[16,64,128]{2,1,0:T(8,128)(2,1)} %copy-done.9, bf16[16,64,128]{2,1,0:T(8,128)(2,1)} %copy-done.18, bf16[16,64,128]{2,1,0:T(8,128)(2,1)} %copy-done.19, bf16[16,64,128]{2,1,0:T(8,128)(2,1)} %copy-done.34, ...), custom_call_target="tpu_custom_call", output_to_operand_aliasing={{}: (9, {})} | custom-call | bytes 4194304 | tf_op jit(solution)/shard_map/place/pallas_call | solution.py:215
  (187 shorter events, 47.1 us)
Async XLA Ops:
  7.2 52.3 %all-gather.2.cloned.1.call-start = ((), (), s32[]{:S(2)}) async-start(), calls=%async_computation | async-start | bytes 4718592 | tf_op jit(solution)/shard_map/all_gather | solution.py:247
  7.9 17.0 %collective-permute-start.2 = (bf16[128,2048]{1,0:T(8,128)(2,1)}, bf16[128,2048]{1,0:T(8,128)(2,1)S(1)}, u32[]{:S(2)}, u32[]{:S(2)}) collective-permute-start(bf16[128,2048]{1,0:T(8,128)(2,1)} %refs_0_.7), channel_id=1, source_target_pairs={{0,24},{8,16},{16,8},{24,0},{1,25},{9,17},{17,9},{25,1},{2,26},{10... | collective-permute-start | bytes 1572872 | tf_op jit(solution)/shard_map/ppermute | solution.py:246
  11.9 23.4 %collective-permute-start.1 = (bf16[128,2048]{1,0:T(8,128)(2,1)}, bf16[128,2048]{1,0:T(8,128)(2,1)S(1)}, u32[]{:S(2)}, u32[]{:S(2)}) collective-permute-start(bf16[128,2048]{1,0:T(8,128)(2,1)} %refs_0_.7), channel_id=1, source_target_pairs={{0,16},{8,24},{16,0},{24,8},{1,17},{9,25},{17,1},{25,9},{2,18},{10... | collective-permute-start | bytes 1572872 | tf_op jit(solution)/shard_map/ppermute | solution.py:246
  12.4 23.2 %collective-permute-start = (bf16[128,2048]{1,0:T(8,128)(2,1)}, bf16[128,2048]{1,0:T(8,128)(2,1)S(1)}, u32[]{:S(2)}, u32[]{:S(2)}) collective-permute-start(bf16[128,2048]{1,0:T(8,128)(2,1)} %refs_0_.7), channel_id=1, source_target_pairs={{0,8},{8,0},{16,24},{24,16},{1,9},{9,1},{17,25},{25,17},{2,10},{10... | collective-permute-start | bytes 1572872 | tf_op jit(solution)/shard_map/ppermute | solution.py:246
  89.5 16.7 %collective-permute-start.6 = (bf16[16,128,128]{2,1,0:T(8,128)(2,1)S(1)}, bf16[16,128,128]{2,1,0:T(8,128)(2,1)S(1)}, u32[]{:S(2)}, u32[]{:S(2)}) collective-permute-start(bf16[16,128,128]{2,1,0:T(8,128)(2,1)S(1)} %get-tuple-element.46.refs_3_), channel_id=1, source_target_pairs={{7,5},{6,4},{5,3},{4,2},{3,1},{2,0},{15,13},{14,12},{13,11},{12,10... | collective-permute-start | bytes 1572872 | tf_op jit(solution)/shard_map/ppermute | solution.py:277
  90.8 17.2 %collective-permute-start.3 = (bf16[16,128,128]{2,1,0:T(8,128)(2,1)S(1)}, bf16[16,128,128]{2,1,0:T(8,128)(2,1)S(1)}, u32[]{:S(2)}, u32[]{:S(2)}) collective-permute-start(bf16[16,128,128]{2,1,0:T(8,128)(2,1)S(1)} %get-tuple-element.46.refs_3_), channel_id=1, source_target_pairs={{0,2},{1,3},{2,4},{3,5},{4,6},{5,7},{8,10},{9,11},{10,12},{11,13},... | collective-permute-start | bytes 1572872 | tf_op jit(solution)/shard_map/ppermute | solution.py:276
  95.4 22.0 %collective-permute-start.19 = (bf16[16,128,128]{2,1,0:T(8,128)(2,1)S(1)}, bf16[16,128,128]{2,1,0:T(8,128)(2,1)S(1)}, u32[]{:S(2)}, u32[]{:S(2)}) collective-permute-start(bf16[16,128,128]{2,1,0:T(8,128)(2,1)S(1)} %get-tuple-element.55.refs_3_), channel_id=1, source_target_pairs={{7,5},{6,4},{5,3},{4,2},{3,1},{2,0},{15,13},{14,12},{13,11},{12,10... | collective-permute-start | bytes 1572872 | tf_op jit(solution)/shard_map/ppermute | solution.py:277
  96.7 22.6 %collective-permute-start.16 = (bf16[16,128,128]{2,1,0:T(8,128)(2,1)S(1)}, bf16[16,128,128]{2,1,0:T(8,128)(2,1)S(1)}, u32[]{:S(2)}, u32[]{:S(2)}) collective-permute-start(bf16[16,128,128]{2,1,0:T(8,128)(2,1)S(1)} %get-tuple-element.55.refs_3_), channel_id=1, source_target_pairs={{0,2},{1,3},{2,4},{3,5},{4,6},{5,7},{8,10},{9,11},{10,12},{11,13},... | collective-permute-start | bytes 1572872 | tf_op jit(solution)/shard_map/ppermute | solution.py:276
  101.3 27.3 %collective-permute-start.32 = (bf16[16,128,128]{2,1,0:T(8,128)(2,1)S(1)}, bf16[16,128,128]{2,1,0:T(8,128)(2,1)S(1)}, u32[]{:S(2)}, u32[]{:S(2)}) collective-permute-start(bf16[16,128,128]{2,1,0:T(8,128)(2,1)S(1)} %get-tuple-element.64.refs_3_), channel_id=1, source_target_pairs={{7,5},{6,4},{5,3},{4,2},{3,1},{2,0},{15,13},{14,12},{13,11},{12,10... | collective-permute-start | bytes 1572872 | tf_op jit(solution)/shard_map/ppermute | solution.py:277
  106.1 24.7 %collective-permute-start.29 = (bf16[16,128,128]{2,1,0:T(8,128)(2,1)S(1)}, bf16[16,128,128]{2,1,0:T(8,128)(2,1)S(1)}, u32[]{:S(2)}, u32[]{:S(2)}) collective-permute-start(bf16[16,128,128]{2,1,0:T(8,128)(2,1)S(1)} %get-tuple-element.64.refs_3_), channel_id=1, source_target_pairs={{0,2},{1,3},{2,4},{3,5},{4,6},{5,7},{8,10},{9,11},{10,12},{11,13},... | collective-permute-start | bytes 1572872 | tf_op jit(solution)/shard_map/ppermute | solution.py:276
  108.0 31.9 %collective-permute-start.45 = (bf16[16,128,128]{2,1,0:T(8,128)(2,1)S(1)}, bf16[16,128,128]{2,1,0:T(8,128)(2,1)}, u32[]{:S(2)}, u32[]{:S(2)}) collective-permute-start(bf16[16,128,128]{2,1,0:T(8,128)(2,1)S(1)} %get-tuple-element.73.refs_3_), channel_id=1, source_target_pairs={{7,5},{6,4},{5,3},{4,2},{3,1},{2,0},{15,13},{14,12},{13,11},{12,10... | collective-permute-start | bytes 1572872 | tf_op jit(solution)/shard_map/ppermute | solution.py:277
  117.4 24.1 %collective-permute-start.42 = (bf16[16,128,128]{2,1,0:T(8,128)(2,1)S(1)}, bf16[16,128,128]{2,1,0:T(8,128)(2,1)S(1)}, u32[]{:S(2)}, u32[]{:S(2)}) collective-permute-start(bf16[16,128,128]{2,1,0:T(8,128)(2,1)S(1)} %get-tuple-element.73.refs_3_), channel_id=1, source_target_pairs={{0,2},{1,3},{2,4},{3,5},{4,6},{5,7},{8,10},{9,11},{10,12},{11,13},... | collective-permute-start | bytes 1572872 | tf_op jit(solution)/shard_map/ppermute | solution.py:276
  119.3 31.9 %collective-permute-start.7 = (bf16[16,128,128]{2,1,0:T(8,128)(2,1)S(1)}, bf16[16,128,128]{2,1,0:T(8,128)(2,1)}, u32[]{:S(2)}, u32[]{:S(2)}) collective-permute-start(bf16[16,128,128]{2,1,0:T(8,128)(2,1)S(1)} %collective-permute-done.6.refs_4_), channel_id=1, source_target_pairs={{5,3},{4,2},{3,1},{2,0},{13,11},{12,10},{11,9},{10,8},{21,19},{20,... | collective-permute-start | bytes 1572872 | tf_op jit(solution)/shard_map/ppermute | solution.py:277
  128.6 23.3 %collective-permute-start.4 = (bf16[16,128,128]{2,1,0:T(8,128)(2,1)S(1)}, bf16[16,128,128]{2,1,0:T(8,128)(2,1)}, u32[]{:S(2)}, u32[]{:S(2)}) collective-permute-start(bf16[16,128,128]{2,1,0:T(8,128)(2,1)S(1)} %collective-permute-done.3.refs_2_), channel_id=1, source_target_pairs={{2,4},{3,5},{4,6},{5,7},{10,12},{11,13},{12,14},{13,15},{18,20},{1... | collective-permute-start | bytes 1572872 | tf_op jit(solution)/shard_map/ppermute | solution.py:276
  130.9 31.6 %collective-permute-start.20 = (bf16[16,128,128]{2,1,0:T(8,128)(2,1)S(1)}, bf16[16,128,128]{2,1,0:T(8,128)(2,1)}, u32[]{:S(2)}, u32[]{:S(2)}) collective-permute-start(bf16[16,128,128]{2,1,0:T(8,128)(2,1)S(1)} %collective-permute-done.19.refs_4_), channel_id=1, source_target_pairs={{5,3},{4,2},{3,1},{2,0},{13,11},{12,10},{11,9},{10,8},{21,19},{20,... | collective-permute-start | bytes 1572872 | tf_op jit(solution)/shard_map/ppermute | solution.py:277
  139.9 23.2 %collective-permute-start.17 = (bf16[16,128,128]{2,1,0:T(8,128)(2,1)S(1)}, bf16[16,128,128]{2,1,0:T(8,128)(2,1)S(1)}, u32[]{:S(2)}, u32[]{:S(2)}) collective-permute-start(bf16[16,128,128]{2,1,0:T(8,128)(2,1)S(1)} %collective-permute-done.16.refs_2_), channel_id=1, source_target_pairs={{2,4},{3,5},{4,6},{5,7},{10,12},{11,13},{12,14},{13,15},{18,20},{1... | collective-permute-start | bytes 1572872 | tf_op jit(solution)/shard_map/ppermute | solution.py:276
  141.4 32.1 %collective-permute-start.33 = (bf16[16,128,128]{2,1,0:T(8,128)(2,1)S(1)}, bf16[16,128,128]{2,1,0:T(8,128)(2,1)S(1)}, u32[]{:S(2)}, u32[]{:S(2)}) collective-permute-start(bf16[16,128,128]{2,1,0:T(8,128)(2,1)S(1)} %collective-permute-done.32.refs_4_), channel_id=1, source_target_pairs={{5,3},{4,2},{3,1},{2,0},{13,11},{12,10},{11,9},{10,8},{21,19},{20,... | collective-permute-start | bytes 1572872 | tf_op jit(solution)/shard_map/ppermute | solution.py:277
  151.2 23.9 %collective-permute-start.30 = (bf16[16,128,128]{2,1,0:T(8,128)(2,1)S(1)}, bf16[16,128,128]{2,1,0:T(8,128)(2,1)S(1)}, u32[]{:S(2)}, u32[]{:S(2)}) collective-permute-start(bf16[16,128,128]{2,1,0:T(8,128)(2,1)S(1)} %collective-permute-done.29.refs_2_), channel_id=1, source_target_pairs={{2,4},{3,5},{4,6},{5,7},{10,12},{11,13},{12,14},{13,15},{18,20},{1... | collective-permute-start | bytes 1572872 | tf_op jit(solution)/shard_map/ppermute | solution.py:276
  151.9 33.0 %collective-permute-start.46 = (bf16[16,128,128]{2,1,0:T(8,128)(2,1)}, bf16[16,128,128]{2,1,0:T(8,128)(2,1)}, u32[]{:S(2)}, u32[]{:S(2)}) collective-permute-start(bf16[16,128,128]{2,1,0:T(8,128)(2,1)} %collective-permute-done.45.refs_4_), channel_id=1, source_target_pairs={{5,3},{4,2},{3,1},{2,0},{13,11},{12,10},{11,9},{10,8},{21,19},{20,... | collective-permute-start | bytes 1572872 | tf_op jit(solution)/shard_map/ppermute | solution.py:277
  162.4 23.9 %collective-permute-start.43 = (bf16[16,128,128]{2,1,0:T(8,128)(2,1)S(1)}, bf16[16,128,128]{2,1,0:T(8,128)(2,1)S(1)}, u32[]{:S(2)}, u32[]{:S(2)}) collective-permute-start(bf16[16,128,128]{2,1,0:T(8,128)(2,1)S(1)} %collective-permute-done.42.refs_2_), channel_id=1, source_target_pairs={{2,4},{3,5},{4,6},{5,7},{10,12},{11,13},{12,14},{13,15},{18,20},{1... | collective-permute-start | bytes 1572872 | tf_op jit(solution)/shard_map/ppermute | solution.py:276
  163.1 33.0 %collective-permute-start.8 = (bf16[16,128,128]{2,1,0:T(8,128)(2,1)}, bf16[16,128,128]{2,1,0:T(8,128)(2,1)}, u32[]{:S(2)}, u32[]{:S(2)}) collective-permute-start(bf16[16,128,128]{2,1,0:T(8,128)(2,1)} %collective-permute-done.7.refs_5_), channel_id=1, source_target_pairs={{3,1},{2,0},{11,9},{10,8},{19,17},{18,16},{27,25},{26,24}} | collective-permute-start | bytes 1572872 | tf_op jit(solution)/shard_map/ppermute | solution.py:277
  173.5 24.6 %collective-permute-start.5 = (bf16[16,128,128]{2,1,0:T(8,128)(2,1)}, bf16[16,128,128]{2,1,0:T(8,128)(2,1)}, u32[]{:S(2)}, u32[]{:S(2)}) collective-permute-start(bf16[16,128,128]{2,1,0:T(8,128)(2,1)} %collective-permute-done.4.refs_1_), channel_id=1, source_target_pairs={{4,6},{5,7},{12,14},{13,15},{20,22},{21,23},{28,30},{29,31}} | collective-permute-start | bytes 1572872 | tf_op jit(solution)/shard_map/ppermute | solution.py:276
  175.1 32.3 %collective-permute-start.21 = (bf16[16,128,128]{2,1,0:T(8,128)(2,1)}, bf16[16,128,128]{2,1,0:T(8,128)(2,1)}, u32[]{:S(2)}, u32[]{:S(2)}) collective-permute-start(bf16[16,128,128]{2,1,0:T(8,128)(2,1)} %collective-permute-done.20.refs_5_), channel_id=1, source_target_pairs={{3,1},{2,0},{11,9},{10,8},{19,17},{18,16},{27,25},{26,24}} | collective-permute-start | bytes 1572872 | tf_op jit(solution)/shard_map/ppermute | solution.py:277
  184.9 30.7 %collective-permute-start.18 = (bf16[16,128,128]{2,1,0:T(8,128)(2,1)S(1)}, bf16[16,128,128]{2,1,0:T(8,128)(2,1)}, u32[]{:S(2)}, u32[]{:S(2)}) collective-permute-start(bf16[16,128,128]{2,1,0:T(8,128)(2,1)S(1)} %collective-permute-done.17.refs_1_), channel_id=1, source_target_pairs={{4,6},{5,7},{12,14},{13,15},{20,22},{21,23},{28,30},{29,31}} | collective-permute-start | bytes 1572872 | tf_op jit(solution)/shard_map/ppermute | solution.py:276
  186.3 33.4 %collective-permute-start.34 = (bf16[16,128,128]{2,1,0:T(8,128)(2,1)}, bf16[16,128,128]{2,1,0:T(8,128)(2,1)}, u32[]{:S(2)}, u32[]{:S(2)}) collective-permute-start(bf16[16,128,128]{2,1,0:T(8,128)(2,1)} %copy-done.15), channel_id=1, source_target_pairs={{3,1},{2,0},{11,9},{10,8},{19,17},{18,16},{27,25},{26,24}} | collective-permute-start | bytes 1572872 | tf_op jit(solution)/shard_map/ppermute | solution.py:277
  196.1 25.2 %collective-permute-start.31 = (bf16[16,128,128]{2,1,0:T(8,128)(2,1)S(1)}, bf16[16,128,128]{2,1,0:T(8,128)(2,1)}, u32[]{:S(2)}, u32[]{:S(2)}) collective-permute-start(bf16[16,128,128]{2,1,0:T(8,128)(2,1)S(1)} %collective-permute-done.30.refs_1_), channel_id=1, source_target_pairs={{4,6},{5,7},{12,14},{13,15},{20,22},{21,23},{28,30},{29,31}} | collective-permute-start | bytes 1572872 | tf_op jit(solution)/shard_map/ppermute | solution.py:276
  198.1 31.0 %collective-permute-start.47 = (bf16[16,128,128]{2,1,0:T(8,128)(2,1)}, bf16[16,128,128]{2,1,0:T(8,128)(2,1)}, u32[]{:S(2)}, u32[]{:S(2)}) collective-permute-start(bf16[16,128,128]{2,1,0:T(8,128)(2,1)} %collective-permute-done.46.refs_5_), channel_id=1, source_target_pairs={{3,1},{2,0},{11,9},{10,8},{19,17},{18,16},{27,25},{26,24}} | collective-permute-start | bytes 1572872 | tf_op jit(solution)/shard_map/ppermute | solution.py:277
  207.4 23.3 %collective-permute-start.44 = (bf16[16,128,128]{2,1,0:T(8,128)(2,1)S(1)}, bf16[16,128,128]{2,1,0:T(8,128)(2,1)}, u32[]{:S(2)}, u32[]{:S(2)}) collective-permute-start(bf16[16,128,128]{2,1,0:T(8,128)(2,1)S(1)} %collective-permute-done.43.refs_1_), channel_id=1, source_target_pairs={{4,6},{5,7},{12,14},{13,15},{20,22},{21,23},{28,30},{29,31}} | collective-permute-start | bytes 1572872 | tf_op jit(solution)/shard_map/ppermute | solution.py:276
  215.6 15.0 %collective-permute-start.9 = (bf16[16,64,128]{2,1,0:T(8,128)(2,1)S(1)}, bf16[16,64,128]{2,1,0:T(8,128)(2,1)S(1)}, u32[]{:S(2)}, u32[]{:S(2)}) collective-permute-start(bf16[16,64,128]{2,1,0:T(8,128)(2,1)S(1)} %get-tuple-element.48), channel_id=1, source_target_pairs={{0,1},{1,0},{2,3},{3,2},{4,5},{5,4},{6,7},{7,6},{8,9},{9,8},{10,11... | collective-permute-start | bytes 786440 | tf_op jit(solution)/shard_map/ppermute | solution.py:294
  232.2 23.7 %collective-permute-start.26 = (bf16[16,64,128]{2,1,0:T(8,128)(2,1)S(1)}, bf16[16,64,128]{2,1,0:T(8,128)(2,1)S(1)}, u32[]{:S(2)}, u32[]{:S(2)}) collective-permute-start(bf16[16,64,128]{2,1,0:T(8,128)(2,1)S(1)} %get-tuple-element.61), channel_id=1, source_target_pairs={{0,17},{1,16},{2,19},{3,18},{4,21},{5,20},{6,23},{7,22},{8,25},{9,... | collective-permute-start | bytes 786440 | tf_op jit(solution)/shard_map/ppermute | solution.py:294
  233.3 23.1 %collective-permute-start.27 = (bf16[16,64,128]{2,1,0:T(8,128)(2,1)S(1)}, bf16[16,64,128]{2,1,0:T(8,128)(2,1)S(1)}, u32[]{:S(2)}, u32[]{:S(2)}) collective-permute-start(bf16[16,64,128]{2,1,0:T(8,128)(2,1)S(1)} %get-tuple-element.62), channel_id=1, source_target_pairs={{0,24},{1,25},{2,26},{3,27},{4,28},{5,29},{6,30},{7,31},{8,16},{9,... | collective-permute-start | bytes 786440 | tf_op jit(solution)/shard_map/ppermute | solution.py:294
  240.1 23.1 %collective-permute-start.28 = (bf16[16,64,128]{2,1,0:T(8,128)(2,1)S(1)}, bf16[16,64,128]{2,1,0:T(8,128)(2,1)S(1)}, u32[]{:S(2)}, u32[]{:S(2)}) collective-permute-start(bf16[16,64,128]{2,1,0:T(8,128)(2,1)S(1)} %get-tuple-element.63), channel_id=1, source_target_pairs={{0,25},{1,24},{2,27},{3,26},{4,29},{5,28},{6,31},{7,30},{8,17},{9,... | collective-permute-start | bytes 786440 | tf_op jit(solution)/shard_map/ppermute | solution.py:294
  243.0 20.7 %collective-permute-start.35 = (bf16[16,64,128]{2,1,0:T(8,128)(2,1)S(1)}, bf16[16,64,128]{2,1,0:T(8,128)(2,1)S(1)}, u32[]{:S(2)}, u32[]{:S(2)}) collective-permute-start(bf16[16,64,128]{2,1,0:T(8,128)(2,1)S(1)} %get-tuple-element.66), channel_id=1, source_target_pairs={{0,1},{1,0},{2,3},{3,2},{4,5},{5,4},{6,7},{7,6},{8,9},{9,8},{10,11... | collective-permute-start | bytes 786440 | tf_op jit(solution)/shard_map/ppermute | solution.py:294
  244.1 21.4 %collective-permute-start.36 = (bf16[16,64,128]{2,1,0:T(8,128)(2,1)S(1)}, bf16[16,64,128]{2,1,0:T(8,128)(2,1)S(1)}, u32[]{:S(2)}, u32[]{:S(2)}) collective-permute-start(bf16[16,64,128]{2,1,0:T(8,128)(2,1)S(1)} %get-tuple-element.67), channel_id=1, source_target_pairs={{0,8},{1,9},{2,10},{3,11},{4,12},{5,13},{6,14},{7,15},{8,0},{9,1},... | collective-permute-start | bytes 786440 | tf_op jit(solution)/shard_map/ppermute | solution.py:294
  263.3 19.3 %collective-permute-start.39 = (bf16[16,64,128]{2,1,0:T(8,128)(2,1)S(1)}, bf16[16,64,128]{2,1,0:T(8,128)(2,1)S(1)}, u32[]{:S(2)}, u32[]{:S(2)}) collective-permute-start(bf16[16,64,128]{2,1,0:T(8,128)(2,1)S(1)} %get-tuple-element.70), channel_id=1, source_target_pairs={{0,17},{1,16},{2,19},{3,18},{4,21},{5,20},{6,23},{7,22},{8,25},{9,... | collective-permute-start | bytes 786440 | tf_op jit(solution)/shard_map/ppermute | solution.py:294
  263.7 20.4 %collective-permute-start.40 = (bf16[16,64,128]{2,1,0:T(8,128)(2,1)S(1)}, bf16[16,64,128]{2,1,0:T(8,128)(2,1)S(1)}, u32[]{:S(2)}, u32[]{:S(2)}) collective-permute-start(bf16[16,64,128]{2,1,0:T(8,128)(2,1)S(1)} %get-tuple-element.71), channel_id=1, source_target_pairs={{0,24},{1,25},{2,26},{3,27},{4,28},{5,29},{6,30},{7,31},{8,16},{9,... | collective-permute-start | bytes 786440 | tf_op jit(solution)/shard_map/ppermute | solution.py:294
  265.5 19.2 %collective-permute-start.41 = (bf16[16,64,128]{2,1,0:T(8,128)(2,1)S(1)}, bf16[16,64,128]{2,1,0:T(8,128)(2,1)S(1)}, u32[]{:S(2)}, u32[]{:S(2)}) collective-permute-start(bf16[16,64,128]{2,1,0:T(8,128)(2,1)S(1)} %get-tuple-element.72), channel_id=1, source_target_pairs={{0,25},{1,24},{2,27},{3,26},{4,29},{5,28},{6,31},{7,30},{8,17},{9,... | collective-permute-start | bytes 786440 | tf_op jit(solution)/shard_map/ppermute | solution.py:294
  266.1 19.8 %collective-permute-start.48 = (bf16[16,64,128]{2,1,0:T(8,128)(2,1)S(1)}, bf16[16,64,128]{2,1,0:T(8,128)(2,1)S(1)}, u32[]{:S(2)}, u32[]{:S(2)}) collective-permute-start(bf16[16,64,128]{2,1,0:T(8,128)(2,1)S(1)} %get-tuple-element.75), channel_id=1, source_target_pairs={{0,1},{1,0},{2,3},{3,2},{4,5},{5,4},{6,7},{7,6},{8,9},{9,8},{10,11... | collective-permute-start | bytes 786440 | tf_op jit(solution)/shard_map/ppermute | solution.py:294
  266.8 20.1 %collective-permute-start.49 = (bf16[16,64,128]{2,1,0:T(8,128)(2,1)S(1)}, bf16[16,64,128]{2,1,0:T(8,128)(2,1)S(1)}, u32[]{:S(2)}, u32[]{:S(2)}) collective-permute-start(bf16[16,64,128]{2,1,0:T(8,128)(2,1)S(1)} %get-tuple-element.76), channel_id=1, source_target_pairs={{0,8},{1,9},{2,10},{3,11},{4,12},{5,13},{6,14},{7,15},{8,0},{9,1},... | collective-permute-start | bytes 786440 | tf_op jit(solution)/shard_map/ppermute | solution.py:294
  284.1 20.4 %collective-permute-start.51 = (bf16[16,64,128]{2,1,0:T(8,128)(2,1)S(1)}, bf16[16,64,128]{2,1,0:T(8,128)(2,1)S(1)}, u32[]{:S(2)}, u32[]{:S(2)}) collective-permute-start(bf16[16,64,128]{2,1,0:T(8,128)(2,1)S(1)} %get-tuple-element.78), channel_id=1, source_target_pairs={{0,16},{1,17},{2,18},{3,19},{4,20},{5,21},{6,22},{7,23},{8,24},{9,... | collective-permute-start | bytes 786440 | tf_op jit(solution)/shard_map/ppermute | solution.py:294
  284.7 24.4 %collective-permute-start.52 = (bf16[16,64,128]{2,1,0:T(8,128)(2,1)S(1)}, bf16[16,64,128]{2,1,0:T(8,128)(2,1)S(1)}, u32[]{:S(2)}, u32[]{:S(2)}) collective-permute-start(bf16[16,64,128]{2,1,0:T(8,128)(2,1)S(1)} %get-tuple-element.79), channel_id=1, source_target_pairs={{0,17},{1,16},{2,19},{3,18},{4,21},{5,20},{6,23},{7,22},{8,25},{9,... | collective-permute-start | bytes 786440 | tf_op jit(solution)/shard_map/ppermute | solution.py:294
  285.9 24.2 %collective-permute-start.53 = (bf16[16,64,128]{2,1,0:T(8,128)(2,1)S(1)}, bf16[16,64,128]{2,1,0:T(8,128)(2,1)S(1)}, u32[]{:S(2)}, u32[]{:S(2)}) collective-permute-start(bf16[16,64,128]{2,1,0:T(8,128)(2,1)S(1)} %get-tuple-element.80), channel_id=1, source_target_pairs={{0,24},{1,25},{2,26},{3,27},{4,28},{5,29},{6,30},{7,31},{8,16},{9,... | collective-permute-start | bytes 786440 | tf_op jit(solution)/shard_map/ppermute | solution.py:294
  286.9 25.0 %collective-permute-start.54 = (bf16[16,64,128]{2,1,0:T(8,128)(2,1)S(1)}, bf16[16,64,128]{2,1,0:T(8,128)(2,1)S(1)}, u32[]{:S(2)}, u32[]{:S(2)}) collective-permute-start(bf16[16,64,128]{2,1,0:T(8,128)(2,1)S(1)} %get-tuple-element.81), channel_id=1, source_target_pairs={{0,25},{1,24},{2,27},{3,26},{4,29},{5,28},{6,31},{7,30},{8,17},{9,... | collective-permute-start | bytes 786440 | tf_op jit(solution)/shard_map/ppermute | solution.py:294
  290.8 218.0 %collective-permute-start.11 = (bf16[16,64,128]{2,1,0:T(8,128)(2,1)}, bf16[16,64,128]{2,1,0:T(8,128)(2,1)S(1)}, u32[]{:S(2)}, u32[]{:S(2)}) collective-permute-start(bf16[16,64,128]{2,1,0:T(8,128)(2,1)} %get-tuple-element.50), channel_id=1, source_target_pairs={{0,9},{1,8},{2,11},{3,10},{4,13},{5,12},{6,15},{7,14},{8,1},{9,0},... | collective-permute-start | bytes 786440 | tf_op jit(solution)/shard_map/ppermute | solution.py:294
  304.5 204.3 %collective-permute-start.12 = (bf16[16,64,128]{2,1,0:T(8,128)(2,1)}, bf16[16,64,128]{2,1,0:T(8,128)(2,1)S(1)}, u32[]{:S(2)}, u32[]{:S(2)}) collective-permute-start(bf16[16,64,128]{2,1,0:T(8,128)(2,1)} %get-tuple-element.51), channel_id=1, source_target_pairs={{0,16},{1,17},{2,18},{3,19},{4,20},{5,21},{6,22},{7,23},{8,24},{9,... | collective-permute-start | bytes 786440 | tf_op jit(solution)/shard_map/ppermute | solution.py:294
  309.2 199.7 %collective-permute-start.13 = (bf16[16,64,128]{2,1,0:T(8,128)(2,1)}, bf16[16,64,128]{2,1,0:T(8,128)(2,1)S(1)}, u32[]{:S(2)}, u32[]{:S(2)}) collective-permute-start(bf16[16,64,128]{2,1,0:T(8,128)(2,1)} %get-tuple-element.52), channel_id=1, source_target_pairs={{0,17},{1,16},{2,19},{3,18},{4,21},{5,20},{6,23},{7,22},{8,25},{9,... | collective-permute-start | bytes 786440 | tf_op jit(solution)/shard_map/ppermute | solution.py:294
  310.1 198.7 %collective-permute-start.14 = (bf16[16,64,128]{2,1,0:T(8,128)(2,1)}, bf16[16,64,128]{2,1,0:T(8,128)(2,1)S(1)}, u32[]{:S(2)}, u32[]{:S(2)}) collective-permute-start(bf16[16,64,128]{2,1,0:T(8,128)(2,1)} %get-tuple-element.53), channel_id=1, source_target_pairs={{0,24},{1,25},{2,26},{3,27},{4,28},{5,29},{6,30},{7,31},{8,16},{9,... | collective-permute-start | bytes 786440 | tf_op jit(solution)/shard_map/ppermute | solution.py:294
  311.9 197.0 %collective-permute-start.15 = (bf16[16,64,128]{2,1,0:T(8,128)(2,1)S(1)}, bf16[16,64,128]{2,1,0:T(8,128)(2,1)S(1)}, u32[]{:S(2)}, u32[]{:S(2)}) collective-permute-start(bf16[16,64,128]{2,1,0:T(8,128)(2,1)S(1)} %get-tuple-element.54), channel_id=1, source_target_pairs={{0,25},{1,24},{2,27},{3,26},{4,29},{5,28},{6,31},{7,30},{8,17},{9,... | collective-permute-start | bytes 786440 | tf_op jit(solution)/shard_map/ppermute | solution.py:294
  (56 other events, 1903.1 us)
Sparse Core Ops, SparseCore 0:
  9.6 49.8 all-gather.1

commit v2 on v1

--- a/solution.py
+++ b/solution.py
@@ -185,21 +185,18 @@
 
 def place_kernel(parts, part, tile_cols, where_ref, *refs):
     pieces = refs[: CORES * parts]
-    out_ref, sems = refs[-2:]
+    out_ref, rows, sems = refs[-3:]
     mine, core = where_ref[0], where_ref[2]
     step, group, lanes = pieces[0].shape
     copies = []
-    for d in range(parts):
-        for e in range(CORES):
-            row = pl.multiple_of((core ^ e) * tile_cols + part * STEP, STEP)
+    for e in range(CORES):
+        for d in range(parts):
             column = pl.multiple_of((mine ^ d) * lanes, lanes)
-            copy = pltpu.make_async_copy(
-                pieces[d * CORES + e],
-                out_ref.at[pl.ds(row, step), :, pl.ds(column, lanes)],
-                sems.at[d * CORES + e],
-            )
-            copy.start()
-            copies.append(copy)
+            rows[e, :, :, pl.ds(column, lanes)] = pieces[d * CORES + e][...]
+        row = pl.multiple_of((core ^ e) * tile_cols + part * STEP, STEP)
+        copy = pltpu.make_async_copy(rows.at[e], out_ref.at[pl.ds(row, step)], sems.at[e])
+        copy.start()
+        copies.append(copy)
     for copy in copies:
         copy.wait()
 
@@ -207,19 +204,26 @@
 def place_call(where, pieces, earlier, part, parts, tile_cols):
     step, group, lanes = pieces[0].shape
     far = pl.BlockSpec(memory_space=pl.ANY)
+    whole = pl.BlockSpec(memory_space=pltpu.VMEM)
     args = [where, *pieces]
+    specs = [pl.BlockSpec(memory_space=pltpu.SMEM), *[whole] * len(pieces)]
     aliases = {}
     if earlier is not None:
         aliases = {len(args): 0}
         args.append(earlier)
+        specs.append(far)
     return pl.pallas_call(
         functools.partial(place_kernel, parts, part, tile_cols),
-        in_specs=[pl.BlockSpec(memory_space=pltpu.SMEM), *[far] * (len(args) - 1)],
+        in_specs=specs,
         out_specs=far,
         out_shape=jax.ShapeDtypeStruct((CORES * tile_cols, group, parts * lanes), jnp.bfloat16),
-        scratch_shapes=[pltpu.SemaphoreType.DMA((CORES * parts,))],
+        scratch_shapes=[
+            pltpu.VMEM((CORES, step, group, parts * lanes), jnp.bfloat16),
+            pltpu.SemaphoreType.DMA((CORES,)),
+        ],
         input_output_aliases=aliases,
-        cost_estimate=pl.CostEstimate(flops=0, bytes_accessed=4 * 2**20, transcendentals=0),
+        compiler_params=pltpu.CompilerParams(vmem_limit_bytes=VMEM_LIMIT),
+        cost_estimate=pl.CostEstimate(flops=0, bytes_accessed=8 * 2**20, transcendentals=0),
         name="place",
     )(*args)
 
@@ -264,26 +268,37 @@
 
     my_weight, my_offsets, my_gates = chosen(turned), chosen(offsets), chosen(gates)
 
-    new_pair, result = None, None
-    for part in range(tile_cols // STEP):
-        new_pair, normed = update_call(
-            where, left, rights, pair_features, weight, bias, gain, new_pair, part
-        )
-        tiles = {0: normed}
-        for s in range(1, line):
-            up = [(z * CORES + k, (z + 1) * CORES + k) for z in range(s - 1, line - 1) for k in range(CORES)]
-            down = [(cols - 1 - a, cols - 1 - b) for a, b in up]
-            tiles[-s] = lax.ppermute(tiles[-(s - 1)], "col", up)
-            tiles[s] = lax.ppermute(tiles[s - 1], "col", down)
+    count = tile_cols // STEP
+    state = {"new_pair": None, "result": None}
+    tiles = [{} for _ in range(count)]
+    moved = [None] * count
+
+    def after(value, *others):
+        return lax.optimization_barrier((value, others))[0]
+
+    def update(part, *others):
+        state["new_pair"], tiles[part][0] = update_call(
+            after(where, *others), left, rights, pair_features, weight, bias, gain, state["new_pair"], part
+        )
+
+    def shift(part, s, *others):
+        up = [(z * CORES + k, (z + 1) * CORES + k) for z in range(s - 1, line - 1) for k in range(CORES)]
+        down = [(cols - 1 - a, cols - 1 - b) for a, b in up]
+        here = tiles[part]
+        here[-s] = lax.ppermute(after(here[-(s - 1)], *others), "col", up)
+        here[s] = lax.ppermute(after(here[s - 1], *others), "col", down)
+
+    def send(part, *others):
+        here = tiles[part]
         pieces = project_call(
-            where,
+            after(where, *others),
             my_weight,
             my_offsets,
             my_gates,
-            [tiles[o] for o in range(-(line - 1), line)],
+            [here[o] for o in range(-(line - 1), line)],
             parts,
         )
-        moved = []
+        moved[part] = []
         for d in range(parts):
             for e in range(CORES):
                 piece = pieces[d * CORES + e]
@@ -292,9 +307,22 @@
                         (a * cols + c, (a ^ d) * cols + (c ^ e)) for a in range(parts) for c in range(cols)
                     ]
                     piece = lax.ppermute(piece, ("row", "col"), pairs)
-                moved.append(piece)
-        result = place_call(where, moved, result, part, parts, tile_cols)
-    return (new_pair, result)
+                moved[part].append(piece)
+
+    def place(part):
+        state["result"] = place_call(where, moved[part], state["result"], part, parts, tile_cols)
+
+    update(0)
+    for part in range(count):
+        for s in range(1, line):
+            others = moved[part - 1] if part and s == line - 1 else []
+            shift(part, s, *others)
+            if s == 1 and part + 1 < count:
+                update(part + 1, tiles[part][-1])
+        send(part)
+    for part in range(count):
+        place(part)
+    return (state["new_pair"], state["result"])
 
 
 def solution(mesh):

time: 583 us -> 329 us (0.56)
  Pallas kernels: 308 us -> 52.4 us
    pallas_call x4, Pallas kernels: 261 us -> 8.24 us  [place_call(): pl.pallas_call(functools.partial(place_kernel, parts, part, tile_cols), i...]
  transfers between devices with their start and end apart: 56 -> 56, of which waited for: 21 -> 29; matrix products, arithmetic and copies ran while one was open for 1% -> 1% of each run, Pallas kernels for 37% -> 12%
where the time goes in v2:
time: 329 us; the launch traced here: 328 us
  waiting for transfers between devices  179 us (54%)
  starting transfers between devices  75.4 us (23%)
  Pallas kernels  52.4 us (16%)
  between operations  14.6 us (4%)
  local copies, waits for them, and re-layouts  6.73 us (2%)
    ppermute x12, waiting for transfers between devices, shift(): here[s] = lax.ppermute(after(here[s - 1], *others), 'col', down)  81.5 us
    ppermute x28, waiting for transfers between devices, send(): piece = lax.ppermute(piece, ('row', 'col'), pairs)  52.4 us
    ppermute x12, starting transfers between devices, shift(): here[-s] = lax.ppermute(after(here[-(s - 1)], *others), 'col', up)  28 us
    pallas_call x4, Pallas kernels, update_call(): pl.pallas_call(functools.partial(update_kernel, parts, part), grid=(1,),...  27.8 us
    ppermute x28, starting transfers between devices, send(): piece = lax.ppermute(piece, ('row', 'col'), pairs)  27.2 us
    all_gather x1, waiting for transfers between devices, shards(): left = lax.all_gather(alignment_left, 'col', axis=0, tiled=True)  24 us
    ppermute x3, waiting for transfers between devices, shards(): lax.ppermute(alignment_right, 'row', [(a, a ^ d) for a in range(parts)])  20.3 us
    pallas_call x4, Pallas kernels, project_call(): pl.pallas_call(functools.partial(project_kernel, line, parts), in_specs=[...  16.4 us
  transfers between devices with their start and end apart: 56, of which 29 were waited for; matrix products, arithmetic and copies ran while one was open for 1% of the time, Pallas kernels for 12%

profile of v2, /device:TPU:0, one launch (start us, length us, event | category | flops | bytes accessed | tf_op | source)
XLA Modules:
  0.0 328.3 jit_solution(7128977657506165809)
XLA Ops:
  7.9 4.0 %collective-permute-start.2 = (bf16[128,2048]{1,0:T(8,128)(2,1)}, bf16[128,2048]{1,0:T(8,128)(2,1)S(1)}, u32[]{:S(2)}, u32[]{:S(2)}) collective-permute-start(bf16[128,2048]{1,0:T(8,128)(2,1)} %refs_0_.7), channel_id=1, source_target_pairs={{0,24},{8,16},{16,8},{24,0},{1,25},{9,17},{17,9},{25,1},{2,26},{10... | collective-permute-start | bytes 1572872 | tf_op jit(solution)/shard_map/ppermute | solution.py:250
  15.2 9.7 %collective-permute-done.2.refs_3_ = bf16[128,2048]{1,0:T(8,128)(2,1)S(1)} collective-permute-done((bf16[128,2048]{1,0:T(8,128)(2,1)}, bf16[128,2048]{1,0:T(8,128)(2,1)S(1)}, u32[]{:S(2)}, u32[]{:S(2)}) %collective-permute-start.2) | collective-permute-done | bytes 524320 | tf_op jit(solution)/shard_map/ppermute | solution.py:250
  24.9 10.4 %collective-permute-done.1.refs_2_ = bf16[128,2048]{1,0:T(8,128)(2,1)S(1)} collective-permute-done((bf16[128,2048]{1,0:T(8,128)(2,1)}, bf16[128,2048]{1,0:T(8,128)(2,1)S(1)}, u32[]{:S(2)}, u32[]{:S(2)}) %collective-permute-start.1) | collective-permute-done | bytes 524320 | tf_op jit(solution)/shard_map/ppermute | solution.py:250
  35.5 24.0 %all-gather.2.cloned.1.call-done.left_ref = bf16[128,16384]{1,0:T(8,128)(2,1)} async-done(((bf16[16,16384]{1,0:T(8,128)(2,1)}), bf16[128,16384]{1,0:T(8,128)(2,1)}) %all-gather.2.cloned.1.call-update) | async-done | bytes 4194320 | tf_op jit(solution)/shard_map/all_gather | solution.py:251
  60.5 6.9 %update.4 = (bf16[128,64,128]{2,1,0:T(8,128)(2,1)}, bf16[16,128,128]{2,1,0:T(8,128)(2,1)S(1)}) custom-call(s32[3]{0:T(128)S(1)} %pad_add_fusion.where_ref, bf16[128,16384]{1,0:T(8,128)(2,1)} %all-gather.2.cloned.1.call-done.left_ref, bf16[128,2048]{1,0:T(8,128)(2,1)S(1)} %copy-done, bf16[128,2048]{1,0:T(8,128)(2,1)S(1)} %collective-permute-done.refs_1_, ...), custom_call_target="tpu_custom_call" | custom-call | flops 2684354560 | bytes 8388608 | tf_op jit(solution)/shard_map/update/pallas_call | solution.py:105
  68.8 5.3 %collective-permute-start.3 = (bf16[16,128,128]{2,1,0:T(8,128)(2,1)S(1)}, bf16[16,128,128]{2,1,0:T(8,128)(2,1)}, u32[]{:S(2)}, u32[]{:S(2)}) collective-permute-start(bf16[16,128,128]{2,1,0:T(8,128)(2,1)S(1)} %get-tuple-element.51.refs_3_), channel_id=1, source_target_pairs={{0,2},{1,3},{2,4},{3,5},{4,6},{5,7},{8,10},{9,11},{10,12},{11,13},... | collective-permute-start | bytes 1572872 | tf_op jit(solution)/shard_map/ppermute | solution.py:288
  74.1 9.4 %collective-permute-done.12.refs_4_ = bf16[16,128,128]{2,1,0:T(8,128)(2,1)} collective-permute-done((bf16[16,128,128]{2,1,0:T(8,128)(2,1)S(1)}, bf16[16,128,128]{2,1,0:T(8,128)(2,1)}, u32[]{:S(2)}, u32[]{:S(2)}) %collective-permute-start.12) | collective-permute-done | bytes 524320 | tf_op jit(solution)/shard_map/ppermute | solution.py:289
  86.3 7.0 %update.5 = (bf16[128,64,128]{2,1,0:T(8,128)(2,1)}, bf16[16,128,128]{2,1,0:T(8,128)(2,1)S(1)}) custom-call(s32[3]{0:T(128)S(1)} %pad_add_fusion.where_ref, bf16[128,16384]{1,0:T(8,128)(2,1)} %all-gather.2.cloned.1.call-done.left_ref, bf16[128,2048]{1,0:T(8,128)(2,1)S(1)} %copy-done, ...), custom_call_target="tpu_custom_call", output_to_operand_aliasing={{0}: (10, {})} | custom-call | flops 2684354560 | bytes 8388608 | tf_op jit(solution)/shard_map/update/pallas_call | solution.py:105
  94.8 4.2 %collective-permute-done.13.refs_5_ = bf16[16,128,128]{2,1,0:T(8,128)(2,1)} collective-permute-done((bf16[16,128,128]{2,1,0:T(8,128)(2,1)}, bf16[16,128,128]{2,1,0:T(8,128)(2,1)}, u32[]{:S(2)}, u32[]{:S(2)}) %collective-permute-start.13) | collective-permute-done | bytes 524320 | tf_op jit(solution)/shard_map/ppermute | solution.py:289
  101.9 6.2 %collective-permute-start.4 = (bf16[16,128,128]{2,1,0:T(8,128)(2,1)S(1)}, bf16[16,128,128]{2,1,0:T(8,128)(2,1)}, u32[]{:S(2)}, u32[]{:S(2)}) collective-permute-start(bf16[16,128,128]{2,1,0:T(8,128)(2,1)S(1)} %get-tuple-element.54.refs_3_), channel_id=1, source_target_pairs={{0,2},{1,3},{2,4},{3,5},{4,6},{5,7},{8,10},{9,11},{10,12},{11,13},... | collective-permute-start | bytes 1572872 | tf_op jit(solution)/shard_map/ppermute | solution.py:288
  108.1 4.8 %collective-permute-done.23.refs_4_ = bf16[16,128,128]{2,1,0:T(8,128)(2,1)} collective-permute-done((bf16[16,128,128]{2,1,0:T(8,128)(2,1)S(1)}, bf16[16,128,128]{2,1,0:T(8,128)(2,1)}, u32[]{:S(2)}, u32[]{:S(2)}) %collective-permute-start.23) | collective-permute-done | bytes 524320 | tf_op jit(solution)/shard_map/ppermute | solution.py:289
  114.8 9.4 %collective-permute-done.14.refs_6_ = bf16[16,128,128]{2,1,0:T(8,128)(2,1)} collective-permute-done((bf16[16,128,128]{2,1,0:T(8,128)(2,1)}, bf16[16,128,128]{2,1,0:T(8,128)(2,1)}, u32[]{:S(2)}, u32[]{:S(2)}) %collective-permute-start.14) | collective-permute-done | bytes 524320 | tf_op jit(solution)/shard_map/ppermute | solution.py:289
  124.2 3.8 %project.4 = (bf16[16,64,128]{2,1,0:T(8,128)(2,1)S(1)}, bf16[16,64,128]{2,1,0:T(8,128)(2,1)S(1)}, bf16[16,64,128]{2,1,0:T(8,128)(2,1)S(1)}, bf16[16,64,128]{2,1,...) custom-call(s32[3]{0:T(128)S(1)} %pad_add_fusion.where_ref, ...), custom_call_target="tpu_custom_call" | custom-call | flops 268435456 | bytes 4194304 | tf_op jit(solution)/shard_map/project/pallas_call | solution.py:167
  130.8 2.7 collective-permute-done.24.refs_5_
  135.0 2.2 collective-permute-done.16.refs_2_
  137.2 2.4 collective-permute-start.20
  139.6 2.3 collective-permute-done.17.refs_3_
  141.9 3.0 collective-permute-start.21
  144.9 6.9 %update.6 = (bf16[128,64,128]{2,1,0:T(8,128)(2,1)}, bf16[16,128,128]{2,1,0:T(8,128)(2,1)S(1)}) custom-call(s32[3]{0:T(128)S(1)} %pad_add_fusion.where_ref, bf16[128,16384]{1,0:T(8,128)(2,1)} %all-gather.2.cloned.1.call-done.left_ref, bf16[128,2048]{1,0:T(8,128)(2,1)S(1)} %copy-done.1, ...), custom_call_target="tpu_custom_call", output_to_operand_aliasing={{0}: (10, {})} | custom-call | flops 2684354560 | bytes 8388608 | tf_op jit(solution)/shard_map/update/pallas_call | solution.py:105
  157.8 4.6 %collective-permute-start.5 = (bf16[16,128,128]{2,1,0:T(8,128)(2,1)S(1)}, bf16[16,128,128]{2,1,0:T(8,128)(2,1)S(1)}, u32[]{:S(2)}, u32[]{:S(2)}) collective-permute-start(bf16[16,128,128]{2,1,0:T(8,128)(2,1)S(1)} %get-tuple-element.57.refs_3_), channel_id=1, source_target_pairs={{0,2},{1,3},{2,4},{3,5},{4,6},{5,7},{8,10},{9,11},{10,12},{11,13},... | collective-permute-start | bytes 1572872 | tf_op jit(solution)/shard_map/ppermute | solution.py:288
  162.4 7.3 %collective-permute-done.34.refs_4_ = bf16[16,128,128]{2,1,0:T(8,128)(2,1)S(1)} collective-permute-done((bf16[16,128,128]{2,1,0:T(8,128)(2,1)S(1)}, bf16[16,128,128]{2,1,0:T(8,128)(2,1)S(1)}, u32[]{:S(2)}, u32[]{:S(2)}) %collective-permute-start.34) | collective-permute-done | bytes 524320 | tf_op jit(solution)/shard_map/ppermute | solution.py:289
  171.1 9.9 %collective-permute-done.25.refs_6_ = bf16[16,128,128]{2,1,0:T(8,128)(2,1)S(1)} collective-permute-done((bf16[16,128,128]{2,1,0:T(8,128)(2,1)}, bf16[16,128,128]{2,1,0:T(8,128)(2,1)S(1)}, u32[]{:S(2)}, u32[]{:S(2)}) %collective-permute-start.25) | collective-permute-done | bytes 524320 | tf_op jit(solution)/shard_map/ppermute | solution.py:289
  181.8 4.1 %project.5 = (bf16[16,64,128]{2,1,0:T(8,128)(2,1)S(1)}, bf16[16,64,128]{2,1,0:T(8,128)(2,1)S(1)}, bf16[16,64,128]{2,1,0:T(8,128)(2,1)S(1)}, bf16[16,64,128]{2,1,...) custom-call(s32[3]{0:T(128)S(1)} %pad_add_fusion.where_ref, ...), custom_call_target="tpu_custom_call" | custom-call | flops 268435456 | bytes 4194304 | tf_op jit(solution)/shard_map/project/pallas_call | solution.py:167
  186.1 1.8 collective-permute-start.28
  190.8 4.4 %collective-permute-done.27.refs_2_ = bf16[16,64,128]{2,1,0:T(8,128)(2,1)S(1)} collective-permute-done((bf16[16,64,128]{2,1,0:T(8,128)(2,1)S(1)}, bf16[16,64,128]{2,1,0:T(8,128)(2,1)S(1)}, u32[]{:S(2)}, u32[]{:S(2)}) %collective-permute-start.27) | collective-permute-done | bytes 262176 | tf_op jit(solution)/shard_map/ppermute | solution.py:309
  195.2 1.8 collective-permute-start.31
  197.0 2.9 collective-permute-done.28.refs_3_
  199.9 2.5 collective-permute-start.32
  202.4 6.9 %update.7 = (bf16[128,64,128]{2,1,0:T(8,128)(2,1)}, bf16[16,128,128]{2,1,0:T(8,128)(2,1)S(1)}) custom-call(s32[3]{0:T(128)S(1)} %pad_add_fusion.where_ref, bf16[128,16384]{1,0:T(8,128)(2,1)} %all-gather.2.cloned.1.call-done.left_ref, bf16[128,2048]{1,0:T(8,128)(2,1)S(1)} %copy-done.1, ...), custom_call_target="tpu_custom_call", output_to_operand_aliasing={{0}: (10, {})} | custom-call | flops 2684354560 | bytes 8388608 | tf_op jit(solution)/shard_map/update/pallas_call | solution.py:105
  210.6 3.0 collective-permute-done.30.refs_5_
  215.7 4.6 %collective-permute-start.6 = (bf16[16,128,128]{2,1,0:T(8,128)(2,1)S(1)}, bf16[16,128,128]{2,1,0:T(8,128)(2,1)S(1)}, u32[]{:S(2)}, u32[]{:S(2)}) collective-permute-start(bf16[16,128,128]{2,1,0:T(8,128)(2,1)S(1)} %get-tuple-element.61.refs_3_), channel_id=1, source_target_pairs={{0,2},{1,3},{2,4},{3,5},{4,6},{5,7},{8,10},{9,11},{10,12},{11,13},... | collective-permute-start | bytes 1572872 | tf_op jit(solution)/shard_map/ppermute | solution.py:288
  220.3 5.8 %collective-permute-done.45.refs_4_ = bf16[16,128,128]{2,1,0:T(8,128)(2,1)S(1)} collective-permute-done((bf16[16,128,128]{2,1,0:T(8,128)(2,1)S(1)}, bf16[16,128,128]{2,1,0:T(8,128)(2,1)S(1)}, u32[]{:S(2)}, u32[]{:S(2)}) %collective-permute-start.45) | collective-permute-done | bytes 524320 | tf_op jit(solution)/shard_map/ppermute | solution.py:289
  227.4 9.9 %collective-permute-done.36.refs_6_ = bf16[16,128,128]{2,1,0:T(8,128)(2,1)S(1)} collective-permute-done((bf16[16,128,128]{2,1,0:T(8,128)(2,1)S(1)}, bf16[16,128,128]{2,1,0:T(8,128)(2,1)S(1)}, u32[]{:S(2)}, u32[]{:S(2)}) %collective-permute-start.36) | collective-permute-done | bytes 524320 | tf_op jit(solution)/shard_map/ppermute | solution.py:289
  238.1 4.3 %project.6 = (bf16[16,64,128]{2,1,0:T(8,128)(2,1)S(1)}, bf16[16,64,128]{2,1,0:T(8,128)(2,1)S(1)}, bf16[16,64,128]{2,1,0:T(8,128)(2,1)S(1)}, bf16[16,64,128]{2,1,...) custom-call(s32[3]{0:T(128)S(1)} %pad_add_fusion.where_ref, ...), custom_call_target="tpu_custom_call" | custom-call | flops 268435456 | bytes 4194304 | tf_op jit(solution)/shard_map/project/pallas_call | solution.py:167
  245.1 2.0 collective-permute-done.46.refs_5_
  248.2 3.6 %collective-permute-done.38.refs_2_ = bf16[16,64,128]{2,1,0:T(8,128)(2,1)S(1)} collective-permute-done((bf16[16,64,128]{2,1,0:T(8,128)(2,1)S(1)}, bf16[16,64,128]{2,1,0:T(8,128)(2,1)S(1)}, u32[]{:S(2)}, u32[]{:S(2)}) %collective-permute-start.38) | collective-permute-done | bytes 262176 | tf_op jit(solution)/shard_map/ppermute | solution.py:309
  252.9 3.7 %collective-permute-done.39.refs_3_ = bf16[16,64,128]{2,1,0:T(8,128)(2,1)S(1)} collective-permute-done((bf16[16,64,128]{2,1,0:T(8,128)(2,1)S(1)}, bf16[16,64,128]{2,1,0:T(8,128)(2,1)S(1)}, u32[]{:S(2)}, u32[]{:S(2)}) %collective-permute-start.39) | collective-permute-done | bytes 262176 | tf_op jit(solution)/shard_map/ppermute | solution.py:309
  258.2 9.4 %collective-permute-done.40.refs_4_ = bf16[16,64,128]{2,1,0:T(8,128)(2,1)S(1)} collective-permute-done((bf16[16,64,128]{2,1,0:T(8,128)(2,1)S(1)}, bf16[16,64,128]{2,1,0:T(8,128)(2,1)S(1)}, u32[]{:S(2)}, u32[]{:S(2)}) %collective-permute-start.40) | collective-permute-done | bytes 262176 | tf_op jit(solution)/shard_map/ppermute | solution.py:309
  267.6 3.2 collective-permute-done.41.refs_5_
  272.8 15.0 %collective-permute-done.47.refs_6_ = bf16[16,128,128]{2,1,0:T(8,128)(2,1)S(1)} collective-permute-done((bf16[16,128,128]{2,1,0:T(8,128)(2,1)S(1)}, bf16[16,128,128]{2,1,0:T(8,128)(2,1)S(1)}, u32[]{:S(2)}, u32[]{:S(2)}) %collective-permute-start.47) | collective-permute-done | bytes 524320 | tf_op jit(solution)/shard_map/ppermute | solution.py:289
  288.6 4.1 %project.7 = (bf16[16,64,128]{2,1,0:T(8,128)(2,1)S(1)}, bf16[16,64,128]{2,1,0:T(8,128)(2,1)S(1)}, bf16[16,64,128]{2,1,0:T(8,128)(2,1)S(1)}, bf16[16,64,128]{2,1,...) custom-call(s32[3]{0:T(128)S(1)} %pad_add_fusion.where_ref, ...), custom_call_target="tpu_custom_call" | custom-call | flops 268435456 | bytes 4194304 | tf_op jit(solution)/shard_map/project/pallas_call | solution.py:167
  292.9 1.8 collective-permute-start.50
  297.6 4.3 %collective-permute-done.49.refs_2_ = bf16[16,64,128]{2,1,0:T(8,128)(2,1)S(1)} collective-permute-done((bf16[16,64,128]{2,1,0:T(8,128)(2,1)S(1)}, bf16[16,64,128]{2,1,0:T(8,128)(2,1)S(1)}, u32[]{:S(2)}, u32[]{:S(2)}) %collective-permute-start.49) | collective-permute-done | bytes 262176 | tf_op jit(solution)/shard_map/ppermute | solution.py:309
  302.4 2.1 place.4.refs_8_
  304.5 2.1 place.5.refs_8_
  306.6 2.1 place.6.refs_8_
  308.7 10.7 %collective-permute-done.52.refs_5_ = bf16[16,64,128]{2,1,0:T(8,128)(2,1)S(1)} collective-permute-done((bf16[16,64,128]{2,1,0:T(8,128)(2,1)S(1)}, bf16[16,64,128]{2,1,0:T(8,128)(2,1)S(1)}, u32[]{:S(2)}, u32[]{:S(2)}) %collective-permute-start.52) | collective-permute-done | bytes 262176 | tf_op jit(solution)/shard_map/ppermute | solution.py:309
  319.4 2.1 place.7
  (121 shorter events, 49.1 us)
Async XLA Ops:
  7.2 52.3 %all-gather.2.cloned.1.call-start = ((), (), s32[]{:S(2)}) async-start(), calls=%async_computation | async-start | bytes 4718592 | tf_op jit(solution)/shard_map/all_gather | solution.py:251
  7.9 17.0 %collective-permute-start.2 = (bf16[128,2048]{1,0:T(8,128)(2,1)}, bf16[128,2048]{1,0:T(8,128)(2,1)S(1)}, u32[]{:S(2)}, u32[]{:S(2)}) collective-permute-start(bf16[128,2048]{1,0:T(8,128)(2,1)} %refs_0_.7), channel_id=1, source_target_pairs={{0,24},{8,16},{16,8},{24,0},{1,25},{9,17},{17,9},{25,1},{2,26},{10... | collective-permute-start | bytes 1572872 | tf_op jit(solution)/shard_map/ppermute | solution.py:250
  11.9 23.4 %collective-permute-start.1 = (bf16[128,2048]{1,0:T(8,128)(2,1)}, bf16[128,2048]{1,0:T(8,128)(2,1)S(1)}, u32[]{:S(2)}, u32[]{:S(2)}) collective-permute-start(bf16[128,2048]{1,0:T(8,128)(2,1)} %refs_0_.7), channel_id=1, source_target_pairs={{0,16},{8,24},{16,0},{24,8},{1,17},{9,25},{17,1},{25,9},{2,18},{10... | collective-permute-start | bytes 1572872 | tf_op jit(solution)/shard_map/ppermute | solution.py:250
  12.4 23.2 %collective-permute-start = (bf16[128,2048]{1,0:T(8,128)(2,1)}, bf16[128,2048]{1,0:T(8,128)(2,1)S(1)}, u32[]{:S(2)}, u32[]{:S(2)}) collective-permute-start(bf16[128,2048]{1,0:T(8,128)(2,1)} %refs_0_.7), channel_id=1, source_target_pairs={{0,8},{8,0},{16,24},{24,16},{1,9},{9,1},{17,25},{25,17},{2,10},{10... | collective-permute-start | bytes 1572872 | tf_op jit(solution)/shard_map/ppermute | solution.py:250
  67.5 16.0 %collective-permute-start.12 = (bf16[16,128,128]{2,1,0:T(8,128)(2,1)S(1)}, bf16[16,128,128]{2,1,0:T(8,128)(2,1)}, u32[]{:S(2)}, u32[]{:S(2)}) collective-permute-start(bf16[16,128,128]{2,1,0:T(8,128)(2,1)S(1)} %get-tuple-element.51.refs_3_), channel_id=1, source_target_pairs={{7,5},{6,4},{5,3},{4,2},{3,1},{2,0},{15,13},{14,12},{13,11},{12,10... | collective-permute-start | bytes 1572872 | tf_op jit(solution)/shard_map/ppermute | solution.py:289
  68.8 16.0 %collective-permute-start.3 = (bf16[16,128,128]{2,1,0:T(8,128)(2,1)S(1)}, bf16[16,128,128]{2,1,0:T(8,128)(2,1)}, u32[]{:S(2)}, u32[]{:S(2)}) collective-permute-start(bf16[16,128,128]{2,1,0:T(8,128)(2,1)S(1)} %get-tuple-element.51.refs_3_), channel_id=1, source_target_pairs={{0,2},{1,3},{2,4},{3,5},{4,6},{5,7},{8,10},{9,11},{10,12},{11,13},... | collective-permute-start | bytes 1572872 | tf_op jit(solution)/shard_map/ppermute | solution.py:288
  83.5 15.4 %collective-permute-start.13 = (bf16[16,128,128]{2,1,0:T(8,128)(2,1)}, bf16[16,128,128]{2,1,0:T(8,128)(2,1)}, u32[]{:S(2)}, u32[]{:S(2)}) collective-permute-start(bf16[16,128,128]{2,1,0:T(8,128)(2,1)} %collective-permute-done.12.refs_4_), channel_id=1, source_target_pairs={{5,3},{4,2},{3,1},{2,0},{13,11},{12,10},{11,9},{10,8},{21,19},{20,... | collective-permute-start | bytes 1572872 | tf_op jit(solution)/shard_map/ppermute | solution.py:289
  84.8 15.4 %collective-permute-start.10 = (bf16[16,128,128]{2,1,0:T(8,128)(2,1)}, bf16[16,128,128]{2,1,0:T(8,128)(2,1)}, u32[]{:S(2)}, u32[]{:S(2)}) collective-permute-start(bf16[16,128,128]{2,1,0:T(8,128)(2,1)} %collective-permute-done.3.refs_2_), channel_id=1, source_target_pairs={{2,4},{3,5},{4,6},{5,7},{10,12},{11,13},{12,14},{13,15},{18,20},{1... | collective-permute-start | bytes 1572872 | tf_op jit(solution)/shard_map/ppermute | solution.py:288
  93.3 19.6 %collective-permute-start.23 = (bf16[16,128,128]{2,1,0:T(8,128)(2,1)S(1)}, bf16[16,128,128]{2,1,0:T(8,128)(2,1)}, u32[]{:S(2)}, u32[]{:S(2)}) collective-permute-start(bf16[16,128,128]{2,1,0:T(8,128)(2,1)S(1)} %get-tuple-element.54.refs_3_), channel_id=1, source_target_pairs={{7,5},{6,4},{5,3},{4,2},{3,1},{2,0},{15,13},{14,12},{13,11},{12,10... | collective-permute-start | bytes 1572872 | tf_op jit(solution)/shard_map/ppermute | solution.py:289
  98.9 25.2 %collective-permute-start.14 = (bf16[16,128,128]{2,1,0:T(8,128)(2,1)}, bf16[16,128,128]{2,1,0:T(8,128)(2,1)}, u32[]{:S(2)}, u32[]{:S(2)}) collective-permute-start(bf16[16,128,128]{2,1,0:T(8,128)(2,1)} %collective-permute-done.13.refs_5_), channel_id=1, source_target_pairs={{3,1},{2,0},{11,9},{10,8},{19,17},{18,16},{27,25},{26,24}} | collective-permute-start | bytes 1572872 | tf_op jit(solution)/shard_map/ppermute | solution.py:289
  100.2 23.9 %collective-permute-start.11 = (bf16[16,128,128]{2,1,0:T(8,128)(2,1)}, bf16[16,128,128]{2,1,0:T(8,128)(2,1)}, u32[]{:S(2)}, u32[]{:S(2)}) collective-permute-start(bf16[16,128,128]{2,1,0:T(8,128)(2,1)} %collective-permute-done.10.refs_1_), channel_id=1, source_target_pairs={{4,6},{5,7},{12,14},{13,15},{20,22},{21,23},{28,30},{29,31}} | collective-permute-start | bytes 1572872 | tf_op jit(solution)/shard_map/ppermute | solution.py:288
  101.9 28.0 %collective-permute-start.4 = (bf16[16,128,128]{2,1,0:T(8,128)(2,1)S(1)}, bf16[16,128,128]{2,1,0:T(8,128)(2,1)}, u32[]{:S(2)}, u32[]{:S(2)}) collective-permute-start(bf16[16,128,128]{2,1,0:T(8,128)(2,1)S(1)} %get-tuple-element.54.refs_3_), channel_id=1, source_target_pairs={{0,2},{1,3},{2,4},{3,5},{4,6},{5,7},{8,10},{9,11},{10,12},{11,13},... | collective-permute-start | bytes 1572872 | tf_op jit(solution)/shard_map/ppermute | solution.py:288
  112.9 20.6 %collective-permute-start.24 = (bf16[16,128,128]{2,1,0:T(8,128)(2,1)}, bf16[16,128,128]{2,1,0:T(8,128)(2,1)}, u32[]{:S(2)}, u32[]{:S(2)}) collective-permute-start(bf16[16,128,128]{2,1,0:T(8,128)(2,1)} %collective-permute-done.23.refs_4_), channel_id=1, source_target_pairs={{5,3},{4,2},{3,1},{2,0},{13,11},{12,10},{11,9},{10,8},{21,19},{20,... | collective-permute-start | bytes 1572872 | tf_op jit(solution)/shard_map/ppermute | solution.py:289
  129.6 12.3 %collective-permute-start.17 = (bf16[16,64,128]{2,1,0:T(8,128)(2,1)S(1)}, bf16[16,64,128]{2,1,0:T(8,128)(2,1)S(1)}, u32[]{:S(2)}, u32[]{:S(2)}) collective-permute-start(bf16[16,64,128]{2,1,0:T(8,128)(2,1)S(1)} %get-tuple-element.65), channel_id=1, source_target_pairs={{0,9},{1,8},{2,11},{3,10},{4,13},{5,12},{6,15},{7,14},{8,1},{9,0},... | collective-permute-start | bytes 786440 | tf_op jit(solution)/shard_map/ppermute | solution.py:309
  129.9 25.9 %collective-permute-start.9 = (bf16[16,128,128]{2,1,0:T(8,128)(2,1)}, bf16[16,128,128]{2,1,0:T(8,128)(2,1)S(1)}, u32[]{:S(2)}, u32[]{:S(2)}) collective-permute-start(bf16[16,128,128]{2,1,0:T(8,128)(2,1)} %collective-permute-done.4.refs_2_), channel_id=1, source_target_pairs={{2,4},{3,5},{4,6},{5,7},{10,12},{11,13},{12,14},{13,15},{18,20},{1... | collective-permute-start | bytes 1572872 | tf_op jit(solution)/shard_map/ppermute | solution.py:288
  133.5 19.5 %collective-permute-start.18 = (bf16[16,64,128]{2,1,0:T(8,128)(2,1)S(1)}, bf16[16,64,128]{2,1,0:T(8,128)(2,1)S(1)}, u32[]{:S(2)}, u32[]{:S(2)}) collective-permute-start(bf16[16,64,128]{2,1,0:T(8,128)(2,1)S(1)} %get-tuple-element.66), channel_id=1, source_target_pairs={{0,16},{1,17},{2,18},{3,19},{4,20},{5,21},{6,22},{7,23},{8,24},{9,... | collective-permute-start | bytes 786440 | tf_op jit(solution)/shard_map/ppermute | solution.py:309
  135.0 20.8 %collective-permute-start.19 = (bf16[16,64,128]{2,1,0:T(8,128)(2,1)S(1)}, bf16[16,64,128]{2,1,0:T(8,128)(2,1)S(1)}, u32[]{:S(2)}, u32[]{:S(2)}) collective-permute-start(bf16[16,64,128]{2,1,0:T(8,128)(2,1)S(1)} %get-tuple-element.67), channel_id=1, source_target_pairs={{0,17},{1,16},{2,19},{3,18},{4,21},{5,20},{6,23},{7,22},{8,25},{9,... | collective-permute-start | bytes 786440 | tf_op jit(solution)/shard_map/ppermute | solution.py:309
  137.2 18.6 %collective-permute-start.20 = (bf16[16,64,128]{2,1,0:T(8,128)(2,1)S(1)}, bf16[16,64,128]{2,1,0:T(8,128)(2,1)S(1)}, u32[]{:S(2)}, u32[]{:S(2)}) collective-permute-start(bf16[16,64,128]{2,1,0:T(8,128)(2,1)S(1)} %get-tuple-element.68), channel_id=1, source_target_pairs={{0,24},{1,25},{2,26},{3,27},{4,28},{5,29},{6,30},{7,31},{8,16},{9,... | collective-permute-start | bytes 786440 | tf_op jit(solution)/shard_map/ppermute | solution.py:309
  141.9 13.9 %collective-permute-start.21 = (bf16[16,64,128]{2,1,0:T(8,128)(2,1)S(1)}, bf16[16,64,128]{2,1,0:T(8,128)(2,1)S(1)}, u32[]{:S(2)}, u32[]{:S(2)}) collective-permute-start(bf16[16,64,128]{2,1,0:T(8,128)(2,1)S(1)} %get-tuple-element.69), channel_id=1, source_target_pairs={{0,25},{1,24},{2,27},{3,26},{4,29},{5,28},{6,31},{7,30},{8,17},{9,... | collective-permute-start | bytes 786440 | tf_op jit(solution)/shard_map/ppermute | solution.py:309
  153.0 16.7 %collective-permute-start.34 = (bf16[16,128,128]{2,1,0:T(8,128)(2,1)S(1)}, bf16[16,128,128]{2,1,0:T(8,128)(2,1)S(1)}, u32[]{:S(2)}, u32[]{:S(2)}) collective-permute-start(bf16[16,128,128]{2,1,0:T(8,128)(2,1)S(1)} %get-tuple-element.57.refs_3_), channel_id=1, source_target_pairs={{7,5},{6,4},{5,3},{4,2},{3,1},{2,0},{15,13},{14,12},{13,11},{12,10... | collective-permute-start | bytes 1572872 | tf_op jit(solution)/shard_map/ppermute | solution.py:289
  155.8 15.3 %collective-permute-start.22 = (bf16[16,128,128]{2,1,0:T(8,128)(2,1)S(1)}, bf16[16,128,128]{2,1,0:T(8,128)(2,1)S(1)}, u32[]{:S(2)}, u32[]{:S(2)}) collective-permute-start(bf16[16,128,128]{2,1,0:T(8,128)(2,1)S(1)} %collective-permute-done.9.refs_1_), channel_id=1, source_target_pairs={{4,6},{5,7},{12,14},{13,15},{20,22},{21,23},{28,30},{29,31}} | collective-permute-start | bytes 1572872 | tf_op jit(solution)/shard_map/ppermute | solution.py:288
  156.5 24.5 %collective-permute-start.25 = (bf16[16,128,128]{2,1,0:T(8,128)(2,1)}, bf16[16,128,128]{2,1,0:T(8,128)(2,1)S(1)}, u32[]{:S(2)}, u32[]{:S(2)}) collective-permute-start(bf16[16,128,128]{2,1,0:T(8,128)(2,1)} %collective-permute-done.24.refs_5_), channel_id=1, source_target_pairs={{3,1},{2,0},{11,9},{10,8},{19,17},{18,16},{27,25},{26,24}} | collective-permute-start | bytes 1572872 | tf_op jit(solution)/shard_map/ppermute | solution.py:289
  157.8 30.1 %collective-permute-start.5 = (bf16[16,128,128]{2,1,0:T(8,128)(2,1)S(1)}, bf16[16,128,128]{2,1,0:T(8,128)(2,1)S(1)}, u32[]{:S(2)}, u32[]{:S(2)}) collective-permute-start(bf16[16,128,128]{2,1,0:T(8,128)(2,1)S(1)} %get-tuple-element.57.refs_3_), channel_id=1, source_target_pairs={{0,2},{1,3},{2,4},{3,5},{4,6},{5,7},{8,10},{9,11},{10,12},{11,13},... | collective-permute-start | bytes 1572872 | tf_op jit(solution)/shard_map/ppermute | solution.py:288
  169.8 19.8 %collective-permute-start.35 = (bf16[16,128,128]{2,1,0:T(8,128)(2,1)S(1)}, bf16[16,128,128]{2,1,0:T(8,128)(2,1)S(1)}, u32[]{:S(2)}, u32[]{:S(2)}) collective-permute-start(bf16[16,128,128]{2,1,0:T(8,128)(2,1)S(1)} %collective-permute-done.34.refs_4_), channel_id=1, source_target_pairs={{5,3},{4,2},{3,1},{2,0},{13,11},{12,10},{11,9},{10,8},{21,19},{20,... | collective-permute-start | bytes 1572872 | tf_op jit(solution)/shard_map/ppermute | solution.py:289
  186.0 9.2 %collective-permute-start.27 = (bf16[16,64,128]{2,1,0:T(8,128)(2,1)S(1)}, bf16[16,64,128]{2,1,0:T(8,128)(2,1)S(1)}, u32[]{:S(2)}, u32[]{:S(2)}) collective-permute-start(bf16[16,64,128]{2,1,0:T(8,128)(2,1)S(1)} %get-tuple-element.74), channel_id=1, source_target_pairs={{0,8},{1,9},{2,10},{3,11},{4,12},{5,13},{6,14},{7,15},{8,0},{9,1},... | collective-permute-start | bytes 786440 | tf_op jit(solution)/shard_map/ppermute | solution.py:309
  186.1 13.8 %collective-permute-start.28 = (bf16[16,64,128]{2,1,0:T(8,128)(2,1)S(1)}, bf16[16,64,128]{2,1,0:T(8,128)(2,1)S(1)}, u32[]{:S(2)}, u32[]{:S(2)}) collective-permute-start(bf16[16,64,128]{2,1,0:T(8,128)(2,1)S(1)} %get-tuple-element.75), channel_id=1, source_target_pairs={{0,9},{1,8},{2,11},{3,10},{4,13},{5,12},{6,15},{7,14},{8,1},{9,0},... | collective-permute-start | bytes 786440 | tf_op jit(solution)/shard_map/ppermute | solution.py:309
  187.9 25.8 %collective-permute-start.8 = (bf16[16,128,128]{2,1,0:T(8,128)(2,1)S(1)}, bf16[16,128,128]{2,1,0:T(8,128)(2,1)S(1)}, u32[]{:S(2)}, u32[]{:S(2)}) collective-permute-start(bf16[16,128,128]{2,1,0:T(8,128)(2,1)S(1)} %collective-permute-done.5.refs_2_), channel_id=1, source_target_pairs={{2,4},{3,5},{4,6},{5,7},{10,12},{11,13},{12,14},{13,15},{18,20},{1... | collective-permute-start | bytes 1572872 | tf_op jit(solution)/shard_map/ppermute | solution.py:288
  189.6 19.7 %collective-permute-start.29 = (bf16[16,64,128]{2,1,0:T(8,128)(2,1)S(1)}, bf16[16,64,128]{2,1,0:T(8,128)(2,1)S(1)}, u32[]{:S(2)}, u32[]{:S(2)}) collective-permute-start(bf16[16,64,128]{2,1,0:T(8,128)(2,1)S(1)} %get-tuple-element.76), channel_id=1, source_target_pairs={{0,16},{1,17},{2,18},{3,19},{4,20},{5,21},{6,22},{7,23},{8,24},{9,... | collective-permute-start | bytes 786440 | tf_op jit(solution)/shard_map/ppermute | solution.py:309
  190.7 22.9 %collective-permute-start.30 = (bf16[16,64,128]{2,1,0:T(8,128)(2,1)S(1)}, bf16[16,64,128]{2,1,0:T(8,128)(2,1)S(1)}, u32[]{:S(2)}, u32[]{:S(2)}) collective-permute-start(bf16[16,64,128]{2,1,0:T(8,128)(2,1)S(1)} %get-tuple-element.77), channel_id=1, source_target_pairs={{0,17},{1,16},{2,19},{3,18},{4,21},{5,20},{6,23},{7,22},{8,25},{9,... | collective-permute-start | bytes 786440 | tf_op jit(solution)/shard_map/ppermute | solution.py:309
  195.2 18.4 %collective-permute-start.31 = (bf16[16,64,128]{2,1,0:T(8,128)(2,1)S(1)}, bf16[16,64,128]{2,1,0:T(8,128)(2,1)S(1)}, u32[]{:S(2)}, u32[]{:S(2)}) collective-permute-start(bf16[16,64,128]{2,1,0:T(8,128)(2,1)S(1)} %get-tuple-element.78), channel_id=1, source_target_pairs={{0,24},{1,25},{2,26},{3,27},{4,28},{5,29},{6,30},{7,31},{8,16},{9,... | collective-permute-start | bytes 786440 | tf_op jit(solution)/shard_map/ppermute | solution.py:309
  199.9 13.7 %collective-permute-start.32 = (bf16[16,64,128]{2,1,0:T(8,128)(2,1)S(1)}, bf16[16,64,128]{2,1,0:T(8,128)(2,1)S(1)}, u32[]{:S(2)}, u32[]{:S(2)}) collective-permute-start(bf16[16,64,128]{2,1,0:T(8,128)(2,1)S(1)} %get-tuple-element.79), channel_id=1, source_target_pairs={{0,25},{1,24},{2,27},{3,26},{4,29},{5,28},{6,31},{7,30},{8,17},{9,... | collective-permute-start | bytes 786440 | tf_op jit(solution)/shard_map/ppermute | solution.py:309
  209.3 16.7 %collective-permute-start.45 = (bf16[16,128,128]{2,1,0:T(8,128)(2,1)S(1)}, bf16[16,128,128]{2,1,0:T(8,128)(2,1)S(1)}, u32[]{:S(2)}, u32[]{:S(2)}) collective-permute-start(bf16[16,128,128]{2,1,0:T(8,128)(2,1)S(1)} %get-tuple-element.61.refs_3_), channel_id=1, source_target_pairs={{7,5},{6,4},{5,3},{4,2},{3,1},{2,0},{15,13},{14,12},{13,11},{12,10... | collective-permute-start | bytes 1572872 | tf_op jit(solution)/shard_map/ppermute | solution.py:289
  213.7 13.7 %collective-permute-start.33 = (bf16[16,128,128]{2,1,0:T(8,128)(2,1)S(1)}, bf16[16,128,128]{2,1,0:T(8,128)(2,1)S(1)}, u32[]{:S(2)}, u32[]{:S(2)}) collective-permute-start(bf16[16,128,128]{2,1,0:T(8,128)(2,1)S(1)} %collective-permute-done.8.refs_1_), channel_id=1, source_target_pairs={{4,6},{5,7},{12,14},{13,15},{20,22},{21,23},{28,30},{29,31}} | collective-permute-start | bytes 1572872 | tf_op jit(solution)/shard_map/ppermute | solution.py:288
  214.4 22.9 %collective-permute-start.36 = (bf16[16,128,128]{2,1,0:T(8,128)(2,1)S(1)}, bf16[16,128,128]{2,1,0:T(8,128)(2,1)S(1)}, u32[]{:S(2)}, u32[]{:S(2)}) collective-permute-start(bf16[16,128,128]{2,1,0:T(8,128)(2,1)S(1)} %collective-permute-done.35.refs_5_), channel_id=1, source_target_pairs={{3,1},{2,0},{11,9},{10,8},{19,17},{18,16},{27,25},{26,24}} | collective-permute-start | bytes 1572872 | tf_op jit(solution)/shard_map/ppermute | solution.py:289
  215.7 28.8 %collective-permute-start.6 = (bf16[16,128,128]{2,1,0:T(8,128)(2,1)S(1)}, bf16[16,128,128]{2,1,0:T(8,128)(2,1)S(1)}, u32[]{:S(2)}, u32[]{:S(2)}) collective-permute-start(bf16[16,128,128]{2,1,0:T(8,128)(2,1)S(1)} %get-tuple-element.61.refs_3_), channel_id=1, source_target_pairs={{0,2},{1,3},{2,4},{3,5},{4,6},{5,7},{8,10},{9,11},{10,12},{11,13},... | collective-permute-start | bytes 1572872 | tf_op jit(solution)/shard_map/ppermute | solution.py:288
  226.1 21.1 %collective-permute-start.46 = (bf16[16,128,128]{2,1,0:T(8,128)(2,1)S(1)}, bf16[16,128,128]{2,1,0:T(8,128)(2,1)S(1)}, u32[]{:S(2)}, u32[]{:S(2)}) collective-permute-start(bf16[16,128,128]{2,1,0:T(8,128)(2,1)S(1)} %collective-permute-done.45.refs_4_), channel_id=1, source_target_pairs={{5,3},{4,2},{3,1},{2,0},{13,11},{12,10},{11,9},{10,8},{21,19},{20,... | collective-permute-start | bytes 1572872 | tf_op jit(solution)/shard_map/ppermute | solution.py:289
  244.3 12.2 %collective-permute-start.39 = (bf16[16,64,128]{2,1,0:T(8,128)(2,1)S(1)}, bf16[16,64,128]{2,1,0:T(8,128)(2,1)S(1)}, u32[]{:S(2)}, u32[]{:S(2)}) collective-permute-start(bf16[16,64,128]{2,1,0:T(8,128)(2,1)S(1)} %get-tuple-element.85), channel_id=1, source_target_pairs={{0,9},{1,8},{2,11},{3,10},{4,13},{5,12},{6,15},{7,14},{8,1},{9,0},... | collective-permute-start | bytes 786440 | tf_op jit(solution)/shard_map/ppermute | solution.py:309
  244.4 26.4 %collective-permute-start.7 = (bf16[16,128,128]{2,1,0:T(8,128)(2,1)S(1)}, bf16[16,128,128]{2,1,0:T(8,128)(2,1)S(1)}, u32[]{:S(2)}, u32[]{:S(2)}) collective-permute-start(bf16[16,128,128]{2,1,0:T(8,128)(2,1)S(1)} %collective-permute-done.6.refs_2_), channel_id=1, source_target_pairs={{2,4},{3,5},{4,6},{5,7},{10,12},{11,13},{12,14},{13,15},{18,20},{1... | collective-permute-start | bytes 1572872 | tf_op jit(solution)/shard_map/ppermute | solution.py:288
  247.2 20.5 %collective-permute-start.40 = (bf16[16,64,128]{2,1,0:T(8,128)(2,1)S(1)}, bf16[16,64,128]{2,1,0:T(8,128)(2,1)S(1)}, u32[]{:S(2)}, u32[]{:S(2)}) collective-permute-start(bf16[16,64,128]{2,1,0:T(8,128)(2,1)S(1)} %get-tuple-element.86), channel_id=1, source_target_pairs={{0,16},{1,17},{2,18},{3,19},{4,20},{5,21},{6,22},{7,23},{8,24},{9,... | collective-permute-start | bytes 786440 | tf_op jit(solution)/shard_map/ppermute | solution.py:309
  248.2 22.6 %collective-permute-start.41 = (bf16[16,64,128]{2,1,0:T(8,128)(2,1)S(1)}, bf16[16,64,128]{2,1,0:T(8,128)(2,1)S(1)}, u32[]{:S(2)}, u32[]{:S(2)}) collective-permute-start(bf16[16,64,128]{2,1,0:T(8,128)(2,1)S(1)} %get-tuple-element.87), channel_id=1, source_target_pairs={{0,17},{1,16},{2,19},{3,18},{4,21},{5,20},{6,23},{7,22},{8,25},{9,... | collective-permute-start | bytes 786440 | tf_op jit(solution)/shard_map/ppermute | solution.py:309
  251.7 19.1 %collective-permute-start.42 = (bf16[16,64,128]{2,1,0:T(8,128)(2,1)S(1)}, bf16[16,64,128]{2,1,0:T(8,128)(2,1)S(1)}, u32[]{:S(2)}, u32[]{:S(2)}) collective-permute-start(bf16[16,64,128]{2,1,0:T(8,128)(2,1)S(1)} %get-tuple-element.88), channel_id=1, source_target_pairs={{0,24},{1,25},{2,26},{3,27},{4,28},{5,29},{6,30},{7,31},{8,16},{9,... | collective-permute-start | bytes 786440 | tf_op jit(solution)/shard_map/ppermute | solution.py:309
  256.6 14.2 %collective-permute-start.43 = (bf16[16,64,128]{2,1,0:T(8,128)(2,1)S(1)}, bf16[16,64,128]{2,1,0:T(8,128)(2,1)S(1)}, u32[]{:S(2)}, u32[]{:S(2)}) collective-permute-start(bf16[16,64,128]{2,1,0:T(8,128)(2,1)S(1)} %get-tuple-element.89), channel_id=1, source_target_pairs={{0,25},{1,24},{2,27},{3,26},{4,29},{5,28},{6,31},{7,30},{8,17},{9,... | collective-permute-start | bytes 786440 | tf_op jit(solution)/shard_map/ppermute | solution.py:309
  271.5 16.3 %collective-permute-start.47 = (bf16[16,128,128]{2,1,0:T(8,128)(2,1)S(1)}, bf16[16,128,128]{2,1,0:T(8,128)(2,1)S(1)}, u32[]{:S(2)}, u32[]{:S(2)}) collective-permute-start(bf16[16,128,128]{2,1,0:T(8,128)(2,1)S(1)} %collective-permute-done.46.refs_5_), channel_id=1, source_target_pairs={{3,1},{2,0},{11,9},{10,8},{19,17},{18,16},{27,25},{26,24}} | collective-permute-start | bytes 1572872 | tf_op jit(solution)/shard_map/ppermute | solution.py:289
  292.9 15.7 %collective-permute-start.50 = (bf16[16,64,128]{2,1,0:T(8,128)(2,1)S(1)}, bf16[16,64,128]{2,1,0:T(8,128)(2,1)S(1)}, u32[]{:S(2)}, u32[]{:S(2)}) collective-permute-start(bf16[16,64,128]{2,1,0:T(8,128)(2,1)S(1)} %get-tuple-element.95), channel_id=1, source_target_pairs={{0,9},{1,8},{2,11},{3,10},{4,13},{5,12},{6,15},{7,14},{8,1},{9,0},... | collective-permute-start | bytes 786440 | tf_op jit(solution)/shard_map/ppermute | solution.py:309
  294.7 14.0 %collective-permute-start.51 = (bf16[16,64,128]{2,1,0:T(8,128)(2,1)S(1)}, bf16[16,64,128]{2,1,0:T(8,128)(2,1)S(1)}, u32[]{:S(2)}, u32[]{:S(2)}) collective-permute-start(bf16[16,64,128]{2,1,0:T(8,128)(2,1)S(1)} %get-tuple-element.96), channel_id=1, source_target_pairs={{0,16},{1,17},{2,18},{3,19},{4,20},{5,21},{6,22},{7,23},{8,24},{9,... | collective-permute-start | bytes 786440 | tf_op jit(solution)/shard_map/ppermute | solution.py:309
  296.4 22.9 %collective-permute-start.52 = (bf16[16,64,128]{2,1,0:T(8,128)(2,1)S(1)}, bf16[16,64,128]{2,1,0:T(8,128)(2,1)S(1)}, u32[]{:S(2)}, u32[]{:S(2)}) collective-permute-start(bf16[16,64,128]{2,1,0:T(8,128)(2,1)S(1)} %get-tuple-element.97), channel_id=1, source_target_pairs={{0,17},{1,16},{2,19},{3,18},{4,21},{5,20},{6,23},{7,22},{8,25},{9,... | collective-permute-start | bytes 786440 | tf_op jit(solution)/shard_map/ppermute | solution.py:309
  296.4 22.9 %collective-permute-start.53 = (bf16[16,64,128]{2,1,0:T(8,128)(2,1)S(1)}, bf16[16,64,128]{2,1,0:T(8,128)(2,1)S(1)}, u32[]{:S(2)}, u32[]{:S(2)}) collective-permute-start(bf16[16,64,128]{2,1,0:T(8,128)(2,1)S(1)} %get-tuple-element.98), channel_id=1, source_target_pairs={{0,24},{1,25},{2,26},{3,27},{4,28},{5,29},{6,30},{7,31},{8,16},{9,... | collective-permute-start | bytes 786440 | tf_op jit(solution)/shard_map/ppermute | solution.py:309
  302.0 17.4 %collective-permute-start.54 = (bf16[16,64,128]{2,1,0:T(8,128)(2,1)S(1)}, bf16[16,64,128]{2,1,0:T(8,128)(2,1)S(1)}, u32[]{:S(2)}, u32[]{:S(2)}) collective-permute-start(bf16[16,64,128]{2,1,0:T(8,128)(2,1)S(1)} %get-tuple-element.99), channel_id=1, source_target_pairs={{0,25},{1,24},{2,27},{3,26},{4,29},{5,28},{6,31},{7,30},{8,17},{9,... | collective-permute-start | bytes 786440 | tf_op jit(solution)/shard_map/ppermute | solution.py:309
  (23 other events, 523.7 us)
Sparse Core Ops, SparseCore 0:
  9.6 49.8 all-gather.1

commit v3 on v2

--- a/solution.py
+++ b/solution.py
@@ -127,14 +127,14 @@
 
 def project_kernel(line, parts, where_ref, weight_ref, offset_ref, gate_ref, *refs):
     tiles = refs[: 2 * line - 1]
-    outs = refs[2 * line - 1 : 2 * line - 1 + CORES * parts]
+    outs = refs[2 * line - 1 : 2 * line - 1 + parts]
     held, sems = refs[-2:]
-    mine, place = where_ref[0], where_ref[1]
+    mine, place, core = where_ref[0], where_ref[1], where_ref[2]
     group = weight_ref.shape[0] // CORES
     lanes = held.shape[-1]
 
     def fetch(d):
-        distance = (mine ^ d) - place
+        distance = ((mine ^ d) - place) * (1 - 2 * core)
         for index in range(2 * line - 1):
             @pl.when(distance == index - (line - 1))
             def _():
@@ -152,9 +152,7 @@
             result = jnp.where(gate_ref[...] > 0.0, gated, raw).astype(jnp.bfloat16)
             for e in range(CORES):
                 for jj in range(2):
-                    outs[d * CORES + e][j + jj] = result[
-                        e * group : (e + 1) * group, jj * lanes : (jj + 1) * lanes
-                    ]
+                    outs[d][e, j + jj] = result[e * group : (e + 1) * group, jj * lanes : (jj + 1) * lanes]
 
 
 def project_call(where, weight, offset, gate, tiles, parts):
@@ -163,12 +161,12 @@
     group = weight.shape[0] // CORES
     whole = pl.BlockSpec(memory_space=pltpu.VMEM)
     far = pl.BlockSpec(memory_space=pl.ANY)
-    shape = jax.ShapeDtypeStruct((STEP, group, lanes), jnp.bfloat16)
+    shape = jax.ShapeDtypeStruct((CORES, STEP, group, lanes), jnp.bfloat16)
     return pl.pallas_call(
         functools.partial(project_kernel, line, parts),
         in_specs=[pl.BlockSpec(memory_space=pltpu.SMEM), whole, whole, whole, *[far] * len(tiles)],
-        out_specs=[whole] * (CORES * parts),
-        out_shape=[shape] * (CORES * parts),
+        out_specs=[whole] * parts,
+        out_shape=[shape] * parts,
         scratch_shapes=[
             pltpu.VMEM((2, STEP, channels, lanes), jnp.bfloat16),
             pltpu.SemaphoreType.DMA((2,)),
@@ -184,25 +182,23 @@
 
 
 def place_kernel(parts, part, tile_cols, where_ref, *refs):
-    pieces = refs[: CORES * parts]
-    out_ref, rows, sems = refs[-3:]
+    pieces = refs[:parts]
+    out_ref, other_ref, rows, sem = refs[-4:]
     mine, core = where_ref[0], where_ref[2]
-    step, group, lanes = pieces[0].shape
-    copies = []
-    for e in range(CORES):
+    step, group, lanes = pieces[0].shape[1:]
+    for e, target in enumerate((rows, other_ref)):
         for d in range(parts):
             column = pl.multiple_of((mine ^ d) * lanes, lanes)
-            rows[e, :, :, pl.ds(column, lanes)] = pieces[d * CORES + e][...]
-        row = pl.multiple_of((core ^ e) * tile_cols + part * STEP, STEP)
-        copy = pltpu.make_async_copy(rows.at[e], out_ref.at[pl.ds(row, step)], sems.at[e])
-        copy.start()
-        copies.append(copy)
-    for copy in copies:
-        copy.wait()
+            target[:, :, pl.ds(column, lanes)] = pieces[d][e]
+        if e == 0:
+            row = pl.multiple_of(core * tile_cols + part * step, step)
+            copy = pltpu.make_async_copy(rows, out_ref.at[pl.ds(row, step)], sem)
+            copy.start()
+    copy.wait()
 
 
 def place_call(where, pieces, earlier, part, parts, tile_cols):
-    step, group, lanes = pieces[0].shape
+    step, group, lanes = pieces[0].shape[1:]
     far = pl.BlockSpec(memory_space=pl.ANY)
     whole = pl.BlockSpec(memory_space=pltpu.VMEM)
     args = [where, *pieces]
@@ -212,20 +208,44 @@
         aliases = {len(args): 0}
         args.append(earlier)
         specs.append(far)
+    block = (step, group, parts * lanes)
     return pl.pallas_call(
         functools.partial(place_kernel, parts, part, tile_cols),
         in_specs=specs,
-        out_specs=far,
-        out_shape=jax.ShapeDtypeStruct((CORES * tile_cols, group, parts * lanes), jnp.bfloat16),
-        scratch_shapes=[
-            pltpu.VMEM((CORES, step, group, parts * lanes), jnp.bfloat16),
-            pltpu.SemaphoreType.DMA((CORES,)),
-        ],
+        out_specs=(far, whole),
+        out_shape=(
+            jax.ShapeDtypeStruct((CORES * tile_cols, *block[1:]), jnp.bfloat16),
+            jax.ShapeDtypeStruct(block, jnp.bfloat16),
+        ),
+        scratch_shapes=[pltpu.VMEM(block, jnp.bfloat16), pltpu.SemaphoreType.DMA],
         input_output_aliases=aliases,
         compiler_params=pltpu.CompilerParams(vmem_limit_bytes=VMEM_LIMIT),
-        cost_estimate=pl.CostEstimate(flops=0, bytes_accessed=8 * 2**20, transcendentals=0),
+        cost_estimate=pl.CostEstimate(flops=0, bytes_accessed=6 * 2**20, transcendentals=0),
         name="place",
     )(*args)
+
+
+def put_kernel(part, tile_cols, where_ref, rows_ref, earlier_ref, out_ref, sem):
+    del earlier_ref
+    row = pl.multiple_of((1 - where_ref[2]) * tile_cols + part * rows_ref.shape[0], rows_ref.shape[0])
+    copy = pltpu.make_async_copy(rows_ref, out_ref.at[pl.ds(row, rows_ref.shape[0])], sem)
+    copy.start()
+    copy.wait()
+
+
+def put_call(where, rows, earlier, part, tile_cols):
+    far = pl.BlockSpec(memory_space=pl.ANY)
+    return pl.pallas_call(
+        functools.partial(put_kernel, part, tile_cols),
+        in_specs=[pl.BlockSpec(memory_space=pltpu.SMEM), pl.BlockSpec(memory_space=pltpu.VMEM), far],
+        out_specs=far,
+        out_shape=jax.ShapeDtypeStruct(earlier.shape, earlier.dtype),
+        scratch_shapes=[pltpu.SemaphoreType.DMA],
+        input_output_aliases={2: 0},
+        compiler_params=pltpu.CompilerParams(vmem_limit_bytes=VMEM_LIMIT),
+        cost_estimate=pl.CostEstimate(flops=0, bytes_accessed=2 * 2**20, transcendentals=0),
+        name="put",
+    )(where, rows, earlier)
 
 
 def shards(
@@ -281,47 +301,77 @@
             after(where, *others), left, rights, pair_features, weight, bias, gain, state["new_pair"], part
         )
 
+    ring = [z * CORES for z in range(line)] + [z * CORES + 1 for z in reversed(range(line))]
+    onward = [(ring[t], ring[(t + 1) % cols]) for t in range(cols)]
+    back = [(b, a) for a, b in onward]
+
     def shift(part, s, *others):
-        up = [(z * CORES + k, (z + 1) * CORES + k) for z in range(s - 1, line - 1) for k in range(CORES)]
-        down = [(cols - 1 - a, cols - 1 - b) for a, b in up]
         here = tiles[part]
-        here[-s] = lax.ppermute(after(here[-(s - 1)], *others), "col", up)
-        here[s] = lax.ppermute(after(here[s - 1], *others), "col", down)
-
-    def send(part, *others):
+        here[-s] = lax.ppermute(after(here[-(s - 1)], *others), "col", onward)
+        here[s] = lax.ppermute(after(here[s - 1], *others), "col", back)
+
+    def project(part, *others):
         here = tiles[part]
-        pieces = project_call(
-            after(where, *others),
-            my_weight,
-            my_offsets,
-            my_gates,
-            [here[o] for o in range(-(line - 1), line)],
-            parts,
-        )
-        moved[part] = []
-        for d in range(parts):
-            for e in range(CORES):
-                piece = pieces[d * CORES + e]
-                if d or e:
-                    pairs = [
-                        (a * cols + c, (a ^ d) * cols + (c ^ e)) for a in range(parts) for c in range(cols)
-                    ]
-                    piece = lax.ppermute(piece, ("row", "col"), pairs)
-                moved[part].append(piece)
+        moved[part] = list(
+            project_call(
+                after(where, *others),
+                my_weight,
+                my_offsets,
+                my_gates,
+                [here[o] for o in range(-(line - 1), line)],
+                parts,
+            )
+        )
+
+    def send(part, d):
+        moved[part][d] = lax.ppermute(moved[part][d], "row", [(a, a ^ d) for a in range(parts)])
 
     def place(part):
-        state["result"] = place_call(where, moved[part], state["result"], part, parts, tile_cols)
-
+        state["result"], other = place_call(where, moved[part], state["result"], part, parts, tile_cols)
+        swapped[part] = lax.ppermute(other, "col", [(c, c ^ 1) for c in range(cols)])
+
+    def put(part):
+        state["result"] = put_call(where, swapped[part], state["result"], part, tile_cols)
+
+    order = sorted(
+        ((part, s) for part in range(count) for s in range(1, line)),
+        key=lambda step: (step[0] + step[1], step[0]),
+    )
+    swapped = [None] * count
+    done = []
+    pending = []
     update(0)
-    for part in range(count):
-        for s in range(1, line):
-            others = moved[part - 1] if part and s == line - 1 else []
-            shift(part, s, *others)
-            if s == 1 and part + 1 < count:
-                update(part + 1, tiles[part][-1])
-        send(part)
-    for part in range(count):
-        place(part)
+    updated = 1
+    for index, (part, s) in enumerate(order):
+        others = list(done[index - 2]) if index >= 2 else []
+        while updated <= part:
+            update(updated)
+            updated += 1
+        if pending and index >= pending[0][0]:
+            _, owner, d = pending.pop(0)
+            others.append(moved[owner][d])
+        if part == count - 1 and s == line - 1:
+            for owner in range(count - 3):
+                if swapped[owner] is not None:
+                    others.append(swapped[owner])
+        shift(part, s, *others)
+        done.append((tiles[part][-s], tiles[part][s]))
+        if updated < count and any(p == updated for p, _ in order[index + 2 : index + 4]):
+            update(updated, *done[index - 1 if index else 0])
+            updated += 1
+        if s == line - 1 and part < count - 1:
+            project(part)
+            for d in range(1, parts):
+                send(part, d)
+                pending.append((index + 2 + d, part, d))
+            place(part)
+    project(count - 1, *[w for w in swapped[:-2] if w is not None])
+    for d in range(1, parts):
+        send(count - 1, d)
+    for part in range(count - 1):
+        put(part)
+    place(count - 1)
+    put(count - 1)
     return (state["new_pair"], state["result"])
 
 

time: 329 us -> 280 us (0.85)
  starting transfers between devices: 75.4 us -> 41.1 us
  waiting for transfers between devices: 179 us -> 160 us
  Pallas kernels: 52.4 us -> 57.7 us
    ppermute x52 -> x40, starting transfers between devices: 70.7 us -> 36.5 us  [the longest x12 18 us: shift(): here[-s] = lax.ppermute(after(here[-(s - 1)], *others), 'col', onward)]
    ppermute x52 -> x40, waiting for transfers between devices: 134 us -> 115 us  [the longest x12 50.6 us: shift(): here[-s] = lax.ppermute(after(here[-(s - 1)], *others), 'col', onward)]
    pallas_call x0 -> x4, Pallas kernels: none -> 6.1 us  [put_call(): pl.pallas_call(functools.partial(put_kernel, part, tile_cols), in_specs=[...]
  transfers between devices with their start and end apart: 56 -> 44, of which waited for: 29 -> 25; matrix products, arithmetic and copies ran while one was open for 1% -> 1% of each run, Pallas kernels for 12% -> 17%
where the time goes in v3:
time: 280 us
  waiting for transfers between devices  160 us (57%)
  Pallas kernels  57.7 us (21%)
  starting transfers between devices  41.1 us (15%)
  between operations  14.4 us (5%)
  local copies, waits for them, and re-layouts  6.73 us (2%)
    ppermute x12, waiting for transfers between devices, shift(): here[-s] = lax.ppermute(after(here[-(s - 1)], *others), 'col', onward)  50.6 us
    ppermute x12, waiting for transfers between devices, send(): lax.ppermute(moved[part][d], 'row', [(a, a ^ d) for a in range(parts)])  44.8 us
    pallas_call x4, Pallas kernels, update_call(): pl.pallas_call(functools.partial(update_kernel, parts, part), grid=(1,),...  27.9 us
    all_gather x1, waiting for transfers between devices, shards(): left = lax.all_gather(alignment_left, 'col', axis=0, tiled=True)  23.7 us
    ppermute x3, waiting for transfers between devices, shards(): lax.ppermute(alignment_right, 'row', [(a, a ^ d) for a in range(parts)])  20.6 us
    ppermute x12, starting transfers between devices, shift(): here[-s] = lax.ppermute(after(here[-(s - 1)], *others), 'col', onward)  18 us
    ppermute x12, waiting for transfers between devices, shift(): here[s] = lax.ppermute(after(here[s - 1], *others), 'col', back)  16.5 us
    pallas_call x4, Pallas kernels, project_call(): pl.pallas_call(functools.partial(project_kernel, line, parts), in_specs=[...  16.3 us
  transfers between devices with their start and end apart: 44, of which 25 were waited for; matrix products, arithmetic and copies ran while one was open for 1% of the time, Pallas kernels for 17%

profile of v3, /device:TPU:0, one launch (start us, length us, event | category | flops | bytes accessed | tf_op | source)
XLA Modules:
  0.0 279.8 jit_solution(4093329793734292801)
XLA Ops:
  7.9 3.0 %collective-permute-start = (bf16[128,2048]{1,0:T(8,128)(2,1)}, bf16[128,2048]{1,0:T(8,128)(2,1)S(1)}, u32[]{:S(2)}, u32[]{:S(2)}) collective-permute-start(bf16[128,2048]{1,0:T(8,128)(2,1)} %refs_0_.7), channel_id=1, source_target_pairs={{0,8},{8,0},{16,24},{24,16},{1,9},{9,1},{17,25},{25,17},{2,10},{10... | collective-permute-start | bytes 1572872 | tf_op jit(solution)/shard_map/ppermute | solution.py:270
  15.1 8.7 %collective-permute-done.refs_1_ = bf16[128,2048]{1,0:T(8,128)(2,1)S(1)} collective-permute-done((bf16[128,2048]{1,0:T(8,128)(2,1)}, bf16[128,2048]{1,0:T(8,128)(2,1)S(1)}, u32[]{:S(2)}, u32[]{:S(2)}) %collective-permute-start) | collective-permute-done | bytes 524320 | tf_op jit(solution)/shard_map/ppermute | solution.py:270
  23.9 11.9 %collective-permute-done.1.refs_2_ = bf16[128,2048]{1,0:T(8,128)(2,1)S(1)} collective-permute-done((bf16[128,2048]{1,0:T(8,128)(2,1)}, bf16[128,2048]{1,0:T(8,128)(2,1)S(1)}, u32[]{:S(2)}, u32[]{:S(2)}) %collective-permute-start.1) | collective-permute-done | bytes 524320 | tf_op jit(solution)/shard_map/ppermute | solution.py:270
  35.7 23.7 %all-gather.2.cloned.1.call-done.left_ref = bf16[128,16384]{1,0:T(8,128)(2,1)} async-done(((bf16[16,16384]{1,0:T(8,128)(2,1)}), bf16[128,16384]{1,0:T(8,128)(2,1)}) %all-gather.2.cloned.1.call-update) | async-done | bytes 4194320 | tf_op jit(solution)/shard_map/all_gather | solution.py:271
  60.5 7.0 %update.4 = (bf16[128,64,128]{2,1,0:T(8,128)(2,1)}, bf16[16,128,128]{2,1,0:T(8,128)(2,1)S(1)}) custom-call(s32[3]{0:T(128)S(1)} %pad_add_fusion.where_ref, bf16[128,16384]{1,0:T(8,128)(2,1)} %all-gather.2.cloned.1.call-done.left_ref, bf16[128,2048]{1,0:T(8,128)(2,1)S(1)} %copy-done, bf16[128,2048]{1,0:T(8,128)(2,1)S(1)} %collective-permute-done.refs_1_, ...), custom_call_target="tpu_custom_call" | custom-call | flops 2684354560 | bytes 8388608 | tf_op jit(solution)/shard_map/update/pallas_call | solution.py:105
  68.0 10.8 %collective-permute-done.3.refs_2_ = bf16[16,128,128]{2,1,0:T(8,128)(2,1)} collective-permute-done((bf16[16,128,128]{2,1,0:T(8,128)(2,1)S(1)}, bf16[16,128,128]{2,1,0:T(8,128)(2,1)}, u32[]{:S(2)}, u32[]{:S(2)}) %collective-permute-start.3) | collective-permute-done | bytes 524320 | tf_op jit(solution)/shard_map/ppermute | solution.py:310
  78.8 2.6 collective-permute-start.9
  81.7 6.9 %update.5 = (bf16[128,64,128]{2,1,0:T(8,128)(2,1)}, bf16[16,128,128]{2,1,0:T(8,128)(2,1)S(1)}) custom-call(s32[3]{0:T(128)S(1)} %pad_add_fusion.where_ref, bf16[128,16384]{1,0:T(8,128)(2,1)} %all-gather.2.cloned.1.call-done.left_ref, bf16[128,2048]{1,0:T(8,128)(2,1)S(1)} %copy-done, ...), custom_call_target="tpu_custom_call", output_to_operand_aliasing={{0}: (10, {})} | custom-call | flops 2684354560 | bytes 8388608 | tf_op jit(solution)/shard_map/update/pallas_call | solution.py:105
  88.7 2.0 collective-permute-start.5
  91.0 2.7 collective-permute-done.9.refs_1_
  93.7 3.2 %collective-permute-done.10.refs_5_ = bf16[16,128,128]{2,1,0:T(8,128)(2,1)} collective-permute-done((bf16[16,128,128]{2,1,0:T(8,128)(2,1)}, bf16[16,128,128]{2,1,0:T(8,128)(2,1)}, u32[]{:S(2)}, u32[]{:S(2)}) %collective-permute-start.10) | collective-permute-done | bytes 524320 | tf_op jit(solution)/shard_map/ppermute | solution.py:311
  97.7 7.1 %collective-permute-done.5.refs_2_ = bf16[16,128,128]{2,1,0:T(8,128)(2,1)} collective-permute-done((bf16[16,128,128]{2,1,0:T(8,128)(2,1)S(1)}, bf16[16,128,128]{2,1,0:T(8,128)(2,1)}, u32[]{:S(2)}, u32[]{:S(2)}) %collective-permute-start.5) | collective-permute-done | bytes 524320 | tf_op jit(solution)/shard_map/ppermute | solution.py:310
  104.8 3.3 %collective-permute-done.6.refs_4_ = bf16[16,128,128]{2,1,0:T(8,128)(2,1)} collective-permute-done((bf16[16,128,128]{2,1,0:T(8,128)(2,1)S(1)}, bf16[16,128,128]{2,1,0:T(8,128)(2,1)}, u32[]{:S(2)}, u32[]{:S(2)}) %collective-permute-start.6) | collective-permute-done | bytes 524320 | tf_op jit(solution)/shard_map/ppermute | solution.py:311
  108.8 7.3 %collective-permute-done.11.refs_0_ = bf16[16,128,128]{2,1,0:T(8,128)(2,1)} collective-permute-done((bf16[16,128,128]{2,1,0:T(8,128)(2,1)}, bf16[16,128,128]{2,1,0:T(8,128)(2,1)}, u32[]{:S(2)}, u32[]{:S(2)}) %collective-permute-start.11) | collective-permute-done | bytes 524320 | tf_op jit(solution)/shard_map/ppermute | solution.py:310
  116.1 3.2 %collective-permute-done.12.refs_6_ = bf16[16,128,128]{2,1,0:T(8,128)(2,1)} collective-permute-done((bf16[16,128,128]{2,1,0:T(8,128)(2,1)}, bf16[16,128,128]{2,1,0:T(8,128)(2,1)}, u32[]{:S(2)}, u32[]{:S(2)}) %collective-permute-start.12) | collective-permute-done | bytes 524320 | tf_op jit(solution)/shard_map/ppermute | solution.py:311
  119.4 3.8 %project.4 = (bf16[2,16,64,128]{3,2,1,0:T(8,128)(2,1)S(1)}, bf16[2,16,64,128]{3,2,1,0:T(8,128)(2,1)S(1)}, bf16[2,16,64,128]{3,2,1,0:T(8,128)(2,1)S(1)}, bf16[2,16,64,128]{3,2,1,0:T(8,128)(2,1)S(1)}) custom-call(s32[3]{0:T(128)S(1)} %pad_add_fusion.where_ref, bf16[128,128]{1,0:T(8,128)(2,1)S(1)} %pad_maximum_fusion.weight_ref, f32[128,1]{1,0:T(8,128)S(1)} %copy.46.offset_ref, ...), custom_call_target="tpu_custom_call" | custom-call | flops 268435456 | bytes 4194304 | tf_op jit(solution)/shard_map/project/pallas_call | solution.py:165
  123.2 1.6 collective-permute-start.13
  126.2 7.1 %update.6 = (bf16[128,64,128]{2,1,0:T(8,128)(2,1)}, bf16[16,128,128]{2,1,0:T(8,128)(2,1)S(1)}) custom-call(s32[3]{0:T(128)S(1)} %pad_add_fusion.where_ref, bf16[128,16384]{1,0:T(8,128)(2,1)} %all-gather.2.cloned.1.call-done.left_ref, bf16[128,2048]{1,0:T(8,128)(2,1)S(1)} %copy-done.1, ...), custom_call_target="tpu_custom_call", output_to_operand_aliasing={{0}: (10, {})} | custom-call | flops 2684354560 | bytes 8388608 | tf_op jit(solution)/shard_map/update/pallas_call | solution.py:105
  134.7 2.5 collective-permute-start.17
  137.2 2.3 collective-permute-start.15
  139.5 6.1 %collective-permute-done.26.refs_2_ = bf16[16,128,128]{2,1,0:T(8,128)(2,1)S(1)} collective-permute-done((bf16[16,128,128]{2,1,0:T(8,128)(2,1)S(1)}, bf16[16,128,128]{2,1,0:T(8,128)(2,1)S(1)}, u32[]{:S(2)}, u32[]{:S(2)}) %collective-permute-start.26) | collective-permute-done | bytes 524320 | tf_op jit(solution)/shard_map/ppermute | solution.py:310
  145.6 2.7 collective-permute-done.27.refs_4_
  148.3 1.9 collective-permute-start.28
  150.3 6.7 %collective-permute-done.17.refs_0_ = bf16[16,128,128]{2,1,0:T(8,128)(2,1)S(1)} collective-permute-done((bf16[16,128,128]{2,1,0:T(8,128)(2,1)}, bf16[16,128,128]{2,1,0:T(8,128)(2,1)S(1)}, u32[]{:S(2)}, u32[]{:S(2)}) %collective-permute-start.17) | collective-permute-done | bytes 524320 | tf_op jit(solution)/shard_map/ppermute | solution.py:310
  157.0 2.5 collective-permute-done.18.refs_6_
  160.3 4.1 %project.5 = (bf16[2,16,64,128]{3,2,1,0:T(8,128)(2,1)S(1)}, bf16[2,16,64,128]{3,2,1,0:T(8,128)(2,1)S(1)}, bf16[2,16,64,128]{3,2,1,0:T(8,128)(2,1)S(1)}, bf16[2,16,64,128]{3,2,1,0:T(8,128)(2,1)S(1)}) custom-call(s32[3]{0:T(128)S(1)} %pad_add_fusion.where_ref, bf16[128,128]{1,0:T(8,128)(2,1)S(1)} %pad_maximum_fusion.weight_ref, f32[128,1]{1,0:T(8,128)S(1)} %copy.46.offset_ref, ...), custom_call_target="tpu_custom_call" | custom-call | flops 268435456 | bytes 4194304 | tf_op jit(solution)/shard_map/project/pallas_call | solution.py:165
  165.0 6.9 %update.7 = (bf16[128,64,128]{2,1,0:T(8,128)(2,1)}, bf16[16,128,128]{2,1,0:T(8,128)(2,1)S(1)}) custom-call(s32[3]{0:T(128)S(1)} %pad_add_fusion.where_ref, bf16[128,16384]{1,0:T(8,128)(2,1)} %all-gather.2.cloned.1.call-done.left_ref, bf16[128,2048]{1,0:T(8,128)(2,1)S(1)} %copy-done.1, ...), custom_call_target="tpu_custom_call", output_to_operand_aliasing={{0}: (10, {})} | custom-call | flops 2684354560 | bytes 8388608 | tf_op jit(solution)/shard_map/update/pallas_call | solution.py:105
  172.6 1.9 collective-permute-start.23
  174.5 1.8 place.4
  176.5 2.4 collective-permute-start.21
  179.0 15.0 %collective-permute-done.20.refs_2_ = bf16[2,16,64,128]{3,2,1,0:T(8,128)(2,1)S(1)} collective-permute-done((bf16[2,16,64,128]{3,2,1,0:T(8,128)(2,1)S(1)}, bf16[2,16,64,128]{3,2,1,0:T(8,128)(2,1)S(1)}, u32[]{:S(2)}, u32[]{:S(2)}) %collective-permute-start.20) | collective-permute-done | bytes 524320 | tf_op jit(solution)/shard_map/ppermute | solution.py:327
  194.0 2.5 collective-permute-start.30
  196.5 2.0 collective-permute-start.25
  198.5 1.8 place.5
  200.4 8.4 %collective-permute-done.30.refs_0_ = bf16[16,128,128]{2,1,0:T(8,128)(2,1)S(1)} collective-permute-done((bf16[16,128,128]{2,1,0:T(8,128)(2,1)S(1)}, bf16[16,128,128]{2,1,0:T(8,128)(2,1)S(1)}, u32[]{:S(2)}, u32[]{:S(2)}) %collective-permute-start.30) | collective-permute-done | bytes 524320 | tf_op jit(solution)/shard_map/ppermute | solution.py:310
  209.7 4.3 %project.7 = (bf16[2,16,64,128]{3,2,1,0:T(8,128)(2,1)S(1)}, bf16[2,16,64,128]{3,2,1,0:T(8,128)(2,1)S(1)}, bf16[2,16,64,128]{3,2,1,0:T(8,128)(2,1)S(1)}, bf16[2,16,64,128]{3,2,1,0:T(8,128)(2,1)S(1)}) custom-call(s32[3]{0:T(128)S(1)} %pad_add_fusion.where_ref, bf16[128,128]{1,0:T(8,128)(2,1)S(1)} %pad_maximum_fusion.weight_ref, f32[128,1]{1,0:T(8,128)S(1)} %copy.46.offset_ref, ...), custom_call_target="tpu_custom_call" | custom-call | flops 268435456 | bytes 4194304 | tf_op jit(solution)/shard_map/project/pallas_call | solution.py:165
  214.0 1.5 collective-permute-start.38
  219.1 2.5 collective-permute-start.32
  221.6 6.6 %collective-permute-done.38.refs_1_ = bf16[2,16,64,128]{3,2,1,0:T(8,128)(2,1)S(1)} collective-permute-done((bf16[2,16,64,128]{3,2,1,0:T(8,128)(2,1)S(1)}, bf16[2,16,64,128]{3,2,1,0:T(8,128)(2,1)S(1)}, u32[]{:S(2)}, u32[]{:S(2)}) %collective-permute-start.38) | collective-permute-done | bytes 524320 | tf_op jit(solution)/shard_map/ppermute | solution.py:327
  228.2 6.2 %collective-permute-done.39.refs_2_ = bf16[2,16,64,128]{3,2,1,0:T(8,128)(2,1)S(1)} collective-permute-done((bf16[2,16,64,128]{3,2,1,0:T(8,128)(2,1)S(1)}, bf16[2,16,64,128]{3,2,1,0:T(8,128)(2,1)S(1)}, u32[]{:S(2)}, u32[]{:S(2)}) %collective-permute-start.39) | collective-permute-done | bytes 524320 | tf_op jit(solution)/shard_map/ppermute | solution.py:327
  234.4 1.8 place.6
  238.5 4.1 %project.6 = (bf16[2,16,64,128]{3,2,1,0:T(8,128)(2,1)S(1)}, bf16[2,16,64,128]{3,2,1,0:T(8,128)(2,1)S(1)}, bf16[2,16,64,128]{3,2,1,0:T(8,128)(2,1)S(1)}, bf16[2,16,64,128]{3,2,1,0:T(8,128)(2,1)S(1)}) custom-call(s32[3]{0:T(128)S(1)} %pad_add_fusion.where_ref, bf16[128,128]{1,0:T(8,128)(2,1)S(1)} %pad_maximum_fusion.weight_ref, f32[128,1]{1,0:T(8,128)S(1)} %copy.46.offset_ref, ...), custom_call_target="tpu_custom_call" | custom-call | flops 268435456 | bytes 4194304 | tf_op jit(solution)/shard_map/project/pallas_call | solution.py:165
  244.4 1.8 collective-permute-start.37
  247.7 1.5 put.5.earlier_ref
  250.8 6.8 %collective-permute-done.35.refs_1_ = bf16[2,16,64,128]{3,2,1,0:T(8,128)(2,1)S(1)} collective-permute-done((bf16[2,16,64,128]{3,2,1,0:T(8,128)(2,1)S(1)}, bf16[2,16,64,128]{3,2,1,0:T(8,128)(2,1)S(1)}, u32[]{:S(2)}, u32[]{:S(2)}) %collective-permute-start.35) | collective-permute-done | bytes 524320 | tf_op jit(solution)/shard_map/ppermute | solution.py:327
  257.6 9.2 %collective-permute-done.36.refs_2_ = bf16[2,16,64,128]{3,2,1,0:T(8,128)(2,1)S(1)} collective-permute-done((bf16[2,16,64,128]{3,2,1,0:T(8,128)(2,1)S(1)}, bf16[2,16,64,128]{3,2,1,0:T(8,128)(2,1)S(1)}, u32[]{:S(2)}, u32[]{:S(2)}) %collective-permute-start.36) | collective-permute-done | bytes 524320 | tf_op jit(solution)/shard_map/ppermute | solution.py:327
  266.8 1.8 place.7
  268.7 2.6 collective-permute-done.42.rows_ref
  (99 shorter events, 26.7 us)
Async XLA Ops:
  7.2 52.3 %all-gather.2.cloned.1.call-start = ((), (), s32[]{:S(2)}) async-start(), calls=%async_computation | async-start | bytes 4718592 | tf_op jit(solution)/shard_map/all_gather | solution.py:271
  7.9 16.0 %collective-permute-start = (bf16[128,2048]{1,0:T(8,128)(2,1)}, bf16[128,2048]{1,0:T(8,128)(2,1)S(1)}, u32[]{:S(2)}, u32[]{:S(2)}) collective-permute-start(bf16[128,2048]{1,0:T(8,128)(2,1)} %refs_0_.7), channel_id=1, source_target_pairs={{0,8},{8,0},{16,24},{24,16},{1,9},{9,1},{17,25},{25,17},{2,10},{10... | collective-permute-start | bytes 1572872 | tf_op jit(solution)/shard_map/ppermute | solution.py:270
  10.9 24.8 %collective-permute-start.1 = (bf16[128,2048]{1,0:T(8,128)(2,1)}, bf16[128,2048]{1,0:T(8,128)(2,1)S(1)}, u32[]{:S(2)}, u32[]{:S(2)}) collective-permute-start(bf16[128,2048]{1,0:T(8,128)(2,1)} %refs_0_.7), channel_id=1, source_target_pairs={{0,16},{8,24},{16,0},{24,8},{1,17},{9,25},{17,1},{25,9},{2,18},{10... | collective-permute-start | bytes 1572872 | tf_op jit(solution)/shard_map/ppermute | solution.py:270
  12.4 23.3 %collective-permute-start.2 = (bf16[128,2048]{1,0:T(8,128)(2,1)}, bf16[128,2048]{1,0:T(8,128)(2,1)S(1)}, u32[]{:S(2)}, u32[]{:S(2)}) collective-permute-start(bf16[128,2048]{1,0:T(8,128)(2,1)} %refs_0_.7), channel_id=1, source_target_pairs={{0,24},{8,16},{16,8},{24,0},{1,25},{9,17},{17,9},{25,1},{2,26},{10... | collective-permute-start | bytes 1572872 | tf_op jit(solution)/shard_map/ppermute | solution.py:270
  67.5 58.7 %copy-start.1 = (bf16[128,2048]{1,0:T(8,128)(2,1)S(1)}, bf16[128,2048]{1,0:T(8,128)(2,1)}, u32[]{:S(2)}) copy-start(bf16[128,2048]{1,0:T(8,128)(2,1)} %refs_0_.7) | copy-start | bytes 1572868
  67.5 11.3 %collective-permute-start.3 = (bf16[16,128,128]{2,1,0:T(8,128)(2,1)S(1)}, bf16[16,128,128]{2,1,0:T(8,128)(2,1)}, u32[]{:S(2)}, u32[]{:S(2)}) collective-permute-start(bf16[16,128,128]{2,1,0:T(8,128)(2,1)S(1)} %get-tuple-element.55.refs_3_), channel_id=1, source_target_pairs={{0,2},{2,4},{4,6},{6,7},{7,5},{5,3},{3,1},{1,0},{8,10},{10,12},{12... | collective-permute-start | bytes 1572872 | tf_op jit(solution)/shard_map/ppermute | solution.py:310
  67.5 14.2 %collective-permute-start.4 = (bf16[16,128,128]{2,1,0:T(8,128)(2,1)S(1)}, bf16[16,128,128]{2,1,0:T(8,128)(2,1)}, u32[]{:S(2)}, u32[]{:S(2)}) collective-permute-start(bf16[16,128,128]{2,1,0:T(8,128)(2,1)S(1)} %get-tuple-element.55.refs_3_), channel_id=1, source_target_pairs={{2,0},{4,2},{6,4},{7,6},{5,7},{3,5},{1,3},{0,1},{10,8},{12,10},{14... | collective-permute-start | bytes 1572872 | tf_op jit(solution)/shard_map/ppermute | solution.py:311
  78.8 14.8 %collective-permute-start.9 = (bf16[16,128,128]{2,1,0:T(8,128)(2,1)}, bf16[16,128,128]{2,1,0:T(8,128)(2,1)}, u32[]{:S(2)}, u32[]{:S(2)}) collective-permute-start(bf16[16,128,128]{2,1,0:T(8,128)(2,1)} %collective-permute-done.3.refs_2_), channel_id=1, source_target_pairs={{0,2},{2,4},{4,6},{6,7},{7,5},{5,3},{3,1},{1,0},{8,10},{10,12},{12... | collective-permute-start | bytes 1572872 | tf_op jit(solution)/shard_map/ppermute | solution.py:310
  81.7 15.2 %collective-permute-start.10 = (bf16[16,128,128]{2,1,0:T(8,128)(2,1)}, bf16[16,128,128]{2,1,0:T(8,128)(2,1)}, u32[]{:S(2)}, u32[]{:S(2)}) collective-permute-start(bf16[16,128,128]{2,1,0:T(8,128)(2,1)} %collective-permute-done.4.refs_4_), channel_id=1, source_target_pairs={{2,0},{4,2},{6,4},{7,6},{5,7},{3,5},{1,3},{0,1},{10,8},{12,10},{14... | collective-permute-start | bytes 1572872 | tf_op jit(solution)/shard_map/ppermute | solution.py:311
  88.6 70.8 %copy-start.4 = (bf16[16,128,128]{2,1,0:T(8,128)(2,1)}, bf16[16,128,128]{2,1,0:T(8,128)(2,1)S(1)}, u32[]{:S(2)}) copy-start(bf16[16,128,128]{2,1,0:T(8,128)(2,1)S(1)} %get-tuple-element.59.refs_3_) | copy-start | bytes 1572868
  88.7 16.1 %collective-permute-start.5 = (bf16[16,128,128]{2,1,0:T(8,128)(2,1)S(1)}, bf16[16,128,128]{2,1,0:T(8,128)(2,1)}, u32[]{:S(2)}, u32[]{:S(2)}) collective-permute-start(bf16[16,128,128]{2,1,0:T(8,128)(2,1)S(1)} %get-tuple-element.59.refs_3_), channel_id=1, source_target_pairs={{0,2},{2,4},{4,6},{6,7},{7,5},{5,3},{3,1},{1,0},{8,10},{10,12},{12... | collective-permute-start | bytes 1572872 | tf_op jit(solution)/shard_map/ppermute | solution.py:310
  90.7 17.4 %collective-permute-start.6 = (bf16[16,128,128]{2,1,0:T(8,128)(2,1)S(1)}, bf16[16,128,128]{2,1,0:T(8,128)(2,1)}, u32[]{:S(2)}, u32[]{:S(2)}) collective-permute-start(bf16[16,128,128]{2,1,0:T(8,128)(2,1)S(1)} %get-tuple-element.59.refs_3_), channel_id=1, source_target_pairs={{2,0},{4,2},{6,4},{7,6},{5,7},{3,5},{1,3},{0,1},{10,8},{12,10},{14... | collective-permute-start | bytes 1572872 | tf_op jit(solution)/shard_map/ppermute | solution.py:311
  96.9 19.3 %collective-permute-start.11 = (bf16[16,128,128]{2,1,0:T(8,128)(2,1)}, bf16[16,128,128]{2,1,0:T(8,128)(2,1)}, u32[]{:S(2)}, u32[]{:S(2)}) collective-permute-start(bf16[16,128,128]{2,1,0:T(8,128)(2,1)} %collective-permute-done.9.refs_1_), channel_id=1, source_target_pairs={{0,2},{2,4},{4,6},{6,7},{7,5},{5,3},{3,1},{1,0},{8,10},{10,12},{12... | collective-permute-start | bytes 1572872 | tf_op jit(solution)/shard_map/ppermute | solution.py:310
  96.9 22.5 %collective-permute-start.12 = (bf16[16,128,128]{2,1,0:T(8,128)(2,1)}, bf16[16,128,128]{2,1,0:T(8,128)(2,1)}, u32[]{:S(2)}, u32[]{:S(2)}) collective-permute-start(bf16[16,128,128]{2,1,0:T(8,128)(2,1)} %collective-permute-done.10.refs_5_), channel_id=1, source_target_pairs={{2,0},{4,2},{6,4},{7,6},{5,7},{3,5},{1,3},{0,1},{10,8},{12,10},{14... | collective-permute-start | bytes 1572872 | tf_op jit(solution)/shard_map/ppermute | solution.py:311
  108.1 25.2 %collective-permute-start.7 = (bf16[16,128,128]{2,1,0:T(8,128)(2,1)}, bf16[16,128,128]{2,1,0:T(8,128)(2,1)}, u32[]{:S(2)}, u32[]{:S(2)}) collective-permute-start(bf16[16,128,128]{2,1,0:T(8,128)(2,1)} %collective-permute-done.5.refs_2_), channel_id=1, source_target_pairs={{0,2},{2,4},{4,6},{6,7},{7,5},{5,3},{3,1},{1,0},{8,10},{10,12},{12... | collective-permute-start | bytes 1572872 | tf_op jit(solution)/shard_map/ppermute | solution.py:310
  108.3 25.5 %collective-permute-start.8 = (bf16[16,128,128]{2,1,0:T(8,128)(2,1)}, bf16[16,128,128]{2,1,0:T(8,128)(2,1)S(1)}, u32[]{:S(2)}, u32[]{:S(2)}) collective-permute-start(bf16[16,128,128]{2,1,0:T(8,128)(2,1)} %collective-permute-done.6.refs_4_), channel_id=1, source_target_pairs={{2,0},{4,2},{6,4},{7,6},{5,7},{3,5},{1,3},{0,1},{10,8},{12,10},{14... | collective-permute-start | bytes 1572872 | tf_op jit(solution)/shard_map/ppermute | solution.py:311
  123.2 11.5 %collective-permute-start.13 = (bf16[2,16,64,128]{3,2,1,0:T(8,128)(2,1)S(1)}, bf16[2,16,64,128]{3,2,1,0:T(8,128)(2,1)S(1)}, u32[]{:S(2)}, u32[]{:S(2)}) collective-permute-start(bf16[2,16,64,128]{3,2,1,0:T(8,128)(2,1)S(1)} %get-tuple-element.70), channel_id=1, source_target_pairs={{0,8},{8,0},{16,24},{24,16},{1,9},{9,1},{17,25},{25,17},{2,10},{10... | collective-permute-start | bytes 1572872 | tf_op jit(solution)/shard_map/ppermute | solution.py:327
  124.7 12.5 %collective-permute-start.14 = (bf16[2,16,64,128]{3,2,1,0:T(8,128)(2,1)S(1)}, bf16[2,16,64,128]{3,2,1,0:T(8,128)(2,1)S(1)}, u32[]{:S(2)}, u32[]{:S(2)}) collective-permute-start(bf16[2,16,64,128]{3,2,1,0:T(8,128)(2,1)S(1)} %get-tuple-element.71), channel_id=1, source_target_pairs={{0,16},{8,24},{16,0},{24,8},{1,17},{9,25},{17,1},{25,9},{2,18},{10... | collective-permute-start | bytes 1572872 | tf_op jit(solution)/shard_map/ppermute | solution.py:327
  133.3 43.1 %copy-start.3 = (bf16[16,128,128]{2,1,0:T(8,128)(2,1)}, bf16[16,128,128]{2,1,0:T(8,128)(2,1)S(1)}, u32[]{:S(2)}) copy-start(bf16[16,128,128]{2,1,0:T(8,128)(2,1)S(1)} %get-tuple-element.87.refs_3_) | copy-start | bytes 1572868
  133.3 12.3 %collective-permute-start.26 = (bf16[16,128,128]{2,1,0:T(8,128)(2,1)S(1)}, bf16[16,128,128]{2,1,0:T(8,128)(2,1)S(1)}, u32[]{:S(2)}, u32[]{:S(2)}) collective-permute-start(bf16[16,128,128]{2,1,0:T(8,128)(2,1)S(1)} %get-tuple-element.87.refs_3_), channel_id=1, source_target_pairs={{0,2},{2,4},{4,6},{6,7},{7,5},{5,3},{3,1},{1,0},{8,10},{10,12},{12... | collective-permute-start | bytes 1572872 | tf_op jit(solution)/shard_map/ppermute | solution.py:310
  133.3 15.0 %collective-permute-start.27 = (bf16[16,128,128]{2,1,0:T(8,128)(2,1)S(1)}, bf16[16,128,128]{2,1,0:T(8,128)(2,1)}, u32[]{:S(2)}, u32[]{:S(2)}) collective-permute-start(bf16[16,128,128]{2,1,0:T(8,128)(2,1)S(1)} %get-tuple-element.87.refs_3_), channel_id=1, source_target_pairs={{2,0},{4,2},{6,4},{7,6},{5,7},{3,5},{1,3},{0,1},{10,8},{12,10},{14... | collective-permute-start | bytes 1572872 | tf_op jit(solution)/shard_map/ppermute | solution.py:311
  134.7 22.3 %collective-permute-start.17 = (bf16[16,128,128]{2,1,0:T(8,128)(2,1)}, bf16[16,128,128]{2,1,0:T(8,128)(2,1)S(1)}, u32[]{:S(2)}, u32[]{:S(2)}) collective-permute-start(bf16[16,128,128]{2,1,0:T(8,128)(2,1)} %collective-permute-done.7.refs_1_), channel_id=1, source_target_pairs={{0,2},{2,4},{4,6},{6,7},{7,5},{5,3},{3,1},{1,0},{8,10},{10,12},{12... | collective-permute-start | bytes 1572872 | tf_op jit(solution)/shard_map/ppermute | solution.py:310
  137.2 22.3 %collective-permute-start.18 = (bf16[16,128,128]{2,1,0:T(8,128)(2,1)S(1)}, bf16[16,128,128]{2,1,0:T(8,128)(2,1)S(1)}, u32[]{:S(2)}, u32[]{:S(2)}) collective-permute-start(bf16[16,128,128]{2,1,0:T(8,128)(2,1)S(1)} %collective-permute-done.8.refs_5_), channel_id=1, source_target_pairs={{2,0},{4,2},{6,4},{7,6},{5,7},{3,5},{1,3},{0,1},{10,8},{12,10},{14... | collective-permute-start | bytes 1572872 | tf_op jit(solution)/shard_map/ppermute | solution.py:311
  137.2 35.4 %collective-permute-start.15 = (bf16[2,16,64,128]{3,2,1,0:T(8,128)(2,1)S(1)}, bf16[2,16,64,128]{3,2,1,0:T(8,128)(2,1)S(1)}, u32[]{:S(2)}, u32[]{:S(2)}) collective-permute-start(bf16[2,16,64,128]{3,2,1,0:T(8,128)(2,1)S(1)} %get-tuple-element.72), channel_id=1, source_target_pairs={{0,24},{8,16},{16,8},{24,0},{1,25},{9,17},{17,9},{25,1},{2,26},{10... | collective-permute-start | bytes 1572872 | tf_op jit(solution)/shard_map/ppermute | solution.py:327
  148.3 28.1 %collective-permute-start.28 = (bf16[16,128,128]{2,1,0:T(8,128)(2,1)S(1)}, bf16[16,128,128]{2,1,0:T(8,128)(2,1)S(1)}, u32[]{:S(2)}, u32[]{:S(2)}) collective-permute-start(bf16[16,128,128]{2,1,0:T(8,128)(2,1)S(1)} %collective-permute-done.26.refs_2_), channel_id=1, source_target_pairs={{0,2},{2,4},{4,6},{6,7},{7,5},{5,3},{3,1},{1,0},{8,10},{10,12},{12... | collective-permute-start | bytes 1572872 | tf_op jit(solution)/shard_map/ppermute | solution.py:310
  150.3 26.2 %collective-permute-start.29 = (bf16[16,128,128]{2,1,0:T(8,128)(2,1)}, bf16[16,128,128]{2,1,0:T(8,128)(2,1)}, u32[]{:S(2)}, u32[]{:S(2)}) collective-permute-start(bf16[16,128,128]{2,1,0:T(8,128)(2,1)} %collective-permute-done.27.refs_4_), channel_id=1, source_target_pairs={{2,0},{4,2},{6,4},{7,6},{5,7},{3,5},{1,3},{0,1},{10,8},{12,10},{14... | collective-permute-start | bytes 1572872 | tf_op jit(solution)/shard_map/ppermute | solution.py:311
  164.4 12.1 %collective-permute-start.19 = (bf16[2,16,64,128]{3,2,1,0:T(8,128)(2,1)S(1)}, bf16[2,16,64,128]{3,2,1,0:T(8,128)(2,1)S(1)}, u32[]{:S(2)}, u32[]{:S(2)}) collective-permute-start(bf16[2,16,64,128]{3,2,1,0:T(8,128)(2,1)S(1)} %get-tuple-element.77), channel_id=1, source_target_pairs={{0,8},{8,0},{16,24},{24,16},{1,9},{9,1},{17,25},{25,17},{2,10},{10... | collective-permute-start | bytes 1572872 | tf_op jit(solution)/shard_map/ppermute | solution.py:327
  171.9 64.3 %copy-start.2 = (bf16[16,128,128]{2,1,0:T(8,128)(2,1)}, bf16[16,128,128]{2,1,0:T(8,128)(2,1)S(1)}, u32[]{:S(2)}) copy-start(bf16[16,128,128]{2,1,0:T(8,128)(2,1)S(1)} %get-tuple-element.84.refs_3_) | copy-start | bytes 1572868
  172.0 22.0 %collective-permute-start.20 = (bf16[2,16,64,128]{3,2,1,0:T(8,128)(2,1)S(1)}, bf16[2,16,64,128]{3,2,1,0:T(8,128)(2,1)S(1)}, u32[]{:S(2)}, u32[]{:S(2)}) collective-permute-start(bf16[2,16,64,128]{3,2,1,0:T(8,128)(2,1)S(1)} %get-tuple-element.78), channel_id=1, source_target_pairs={{0,16},{8,24},{16,0},{24,8},{1,17},{9,25},{17,1},{25,9},{2,18},{10... | collective-permute-start | bytes 1572872 | tf_op jit(solution)/shard_map/ppermute | solution.py:327
  172.6 23.9 %collective-permute-start.23 = (bf16[16,128,128]{2,1,0:T(8,128)(2,1)S(1)}, bf16[16,128,128]{2,1,0:T(8,128)(2,1)S(1)}, u32[]{:S(2)}, u32[]{:S(2)}) collective-permute-start(bf16[16,128,128]{2,1,0:T(8,128)(2,1)S(1)} %get-tuple-element.84.refs_3_), channel_id=1, source_target_pairs={{0,2},{2,4},{4,6},{6,7},{7,5},{5,3},{3,1},{1,0},{8,10},{10,12},{12... | collective-permute-start | bytes 1572872 | tf_op jit(solution)/shard_map/ppermute | solution.py:310
  176.4 20.1 %collective-permute-start.24 = (bf16[16,128,128]{2,1,0:T(8,128)(2,1)S(1)}, bf16[16,128,128]{2,1,0:T(8,128)(2,1)S(1)}, u32[]{:S(2)}, u32[]{:S(2)}) collective-permute-start(bf16[16,128,128]{2,1,0:T(8,128)(2,1)S(1)} %get-tuple-element.84.refs_3_), channel_id=1, source_target_pairs={{2,0},{4,2},{6,4},{7,6},{5,7},{3,5},{1,3},{0,1},{10,8},{12,10},{14... | collective-permute-start | bytes 1572872 | tf_op jit(solution)/shard_map/ppermute | solution.py:311
  176.4 39.1 %collective-permute-start.16 = (bf16[16,64,512]{2,1,0:T(8,128)(2,1)S(1)}, bf16[16,64,512]{2,1,0:T(8,128)(2,1)S(1)}, u32[]{:S(2)}, u32[]{:S(2)}) collective-permute-start(bf16[16,64,512]{2,1,0:T(8,128)(2,1)S(1)} %get-tuple-element.73), channel_id=1, source_target_pairs={{0,1},{1,0},{2,3},{3,2},{4,5},{5,4},{6,7},{7,6},{8,9},{9,8},{10,11... | collective-permute-start | bytes 3145736 | tf_op jit(solution)/shard_map/ppermute | solution.py:331
  176.5 22.0 %collective-permute-start.21 = (bf16[2,16,64,128]{3,2,1,0:T(8,128)(2,1)S(1)}, bf16[2,16,64,128]{3,2,1,0:T(8,128)(2,1)S(1)}, u32[]{:S(2)}, u32[]{:S(2)}) collective-permute-start(bf16[2,16,64,128]{3,2,1,0:T(8,128)(2,1)S(1)} %get-tuple-element.79), channel_id=1, source_target_pairs={{0,24},{8,16},{16,8},{24,0},{1,25},{9,17},{17,9},{25,1},{2,26},{10... | collective-permute-start | bytes 1572872 | tf_op jit(solution)/shard_map/ppermute | solution.py:327
  194.0 14.9 %collective-permute-start.30 = (bf16[16,128,128]{2,1,0:T(8,128)(2,1)S(1)}, bf16[16,128,128]{2,1,0:T(8,128)(2,1)S(1)}, u32[]{:S(2)}, u32[]{:S(2)}) collective-permute-start(bf16[16,128,128]{2,1,0:T(8,128)(2,1)S(1)} %collective-permute-done.28.refs_1_), channel_id=1, source_target_pairs={{0,2},{2,4},{4,6},{6,7},{7,5},{5,3},{3,1},{1,0},{8,10},{10,12},{12... | collective-permute-start | bytes 1572872 | tf_op jit(solution)/shard_map/ppermute | solution.py:310
  196.5 12.4 %collective-permute-start.31 = (bf16[16,128,128]{2,1,0:T(8,128)(2,1)}, bf16[16,128,128]{2,1,0:T(8,128)(2,1)S(1)}, u32[]{:S(2)}, u32[]{:S(2)}) collective-permute-start(bf16[16,128,128]{2,1,0:T(8,128)(2,1)} %collective-permute-done.29.refs_5_), channel_id=1, source_target_pairs={{2,0},{4,2},{6,4},{7,6},{5,7},{3,5},{1,3},{0,1},{10,8},{12,10},{14... | collective-permute-start | bytes 1572872 | tf_op jit(solution)/shard_map/ppermute | solution.py:311
  196.5 21.1 %collective-permute-start.25 = (bf16[16,128,128]{2,1,0:T(8,128)(2,1)S(1)}, bf16[16,128,128]{2,1,0:T(8,128)(2,1)S(1)}, u32[]{:S(2)}, u32[]{:S(2)}) collective-permute-start(bf16[16,128,128]{2,1,0:T(8,128)(2,1)S(1)} %collective-permute-done.23.refs_2_), channel_id=1, source_target_pairs={{0,2},{2,4},{4,6},{6,7},{7,5},{5,3},{3,1},{1,0},{8,10},{10,12},{12... | collective-permute-start | bytes 1572872 | tf_op jit(solution)/shard_map/ppermute | solution.py:310
  200.3 36.0 %collective-permute-start.22 = (bf16[16,64,512]{2,1,0:T(8,128)(2,1)S(1)}, bf16[16,64,512]{2,1,0:T(8,128)(2,1)S(1)}, u32[]{:S(2)}, u32[]{:S(2)}) collective-permute-start(bf16[16,64,512]{2,1,0:T(8,128)(2,1)S(1)} %get-tuple-element.81), channel_id=1, source_target_pairs={{0,1},{1,0},{2,3},{3,2},{4,5},{5,4},{6,7},{7,6},{8,9},{9,8},{10,11... | collective-permute-start | bytes 3145736 | tf_op jit(solution)/shard_map/ppermute | solution.py:331
  208.8 10.2 %collective-permute-start.33 = (bf16[16,128,128]{2,1,0:T(8,128)(2,1)S(1)}, bf16[16,128,128]{2,1,0:T(8,128)(2,1)S(1)}, u32[]{:S(2)}, u32[]{:S(2)}) collective-permute-start(bf16[16,128,128]{2,1,0:T(8,128)(2,1)S(1)} %collective-permute-done.24.refs_4_), channel_id=1, source_target_pairs={{2,0},{4,2},{6,4},{7,6},{5,7},{3,5},{1,3},{0,1},{10,8},{12,10},{14... | collective-permute-start | bytes 1572872 | tf_op jit(solution)/shard_map/ppermute | solution.py:311
  214.0 14.2 %collective-permute-start.38 = (bf16[2,16,64,128]{3,2,1,0:T(8,128)(2,1)S(1)}, bf16[2,16,64,128]{3,2,1,0:T(8,128)(2,1)S(1)}, u32[]{:S(2)}, u32[]{:S(2)}) collective-permute-start(bf16[2,16,64,128]{3,2,1,0:T(8,128)(2,1)S(1)} %get-tuple-element.100), channel_id=1, source_target_pairs={{0,8},{8,0},{16,24},{24,16},{1,9},{9,1},{17,25},{25,17},{2,10},{10... | collective-permute-start | bytes 1572872 | tf_op jit(solution)/shard_map/ppermute | solution.py:327
  215.5 18.9 %collective-permute-start.39 = (bf16[2,16,64,128]{3,2,1,0:T(8,128)(2,1)S(1)}, bf16[2,16,64,128]{3,2,1,0:T(8,128)(2,1)S(1)}, u32[]{:S(2)}, u32[]{:S(2)}) collective-permute-start(bf16[2,16,64,128]{3,2,1,0:T(8,128)(2,1)S(1)} %get-tuple-element.101), channel_id=1, source_target_pairs={{0,16},{8,24},{16,0},{24,8},{1,17},{9,25},{17,1},{25,9},{2,18},{10... | collective-permute-start | bytes 1572872 | tf_op jit(solution)/shard_map/ppermute | solution.py:327
  217.6 16.9 %collective-permute-start.40 = (bf16[2,16,64,128]{3,2,1,0:T(8,128)(2,1)S(1)}, bf16[2,16,64,128]{3,2,1,0:T(8,128)(2,1)S(1)}, u32[]{:S(2)}, u32[]{:S(2)}) collective-permute-start(bf16[2,16,64,128]{3,2,1,0:T(8,128)(2,1)S(1)} %get-tuple-element.102), channel_id=1, source_target_pairs={{0,24},{8,16},{16,8},{24,0},{1,25},{9,17},{17,9},{25,1},{2,26},{10... | collective-permute-start | bytes 1572872 | tf_op jit(solution)/shard_map/ppermute | solution.py:327
  219.1 17.3 %collective-permute-start.32 = (bf16[16,128,128]{2,1,0:T(8,128)(2,1)S(1)}, bf16[16,128,128]{2,1,0:T(8,128)(2,1)S(1)}, u32[]{:S(2)}, u32[]{:S(2)}) collective-permute-start(bf16[16,128,128]{2,1,0:T(8,128)(2,1)S(1)} %collective-permute-done.25.refs_1_), channel_id=1, source_target_pairs={{0,2},{2,4},{4,6},{6,7},{7,5},{5,3},{3,1},{1,0},{8,10},{10,12},{12... | collective-permute-start | bytes 1572872 | tf_op jit(solution)/shard_map/ppermute | solution.py:310
  228.2 9.5 %collective-permute-start.34 = (bf16[16,128,128]{2,1,0:T(8,128)(2,1)S(1)}, bf16[16,128,128]{2,1,0:T(8,128)(2,1)S(1)}, u32[]{:S(2)}, u32[]{:S(2)}) collective-permute-start(bf16[16,128,128]{2,1,0:T(8,128)(2,1)S(1)} %collective-permute-done.33.refs_5_), channel_id=1, source_target_pairs={{2,0},{4,2},{6,4},{7,6},{5,7},{3,5},{1,3},{0,1},{10,8},{12,10},{14... | collective-permute-start | bytes 1572872 | tf_op jit(solution)/shard_map/ppermute | solution.py:311
  236.3 12.9 %collective-permute-start.41 = (bf16[16,64,512]{2,1,0:T(8,128)(2,1)S(1)}, bf16[16,64,512]{2,1,0:T(8,128)(2,1)S(1)}, u32[]{:S(2)}, u32[]{:S(2)}) collective-permute-start(bf16[16,64,512]{2,1,0:T(8,128)(2,1)S(1)} %get-tuple-element.104), channel_id=1, source_target_pairs={{0,1},{1,0},{2,3},{3,2},{4,5},{5,4},{6,7},{7,6},{8,9},{9,8},{10,11... | collective-permute-start | bytes 3145736 | tf_op jit(solution)/shard_map/ppermute | solution.py:331
  242.6 14.9 %collective-permute-start.35 = (bf16[2,16,64,128]{3,2,1,0:T(8,128)(2,1)S(1)}, bf16[2,16,64,128]{3,2,1,0:T(8,128)(2,1)S(1)}, u32[]{:S(2)}, u32[]{:S(2)}) collective-permute-start(bf16[2,16,64,128]{3,2,1,0:T(8,128)(2,1)S(1)} %get-tuple-element.96), channel_id=1, source_target_pairs={{0,8},{8,0},{16,24},{24,16},{1,9},{9,1},{17,25},{25,17},{2,10},{10... | collective-permute-start | bytes 1572872 | tf_op jit(solution)/shard_map/ppermute | solution.py:327
  244.0 22.7 %collective-permute-start.36 = (bf16[2,16,64,128]{3,2,1,0:T(8,128)(2,1)S(1)}, bf16[2,16,64,128]{3,2,1,0:T(8,128)(2,1)S(1)}, u32[]{:S(2)}, u32[]{:S(2)}) collective-permute-start(bf16[2,16,64,128]{3,2,1,0:T(8,128)(2,1)S(1)} %get-tuple-element.97), channel_id=1, source_target_pairs={{0,16},{8,24},{16,0},{24,8},{1,17},{9,25},{17,1},{25,9},{2,18},{10... | collective-permute-start | bytes 1572872 | tf_op jit(solution)/shard_map/ppermute | solution.py:327
  244.4 22.4 %collective-permute-start.37 = (bf16[2,16,64,128]{3,2,1,0:T(8,128)(2,1)S(1)}, bf16[2,16,64,128]{3,2,1,0:T(8,128)(2,1)S(1)}, u32[]{:S(2)}, u32[]{:S(2)}) collective-permute-start(bf16[2,16,64,128]{3,2,1,0:T(8,128)(2,1)S(1)} %get-tuple-element.98), channel_id=1, source_target_pairs={{0,24},{8,16},{16,8},{24,0},{1,25},{9,17},{17,9},{25,1},{2,26},{10... | collective-permute-start | bytes 1572872 | tf_op jit(solution)/shard_map/ppermute | solution.py:327
  268.6 2.7 collective-permute-start.42
  (10 other events, 175.8 us)
Sparse Core Ops, SparseCore 0:
  9.6 49.8 all-gather.1

commit v4 on v3

--- a/solution.py
+++ b/solution.py
@@ -292,6 +292,7 @@
     state = {"new_pair": None, "result": None}
     tiles = [{} for _ in range(count)]
     moved = [None] * count
+    handed = [None] * count
 
     def after(value, *others):
         return lax.optimization_barrier((value, others))[0]
@@ -324,54 +325,58 @@
         )
 
     def send(part, d):
-        moved[part][d] = lax.ppermute(moved[part][d], "row", [(a, a ^ d) for a in range(parts)])
-
-    def place(part):
-        state["result"], other = place_call(where, moved[part], state["result"], part, parts, tile_cols)
-        swapped[part] = lax.ppermute(other, "col", [(c, c ^ 1) for c in range(cols)])
+        piece = moved[part][d]
+        if d > 2 and part < count - 1:
+            piece = after(piece, moved[part][1], moved[part][2])
+        moved[part][d] = lax.ppermute(piece, "row", [(a, a ^ d) for a in range(parts)])
+
+    def place(part, *others):
+        state["result"], handed[part] = place_call(
+            after(where, *others), moved[part], state["result"], part, parts, tile_cols
+        )
+        swapped[part] = lax.ppermute(handed[part], "col", [(c, c ^ 1) for c in range(cols)])
 
     def put(part):
         state["result"] = put_call(where, swapped[part], state["result"], part, tile_cols)
 
-    order = sorted(
-        ((part, s) for part in range(count) for s in range(1, line)),
-        key=lambda step: (step[0] + step[1], step[0]),
-    )
+    steps = line - 1
     swapped = [None] * count
-    done = []
-    pending = []
+    gate, before = [], []
+
+    def last(part):
+        return steps * (part + 1) - 1
+
     update(0)
-    updated = 1
-    for index, (part, s) in enumerate(order):
-        others = list(done[index - 2]) if index >= 2 else []
-        while updated <= part:
-            update(updated)
-            updated += 1
-        if pending and index >= pending[0][0]:
-            _, owner, d = pending.pop(0)
-            others.append(moved[owner][d])
-        if part == count - 1 and s == line - 1:
-            for owner in range(count - 3):
-                if swapped[owner] is not None:
-                    others.append(swapped[owner])
-        shift(part, s, *others)
-        done.append((tiles[part][-s], tiles[part][s]))
-        if updated < count and any(p == updated for p, _ in order[index + 2 : index + 4]):
-            update(updated, *done[index - 1 if index else 0])
-            updated += 1
-        if s == line - 1 and part < count - 1:
-            project(part)
-            for d in range(1, parts):
-                send(part, d)
-                pending.append((index + 2 + d, part, d))
-            place(part)
-    project(count - 1, *[w for w in swapped[:-2] if w is not None])
+    for index in range(count * steps):
+        shift(index // steps, index % steps + 1, *gate)
+        here = tiles[index // steps]
+        gate = [here[-(index % steps + 1)], here[index % steps + 1]]
+        now = list(gate)
+        if index + 1 < count:
+            update(index + 1, *before)
+            gate.append(tiles[index + 1][0])
+        for part in range(count - 1):
+            if index == last(part) + 1:
+                project(part, *before)
+                gate.append(moved[part][0])
+                for d in range(1, parts):
+                    send(part, d)
+            if index == last(part) + 2:
+                gate += moved[part][1:3]
+            if index == last(part) + 5:
+                place(part, *before)
+                gate.append(handed[part])
+            if index == last(part) + 6:
+                gate.append(swapped[part])
+                put(part)
+        before = now
+    project(count - 1)
     for d in range(1, parts):
         send(count - 1, d)
-    for part in range(count - 1):
-        put(part)
-    place(count - 1)
-    put(count - 1)
+    for part in range(count):
+        if swapped[part] is None:
+            place(part)
+            put(part)
     return (state["new_pair"], state["result"])
 
 

time: 280 us -> 285 us (1.018)
    ppermute x12, waiting for transfers between devices: 50.6 us -> 44.6 us  [shift(): here[-s] = lax.ppermute(after(here[-(s - 1)], *others), 'col', onward)]
    ppermute x12, waiting for transfers between devices: 16.5 us -> 20.2 us  [shift(): here[s] = lax.ppermute(after(here[s - 1], *others), 'col', back)]
    unnamed x31 -> x39, local copies, waits for them, and re-layouts: 4.8 us -> 5.71 us
  transfers between devices with their start and end apart: 44 -> 44, of which waited for: 25 -> 34; matrix products, arithmetic and copies ran while one was open for 1% -> 2% of each run, Pallas kernels for 17% -> 17%
where the time goes in v4:
time: 285 us; the launch traced here: 282 us
  waiting for transfers between devices  158 us (55%)
  Pallas kernels  58.8 us (21%)
  starting transfers between devices  42 us (15%)
  between operations  14.4 us (5%)
  local copies, waits for them, and re-layouts  9.09 us (3%)
    ppermute x12, waiting for transfers between devices, send(): lax.ppermute(piece, 'row', [(a, a ^ d) for a in range(parts)])  45.1 us
    ppermute x12, waiting for transfers between devices, shift(): here[-s] = lax.ppermute(after(here[-(s - 1)], *others), 'col', onward)  44.6 us
    pallas_call x4, Pallas kernels, update_call(): pl.pallas_call(functools.partial(update_kernel, parts, part), grid=(1,),...  28.5 us
    all_gather x1, waiting for transfers between devices, shards(): left = lax.all_gather(alignment_left, 'col', axis=0, tiled=True)  24 us
    ppermute x12, starting transfers between devices, shift(): here[-s] = lax.ppermute(after(here[-(s - 1)], *others), 'col', onward)  20.5 us
    ppermute x3, waiting for transfers between devices, shards(): lax.ppermute(alignment_right, 'row', [(a, a ^ d) for a in range(parts)])  20.3 us
    ppermute x12, waiting for transfers between devices, shift(): here[s] = lax.ppermute(after(here[s - 1], *others), 'col', back)  20.2 us
    pallas_call x4, Pallas kernels, project_call(): pl.pallas_call(functools.partial(project_kernel, line, parts), in_specs=[...  16.9 us
  transfers between devices with their start and end apart: 44, of which 34 were waited for; matrix products, arithmetic and copies ran while one was open for 2% of the time, Pallas kernels for 17%

profile of v4, /device:TPU:0, one launch (start us, length us, event | category | flops | bytes accessed | tf_op | source)
XLA Modules:
  0.0 282.1 jit_solution(3550365921006385201)
XLA Ops:
  7.9 4.0 %collective-permute-start.2 = (bf16[128,2048]{1,0:T(8,128)(2,1)}, bf16[128,2048]{1,0:T(8,128)(2,1)S(1)}, u32[]{:S(2)}, u32[]{:S(2)}) collective-permute-start(bf16[128,2048]{1,0:T(8,128)(2,1)} %refs_0_.7), channel_id=1, source_target_pairs={{0,24},{8,16},{16,8},{24,0},{1,25},{9,17},{17,9},{25,1},{2,26},{10... | collective-permute-start | bytes 1572872 | tf_op jit(solution)/shard_map/ppermute | solution.py:270
  15.2 9.7 %collective-permute-done.2.refs_3_ = bf16[128,2048]{1,0:T(8,128)(2,1)S(1)} collective-permute-done((bf16[128,2048]{1,0:T(8,128)(2,1)}, bf16[128,2048]{1,0:T(8,128)(2,1)S(1)}, u32[]{:S(2)}, u32[]{:S(2)}) %collective-permute-start.2) | collective-permute-done | bytes 524320 | tf_op jit(solution)/shard_map/ppermute | solution.py:270
  24.9 10.4 %collective-permute-done.1.refs_2_ = bf16[128,2048]{1,0:T(8,128)(2,1)S(1)} collective-permute-done((bf16[128,2048]{1,0:T(8,128)(2,1)}, bf16[128,2048]{1,0:T(8,128)(2,1)S(1)}, u32[]{:S(2)}, u32[]{:S(2)}) %collective-permute-start.1) | collective-permute-done | bytes 524320 | tf_op jit(solution)/shard_map/ppermute | solution.py:270
  35.5 24.0 %all-gather.2.cloned.1.call-done.left_ref = bf16[128,16384]{1,0:T(8,128)(2,1)} async-done(((bf16[16,16384]{1,0:T(8,128)(2,1)}), bf16[128,16384]{1,0:T(8,128)(2,1)}) %all-gather.2.cloned.1.call-update) | async-done | bytes 4194320 | tf_op jit(solution)/shard_map/all_gather | solution.py:271
  60.5 7.0 %update.4 = (bf16[128,64,128]{2,1,0:T(8,128)(2,1)}, bf16[16,128,128]{2,1,0:T(8,128)(2,1)S(1)}) custom-call(s32[3]{0:T(128)S(1)} %pad_add_fusion.where_ref, bf16[128,16384]{1,0:T(8,128)(2,1)} %all-gather.2.cloned.1.call-done.left_ref, bf16[128,2048]{1,0:T(8,128)(2,1)S(1)} %copy-done, bf16[128,2048]{1,0:T(8,128)(2,1)S(1)} %collective-permute-done.refs_1_, ...), custom_call_target="tpu_custom_call" | custom-call | flops 2684354560 | bytes 8388608 | tf_op jit(solution)/shard_map/update/pallas_call | solution.py:105
  67.8 1.8 collective-permute-start.3
  69.6 7.3 %update.5 = (bf16[128,64,128]{2,1,0:T(8,128)(2,1)}, bf16[16,128,128]{2,1,0:T(8,128)(2,1)}) custom-call(s32[3]{0:T(128)S(1)} %pad_add_fusion.where_ref, bf16[128,16384]{1,0:T(8,128)(2,1)} %all-gather.2.cloned.1.call-done.left_ref, bf16[128,2048]{1,0:T(8,128)(2,1)S(1)} %copy-done, ...), custom_call_target="tpu_custom_call", output_to_operand_aliasing={{0}: (10, {})} | custom-call | flops 2684354560 | bytes 8388608 | tf_op jit(solution)/shard_map/update/pallas_call | solution.py:105
  76.9 4.8 %collective-permute-done.4.refs_4_ = bf16[16,128,128]{2,1,0:T(8,128)(2,1)S(1)} collective-permute-done((bf16[16,128,128]{2,1,0:T(8,128)(2,1)S(1)}, bf16[16,128,128]{2,1,0:T(8,128)(2,1)S(1)}, u32[]{:S(2)}, u32[]{:S(2)}) %collective-permute-start.4) | collective-permute-done | bytes 524320 | tf_op jit(solution)/shard_map/ppermute | solution.py:312
  82.2 7.0 %update.6 = (bf16[128,64,128]{2,1,0:T(8,128)(2,1)}, bf16[16,128,128]{2,1,0:T(8,128)(2,1)S(1)}) custom-call(s32[3]{0:T(128)S(1)} %pad_add_fusion.where_ref, bf16[128,16384]{1,0:T(8,128)(2,1)} %all-gather.2.cloned.1.call-done.left_ref, bf16[128,2048]{1,0:T(8,128)(2,1)S(1)} %copy-done, ...), custom_call_target="tpu_custom_call", output_to_operand_aliasing={{0}: (10, {})} | custom-call | flops 2684354560 | bytes 8388608 | tf_op jit(solution)/shard_map/update/pallas_call | solution.py:105
  89.2 5.0 %collective-permute-done.5.refs_1_ = bf16[16,128,128]{2,1,0:T(8,128)(2,1)} collective-permute-done((bf16[16,128,128]{2,1,0:T(8,128)(2,1)S(1)}, bf16[16,128,128]{2,1,0:T(8,128)(2,1)}, u32[]{:S(2)}, u32[]{:S(2)}) %collective-permute-start.5) | collective-permute-done | bytes 524320 | tf_op jit(solution)/shard_map/ppermute | solution.py:311
  95.0 1.8 collective-permute-start.7
  98.3 7.2 %update.7 = (bf16[128,64,128]{2,1,0:T(8,128)(2,1)}, bf16[16,128,128]{2,1,0:T(8,128)(2,1)S(1)}) custom-call(s32[3]{0:T(128)S(1)} %pad_add_fusion.where_ref, bf16[128,16384]{1,0:T(8,128)(2,1)} %all-gather.2.cloned.1.call-done.left_ref, bf16[128,2048]{1,0:T(8,128)(2,1)S(1)} %copy-done.1, ...), custom_call_target="tpu_custom_call", output_to_operand_aliasing={{0}: (10, {})} | custom-call | flops 2684354560 | bytes 8388608 | tf_op jit(solution)/shard_map/update/pallas_call | solution.py:105
  105.6 3.0 %collective-permute-done.7.refs_0_ = bf16[16,128,128]{2,1,0:T(8,128)(2,1)} collective-permute-done((bf16[16,128,128]{2,1,0:T(8,128)(2,1)}, bf16[16,128,128]{2,1,0:T(8,128)(2,1)}, u32[]{:S(2)}, u32[]{:S(2)}) %collective-permute-start.7) | collective-permute-done | bytes 524320 | tf_op jit(solution)/shard_map/ppermute | solution.py:311
  109.3 2.0 collective-permute-start.9
  114.5 4.1 %project.4 = (bf16[2,16,64,128]{3,2,1,0:T(8,128)(2,1)S(1)}, bf16[2,16,64,128]{3,2,1,0:T(8,128)(2,1)S(1)}, bf16[2,16,64,128]{3,2,1,0:T(8,128)(2,1)S(1)}, bf16[2,16,64,128]{3,2,1,0:T(8,128)(2,1)S(1)}) custom-call(s32[3]{0:T(128)S(1)} %pad_add_fusion.where_ref, bf16[128,128]{1,0:T(8,128)(2,1)S(1)} %pad_maximum_fusion.weight_ref, f32[128,1]{1,0:T(8,128)S(1)} %copy.52.offset_ref, ...), custom_call_target="tpu_custom_call" | custom-call | flops 268435456 | bytes 4194304 | tf_op jit(solution)/shard_map/project/pallas_call | solution.py:165
  121.7 2.2 collective-permute-done.10.refs_4_
  123.9 1.8 collective-permute-start.11
  125.7 5.3 %collective-permute-done.13.refs_1_ = bf16[2,16,64,128]{3,2,1,0:T(8,128)(2,1)S(1)} collective-permute-done((bf16[2,16,64,128]{3,2,1,0:T(8,128)(2,1)S(1)}, bf16[2,16,64,128]{3,2,1,0:T(8,128)(2,1)S(1)}, u32[]{:S(2)}, u32[]{:S(2)}) %collective-permute-start.13) | collective-permute-done | bytes 524320 | tf_op jit(solution)/shard_map/ppermute | solution.py:331
  132.2 5.3 %collective-permute-done.11.refs_1_ = bf16[16,128,128]{2,1,0:T(8,128)(2,1)S(1)} collective-permute-done((bf16[16,128,128]{2,1,0:T(8,128)(2,1)S(1)}, bf16[16,128,128]{2,1,0:T(8,128)(2,1)S(1)}, u32[]{:S(2)}, u32[]{:S(2)}) %collective-permute-start.11) | collective-permute-done | bytes 524320 | tf_op jit(solution)/shard_map/ppermute | solution.py:311
  138.2 1.8 collective-permute-start.15
  140.0 11.0 %collective-permute-done.15.refs_0_ = bf16[16,128,128]{2,1,0:T(8,128)(2,1)S(1)} collective-permute-done((bf16[16,128,128]{2,1,0:T(8,128)(2,1)S(1)}, bf16[16,128,128]{2,1,0:T(8,128)(2,1)S(1)}, u32[]{:S(2)}, u32[]{:S(2)}) %collective-permute-start.15) | collective-permute-done | bytes 524320 | tf_op jit(solution)/shard_map/ppermute | solution.py:311
  151.7 2.0 collective-permute-start.17
  153.8 2.4 collective-permute-start.21
  156.2 4.2 %project.5 = (bf16[2,16,64,128]{3,2,1,0:T(8,128)(2,1)S(1)}, bf16[2,16,64,128]{3,2,1,0:T(8,128)(2,1)S(1)}, bf16[2,16,64,128]{3,2,1,0:T(8,128)(2,1)S(1)}, bf16[2,16,64,128]{3,2,1,0:T(8,128)(2,1)S(1)}) custom-call(s32[3]{0:T(128)S(1)} %pad_add_fusion.where_ref, bf16[128,128]{1,0:T(8,128)(2,1)S(1)} %pad_maximum_fusion.weight_ref, f32[128,1]{1,0:T(8,128)S(1)} %copy.52.offset_ref, ...), custom_call_target="tpu_custom_call" | custom-call | flops 268435456 | bytes 4194304 | tf_op jit(solution)/shard_map/project/pallas_call | solution.py:165
  161.5 4.9 %collective-permute-done.18.refs_4_ = bf16[16,128,128]{2,1,0:T(8,128)(2,1)S(1)} collective-permute-done((bf16[16,128,128]{2,1,0:T(8,128)(2,1)S(1)}, bf16[16,128,128]{2,1,0:T(8,128)(2,1)S(1)}, u32[]{:S(2)}, u32[]{:S(2)}) %collective-permute-start.18) | collective-permute-done | bytes 524320 | tf_op jit(solution)/shard_map/ppermute | solution.py:312
  166.4 1.7 collective-permute-start.19
  169.6 1.8 place.4
  171.5 6.8 %collective-permute-done.22.refs_1_ = bf16[2,16,64,128]{3,2,1,0:T(8,128)(2,1)S(1)} collective-permute-done((bf16[2,16,64,128]{3,2,1,0:T(8,128)(2,1)S(1)}, bf16[2,16,64,128]{3,2,1,0:T(8,128)(2,1)S(1)}, u32[]{:S(2)}, u32[]{:S(2)}) %collective-permute-start.22) | collective-permute-done | bytes 524320 | tf_op jit(solution)/shard_map/ppermute | solution.py:331
  180.2 1.8 collective-permute-start.24
  182.0 10.5 %collective-permute-done.24.refs_0_ = bf16[16,128,128]{2,1,0:T(8,128)(2,1)S(1)} collective-permute-done((bf16[16,128,128]{2,1,0:T(8,128)(2,1)S(1)}, bf16[16,128,128]{2,1,0:T(8,128)(2,1)S(1)}, u32[]{:S(2)}, u32[]{:S(2)}) %collective-permute-start.24) | collective-permute-done | bytes 524320 | tf_op jit(solution)/shard_map/ppermute | solution.py:311
  193.2 2.0 collective-permute-start.27
  195.2 2.5 collective-permute-start.31
  199.2 4.4 %project.6 = (bf16[2,16,64,128]{3,2,1,0:T(8,128)(2,1)S(1)}, bf16[2,16,64,128]{3,2,1,0:T(8,128)(2,1)S(1)}, bf16[2,16,64,128]{3,2,1,0:T(8,128)(2,1)S(1)}, bf16[2,16,64,128]{3,2,1,0:T(8,128)(2,1)S(1)}) custom-call(s32[3]{0:T(128)S(1)} %pad_add_fusion.where_ref, bf16[128,128]{1,0:T(8,128)(2,1)S(1)} %pad_maximum_fusion.weight_ref, f32[128,1]{1,0:T(8,128)S(1)} %copy.52.offset_ref, ...), custom_call_target="tpu_custom_call" | custom-call | flops 268435456 | bytes 4194304 | tf_op jit(solution)/shard_map/project/pallas_call | solution.py:165
  204.7 2.4 collective-permute-done.28.refs_4_
  207.1 3.8 %collective-permute-done.31.refs_3_ = bf16[2,16,64,128]{3,2,1,0:T(8,128)(2,1)S(1)} collective-permute-done((bf16[2,16,64,128]{3,2,1,0:T(8,128)(2,1)S(1)}, bf16[2,16,64,128]{3,2,1,0:T(8,128)(2,1)S(1)}, u32[]{:S(2)}, u32[]{:S(2)}) %collective-permute-start.31) | collective-permute-done | bytes 524320 | tf_op jit(solution)/shard_map/ppermute | solution.py:331
  211.0 1.8 place.5
  214.6 5.2 %collective-permute-done.32.refs_1_ = bf16[2,16,64,128]{3,2,1,0:T(8,128)(2,1)S(1)} collective-permute-done((bf16[2,16,64,128]{3,2,1,0:T(8,128)(2,1)S(1)}, bf16[2,16,64,128]{3,2,1,0:T(8,128)(2,1)S(1)}, u32[]{:S(2)}, u32[]{:S(2)}) %collective-permute-start.32) | collective-permute-done | bytes 524320 | tf_op jit(solution)/shard_map/ppermute | solution.py:331
  219.8 2.3 collective-permute-start.39
  222.1 4.4 %collective-permute-done.29.refs_1_ = bf16[16,128,128]{2,1,0:T(8,128)(2,1)S(1)} collective-permute-done((bf16[16,128,128]{2,1,0:T(8,128)(2,1)S(1)}, bf16[16,128,128]{2,1,0:T(8,128)(2,1)S(1)}, u32[]{:S(2)}, u32[]{:S(2)}) %collective-permute-start.29) | collective-permute-done | bytes 524320 | tf_op jit(solution)/shard_map/ppermute | solution.py:311
  227.2 1.9 collective-permute-start.34
  230.6 3.1 %collective-permute-done.39.refs_3_ = bf16[2,16,64,128]{3,2,1,0:T(8,128)(2,1)S(1)} collective-permute-done((bf16[2,16,64,128]{3,2,1,0:T(8,128)(2,1)S(1)}, bf16[2,16,64,128]{3,2,1,0:T(8,128)(2,1)S(1)}, u32[]{:S(2)}, u32[]{:S(2)}) %collective-permute-start.39) | collective-permute-done | bytes 524320 | tf_op jit(solution)/shard_map/ppermute | solution.py:331
  233.8 1.8 place.6
  235.7 4.3 %collective-permute-done.34.refs_0_ = bf16[16,128,128]{2,1,0:T(8,128)(2,1)S(1)} collective-permute-done((bf16[16,128,128]{2,1,0:T(8,128)(2,1)S(1)}, bf16[16,128,128]{2,1,0:T(8,128)(2,1)S(1)}, u32[]{:S(2)}, u32[]{:S(2)}) %collective-permute-start.34) | collective-permute-done | bytes 524320 | tf_op jit(solution)/shard_map/ppermute | solution.py:311
  241.6 4.2 %project.7 = (bf16[2,16,64,128]{3,2,1,0:T(8,128)(2,1)S(1)}, bf16[2,16,64,128]{3,2,1,0:T(8,128)(2,1)S(1)}, bf16[2,16,64,128]{3,2,1,0:T(8,128)(2,1)S(1)}, bf16[2,16,64,128]{3,2,1,0:T(8,128)(2,1)S(1)}) custom-call(s32[3]{0:T(128)S(1)} %pad_add_fusion.where_ref, bf16[128,128]{1,0:T(8,128)(2,1)S(1)} %pad_maximum_fusion.weight_ref, f32[128,1]{1,0:T(8,128)S(1)} %copy.52.offset_ref, ...), custom_call_target="tpu_custom_call" | custom-call | flops 268435456 | bytes 4194304 | tf_op jit(solution)/shard_map/project/pallas_call | solution.py:165
  250.9 9.8 %collective-permute-done.36.refs_1_ = bf16[2,16,64,128]{3,2,1,0:T(8,128)(2,1)S(1)} collective-permute-done((bf16[2,16,64,128]{3,2,1,0:T(8,128)(2,1)S(1)}, bf16[2,16,64,128]{3,2,1,0:T(8,128)(2,1)S(1)}, u32[]{:S(2)}, u32[]{:S(2)}) %collective-permute-start.36) | collective-permute-done | bytes 524320 | tf_op jit(solution)/shard_map/ppermute | solution.py:331
  260.7 8.4 %collective-permute-done.37.refs_2_ = bf16[2,16,64,128]{3,2,1,0:T(8,128)(2,1)S(1)} collective-permute-done((bf16[2,16,64,128]{3,2,1,0:T(8,128)(2,1)S(1)}, bf16[2,16,64,128]{3,2,1,0:T(8,128)(2,1)S(1)}, u32[]{:S(2)}, u32[]{:S(2)}) %collective-permute-start.37) | collective-permute-done | bytes 524320 | tf_op jit(solution)/shard_map/ppermute | solution.py:331
  269.1 1.8 place.7
  271.0 2.6 collective-permute-done.42.rows_ref
  (107 shorter events, 38.4 us)
Async XLA Ops:
  7.2 52.3 %all-gather.2.cloned.1.call-start = ((), (), s32[]{:S(2)}) async-start(), calls=%async_computation | async-start | bytes 4718592 | tf_op jit(solution)/shard_map/all_gather | solution.py:271
  7.9 17.0 %collective-permute-start.2 = (bf16[128,2048]{1,0:T(8,128)(2,1)}, bf16[128,2048]{1,0:T(8,128)(2,1)S(1)}, u32[]{:S(2)}, u32[]{:S(2)}) collective-permute-start(bf16[128,2048]{1,0:T(8,128)(2,1)} %refs_0_.7), channel_id=1, source_target_pairs={{0,24},{8,16},{16,8},{24,0},{1,25},{9,17},{17,9},{25,1},{2,26},{10... | collective-permute-start | bytes 1572872 | tf_op jit(solution)/shard_map/ppermute | solution.py:270
  11.9 23.4 %collective-permute-start.1 = (bf16[128,2048]{1,0:T(8,128)(2,1)}, bf16[128,2048]{1,0:T(8,128)(2,1)S(1)}, u32[]{:S(2)}, u32[]{:S(2)}) collective-permute-start(bf16[128,2048]{1,0:T(8,128)(2,1)} %refs_0_.7), channel_id=1, source_target_pairs={{0,16},{8,24},{16,0},{24,8},{1,17},{9,25},{17,1},{25,9},{2,18},{10... | collective-permute-start | bytes 1572872 | tf_op jit(solution)/shard_map/ppermute | solution.py:270
  12.4 23.2 %collective-permute-start = (bf16[128,2048]{1,0:T(8,128)(2,1)}, bf16[128,2048]{1,0:T(8,128)(2,1)S(1)}, u32[]{:S(2)}, u32[]{:S(2)}) collective-permute-start(bf16[128,2048]{1,0:T(8,128)(2,1)} %refs_0_.7), channel_id=1, source_target_pairs={{0,8},{8,0},{16,24},{24,16},{1,9},{9,1},{17,25},{25,17},{2,10},{10... | collective-permute-start | bytes 1572872 | tf_op jit(solution)/shard_map/ppermute | solution.py:270
  67.5 14.1 %collective-permute-start.4 = (bf16[16,128,128]{2,1,0:T(8,128)(2,1)S(1)}, bf16[16,128,128]{2,1,0:T(8,128)(2,1)S(1)}, u32[]{:S(2)}, u32[]{:S(2)}) collective-permute-start(bf16[16,128,128]{2,1,0:T(8,128)(2,1)S(1)} %get-tuple-element.63.refs_3_), channel_id=1, source_target_pairs={{2,0},{4,2},{6,4},{7,6},{5,7},{3,5},{1,3},{0,1},{10,8},{12,10},{14... | collective-permute-start | bytes 1572872 | tf_op jit(solution)/shard_map/ppermute | solution.py:312
  67.8 13.9 %collective-permute-start.3 = (bf16[16,128,128]{2,1,0:T(8,128)(2,1)S(1)}, bf16[16,128,128]{2,1,0:T(8,128)(2,1)S(1)}, u32[]{:S(2)}, u32[]{:S(2)}) collective-permute-start(bf16[16,128,128]{2,1,0:T(8,128)(2,1)S(1)} %get-tuple-element.63.refs_3_), channel_id=1, source_target_pairs={{0,2},{2,4},{4,6},{6,7},{7,5},{5,3},{3,1},{1,0},{8,10},{10,12},{12... | collective-permute-start | bytes 1572872 | tf_op jit(solution)/shard_map/ppermute | solution.py:311
  81.7 12.6 %collective-permute-start.5 = (bf16[16,128,128]{2,1,0:T(8,128)(2,1)S(1)}, bf16[16,128,128]{2,1,0:T(8,128)(2,1)}, u32[]{:S(2)}, u32[]{:S(2)}) collective-permute-start(bf16[16,128,128]{2,1,0:T(8,128)(2,1)S(1)} %collective-permute-done.3.refs_2_), channel_id=1, source_target_pairs={{0,2},{2,4},{4,6},{6,7},{7,5},{5,3},{3,1},{1,0},{8,10},{10,12},{12... | collective-permute-start | bytes 1572872 | tf_op jit(solution)/shard_map/ppermute | solution.py:311
  81.9 13.1 %collective-permute-start.6 = (bf16[16,128,128]{2,1,0:T(8,128)(2,1)S(1)}, bf16[16,128,128]{2,1,0:T(8,128)(2,1)}, u32[]{:S(2)}, u32[]{:S(2)}) collective-permute-start(bf16[16,128,128]{2,1,0:T(8,128)(2,1)S(1)} %collective-permute-done.4.refs_4_), channel_id=1, source_target_pairs={{2,0},{4,2},{6,4},{7,6},{5,7},{3,5},{1,3},{0,1},{10,8},{12,10},{14... | collective-permute-start | bytes 1572872 | tf_op jit(solution)/shard_map/ppermute | solution.py:312
  89.2 71.2 %copy-start.3 = (bf16[16,128,128]{2,1,0:T(8,128)(2,1)}, bf16[16,128,128]{2,1,0:T(8,128)(2,1)S(1)}, u32[]{:S(2)}) copy-start(bf16[16,128,128]{2,1,0:T(8,128)(2,1)S(1)} %get-tuple-element.86.refs_3_) | copy-start | bytes 1572868
  95.0 13.5 %collective-permute-start.7 = (bf16[16,128,128]{2,1,0:T(8,128)(2,1)}, bf16[16,128,128]{2,1,0:T(8,128)(2,1)}, u32[]{:S(2)}, u32[]{:S(2)}) collective-permute-start(bf16[16,128,128]{2,1,0:T(8,128)(2,1)} %collective-permute-done.5.refs_1_), channel_id=1, source_target_pairs={{0,2},{2,4},{4,6},{6,7},{7,5},{5,3},{3,1},{1,0},{8,10},{10,12},{12... | collective-permute-start | bytes 1572872 | tf_op jit(solution)/shard_map/ppermute | solution.py:311
  96.8 12.5 %collective-permute-start.8 = (bf16[16,128,128]{2,1,0:T(8,128)(2,1)}, bf16[16,128,128]{2,1,0:T(8,128)(2,1)}, u32[]{:S(2)}, u32[]{:S(2)}) collective-permute-start(bf16[16,128,128]{2,1,0:T(8,128)(2,1)} %collective-permute-done.6.refs_5_), channel_id=1, source_target_pairs={{2,0},{4,2},{6,4},{7,6},{5,7},{3,5},{1,3},{0,1},{10,8},{12,10},{14... | collective-permute-start | bytes 1572872 | tf_op jit(solution)/shard_map/ppermute | solution.py:312
  105.6 93.7 %copy-start.2 = (bf16[16,128,128]{2,1,0:T(8,128)(2,1)}, bf16[16,128,128]{2,1,0:T(8,128)(2,1)S(1)}, u32[]{:S(2)}) copy-start(bf16[16,128,128]{2,1,0:T(8,128)(2,1)S(1)} %get-tuple-element.99.refs_3_) | copy-start | bytes 1572868
  109.3 14.6 %collective-permute-start.10 = (bf16[16,128,128]{2,1,0:T(8,128)(2,1)}, bf16[16,128,128]{2,1,0:T(8,128)(2,1)S(1)}, u32[]{:S(2)}, u32[]{:S(2)}) collective-permute-start(bf16[16,128,128]{2,1,0:T(8,128)(2,1)} %get-tuple-element.77.refs_3_), channel_id=1, source_target_pairs={{2,0},{4,2},{6,4},{7,6},{5,7},{3,5},{1,3},{0,1},{10,8},{12,10},{14... | collective-permute-start | bytes 1572872 | tf_op jit(solution)/shard_map/ppermute | solution.py:312
  109.3 14.6 %collective-permute-start.9 = (bf16[16,128,128]{2,1,0:T(8,128)(2,1)}, bf16[16,128,128]{2,1,0:T(8,128)(2,1)S(1)}, u32[]{:S(2)}, u32[]{:S(2)}) collective-permute-start(bf16[16,128,128]{2,1,0:T(8,128)(2,1)} %get-tuple-element.77.refs_3_), channel_id=1, source_target_pairs={{0,2},{2,4},{4,6},{6,7},{7,5},{5,3},{3,1},{1,0},{8,10},{10,12},{12... | collective-permute-start | bytes 1572872 | tf_op jit(solution)/shard_map/ppermute | solution.py:311
  118.7 12.3 %collective-permute-start.13 = (bf16[2,16,64,128]{3,2,1,0:T(8,128)(2,1)S(1)}, bf16[2,16,64,128]{3,2,1,0:T(8,128)(2,1)S(1)}, u32[]{:S(2)}, u32[]{:S(2)}) collective-permute-start(bf16[2,16,64,128]{3,2,1,0:T(8,128)(2,1)S(1)} %get-tuple-element.82), channel_id=1, source_target_pairs={{0,8},{8,0},{16,24},{24,16},{1,9},{9,1},{17,25},{25,17},{2,10},{10... | collective-permute-start | bytes 1572872 | tf_op jit(solution)/shard_map/ppermute | solution.py:331
  120.2 12.0 %collective-permute-start.14 = (bf16[2,16,64,128]{3,2,1,0:T(8,128)(2,1)S(1)}, bf16[2,16,64,128]{3,2,1,0:T(8,128)(2,1)S(1)}, u32[]{:S(2)}, u32[]{:S(2)}) collective-permute-start(bf16[2,16,64,128]{3,2,1,0:T(8,128)(2,1)S(1)} %get-tuple-element.83), channel_id=1, source_target_pairs={{0,16},{8,24},{16,0},{24,8},{1,17},{9,25},{17,1},{25,9},{2,18},{10... | collective-permute-start | bytes 1572872 | tf_op jit(solution)/shard_map/ppermute | solution.py:331
  123.9 32.3 %copy-start.9 = (bf16[16,128,128]{2,1,0:T(8,128)(2,1)}, bf16[16,128,128]{2,1,0:T(8,128)(2,1)S(1)}, u32[]{:S(2)}) copy-start(bf16[16,128,128]{2,1,0:T(8,128)(2,1)S(1)} %collective-permute-done.10.refs_4_) | copy-start | bytes 1572868
  123.9 13.6 %collective-permute-start.11 = (bf16[16,128,128]{2,1,0:T(8,128)(2,1)S(1)}, bf16[16,128,128]{2,1,0:T(8,128)(2,1)S(1)}, u32[]{:S(2)}, u32[]{:S(2)}) collective-permute-start(bf16[16,128,128]{2,1,0:T(8,128)(2,1)S(1)} %collective-permute-done.9.refs_2_), channel_id=1, source_target_pairs={{0,2},{2,4},{4,6},{6,7},{7,5},{5,3},{3,1},{1,0},{8,10},{10,12},{12... | collective-permute-start | bytes 1572872 | tf_op jit(solution)/shard_map/ppermute | solution.py:311
  125.7 12.5 %collective-permute-start.12 = (bf16[16,128,128]{2,1,0:T(8,128)(2,1)S(1)}, bf16[16,128,128]{2,1,0:T(8,128)(2,1)S(1)}, u32[]{:S(2)}, u32[]{:S(2)}) collective-permute-start(bf16[16,128,128]{2,1,0:T(8,128)(2,1)S(1)} %collective-permute-done.10.refs_4_), channel_id=1, source_target_pairs={{2,0},{4,2},{6,4},{7,6},{5,7},{3,5},{1,3},{0,1},{10,8},{12,10},{14... | collective-permute-start | bytes 1572872 | tf_op jit(solution)/shard_map/ppermute | solution.py:312
  138.2 12.8 %collective-permute-start.15 = (bf16[16,128,128]{2,1,0:T(8,128)(2,1)S(1)}, bf16[16,128,128]{2,1,0:T(8,128)(2,1)S(1)}, u32[]{:S(2)}, u32[]{:S(2)}) collective-permute-start(bf16[16,128,128]{2,1,0:T(8,128)(2,1)S(1)} %collective-permute-done.11.refs_1_), channel_id=1, source_target_pairs={{0,2},{2,4},{4,6},{6,7},{7,5},{5,3},{3,1},{1,0},{8,10},{10,12},{12... | collective-permute-start | bytes 1572872 | tf_op jit(solution)/shard_map/ppermute | solution.py:311
  140.0 11.8 %collective-permute-start.16 = (bf16[16,128,128]{2,1,0:T(8,128)(2,1)S(1)}, bf16[16,128,128]{2,1,0:T(8,128)(2,1)S(1)}, u32[]{:S(2)}, u32[]{:S(2)}) collective-permute-start(bf16[16,128,128]{2,1,0:T(8,128)(2,1)S(1)} %collective-permute-done.12.refs_5_), channel_id=1, source_target_pairs={{2,0},{4,2},{6,4},{7,6},{5,7},{3,5},{1,3},{0,1},{10,8},{12,10},{14... | collective-permute-start | bytes 1572872 | tf_op jit(solution)/shard_map/ppermute | solution.py:312
  151.7 14.7 %collective-permute-start.18 = (bf16[16,128,128]{2,1,0:T(8,128)(2,1)S(1)}, bf16[16,128,128]{2,1,0:T(8,128)(2,1)S(1)}, u32[]{:S(2)}, u32[]{:S(2)}) collective-permute-start(bf16[16,128,128]{2,1,0:T(8,128)(2,1)S(1)} %get-tuple-element.86.refs_3_), channel_id=1, source_target_pairs={{2,0},{4,2},{6,4},{7,6},{5,7},{3,5},{1,3},{0,1},{10,8},{12,10},{14... | collective-permute-start | bytes 1572872 | tf_op jit(solution)/shard_map/ppermute | solution.py:312
  151.7 14.7 %collective-permute-start.17 = (bf16[16,128,128]{2,1,0:T(8,128)(2,1)S(1)}, bf16[16,128,128]{2,1,0:T(8,128)(2,1)S(1)}, u32[]{:S(2)}, u32[]{:S(2)}) collective-permute-start(bf16[16,128,128]{2,1,0:T(8,128)(2,1)S(1)} %get-tuple-element.86.refs_3_), channel_id=1, source_target_pairs={{0,2},{2,4},{4,6},{6,7},{7,5},{5,3},{3,1},{1,0},{8,10},{10,12},{12... | collective-permute-start | bytes 1572872 | tf_op jit(solution)/shard_map/ppermute | solution.py:311
  153.8 15.8 %collective-permute-start.21 = (bf16[2,16,64,128]{3,2,1,0:T(8,128)(2,1)S(1)}, bf16[2,16,64,128]{3,2,1,0:T(8,128)(2,1)S(1)}, u32[]{:S(2)}, u32[]{:S(2)}) collective-permute-start(bf16[2,16,64,128]{3,2,1,0:T(8,128)(2,1)S(1)} %get-tuple-element.93), channel_id=1, source_target_pairs={{0,24},{8,16},{16,8},{24,0},{1,25},{9,17},{17,9},{25,1},{2,26},{10... | collective-permute-start | bytes 1572872 | tf_op jit(solution)/shard_map/ppermute | solution.py:331
  160.4 17.9 %collective-permute-start.22 = (bf16[2,16,64,128]{3,2,1,0:T(8,128)(2,1)S(1)}, bf16[2,16,64,128]{3,2,1,0:T(8,128)(2,1)S(1)}, u32[]{:S(2)}, u32[]{:S(2)}) collective-permute-start(bf16[2,16,64,128]{3,2,1,0:T(8,128)(2,1)S(1)} %get-tuple-element.95), channel_id=1, source_target_pairs={{0,8},{8,0},{16,24},{24,16},{1,9},{9,1},{17,25},{25,17},{2,10},{10... | collective-permute-start | bytes 1572872 | tf_op jit(solution)/shard_map/ppermute | solution.py:331
  161.0 17.3 %collective-permute-start.23 = (bf16[2,16,64,128]{3,2,1,0:T(8,128)(2,1)S(1)}, bf16[2,16,64,128]{3,2,1,0:T(8,128)(2,1)S(1)}, u32[]{:S(2)}, u32[]{:S(2)}) collective-permute-start(bf16[2,16,64,128]{3,2,1,0:T(8,128)(2,1)S(1)} %get-tuple-element.96), channel_id=1, source_target_pairs={{0,16},{8,24},{16,0},{24,8},{1,17},{9,25},{17,1},{25,9},{2,18},{10... | collective-permute-start | bytes 1572872 | tf_op jit(solution)/shard_map/ppermute | solution.py:331
  166.4 32.8 %copy-start.10 = (bf16[16,128,128]{2,1,0:T(8,128)(2,1)}, bf16[16,128,128]{2,1,0:T(8,128)(2,1)S(1)}, u32[]{:S(2)}) copy-start(bf16[16,128,128]{2,1,0:T(8,128)(2,1)S(1)} %collective-permute-done.18.refs_4_) | copy-start | bytes 1572868
  166.4 13.1 %collective-permute-start.19 = (bf16[16,128,128]{2,1,0:T(8,128)(2,1)S(1)}, bf16[16,128,128]{2,1,0:T(8,128)(2,1)S(1)}, u32[]{:S(2)}, u32[]{:S(2)}) collective-permute-start(bf16[16,128,128]{2,1,0:T(8,128)(2,1)S(1)} %collective-permute-done.17.refs_2_), channel_id=1, source_target_pairs={{0,2},{2,4},{4,6},{6,7},{7,5},{5,3},{3,1},{1,0},{8,10},{10,12},{12... | collective-permute-start | bytes 1572872 | tf_op jit(solution)/shard_map/ppermute | solution.py:311
  168.1 12.1 %collective-permute-start.20 = (bf16[16,128,128]{2,1,0:T(8,128)(2,1)S(1)}, bf16[16,128,128]{2,1,0:T(8,128)(2,1)S(1)}, u32[]{:S(2)}, u32[]{:S(2)}) collective-permute-start(bf16[16,128,128]{2,1,0:T(8,128)(2,1)S(1)} %collective-permute-done.18.refs_4_), channel_id=1, source_target_pairs={{2,0},{4,2},{6,4},{7,6},{5,7},{3,5},{1,3},{0,1},{10,8},{12,10},{14... | collective-permute-start | bytes 1572872 | tf_op jit(solution)/shard_map/ppermute | solution.py:312
  171.4 10.5 %collective-permute-start.26 = (bf16[16,64,512]{2,1,0:T(8,128)(2,1)S(1)}, bf16[16,64,512]{2,1,0:T(8,128)(2,1)S(1)}, u32[]{:S(2)}, u32[]{:S(2)}) collective-permute-start(bf16[16,64,512]{2,1,0:T(8,128)(2,1)S(1)} %get-tuple-element.94), channel_id=1, source_target_pairs={{0,1},{1,0},{2,3},{3,2},{4,5},{5,4},{6,7},{7,6},{8,9},{9,8},{10,11... | collective-permute-start | bytes 3145736 | tf_op jit(solution)/shard_map/ppermute | solution.py:337
  180.2 12.2 %collective-permute-start.24 = (bf16[16,128,128]{2,1,0:T(8,128)(2,1)S(1)}, bf16[16,128,128]{2,1,0:T(8,128)(2,1)S(1)}, u32[]{:S(2)}, u32[]{:S(2)}) collective-permute-start(bf16[16,128,128]{2,1,0:T(8,128)(2,1)S(1)} %collective-permute-done.19.refs_1_), channel_id=1, source_target_pairs={{0,2},{2,4},{4,6},{6,7},{7,5},{5,3},{3,1},{1,0},{8,10},{10,12},{12... | collective-permute-start | bytes 1572872 | tf_op jit(solution)/shard_map/ppermute | solution.py:311
  182.0 11.2 %collective-permute-start.25 = (bf16[16,128,128]{2,1,0:T(8,128)(2,1)S(1)}, bf16[16,128,128]{2,1,0:T(8,128)(2,1)S(1)}, u32[]{:S(2)}, u32[]{:S(2)}) collective-permute-start(bf16[16,128,128]{2,1,0:T(8,128)(2,1)S(1)} %collective-permute-done.20.refs_5_), channel_id=1, source_target_pairs={{2,0},{4,2},{6,4},{7,6},{5,7},{3,5},{1,3},{0,1},{10,8},{12,10},{14... | collective-permute-start | bytes 1572872 | tf_op jit(solution)/shard_map/ppermute | solution.py:312
  193.1 14.0 %collective-permute-start.28 = (bf16[16,128,128]{2,1,0:T(8,128)(2,1)S(1)}, bf16[16,128,128]{2,1,0:T(8,128)(2,1)S(1)}, u32[]{:S(2)}, u32[]{:S(2)}) collective-permute-start(bf16[16,128,128]{2,1,0:T(8,128)(2,1)S(1)} %get-tuple-element.99.refs_3_), channel_id=1, source_target_pairs={{2,0},{4,2},{6,4},{7,6},{5,7},{3,5},{1,3},{0,1},{10,8},{12,10},{14... | collective-permute-start | bytes 1572872 | tf_op jit(solution)/shard_map/ppermute | solution.py:312
  193.2 14.0 %collective-permute-start.27 = (bf16[16,128,128]{2,1,0:T(8,128)(2,1)S(1)}, bf16[16,128,128]{2,1,0:T(8,128)(2,1)S(1)}, u32[]{:S(2)}, u32[]{:S(2)}) collective-permute-start(bf16[16,128,128]{2,1,0:T(8,128)(2,1)S(1)} %get-tuple-element.99.refs_3_), channel_id=1, source_target_pairs={{0,2},{2,4},{4,6},{6,7},{7,5},{5,3},{3,1},{1,0},{8,10},{10,12},{12... | collective-permute-start | bytes 1572872 | tf_op jit(solution)/shard_map/ppermute | solution.py:311
  195.2 15.8 %collective-permute-start.31 = (bf16[2,16,64,128]{3,2,1,0:T(8,128)(2,1)S(1)}, bf16[2,16,64,128]{3,2,1,0:T(8,128)(2,1)S(1)}, u32[]{:S(2)}, u32[]{:S(2)}) collective-permute-start(bf16[2,16,64,128]{3,2,1,0:T(8,128)(2,1)S(1)} %get-tuple-element.106), channel_id=1, source_target_pairs={{0,24},{8,16},{16,8},{24,0},{1,25},{9,17},{17,9},{25,1},{2,26},{10... | collective-permute-start | bytes 1572872 | tf_op jit(solution)/shard_map/ppermute | solution.py:331
  203.7 16.1 %collective-permute-start.32 = (bf16[2,16,64,128]{3,2,1,0:T(8,128)(2,1)S(1)}, bf16[2,16,64,128]{3,2,1,0:T(8,128)(2,1)S(1)}, u32[]{:S(2)}, u32[]{:S(2)}) collective-permute-start(bf16[2,16,64,128]{3,2,1,0:T(8,128)(2,1)S(1)} %get-tuple-element.109), channel_id=1, source_target_pairs={{0,8},{8,0},{16,24},{24,16},{1,9},{9,1},{17,25},{25,17},{2,10},{10... | collective-permute-start | bytes 1572872 | tf_op jit(solution)/shard_map/ppermute | solution.py:331
  204.3 15.5 %collective-permute-start.33 = (bf16[2,16,64,128]{3,2,1,0:T(8,128)(2,1)S(1)}, bf16[2,16,64,128]{3,2,1,0:T(8,128)(2,1)S(1)}, u32[]{:S(2)}, u32[]{:S(2)}) collective-permute-start(bf16[2,16,64,128]{3,2,1,0:T(8,128)(2,1)S(1)} %get-tuple-element.110), channel_id=1, source_target_pairs={{0,16},{8,24},{16,0},{24,8},{1,17},{9,25},{17,1},{25,9},{2,18},{10... | collective-permute-start | bytes 1572872 | tf_op jit(solution)/shard_map/ppermute | solution.py:331
  212.8 16.3 %collective-permute-start.40 = (bf16[16,64,512]{2,1,0:T(8,128)(2,1)S(1)}, bf16[16,64,512]{2,1,0:T(8,128)(2,1)S(1)}, u32[]{:S(2)}, u32[]{:S(2)}) collective-permute-start(bf16[16,64,512]{2,1,0:T(8,128)(2,1)S(1)} %get-tuple-element.108), channel_id=1, source_target_pairs={{0,1},{1,0},{2,3},{3,2},{4,5},{5,4},{6,7},{7,6},{8,9},{9,8},{10,11... | collective-permute-start | bytes 3145736 | tf_op jit(solution)/shard_map/ppermute | solution.py:337
  212.9 13.6 %collective-permute-start.29 = (bf16[16,128,128]{2,1,0:T(8,128)(2,1)S(1)}, bf16[16,128,128]{2,1,0:T(8,128)(2,1)S(1)}, u32[]{:S(2)}, u32[]{:S(2)}) collective-permute-start(bf16[16,128,128]{2,1,0:T(8,128)(2,1)S(1)} %collective-permute-done.27.refs_2_), channel_id=1, source_target_pairs={{0,2},{2,4},{4,6},{6,7},{7,5},{5,3},{3,1},{1,0},{8,10},{10,12},{12... | collective-permute-start | bytes 1572872 | tf_op jit(solution)/shard_map/ppermute | solution.py:311
  214.6 12.6 %collective-permute-start.30 = (bf16[16,128,128]{2,1,0:T(8,128)(2,1)S(1)}, bf16[16,128,128]{2,1,0:T(8,128)(2,1)S(1)}, u32[]{:S(2)}, u32[]{:S(2)}) collective-permute-start(bf16[16,128,128]{2,1,0:T(8,128)(2,1)S(1)} %collective-permute-done.28.refs_4_), channel_id=1, source_target_pairs={{2,0},{4,2},{6,4},{7,6},{5,7},{3,5},{1,3},{0,1},{10,8},{12,10},{14... | collective-permute-start | bytes 1572872 | tf_op jit(solution)/shard_map/ppermute | solution.py:312
  219.8 14.0 %collective-permute-start.39 = (bf16[2,16,64,128]{3,2,1,0:T(8,128)(2,1)S(1)}, bf16[2,16,64,128]{3,2,1,0:T(8,128)(2,1)S(1)}, u32[]{:S(2)}, u32[]{:S(2)}) collective-permute-start(bf16[2,16,64,128]{3,2,1,0:T(8,128)(2,1)S(1)} %get-tuple-element.118), channel_id=1, source_target_pairs={{0,24},{8,16},{16,8},{24,0},{1,25},{9,17},{17,9},{25,1},{2,26},{10... | collective-permute-start | bytes 1572872 | tf_op jit(solution)/shard_map/ppermute | solution.py:331
  227.2 12.8 %collective-permute-start.34 = (bf16[16,128,128]{2,1,0:T(8,128)(2,1)S(1)}, bf16[16,128,128]{2,1,0:T(8,128)(2,1)S(1)}, u32[]{:S(2)}, u32[]{:S(2)}) collective-permute-start(bf16[16,128,128]{2,1,0:T(8,128)(2,1)S(1)} %collective-permute-done.29.refs_1_), channel_id=1, source_target_pairs={{0,2},{2,4},{4,6},{6,7},{7,5},{5,3},{3,1},{1,0},{8,10},{10,12},{12... | collective-permute-start | bytes 1572872 | tf_op jit(solution)/shard_map/ppermute | solution.py:311
  229.1 11.7 %collective-permute-start.35 = (bf16[16,128,128]{2,1,0:T(8,128)(2,1)S(1)}, bf16[16,128,128]{2,1,0:T(8,128)(2,1)S(1)}, u32[]{:S(2)}, u32[]{:S(2)}) collective-permute-start(bf16[16,128,128]{2,1,0:T(8,128)(2,1)S(1)} %collective-permute-done.30.refs_5_), channel_id=1, source_target_pairs={{2,0},{4,2},{6,4},{7,6},{5,7},{3,5},{1,3},{0,1},{10,8},{12,10},{14... | collective-permute-start | bytes 1572872 | tf_op jit(solution)/shard_map/ppermute | solution.py:312
  235.6 13.7 %collective-permute-start.41 = (bf16[16,64,512]{2,1,0:T(8,128)(2,1)S(1)}, bf16[16,64,512]{2,1,0:T(8,128)(2,1)S(1)}, u32[]{:S(2)}, u32[]{:S(2)}) collective-permute-start(bf16[16,64,512]{2,1,0:T(8,128)(2,1)S(1)} %get-tuple-element.120), channel_id=1, source_target_pairs={{0,1},{1,0},{2,3},{3,2},{4,5},{5,4},{6,7},{7,6},{8,9},{9,8},{10,11... | collective-permute-start | bytes 3145736 | tf_op jit(solution)/shard_map/ppermute | solution.py:337
  245.8 14.9 %collective-permute-start.36 = (bf16[2,16,64,128]{3,2,1,0:T(8,128)(2,1)S(1)}, bf16[2,16,64,128]{3,2,1,0:T(8,128)(2,1)S(1)}, u32[]{:S(2)}, u32[]{:S(2)}) collective-permute-start(bf16[2,16,64,128]{3,2,1,0:T(8,128)(2,1)S(1)} %get-tuple-element.114), channel_id=1, source_target_pairs={{0,8},{8,0},{16,24},{24,16},{1,9},{9,1},{17,25},{25,17},{2,10},{10... | collective-permute-start | bytes 1572872 | tf_op jit(solution)/shard_map/ppermute | solution.py:331
  247.4 21.7 %collective-permute-start.37 = (bf16[2,16,64,128]{3,2,1,0:T(8,128)(2,1)S(1)}, bf16[2,16,64,128]{3,2,1,0:T(8,128)(2,1)S(1)}, u32[]{:S(2)}, u32[]{:S(2)}) collective-permute-start(bf16[2,16,64,128]{3,2,1,0:T(8,128)(2,1)S(1)} %get-tuple-element.115), channel_id=1, source_target_pairs={{0,16},{8,24},{16,0},{24,8},{1,17},{9,25},{17,1},{25,9},{2,18},{10... | collective-permute-start | bytes 1572872 | tf_op jit(solution)/shard_map/ppermute | solution.py:331
  248.9 20.2 %collective-permute-start.38 = (bf16[2,16,64,128]{3,2,1,0:T(8,128)(2,1)S(1)}, bf16[2,16,64,128]{3,2,1,0:T(8,128)(2,1)S(1)}, u32[]{:S(2)}, u32[]{:S(2)}) collective-permute-start(bf16[2,16,64,128]{3,2,1,0:T(8,128)(2,1)S(1)} %get-tuple-element.116), channel_id=1, source_target_pairs={{0,24},{8,16},{16,8},{24,0},{1,25},{9,17},{17,9},{25,1},{2,26},{10... | collective-permute-start | bytes 1572872 | tf_op jit(solution)/shard_map/ppermute | solution.py:331
  271.0 2.7 collective-permute-start.42
  (14 other events, 187.9 us)
Sparse Core Ops, SparseCore 0:
  9.6 49.8 all-gather.1

commit v5 on v3

--- a/solution.py
+++ b/solution.py
@@ -292,6 +292,7 @@
     state = {"new_pair": None, "result": None}
     tiles = [{} for _ in range(count)]
     moved = [None] * count
+    handed = [None] * count
 
     def after(value, *others):
         return lax.optimization_barrier((value, others))[0]
@@ -323,12 +324,18 @@
             )
         )
 
-    def send(part, d):
-        moved[part][d] = lax.ppermute(moved[part][d], "row", [(a, a ^ d) for a in range(parts)])
-
-    def place(part):
-        state["result"], other = place_call(where, moved[part], state["result"], part, parts, tile_cols)
-        swapped[part] = lax.ppermute(other, "col", [(c, c ^ 1) for c in range(cols)])
+    def send(part, d, *others):
+        piece = after(moved[part][d], *others)
+        moved[part][d] = lax.ppermute(piece, "row", [(a, a ^ d) for a in range(parts)])
+
+    def place(part, *others):
+        state["result"], handed[part] = place_call(
+            after(where, *others), moved[part], state["result"], part, parts, tile_cols
+        )
+
+    def exchange(part, *others):
+        handed[part] = after(handed[part], *others)
+        swapped[part] = lax.ppermute(handed[part], "col", [(c, c ^ 1) for c in range(cols)])
 
     def put(part):
         state["result"] = put_call(where, swapped[part], state["result"], part, tile_cols)
@@ -337,41 +344,43 @@
         ((part, s) for part in range(count) for s in range(1, line)),
         key=lambda step: (step[0] + step[1], step[0]),
     )
+    first = [order.index((part, 1)) for part in range(count)]
+    last = [order.index((part, line - 1)) for part in range(count)]
+    gates = [[] for _ in range(len(order) + 2)]
     swapped = [None] * count
     done = []
-    pending = []
+
     update(0)
-    updated = 1
     for index, (part, s) in enumerate(order):
-        others = list(done[index - 2]) if index >= 2 else []
-        while updated <= part:
-            update(updated)
-            updated += 1
-        if pending and index >= pending[0][0]:
-            _, owner, d = pending.pop(0)
-            others.append(moved[owner][d])
-        if part == count - 1 and s == line - 1:
-            for owner in range(count - 3):
-                if swapped[owner] is not None:
-                    others.append(swapped[owner])
-        shift(part, s, *others)
-        done.append((tiles[part][-s], tiles[part][s]))
-        if updated < count and any(p == updated for p, _ in order[index + 2 : index + 4]):
-            update(updated, *done[index - 1 if index else 0])
-            updated += 1
-        if s == line - 1 and part < count - 1:
-            project(part)
+        shift(part, s, *gates[index])
+        done.append([tiles[part][-s], tiles[part][s]])
+        gates[index + 2] += done[index]
+        before = done[index - 1] if index else []
+        for p in range(1, count):
+            if index == max(0, first[p] - 2):
+                update(p, *before)
+                gates[index + 2].append(tiles[p][0])
+        for p in range(count - 1):
+            if index == last[p] + 1:
+                project(p, *before)
+                gates[min(index + 2, len(order) - 1)].append(moved[p][0])
             for d in range(1, parts):
-                send(part, d)
-                pending.append((index + 2 + d, part, d))
-            place(part)
-    project(count - 1, *[w for w in swapped[:-2] if w is not None])
+                if index == last[p] + d and p < count - 2:
+                    send(p, d, *before)
+                    gates[index + 2].append(moved[p][d])
+            if p < count - 2 and index == min(last[p] + parts + 1, len(order) - 1):
+                place(p, *before)
+                gates[min(index + 2, len(order) - 1)].append(handed[p])
+    for d in range(1, parts):
+        send(count - 2, d, *(moved[count - 2][1:3] if d > 2 else []))
+    project(count - 1, *moved[count - 2][1:])
     for d in range(1, parts):
         send(count - 1, d)
-    for part in range(count - 1):
+    place(count - 2)
+    place(count - 1, *handed[:-1])
+    for part in range(count):
+        exchange(part, *moved[-1][1:])
         put(part)
-    place(count - 1)
-    put(count - 1)
     return (state["new_pair"], state["result"])
 
 

time: 280 us -> 269 us (0.961)
  waiting for transfers between devices: 160 us -> 148 us
    ppermute x12, waiting for transfers between devices: 50.6 us -> 31.8 us  [shift(): here[-s] = lax.ppermute(after(here[-(s - 1)], *others), 'col', onward)]
    ppermute x12, waiting for transfers between devices: 16.5 us -> 33.5 us  [shift(): here[s] = lax.ppermute(after(here[s - 1], *others), 'col', back)]
    ppermute x16, waiting for transfers between devices: 47.4 us -> 38.2 us  [the longest x12 38.1 us: send(): lax.ppermute(piece, 'row', [(a, a ^ d) for a in range(parts)])]
    ppermute x16, starting transfers between devices: 16.5 us -> 12.8 us  [the longest x12 11.7 us: send(): lax.ppermute(piece, 'row', [(a, a ^ d) for a in range(parts)])]
    ppermute x12, starting transfers between devices: 18 us -> 21.4 us  [shift(): here[-s] = lax.ppermute(after(here[-(s - 1)], *others), 'col', onward)]
  transfers between devices with their start and end apart: 44 -> 44, of which waited for: 25 -> 26; matrix products, arithmetic and copies ran while one was open for 1% -> 1% of each run, Pallas kernels for 17% -> 17%
where the time goes in v5:
time: 269 us; the launch traced here: 268 us
  waiting for transfers between devices  148 us (55%)
  Pallas kernels  57.7 us (21%)
  starting transfers between devices  40 us (15%)
  between operations  14.4 us (5%)
  local copies, waits for them, and re-layouts  6.65 us (2%)
    ppermute x12, waiting for transfers between devices, send(): lax.ppermute(piece, 'row', [(a, a ^ d) for a in range(parts)])  38.1 us
    ppermute x12, waiting for transfers between devices, shift(): here[s] = lax.ppermute(after(here[s - 1], *others), 'col', back)  33.5 us
    ppermute x12, waiting for transfers between devices, shift(): here[-s] = lax.ppermute(after(here[-(s - 1)], *others), 'col', onward)  31.8 us
    pallas_call x4, Pallas kernels, update_call(): pl.pallas_call(functools.partial(update_kernel, parts, part), grid=(1,),...  27.9 us
    all_gather x1, waiting for transfers between devices, shards(): left = lax.all_gather(alignment_left, 'col', axis=0, tiled=True)  23.7 us
    ppermute x12, starting transfers between devices, shift(): here[-s] = lax.ppermute(after(here[-(s - 1)], *others), 'col', onward)  21.4 us
    ppermute x3, waiting for transfers between devices, shards(): lax.ppermute(alignment_right, 'row', [(a, a ^ d) for a in range(parts)])  20.6 us
    pallas_call x4, Pallas kernels, project_call(): pl.pallas_call(functools.partial(project_kernel, line, parts), in_specs=[...  16.3 us
  transfers between devices with their start and end apart: 44, of which 26 were waited for; matrix products, arithmetic and copies ran while one was open for 1% of the time, Pallas kernels for 17%

profile of v5, /device:TPU:0, one launch (start us, length us, event | category | flops | bytes accessed | tf_op | source)
XLA Modules:
  0.0 267.5 jit_solution(14058987374076950385)
XLA Ops:
  7.9 3.0 %collective-permute-start = (bf16[128,2048]{1,0:T(8,128)(2,1)}, bf16[128,2048]{1,0:T(8,128)(2,1)S(1)}, u32[]{:S(2)}, u32[]{:S(2)}) collective-permute-start(bf16[128,2048]{1,0:T(8,128)(2,1)} %refs_0_.7), channel_id=1, source_target_pairs={{0,8},{8,0},{16,24},{24,16},{1,9},{9,1},{17,25},{25,17},{2,10},{10... | collective-permute-start | bytes 1572872 | tf_op jit(solution)/shard_map/ppermute | solution.py:270
  15.2 8.7 %collective-permute-done.refs_1_ = bf16[128,2048]{1,0:T(8,128)(2,1)S(1)} collective-permute-done((bf16[128,2048]{1,0:T(8,128)(2,1)}, bf16[128,2048]{1,0:T(8,128)(2,1)S(1)}, u32[]{:S(2)}, u32[]{:S(2)}) %collective-permute-start) | collective-permute-done | bytes 524320 | tf_op jit(solution)/shard_map/ppermute | solution.py:270
  23.9 11.9 %collective-permute-done.1.refs_2_ = bf16[128,2048]{1,0:T(8,128)(2,1)S(1)} collective-permute-done((bf16[128,2048]{1,0:T(8,128)(2,1)}, bf16[128,2048]{1,0:T(8,128)(2,1)S(1)}, u32[]{:S(2)}, u32[]{:S(2)}) %collective-permute-start.1) | collective-permute-done | bytes 524320 | tf_op jit(solution)/shard_map/ppermute | solution.py:270
  35.7 23.7 %all-gather.2.cloned.1.call-done.left_ref = bf16[128,16384]{1,0:T(8,128)(2,1)} async-done(((bf16[16,16384]{1,0:T(8,128)(2,1)}), bf16[128,16384]{1,0:T(8,128)(2,1)}) %all-gather.2.cloned.1.call-update) | async-done | bytes 4194320 | tf_op jit(solution)/shard_map/all_gather | solution.py:271
  60.5 7.0 %update.4 = (bf16[128,64,128]{2,1,0:T(8,128)(2,1)}, bf16[16,128,128]{2,1,0:T(8,128)(2,1)S(1)}) custom-call(s32[3]{0:T(128)S(1)} %pad_add_fusion.where_ref, bf16[128,16384]{1,0:T(8,128)(2,1)} %all-gather.2.cloned.1.call-done.left_ref, bf16[128,2048]{1,0:T(8,128)(2,1)S(1)} %copy-done, bf16[128,2048]{1,0:T(8,128)(2,1)S(1)} %collective-permute-done.refs_1_, ...), custom_call_target="tpu_custom_call" | custom-call | flops 2684354560 | bytes 8388608 | tf_op jit(solution)/shard_map/update/pallas_call | solution.py:105
  68.6 10.3 %collective-permute-done.3.refs_2_ = bf16[16,128,128]{2,1,0:T(8,128)(2,1)} collective-permute-done((bf16[16,128,128]{2,1,0:T(8,128)(2,1)S(1)}, bf16[16,128,128]{2,1,0:T(8,128)(2,1)}, u32[]{:S(2)}, u32[]{:S(2)}) %collective-permute-start.3) | collective-permute-done | bytes 524320 | tf_op jit(solution)/shard_map/ppermute | solution.py:311
  78.8 2.6 collective-permute-start.7
  81.7 6.9 %update.5 = (bf16[128,64,128]{2,1,0:T(8,128)(2,1)}, bf16[16,128,128]{2,1,0:T(8,128)(2,1)S(1)}) custom-call(s32[3]{0:T(128)S(1)} %pad_add_fusion.where_ref, bf16[128,16384]{1,0:T(8,128)(2,1)} %all-gather.2.cloned.1.call-done.left_ref, bf16[128,2048]{1,0:T(8,128)(2,1)S(1)} %copy-done.1, ...), custom_call_target="tpu_custom_call", output_to_operand_aliasing={{0}: (10, {})} | custom-call | flops 2684354560 | bytes 8388608 | tf_op jit(solution)/shard_map/update/pallas_call | solution.py:105
  88.7 2.3 collective-permute-start.5
  91.0 3.1 %collective-permute-done.7.refs_1_ = bf16[16,128,128]{2,1,0:T(8,128)(2,1)} collective-permute-done((bf16[16,128,128]{2,1,0:T(8,128)(2,1)}, bf16[16,128,128]{2,1,0:T(8,128)(2,1)}, u32[]{:S(2)}, u32[]{:S(2)}) %collective-permute-start.7) | collective-permute-done | bytes 524320 | tf_op jit(solution)/shard_map/ppermute | solution.py:311
  94.1 3.0 %collective-permute-done.8.refs_5_ = bf16[16,128,128]{2,1,0:T(8,128)(2,1)} collective-permute-done((bf16[16,128,128]{2,1,0:T(8,128)(2,1)}, bf16[16,128,128]{2,1,0:T(8,128)(2,1)}, u32[]{:S(2)}, u32[]{:S(2)}) %collective-permute-start.8) | collective-permute-done | bytes 524320 | tf_op jit(solution)/shard_map/ppermute | solution.py:312
  97.0 2.0 collective-permute-start.9
  99.8 5.3 %collective-permute-done.5.refs_2_ = bf16[16,128,128]{2,1,0:T(8,128)(2,1)} collective-permute-done((bf16[16,128,128]{2,1,0:T(8,128)(2,1)S(1)}, bf16[16,128,128]{2,1,0:T(8,128)(2,1)}, u32[]{:S(2)}, u32[]{:S(2)}) %collective-permute-start.5) | collective-permute-done | bytes 524320 | tf_op jit(solution)/shard_map/ppermute | solution.py:311
  105.2 3.1 %collective-permute-done.6.refs_4_ = bf16[16,128,128]{2,1,0:T(8,128)(2,1)} collective-permute-done((bf16[16,128,128]{2,1,0:T(8,128)(2,1)S(1)}, bf16[16,128,128]{2,1,0:T(8,128)(2,1)}, u32[]{:S(2)}, u32[]{:S(2)}) %collective-permute-start.6) | collective-permute-done | bytes 524320 | tf_op jit(solution)/shard_map/ppermute | solution.py:312
  108.8 10.7 %collective-permute-done.10.refs_6_ = bf16[16,128,128]{2,1,0:T(8,128)(2,1)} collective-permute-done((bf16[16,128,128]{2,1,0:T(8,128)(2,1)}, bf16[16,128,128]{2,1,0:T(8,128)(2,1)}, u32[]{:S(2)}, u32[]{:S(2)}) %collective-permute-start.10) | collective-permute-done | bytes 524320 | tf_op jit(solution)/shard_map/ppermute | solution.py:312
  119.5 3.8 %project.4 = (bf16[2,16,64,128]{3,2,1,0:T(8,128)(2,1)S(1)}, bf16[2,16,64,128]{3,2,1,0:T(8,128)(2,1)S(1)}, bf16[2,16,64,128]{3,2,1,0:T(8,128)(2,1)S(1)}, bf16[2,16,64,128]{3,2,1,0:T(8,128)(2,1)S(1)}) custom-call(s32[3]{0:T(128)S(1)} %pad_add_fusion.where_ref, bf16[128,128]{1,0:T(8,128)(2,1)S(1)} %pad_maximum_fusion.weight_ref, f32[128,1]{1,0:T(8,128)S(1)} %copy.46.offset_ref, ...), custom_call_target="tpu_custom_call" | custom-call | flops 268435456 | bytes 4194304 | tf_op jit(solution)/shard_map/project/pallas_call | solution.py:165
  124.8 7.1 %update.6 = (bf16[128,64,128]{2,1,0:T(8,128)(2,1)}, bf16[16,128,128]{2,1,0:T(8,128)(2,1)S(1)}) custom-call(s32[3]{0:T(128)S(1)} %pad_add_fusion.where_ref, bf16[128,16384]{1,0:T(8,128)(2,1)} %all-gather.2.cloned.1.call-done.left_ref, bf16[128,2048]{1,0:T(8,128)(2,1)S(1)} %copy-done.1, ...), custom_call_target="tpu_custom_call", output_to_operand_aliasing={{0}: (10, {})} | custom-call | flops 2684354560 | bytes 8388608 | tf_op jit(solution)/shard_map/update/pallas_call | solution.py:105
  134.1 2.5 collective-permute-start.20
  136.6 5.9 %collective-permute-done.15.refs_2_ = bf16[2,16,64,128]{3,2,1,0:T(8,128)(2,1)S(1)} collective-permute-done((bf16[2,16,64,128]{3,2,1,0:T(8,128)(2,1)S(1)}, bf16[2,16,64,128]{3,2,1,0:T(8,128)(2,1)S(1)}, u32[]{:S(2)}, u32[]{:S(2)}) %collective-permute-start.15) | collective-permute-done | bytes 524320 | tf_op jit(solution)/shard_map/ppermute | solution.py:329
  142.5 3.2 %collective-permute-done.11.refs_2_ = bf16[16,128,128]{2,1,0:T(8,128)(2,1)S(1)} collective-permute-done((bf16[16,128,128]{2,1,0:T(8,128)(2,1)S(1)}, bf16[16,128,128]{2,1,0:T(8,128)(2,1)S(1)}, u32[]{:S(2)}, u32[]{:S(2)}) %collective-permute-start.11) | collective-permute-done | bytes 524320 | tf_op jit(solution)/shard_map/ppermute | solution.py:311
  145.7 2.7 %collective-permute-done.12.refs_4_ = bf16[16,128,128]{2,1,0:T(8,128)(2,1)S(1)} collective-permute-done((bf16[16,128,128]{2,1,0:T(8,128)(2,1)S(1)}, bf16[16,128,128]{2,1,0:T(8,128)(2,1)S(1)}, u32[]{:S(2)}, u32[]{:S(2)}) %collective-permute-start.12) | collective-permute-done | bytes 524320 | tf_op jit(solution)/shard_map/ppermute | solution.py:312
  148.5 2.0 collective-permute-start.16
  151.0 8.7 %collective-permute-done.21.refs_6_ = bf16[16,128,128]{2,1,0:T(8,128)(2,1)S(1)} collective-permute-done((bf16[16,128,128]{2,1,0:T(8,128)(2,1)S(1)}, bf16[16,128,128]{2,1,0:T(8,128)(2,1)S(1)}, u32[]{:S(2)}, u32[]{:S(2)}) %collective-permute-start.21) | collective-permute-done | bytes 524320 | tf_op jit(solution)/shard_map/ppermute | solution.py:312
  160.6 4.1 %project.5 = (bf16[2,16,64,128]{3,2,1,0:T(8,128)(2,1)S(1)}, bf16[2,16,64,128]{3,2,1,0:T(8,128)(2,1)S(1)}, bf16[2,16,64,128]{3,2,1,0:T(8,128)(2,1)S(1)}, bf16[2,16,64,128]{3,2,1,0:T(8,128)(2,1)S(1)}) custom-call(s32[3]{0:T(128)S(1)} %pad_add_fusion.where_ref, bf16[128,128]{1,0:T(8,128)(2,1)S(1)} %pad_maximum_fusion.weight_ref, f32[128,1]{1,0:T(8,128)S(1)} %copy.46.offset_ref, ...), custom_call_target="tpu_custom_call" | custom-call | flops 268435456 | bytes 4194304 | tf_op jit(solution)/shard_map/project/pallas_call | solution.py:165
  165.2 6.9 %update.7 = (bf16[128,64,128]{2,1,0:T(8,128)(2,1)}, bf16[16,128,128]{2,1,0:T(8,128)(2,1)S(1)}) custom-call(s32[3]{0:T(128)S(1)} %pad_add_fusion.where_ref, bf16[128,16384]{1,0:T(8,128)(2,1)} %all-gather.2.cloned.1.call-done.left_ref, bf16[128,2048]{1,0:T(8,128)(2,1)S(1)} %copy-done.1, ...), custom_call_target="tpu_custom_call", output_to_operand_aliasing={{0}: (10, {})} | custom-call | flops 2684354560 | bytes 8388608 | tf_op jit(solution)/shard_map/update/pallas_call | solution.py:105
  172.2 2.1 collective-permute-start.22
  175.0 3.0 %collective-permute-start.29 = (bf16[16,128,128]{2,1,0:T(8,128)(2,1)S(1)}, bf16[16,128,128]{2,1,0:T(8,128)(2,1)S(1)}, u32[]{:S(2)}, u32[]{:S(2)}) collective-permute-start(bf16[16,128,128]{2,1,0:T(8,128)(2,1)S(1)} %collective-permute-done.16.refs_1_), channel_id=1, source_target_pairs={{0,2},{2,4},{4,6},{6,7},{7,5},{5,3},{3,1},{1,0},{8,10},{10,12},{12... | collective-permute-start | bytes 1572872 | tf_op jit(solution)/shard_map/ppermute | solution.py:311
  178.0 1.8 place.4
  179.9 6.8 %collective-permute-done.22.refs_2_ = bf16[16,128,128]{2,1,0:T(8,128)(2,1)S(1)} collective-permute-done((bf16[16,128,128]{2,1,0:T(8,128)(2,1)S(1)}, bf16[16,128,128]{2,1,0:T(8,128)(2,1)S(1)}, u32[]{:S(2)}, u32[]{:S(2)}) %collective-permute-start.22) | collective-permute-done | bytes 524320 | tf_op jit(solution)/shard_map/ppermute | solution.py:311
  186.6 2.5 collective-permute-done.23.refs_4_
  190.6 1.7 collective-permute-done.24.refs_2_
  192.2 2.5 collective-permute-done.30.refs_6_
  194.8 3.1 %collective-permute-done.29.refs_0_ = bf16[16,128,128]{2,1,0:T(8,128)(2,1)S(1)} collective-permute-done((bf16[16,128,128]{2,1,0:T(8,128)(2,1)S(1)}, bf16[16,128,128]{2,1,0:T(8,128)(2,1)S(1)}, u32[]{:S(2)}, u32[]{:S(2)}) %collective-permute-start.29) | collective-permute-done | bytes 524320 | tf_op jit(solution)/shard_map/ppermute | solution.py:311
  197.9 4.3 %project.6 = (bf16[2,16,64,128]{3,2,1,0:T(8,128)(2,1)S(1)}, bf16[2,16,64,128]{3,2,1,0:T(8,128)(2,1)S(1)}, bf16[2,16,64,128]{3,2,1,0:T(8,128)(2,1)S(1)}, bf16[2,16,64,128]{3,2,1,0:T(8,128)(2,1)S(1)}) custom-call(s32[3]{0:T(128)S(1)} %pad_add_fusion.where_ref, bf16[128,128]{1,0:T(8,128)(2,1)S(1)} %pad_maximum_fusion.weight_ref, f32[128,1]{1,0:T(8,128)S(1)} %copy.46.offset_ref, ...), custom_call_target="tpu_custom_call" | custom-call | flops 268435456 | bytes 4194304 | tf_op jit(solution)/shard_map/project/pallas_call | solution.py:165
  202.2 1.6 collective-permute-start.31
  204.3 2.2 collective-permute-start.25
  206.5 7.6 %collective-permute-done.31.refs_1_ = bf16[2,16,64,128]{3,2,1,0:T(8,128)(2,1)S(1)} collective-permute-done((bf16[2,16,64,128]{3,2,1,0:T(8,128)(2,1)S(1)}, bf16[2,16,64,128]{3,2,1,0:T(8,128)(2,1)S(1)}, u32[]{:S(2)}, u32[]{:S(2)}) %collective-permute-start.31) | collective-permute-done | bytes 524320 | tf_op jit(solution)/shard_map/ppermute | solution.py:329
  214.1 4.5 %collective-permute-done.32.refs_2_ = bf16[2,16,64,128]{3,2,1,0:T(8,128)(2,1)S(1)} collective-permute-done((bf16[2,16,64,128]{3,2,1,0:T(8,128)(2,1)S(1)}, bf16[2,16,64,128]{3,2,1,0:T(8,128)(2,1)S(1)}, u32[]{:S(2)}, u32[]{:S(2)}) %collective-permute-start.32) | collective-permute-done | bytes 524320 | tf_op jit(solution)/shard_map/ppermute | solution.py:329
  218.6 2.7 %collective-permute-start.34 = (bf16[16,128,128]{2,1,0:T(8,128)(2,1)S(1)}, bf16[16,128,128]{2,1,0:T(8,128)(2,1)S(1)}, u32[]{:S(2)}, u32[]{:S(2)}) collective-permute-start(bf16[16,128,128]{2,1,0:T(8,128)(2,1)S(1)} %collective-permute-done.25.refs_1_), channel_id=1, source_target_pairs={{0,2},{2,4},{4,6},{6,7},{7,5},{5,3},{3,1},{1,0},{8,10},{10,12},{12... | collective-permute-start | bytes 1572872 | tf_op jit(solution)/shard_map/ppermute | solution.py:311
  221.3 7.5 %collective-permute-done.33.refs_3_ = bf16[2,16,64,128]{3,2,1,0:T(8,128)(2,1)S(1)} collective-permute-done((bf16[2,16,64,128]{3,2,1,0:T(8,128)(2,1)S(1)}, bf16[2,16,64,128]{3,2,1,0:T(8,128)(2,1)S(1)}, u32[]{:S(2)}, u32[]{:S(2)}) %collective-permute-start.33) | collective-permute-done | bytes 524320 | tf_op jit(solution)/shard_map/ppermute | solution.py:329
  229.6 4.1 %project.7 = (bf16[2,16,64,128]{3,2,1,0:T(8,128)(2,1)S(1)}, bf16[2,16,64,128]{3,2,1,0:T(8,128)(2,1)S(1)}, bf16[2,16,64,128]{3,2,1,0:T(8,128)(2,1)S(1)}, bf16[2,16,64,128]{3,2,1,0:T(8,128)(2,1)S(1)}) custom-call(s32[3]{0:T(128)S(1)} %pad_add_fusion.where_ref, bf16[128,128]{1,0:T(8,128)(2,1)S(1)} %pad_maximum_fusion.weight_ref, f32[128,1]{1,0:T(8,128)S(1)} %copy.46.offset_ref, ...), custom_call_target="tpu_custom_call" | custom-call | flops 268435456 | bytes 4194304 | tf_op jit(solution)/shard_map/project/pallas_call | solution.py:165
  235.7 1.6 collective-permute-start.38
  237.3 1.8 place.5
  239.1 1.8 place.6
  241.0 3.3 %collective-permute-done.36.refs_1_ = bf16[2,16,64,128]{3,2,1,0:T(8,128)(2,1)S(1)} collective-permute-done((bf16[2,16,64,128]{3,2,1,0:T(8,128)(2,1)S(1)}, bf16[2,16,64,128]{3,2,1,0:T(8,128)(2,1)S(1)}, u32[]{:S(2)}, u32[]{:S(2)}) %collective-permute-start.36) | collective-permute-done | bytes 524320 | tf_op jit(solution)/shard_map/ppermute | solution.py:329
  244.3 7.3 %collective-permute-done.37.refs_2_ = bf16[2,16,64,128]{3,2,1,0:T(8,128)(2,1)S(1)} collective-permute-done((bf16[2,16,64,128]{3,2,1,0:T(8,128)(2,1)S(1)}, bf16[2,16,64,128]{3,2,1,0:T(8,128)(2,1)S(1)}, u32[]{:S(2)}, u32[]{:S(2)}) %collective-permute-start.37) | collective-permute-done | bytes 524320 | tf_op jit(solution)/shard_map/ppermute | solution.py:329
  252.1 1.8 place.7
  256.1 1.5 put.5.earlier_ref
  (101 shorter events, 25.4 us)
Async XLA Ops:
  7.2 74.6 %copy-start.1 = (bf16[128,2048]{1,0:T(8,128)(2,1)S(1)}, bf16[128,2048]{1,0:T(8,128)(2,1)}, u32[]{:S(2)}) copy-start(bf16[128,2048]{1,0:T(8,128)(2,1)} %refs_0_.7) | copy-start | bytes 1572868
  7.2 52.3 %all-gather.2.cloned.1.call-start = ((), (), s32[]{:S(2)}) async-start(), calls=%async_computation | async-start | bytes 4718592 | tf_op jit(solution)/shard_map/all_gather | solution.py:271
  7.9 16.0 %collective-permute-start = (bf16[128,2048]{1,0:T(8,128)(2,1)}, bf16[128,2048]{1,0:T(8,128)(2,1)S(1)}, u32[]{:S(2)}, u32[]{:S(2)}) collective-permute-start(bf16[128,2048]{1,0:T(8,128)(2,1)} %refs_0_.7), channel_id=1, source_target_pairs={{0,8},{8,0},{16,24},{24,16},{1,9},{9,1},{17,25},{25,17},{2,10},{10... | collective-permute-start | bytes 1572872 | tf_op jit(solution)/shard_map/ppermute | solution.py:270
  10.9 24.8 %collective-permute-start.1 = (bf16[128,2048]{1,0:T(8,128)(2,1)}, bf16[128,2048]{1,0:T(8,128)(2,1)S(1)}, u32[]{:S(2)}, u32[]{:S(2)}) collective-permute-start(bf16[128,2048]{1,0:T(8,128)(2,1)} %refs_0_.7), channel_id=1, source_target_pairs={{0,16},{8,24},{16,0},{24,8},{1,17},{9,25},{17,1},{25,9},{2,18},{10... | collective-permute-start | bytes 1572872 | tf_op jit(solution)/shard_map/ppermute | solution.py:270
  12.4 23.3 %collective-permute-start.2 = (bf16[128,2048]{1,0:T(8,128)(2,1)}, bf16[128,2048]{1,0:T(8,128)(2,1)S(1)}, u32[]{:S(2)}, u32[]{:S(2)}) collective-permute-start(bf16[128,2048]{1,0:T(8,128)(2,1)} %refs_0_.7), channel_id=1, source_target_pairs={{0,24},{8,16},{16,8},{24,0},{1,25},{9,17},{17,9},{25,1},{2,26},{10... | collective-permute-start | bytes 1572872 | tf_op jit(solution)/shard_map/ppermute | solution.py:270
  67.5 11.3 %collective-permute-start.3 = (bf16[16,128,128]{2,1,0:T(8,128)(2,1)S(1)}, bf16[16,128,128]{2,1,0:T(8,128)(2,1)}, u32[]{:S(2)}, u32[]{:S(2)}) collective-permute-start(bf16[16,128,128]{2,1,0:T(8,128)(2,1)S(1)} %get-tuple-element.73.refs_3_), channel_id=1, source_target_pairs={{0,2},{2,4},{4,6},{6,7},{7,5},{5,3},{3,1},{1,0},{8,10},{10,12},{12... | collective-permute-start | bytes 1572872 | tf_op jit(solution)/shard_map/ppermute | solution.py:311
  68.3 13.4 %collective-permute-start.4 = (bf16[16,128,128]{2,1,0:T(8,128)(2,1)S(1)}, bf16[16,128,128]{2,1,0:T(8,128)(2,1)}, u32[]{:S(2)}, u32[]{:S(2)}) collective-permute-start(bf16[16,128,128]{2,1,0:T(8,128)(2,1)S(1)} %get-tuple-element.73.refs_3_), channel_id=1, source_target_pairs={{2,0},{4,2},{6,4},{7,6},{5,7},{3,5},{1,3},{0,1},{10,8},{12,10},{14... | collective-permute-start | bytes 1572872 | tf_op jit(solution)/shard_map/ppermute | solution.py:312
  78.8 15.2 %collective-permute-start.7 = (bf16[16,128,128]{2,1,0:T(8,128)(2,1)}, bf16[16,128,128]{2,1,0:T(8,128)(2,1)}, u32[]{:S(2)}, u32[]{:S(2)}) collective-permute-start(bf16[16,128,128]{2,1,0:T(8,128)(2,1)} %collective-permute-done.3.refs_2_), channel_id=1, source_target_pairs={{0,2},{2,4},{4,6},{6,7},{7,5},{5,3},{3,1},{1,0},{8,10},{10,12},{12... | collective-permute-start | bytes 1572872 | tf_op jit(solution)/shard_map/ppermute | solution.py:311
  81.7 15.3 %collective-permute-start.8 = (bf16[16,128,128]{2,1,0:T(8,128)(2,1)}, bf16[16,128,128]{2,1,0:T(8,128)(2,1)}, u32[]{:S(2)}, u32[]{:S(2)}) collective-permute-start(bf16[16,128,128]{2,1,0:T(8,128)(2,1)} %collective-permute-done.4.refs_4_), channel_id=1, source_target_pairs={{2,0},{4,2},{6,4},{7,6},{5,7},{3,5},{1,3},{0,1},{10,8},{12,10},{14... | collective-permute-start | bytes 1572872 | tf_op jit(solution)/shard_map/ppermute | solution.py:312
  88.7 71.1 %copy-start.3 = (bf16[16,128,128]{2,1,0:T(8,128)(2,1)}, bf16[16,128,128]{2,1,0:T(8,128)(2,1)S(1)}, u32[]{:S(2)}) copy-start(bf16[16,128,128]{2,1,0:T(8,128)(2,1)S(1)} %get-tuple-element.74.refs_3_) | copy-start | bytes 1572868
  88.7 16.5 %collective-permute-start.5 = (bf16[16,128,128]{2,1,0:T(8,128)(2,1)S(1)}, bf16[16,128,128]{2,1,0:T(8,128)(2,1)}, u32[]{:S(2)}, u32[]{:S(2)}) collective-permute-start(bf16[16,128,128]{2,1,0:T(8,128)(2,1)S(1)} %get-tuple-element.74.refs_3_), channel_id=1, source_target_pairs={{0,2},{2,4},{4,6},{6,7},{7,5},{5,3},{3,1},{1,0},{8,10},{10,12},{12... | collective-permute-start | bytes 1572872 | tf_op jit(solution)/shard_map/ppermute | solution.py:311
  91.0 17.3 %collective-permute-start.6 = (bf16[16,128,128]{2,1,0:T(8,128)(2,1)S(1)}, bf16[16,128,128]{2,1,0:T(8,128)(2,1)}, u32[]{:S(2)}, u32[]{:S(2)}) collective-permute-start(bf16[16,128,128]{2,1,0:T(8,128)(2,1)S(1)} %get-tuple-element.74.refs_3_), channel_id=1, source_target_pairs={{2,0},{4,2},{6,4},{7,6},{5,7},{3,5},{1,3},{0,1},{10,8},{12,10},{14... | collective-permute-start | bytes 1572872 | tf_op jit(solution)/shard_map/ppermute | solution.py:312
  97.0 22.5 %collective-permute-start.10 = (bf16[16,128,128]{2,1,0:T(8,128)(2,1)}, bf16[16,128,128]{2,1,0:T(8,128)(2,1)}, u32[]{:S(2)}, u32[]{:S(2)}) collective-permute-start(bf16[16,128,128]{2,1,0:T(8,128)(2,1)} %collective-permute-done.8.refs_5_), channel_id=1, source_target_pairs={{2,0},{4,2},{6,4},{7,6},{5,7},{3,5},{1,3},{0,1},{10,8},{12,10},{14... | collective-permute-start | bytes 1572872 | tf_op jit(solution)/shard_map/ppermute | solution.py:312
  97.0 22.5 %collective-permute-start.9 = (bf16[16,128,128]{2,1,0:T(8,128)(2,1)}, bf16[16,128,128]{2,1,0:T(8,128)(2,1)}, u32[]{:S(2)}, u32[]{:S(2)}) collective-permute-start(bf16[16,128,128]{2,1,0:T(8,128)(2,1)} %collective-permute-done.7.refs_1_), channel_id=1, source_target_pairs={{0,2},{2,4},{4,6},{6,7},{7,5},{5,3},{3,1},{1,0},{8,10},{10,12},{12... | collective-permute-start | bytes 1572872 | tf_op jit(solution)/shard_map/ppermute | solution.py:311
  108.3 23.7 %collective-permute-start.13 = (bf16[16,128,128]{2,1,0:T(8,128)(2,1)}, bf16[16,128,128]{2,1,0:T(8,128)(2,1)S(1)}, u32[]{:S(2)}, u32[]{:S(2)}) collective-permute-start(bf16[16,128,128]{2,1,0:T(8,128)(2,1)} %collective-permute-done.5.refs_2_), channel_id=1, source_target_pairs={{0,2},{2,4},{4,6},{6,7},{7,5},{5,3},{3,1},{1,0},{8,10},{10,12},{12... | collective-permute-start | bytes 1572872 | tf_op jit(solution)/shard_map/ppermute | solution.py:311
  108.3 23.7 %collective-permute-start.14 = (bf16[16,128,128]{2,1,0:T(8,128)(2,1)}, bf16[16,128,128]{2,1,0:T(8,128)(2,1)S(1)}, u32[]{:S(2)}, u32[]{:S(2)}) collective-permute-start(bf16[16,128,128]{2,1,0:T(8,128)(2,1)} %collective-permute-done.6.refs_4_), channel_id=1, source_target_pairs={{2,0},{4,2},{6,4},{7,6},{5,7},{3,5},{1,3},{0,1},{10,8},{12,10},{14... | collective-permute-start | bytes 1572872 | tf_op jit(solution)/shard_map/ppermute | solution.py:312
  123.3 10.8 %collective-permute-start.18 = (bf16[2,16,64,128]{3,2,1,0:T(8,128)(2,1)S(1)}, bf16[2,16,64,128]{3,2,1,0:T(8,128)(2,1)S(1)}, u32[]{:S(2)}, u32[]{:S(2)}) collective-permute-start(bf16[2,16,64,128]{3,2,1,0:T(8,128)(2,1)S(1)} %get-tuple-element.94), channel_id=1, source_target_pairs={{0,8},{8,0},{16,24},{24,16},{1,9},{9,1},{17,25},{25,17},{2,10},{10... | collective-permute-start | bytes 1572872 | tf_op jit(solution)/shard_map/ppermute | solution.py:329
  131.9 47.9 %copy-start.2 = (bf16[16,128,128]{2,1,0:T(8,128)(2,1)}, bf16[16,128,128]{2,1,0:T(8,128)(2,1)S(1)}, u32[]{:S(2)}) copy-start(bf16[16,128,128]{2,1,0:T(8,128)(2,1)S(1)} %get-tuple-element.80.refs_3_) | copy-start | bytes 1572868
  132.0 10.5 %collective-permute-start.15 = (bf16[2,16,64,128]{3,2,1,0:T(8,128)(2,1)S(1)}, bf16[2,16,64,128]{3,2,1,0:T(8,128)(2,1)S(1)}, u32[]{:S(2)}, u32[]{:S(2)}) collective-permute-start(bf16[2,16,64,128]{3,2,1,0:T(8,128)(2,1)S(1)} %get-tuple-element.88), channel_id=1, source_target_pairs={{0,16},{8,24},{16,0},{24,8},{1,17},{9,25},{17,1},{25,9},{2,18},{10... | collective-permute-start | bytes 1572872 | tf_op jit(solution)/shard_map/ppermute | solution.py:329
  133.4 12.3 %collective-permute-start.11 = (bf16[16,128,128]{2,1,0:T(8,128)(2,1)S(1)}, bf16[16,128,128]{2,1,0:T(8,128)(2,1)S(1)}, u32[]{:S(2)}, u32[]{:S(2)}) collective-permute-start(bf16[16,128,128]{2,1,0:T(8,128)(2,1)S(1)} %get-tuple-element.80.refs_3_), channel_id=1, source_target_pairs={{0,2},{2,4},{4,6},{6,7},{7,5},{5,3},{3,1},{1,0},{8,10},{10,12},{12... | collective-permute-start | bytes 1572872 | tf_op jit(solution)/shard_map/ppermute | solution.py:311
  133.4 15.1 %collective-permute-start.12 = (bf16[16,128,128]{2,1,0:T(8,128)(2,1)S(1)}, bf16[16,128,128]{2,1,0:T(8,128)(2,1)S(1)}, u32[]{:S(2)}, u32[]{:S(2)}) collective-permute-start(bf16[16,128,128]{2,1,0:T(8,128)(2,1)S(1)} %get-tuple-element.80.refs_3_), channel_id=1, source_target_pairs={{2,0},{4,2},{6,4},{7,6},{5,7},{3,5},{1,3},{0,1},{10,8},{12,10},{14... | collective-permute-start | bytes 1572872 | tf_op jit(solution)/shard_map/ppermute | solution.py:312
  134.1 25.6 %collective-permute-start.21 = (bf16[16,128,128]{2,1,0:T(8,128)(2,1)S(1)}, bf16[16,128,128]{2,1,0:T(8,128)(2,1)S(1)}, u32[]{:S(2)}, u32[]{:S(2)}) collective-permute-start(bf16[16,128,128]{2,1,0:T(8,128)(2,1)S(1)} %collective-permute-done.14.refs_5_), channel_id=1, source_target_pairs={{2,0},{4,2},{6,4},{7,6},{5,7},{3,5},{1,3},{0,1},{10,8},{12,10},{14... | collective-permute-start | bytes 1572872 | tf_op jit(solution)/shard_map/ppermute | solution.py:312
  134.1 25.6 %collective-permute-start.20 = (bf16[16,128,128]{2,1,0:T(8,128)(2,1)S(1)}, bf16[16,128,128]{2,1,0:T(8,128)(2,1)S(1)}, u32[]{:S(2)}, u32[]{:S(2)}) collective-permute-start(bf16[16,128,128]{2,1,0:T(8,128)(2,1)S(1)} %collective-permute-done.13.refs_1_), channel_id=1, source_target_pairs={{0,2},{2,4},{4,6},{6,7},{7,5},{5,3},{3,1},{1,0},{8,10},{10,12},{12... | collective-permute-start | bytes 1572872 | tf_op jit(solution)/shard_map/ppermute | solution.py:311
  148.5 25.8 %collective-permute-start.17 = (bf16[16,128,128]{2,1,0:T(8,128)(2,1)S(1)}, bf16[16,128,128]{2,1,0:T(8,128)(2,1)}, u32[]{:S(2)}, u32[]{:S(2)}) collective-permute-start(bf16[16,128,128]{2,1,0:T(8,128)(2,1)S(1)} %collective-permute-done.12.refs_4_), channel_id=1, source_target_pairs={{2,0},{4,2},{6,4},{7,6},{5,7},{3,5},{1,3},{0,1},{10,8},{12,10},{14... | collective-permute-start | bytes 1572872 | tf_op jit(solution)/shard_map/ppermute | solution.py:312
  148.5 25.8 %collective-permute-start.16 = (bf16[16,128,128]{2,1,0:T(8,128)(2,1)S(1)}, bf16[16,128,128]{2,1,0:T(8,128)(2,1)S(1)}, u32[]{:S(2)}, u32[]{:S(2)}) collective-permute-start(bf16[16,128,128]{2,1,0:T(8,128)(2,1)S(1)} %collective-permute-done.11.refs_2_), channel_id=1, source_target_pairs={{0,2},{2,4},{4,6},{6,7},{7,5},{5,3},{3,1},{1,0},{8,10},{10,12},{12... | collective-permute-start | bytes 1572872 | tf_op jit(solution)/shard_map/ppermute | solution.py:311
  150.5 21.7 %collective-permute-start.19 = (bf16[2,16,64,128]{3,2,1,0:T(8,128)(2,1)S(1)}, bf16[2,16,64,128]{3,2,1,0:T(8,128)(2,1)S(1)}, u32[]{:S(2)}, u32[]{:S(2)}) collective-permute-start(bf16[2,16,64,128]{3,2,1,0:T(8,128)(2,1)S(1)} %get-tuple-element.96), channel_id=1, source_target_pairs={{0,24},{8,16},{16,8},{24,0},{1,25},{9,17},{17,9},{25,1},{2,26},{10... | collective-permute-start | bytes 1572872 | tf_op jit(solution)/shard_map/ppermute | solution.py:329
  164.7 10.4 %collective-permute-start.27 = (bf16[2,16,64,128]{3,2,1,0:T(8,128)(2,1)S(1)}, bf16[2,16,64,128]{3,2,1,0:T(8,128)(2,1)S(1)}, u32[]{:S(2)}, u32[]{:S(2)}) collective-permute-start(bf16[2,16,64,128]{3,2,1,0:T(8,128)(2,1)S(1)} %get-tuple-element.110), channel_id=1, source_target_pairs={{0,8},{8,0},{16,24},{24,16},{1,9},{9,1},{17,25},{25,17},{2,10},{10... | collective-permute-start | bytes 1572872 | tf_op jit(solution)/shard_map/ppermute | solution.py:329
  172.2 56.6 %copy-start.4 = (bf16[16,128,128]{2,1,0:T(8,128)(2,1)}, bf16[16,128,128]{2,1,0:T(8,128)(2,1)S(1)}, u32[]{:S(2)}) copy-start(bf16[16,128,128]{2,1,0:T(8,128)(2,1)S(1)} %get-tuple-element.101.refs_3_) | copy-start | bytes 1572868
  172.2 14.4 %collective-permute-start.22 = (bf16[16,128,128]{2,1,0:T(8,128)(2,1)S(1)}, bf16[16,128,128]{2,1,0:T(8,128)(2,1)S(1)}, u32[]{:S(2)}, u32[]{:S(2)}) collective-permute-start(bf16[16,128,128]{2,1,0:T(8,128)(2,1)S(1)} %get-tuple-element.101.refs_3_), channel_id=1, source_target_pairs={{0,2},{2,4},{4,6},{6,7},{7,5},{5,3},{3,1},{1,0},{8,10},{10,12},{12... | collective-permute-start | bytes 1572872 | tf_op jit(solution)/shard_map/ppermute | solution.py:311
  174.2 14.9 %collective-permute-start.23 = (bf16[16,128,128]{2,1,0:T(8,128)(2,1)S(1)}, bf16[16,128,128]{2,1,0:T(8,128)(2,1)S(1)}, u32[]{:S(2)}, u32[]{:S(2)}) collective-permute-start(bf16[16,128,128]{2,1,0:T(8,128)(2,1)S(1)} %get-tuple-element.101.refs_3_), channel_id=1, source_target_pairs={{2,0},{4,2},{6,4},{7,6},{5,7},{3,5},{1,3},{0,1},{10,8},{12,10},{14... | collective-permute-start | bytes 1572872 | tf_op jit(solution)/shard_map/ppermute | solution.py:312
  174.3 18.0 %collective-permute-start.24 = (bf16[2,16,64,128]{3,2,1,0:T(8,128)(2,1)S(1)}, bf16[2,16,64,128]{3,2,1,0:T(8,128)(2,1)S(1)}, u32[]{:S(2)}, u32[]{:S(2)}) collective-permute-start(bf16[2,16,64,128]{3,2,1,0:T(8,128)(2,1)S(1)} %get-tuple-element.104), channel_id=1, source_target_pairs={{0,16},{8,24},{16,0},{24,8},{1,17},{9,25},{17,1},{25,9},{2,18},{10... | collective-permute-start | bytes 1572872 | tf_op jit(solution)/shard_map/ppermute | solution.py:329
  175.0 19.7 %collective-permute-start.30 = (bf16[16,128,128]{2,1,0:T(8,128)(2,1)}, bf16[16,128,128]{2,1,0:T(8,128)(2,1)S(1)}, u32[]{:S(2)}, u32[]{:S(2)}) collective-permute-start(bf16[16,128,128]{2,1,0:T(8,128)(2,1)} %collective-permute-done.17.refs_5_), channel_id=1, source_target_pairs={{2,0},{4,2},{6,4},{7,6},{5,7},{3,5},{1,3},{0,1},{10,8},{12,10},{14... | collective-permute-start | bytes 1572872 | tf_op jit(solution)/shard_map/ppermute | solution.py:312
  175.0 22.8 %collective-permute-start.29 = (bf16[16,128,128]{2,1,0:T(8,128)(2,1)S(1)}, bf16[16,128,128]{2,1,0:T(8,128)(2,1)S(1)}, u32[]{:S(2)}, u32[]{:S(2)}) collective-permute-start(bf16[16,128,128]{2,1,0:T(8,128)(2,1)S(1)} %collective-permute-done.16.refs_1_), channel_id=1, source_target_pairs={{0,2},{2,4},{4,6},{6,7},{7,5},{5,3},{3,1},{1,0},{8,10},{10,12},{12... | collective-permute-start | bytes 1572872 | tf_op jit(solution)/shard_map/ppermute | solution.py:311
  189.1 17.4 %collective-permute-start.28 = (bf16[2,16,64,128]{3,2,1,0:T(8,128)(2,1)S(1)}, bf16[2,16,64,128]{3,2,1,0:T(8,128)(2,1)S(1)}, u32[]{:S(2)}, u32[]{:S(2)}) collective-permute-start(bf16[2,16,64,128]{3,2,1,0:T(8,128)(2,1)S(1)} %get-tuple-element.112), channel_id=1, source_target_pairs={{0,24},{8,16},{16,8},{24,0},{1,25},{9,17},{17,9},{25,1},{2,26},{10... | collective-permute-start | bytes 1572872 | tf_op jit(solution)/shard_map/ppermute | solution.py:329
  192.2 14.3 %collective-permute-start.26 = (bf16[16,128,128]{2,1,0:T(8,128)(2,1)S(1)}, bf16[16,128,128]{2,1,0:T(8,128)(2,1)S(1)}, u32[]{:S(2)}, u32[]{:S(2)}) collective-permute-start(bf16[16,128,128]{2,1,0:T(8,128)(2,1)S(1)} %collective-permute-done.23.refs_4_), channel_id=1, source_target_pairs={{2,0},{4,2},{6,4},{7,6},{5,7},{3,5},{1,3},{0,1},{10,8},{12,10},{14... | collective-permute-start | bytes 1572872 | tf_op jit(solution)/shard_map/ppermute | solution.py:312
  202.2 11.9 %collective-permute-start.31 = (bf16[2,16,64,128]{3,2,1,0:T(8,128)(2,1)S(1)}, bf16[2,16,64,128]{3,2,1,0:T(8,128)(2,1)S(1)}, u32[]{:S(2)}, u32[]{:S(2)}) collective-permute-start(bf16[2,16,64,128]{3,2,1,0:T(8,128)(2,1)S(1)} %get-tuple-element.119), channel_id=1, source_target_pairs={{0,8},{8,0},{16,24},{24,16},{1,9},{9,1},{17,25},{25,17},{2,10},{10... | collective-permute-start | bytes 1572872 | tf_op jit(solution)/shard_map/ppermute | solution.py:329
  203.8 14.8 %collective-permute-start.32 = (bf16[2,16,64,128]{3,2,1,0:T(8,128)(2,1)S(1)}, bf16[2,16,64,128]{3,2,1,0:T(8,128)(2,1)S(1)}, u32[]{:S(2)}, u32[]{:S(2)}) collective-permute-start(bf16[2,16,64,128]{3,2,1,0:T(8,128)(2,1)S(1)} %get-tuple-element.120), channel_id=1, source_target_pairs={{0,16},{8,24},{16,0},{24,8},{1,17},{9,25},{17,1},{25,9},{2,18},{10... | collective-permute-start | bytes 1572872 | tf_op jit(solution)/shard_map/ppermute | solution.py:329
  204.3 14.3 %collective-permute-start.25 = (bf16[16,128,128]{2,1,0:T(8,128)(2,1)S(1)}, bf16[16,128,128]{2,1,0:T(8,128)(2,1)S(1)}, u32[]{:S(2)}, u32[]{:S(2)}) collective-permute-start(bf16[16,128,128]{2,1,0:T(8,128)(2,1)S(1)} %collective-permute-done.22.refs_2_), channel_id=1, source_target_pairs={{0,2},{2,4},{4,6},{6,7},{7,5},{5,3},{3,1},{1,0},{8,10},{10,12},{12... | collective-permute-start | bytes 1572872 | tf_op jit(solution)/shard_map/ppermute | solution.py:311
  206.5 22.3 %collective-permute-start.35 = (bf16[16,128,128]{2,1,0:T(8,128)(2,1)S(1)}, bf16[16,128,128]{2,1,0:T(8,128)(2,1)S(1)}, u32[]{:S(2)}, u32[]{:S(2)}) collective-permute-start(bf16[16,128,128]{2,1,0:T(8,128)(2,1)S(1)} %collective-permute-done.26.refs_5_), channel_id=1, source_target_pairs={{2,0},{4,2},{6,4},{7,6},{5,7},{3,5},{1,3},{0,1},{10,8},{12,10},{14... | collective-permute-start | bytes 1572872 | tf_op jit(solution)/shard_map/ppermute | solution.py:312
  218.6 10.2 %collective-permute-start.33 = (bf16[2,16,64,128]{3,2,1,0:T(8,128)(2,1)S(1)}, bf16[2,16,64,128]{3,2,1,0:T(8,128)(2,1)S(1)}, u32[]{:S(2)}, u32[]{:S(2)}) collective-permute-start(bf16[2,16,64,128]{3,2,1,0:T(8,128)(2,1)S(1)} %get-tuple-element.122), channel_id=1, source_target_pairs={{0,24},{8,16},{16,8},{24,0},{1,25},{9,17},{17,9},{25,1},{2,26},{10... | collective-permute-start | bytes 1572872 | tf_op jit(solution)/shard_map/ppermute | solution.py:329
  218.6 10.2 %collective-permute-start.34 = (bf16[16,128,128]{2,1,0:T(8,128)(2,1)S(1)}, bf16[16,128,128]{2,1,0:T(8,128)(2,1)S(1)}, u32[]{:S(2)}, u32[]{:S(2)}) collective-permute-start(bf16[16,128,128]{2,1,0:T(8,128)(2,1)S(1)} %collective-permute-done.25.refs_1_), channel_id=1, source_target_pairs={{0,2},{2,4},{4,6},{6,7},{7,5},{5,3},{3,1},{1,0},{8,10},{10,12},{12... | collective-permute-start | bytes 1572872 | tf_op jit(solution)/shard_map/ppermute | solution.py:311
  233.7 10.6 %collective-permute-start.36 = (bf16[2,16,64,128]{3,2,1,0:T(8,128)(2,1)S(1)}, bf16[2,16,64,128]{3,2,1,0:T(8,128)(2,1)S(1)}, u32[]{:S(2)}, u32[]{:S(2)}) collective-permute-start(bf16[2,16,64,128]{3,2,1,0:T(8,128)(2,1)S(1)} %get-tuple-element.130), channel_id=1, source_target_pairs={{0,8},{8,0},{16,24},{24,16},{1,9},{9,1},{17,25},{25,17},{2,10},{10... | collective-permute-start | bytes 1572872 | tf_op jit(solution)/shard_map/ppermute | solution.py:329
  234.5 17.1 %collective-permute-start.37 = (bf16[2,16,64,128]{3,2,1,0:T(8,128)(2,1)S(1)}, bf16[2,16,64,128]{3,2,1,0:T(8,128)(2,1)S(1)}, u32[]{:S(2)}, u32[]{:S(2)}) collective-permute-start(bf16[2,16,64,128]{3,2,1,0:T(8,128)(2,1)S(1)} %get-tuple-element.131), channel_id=1, source_target_pairs={{0,16},{8,24},{16,0},{24,8},{1,17},{9,25},{17,1},{25,9},{2,18},{10... | collective-permute-start | bytes 1572872 | tf_op jit(solution)/shard_map/ppermute | solution.py:329
  235.7 15.9 %collective-permute-start.38 = (bf16[2,16,64,128]{3,2,1,0:T(8,128)(2,1)S(1)}, bf16[2,16,64,128]{3,2,1,0:T(8,128)(2,1)S(1)}, u32[]{:S(2)}, u32[]{:S(2)}) collective-permute-start(bf16[2,16,64,128]{3,2,1,0:T(8,128)(2,1)S(1)} %get-tuple-element.132), channel_id=1, source_target_pairs={{0,24},{8,16},{16,8},{24,0},{1,25},{9,17},{17,9},{25,1},{2,26},{10... | collective-permute-start | bytes 1572872 | tf_op jit(solution)/shard_map/ppermute | solution.py:329
  251.6 2.9 %collective-permute-start.42 = (bf16[16,64,512]{2,1,0:T(8,128)(2,1)S(1)}, bf16[16,64,512]{2,1,0:T(8,128)(2,1)S(1)}, u32[]{:S(2)}, u32[]{:S(2)}) collective-permute-start(bf16[16,64,512]{2,1,0:T(8,128)(2,1)S(1)} %get-tuple-element.138), channel_id=1, source_target_pairs={{0,1},{1,0},{2,3},{3,2},{4,5},{5,4},{6,7},{7,6},{8,9},{9,8},{10,11... | collective-permute-start | bytes 3145736 | tf_op jit(solution)/shard_map/ppermute | solution.py:338
  251.6 4.5 %collective-permute-start.41 = (bf16[16,64,512]{2,1,0:T(8,128)(2,1)S(1)}, bf16[16,64,512]{2,1,0:T(8,128)(2,1)S(1)}, u32[]{:S(2)}, u32[]{:S(2)}) collective-permute-start(bf16[16,64,512]{2,1,0:T(8,128)(2,1)S(1)} %get-tuple-element.137), channel_id=1, source_target_pairs={{0,1},{1,0},{2,3},{3,2},{4,5},{5,4},{6,7},{7,6},{8,9},{9,8},{10,11... | collective-permute-start | bytes 3145736 | tf_op jit(solution)/shard_map/ppermute | solution.py:338
  252.1 5.5 %collective-permute-start.40 = (bf16[16,64,512]{2,1,0:T(8,128)(2,1)S(1)}, bf16[16,64,512]{2,1,0:T(8,128)(2,1)S(1)}, u32[]{:S(2)}, u32[]{:S(2)}) collective-permute-start(bf16[16,64,512]{2,1,0:T(8,128)(2,1)S(1)} %get-tuple-element.136), channel_id=1, source_target_pairs={{0,1},{1,0},{2,3},{3,2},{4,5},{5,4},{6,7},{7,6},{8,9},{9,8},{10,11... | collective-permute-start | bytes 3145736 | tf_op jit(solution)/shard_map/ppermute | solution.py:338
  253.9 5.2 %collective-permute-start.39 = (bf16[16,64,512]{2,1,0:T(8,128)(2,1)S(1)}, bf16[16,64,512]{2,1,0:T(8,128)(2,1)S(1)}, u32[]{:S(2)}, u32[]{:S(2)}) collective-permute-start(bf16[16,64,512]{2,1,0:T(8,128)(2,1)S(1)} %get-tuple-element.135), channel_id=1, source_target_pairs={{0,1},{1,0},{2,3},{3,2},{4,5},{5,4},{6,7},{7,6},{8,9},{9,8},{10,11... | collective-permute-start | bytes 3145736 | tf_op jit(solution)/shard_map/ppermute | solution.py:338
  (11 other events, 205.3 us)
Sparse Core Ops, SparseCore 0:
  9.6 49.8 all-gather.1

commit v6 on v5

--- a/solution.py
+++ b/solution.py
@@ -20,13 +20,15 @@
 def update_kernel(
     parts,
     part,
+    cols,
+    plan,
     where_ref,
-    left_ref,
     *refs,
 ):
+    lefts, refs = refs[: len(plan)], refs[len(plan) :]
     rights = refs[:parts]
     pair_ref, weight_ref, bias_ref, gain_ref = refs[parts : parts + 4]
-    new_ref, normed_ref, right_all, right_turned, outer, rows, sems = refs[-7:]
+    new_ref, normed_ref, left_ref, right_all, right_turned, outer, rows, sems = refs[-8:]
     tile_rows = pair_ref.shape[0]
     share = rights[0].shape[0]
     depth = share * parts
@@ -39,10 +41,25 @@
         copy = pltpu.make_async_copy(source, right_all.at[pl.ds(place, share), :], sems.at[d])
         copy.start()
         copies.append(copy)
+    chip, core = where_ref[1], where_ref[2]
+    spot = chip + core * (cols - 1 - 2 * chip)
+    for n, (offset, column) in enumerate(plan):
+        height, length = lefts[n].shape
+        row = 0
+        if offset is not None:
+            owner = lax.rem(spot + offset + cols, cols)
+            owner = jnp.where(owner < cols // 2, CORES * owner, CORES * (cols - 1 - owner) + 1)
+            row = pl.multiple_of(owner * height, height)
+        target = left_ref.at[pl.ds(row, height), pl.ds(column, length)]
+        copy = pltpu.make_async_copy(lefts[n], target, sems.at[parts + n])
+        copy.start()
+        copies.append(copy)
     rows[...] = pair_ref[...].astype(jnp.float32).reshape(tile_rows * STEP, -1)
-    for copy in copies:
+    for copy in copies[:parts]:
         copy.wait()
     right_turned[...] = right_all[...].T
+    for copy in copies[parts:]:
+        copy.wait()
     for c1 in range(0, CHANNEL_WIDTH, 2):
         both = jnp.concatenate(
             [left_ref[:, c * depth : (c + 1) * depth] for c in (c1, c1 + 1)], axis=0
@@ -78,7 +95,7 @@
     new_ref[...] = rows[...].reshape(tile_rows, STEP, -1).astype(jnp.bfloat16)
 
 
-def update_call(where, left, rights, pair, weight, bias, gain, earlier, part):
+def update_call(where, lefts, plan, cols, rights, pair, weight, bias, gain, earlier, part):
     tile_rows, tile_cols, channels = pair.shape
     parts = len(rights)
     depth = rights[0].shape[0] * parts
@@ -86,11 +103,10 @@
     whole = pl.BlockSpec(memory_space=pltpu.VMEM)
     far = pl.BlockSpec(memory_space=pl.ANY)
     block = pl.BlockSpec((tile_rows, STEP, channels), lambda g: (0, part, 0))
-    args = [where, left, *rights, pair, weight, bias, gain]
+    args = [where, *lefts, *rights, pair, weight, bias, gain]
     specs = [
         pl.BlockSpec(memory_space=pltpu.SMEM),
-        whole,
-        *[far] * parts,
+        *[far] * (len(lefts) + parts),
         block,
         whole,
         whole,
@@ -103,7 +119,7 @@
         specs.append(far)
     flops = 2 * width * CHANNEL_WIDTH * tile_rows * depth + 2 * STEP * tile_rows * CHANNEL_WIDTH**2 * channels
     return pl.pallas_call(
-        functools.partial(update_kernel, parts, part),
+        functools.partial(update_kernel, parts, part, cols, plan),
         grid=(1,),
         in_specs=specs,
         out_specs=(block, pl.BlockSpec((STEP, channels, tile_rows), lambda g: (0, 0, 0))),
@@ -112,11 +128,12 @@
             jax.ShapeDtypeStruct((STEP, channels, tile_rows), jnp.bfloat16),
         ),
         scratch_shapes=[
+            pltpu.VMEM((tile_rows, CHANNEL_WIDTH * depth), jnp.bfloat16),
             pltpu.VMEM((depth, width), jnp.bfloat16),
             pltpu.VMEM((width, depth), jnp.bfloat16),
             pltpu.VMEM((width, CHANNEL_WIDTH * tile_rows), jnp.bfloat16),
             pltpu.VMEM((tile_rows * STEP, channels), jnp.float32),
-            pltpu.SemaphoreType.DMA((parts,)),
+            pltpu.SemaphoreType.DMA((parts + len(plan),)),
         ],
         input_output_aliases=aliases,
         compiler_params=pltpu.CompilerParams(vmem_limit_bytes=VMEM_LIMIT),
@@ -225,27 +242,33 @@
     )(*args)
 
 
-def put_kernel(part, tile_cols, where_ref, rows_ref, earlier_ref, out_ref, sem):
-    del earlier_ref
-    row = pl.multiple_of((1 - where_ref[2]) * tile_cols + part * rows_ref.shape[0], rows_ref.shape[0])
-    copy = pltpu.make_async_copy(rows_ref, out_ref.at[pl.ds(row, rows_ref.shape[0])], sem)
-    copy.start()
-    copy.wait()
-
-
-def put_call(where, rows, earlier, part, tile_cols):
+def put_kernel(tile_cols, where_ref, *refs):
+    out_ref, sems = refs[-2:]
+    copies = []
+    for part, rows_ref in enumerate(refs[:-3]):
+        step = rows_ref.shape[0]
+        row = pl.multiple_of((1 - where_ref[2]) * tile_cols + part * step, step)
+        copy = pltpu.make_async_copy(rows_ref, out_ref.at[pl.ds(row, step)], sems.at[part])
+        copy.start()
+        copies.append(copy)
+    for copy in copies:
+        copy.wait()
+
+
+def put_call(where, rows, earlier, tile_cols):
     far = pl.BlockSpec(memory_space=pl.ANY)
+    whole = pl.BlockSpec(memory_space=pltpu.VMEM)
     return pl.pallas_call(
-        functools.partial(put_kernel, part, tile_cols),
-        in_specs=[pl.BlockSpec(memory_space=pltpu.SMEM), pl.BlockSpec(memory_space=pltpu.VMEM), far],
+        functools.partial(put_kernel, tile_cols),
+        in_specs=[pl.BlockSpec(memory_space=pltpu.SMEM), *[whole] * len(rows), far],
         out_specs=far,
         out_shape=jax.ShapeDtypeStruct(earlier.shape, earlier.dtype),
-        scratch_shapes=[pltpu.SemaphoreType.DMA],
-        input_output_aliases={2: 0},
+        scratch_shapes=[pltpu.SemaphoreType.DMA((len(rows),))],
+        input_output_aliases={1 + len(rows): 0},
         compiler_params=pltpu.CompilerParams(vmem_limit_bytes=VMEM_LIMIT),
-        cost_estimate=pl.CostEstimate(flops=0, bytes_accessed=2 * 2**20, transcendentals=0),
+        cost_estimate=pl.CostEstimate(flops=0, bytes_accessed=8 * 2**20, transcendentals=0),
         name="put",
-    )(where, rows, earlier)
+    )(where, *rows, earlier)
 
 
 def shards(
@@ -268,7 +291,27 @@
     rights = [alignment_right]
     for d in range(1, parts):
         rights.append(lax.ppermute(alignment_right, "row", [(a, a ^ d) for a in range(parts)]))
-    left = lax.all_gather(alignment_left, "col", axis=0, tiled=True)
+
+    ring = [z * CORES for z in range(line)] + [z * CORES + 1 for z in reversed(range(line))]
+    onward = [(ring[t], ring[(t + 1) % cols]) for t in range(cols)]
+    back = [(b, a) for a, b in onward]
+
+    if alignment_left.shape[0] % 16 == 0:
+        held = {0: alignment_left}
+        for s in range(1, line):
+            ahead, behind = held[-(s - 1)], held[s - 1]
+            if s == line - 1:
+                ahead, behind, _ = lax.optimization_barrier((ahead, behind, rights[1:]))
+            held[-s] = lax.ppermute(ahead, "col", onward)
+            held[s] = lax.ppermute(behind, "col", back)
+        half = alignment_left.shape[1] // 2
+        plan = tuple((offset, 0) for offset in sorted(held)) + ((line, 0), (line, half))
+        lefts = [held[offset] for offset in sorted(held)]
+        lefts.append(lax.ppermute(held[1 - line][:, :half], "col", onward))
+        lefts.append(lax.ppermute(held[line - 1][:, half:], "col", back))
+    else:
+        plan = ((None, 0),)
+        lefts = [lax.all_gather(alignment_left, "col", axis=0, tiled=True)]
 
     weight = output_weight.T
     bias = output_bias.reshape(channels, 1)
@@ -299,12 +342,18 @@
 
     def update(part, *others):
         state["new_pair"], tiles[part][0] = update_call(
-            after(where, *others), left, rights, pair_features, weight, bias, gain, state["new_pair"], part
-        )
-
-    ring = [z * CORES for z in range(line)] + [z * CORES + 1 for z in reversed(range(line))]
-    onward = [(ring[t], ring[(t + 1) % cols]) for t in range(cols)]
-    back = [(b, a) for a, b in onward]
+            after(where, *others),
+            lefts,
+            plan,
+            cols,
+            rights,
+            pair_features,
+            weight,
+            bias,
+            gain,
+            state["new_pair"],
+            part,
+        )
 
     def shift(part, s, *others):
         here = tiles[part]
@@ -336,9 +385,6 @@
     def exchange(part, *others):
         handed[part] = after(handed[part], *others)
         swapped[part] = lax.ppermute(handed[part], "col", [(c, c ^ 1) for c in range(cols)])
-
-    def put(part):
-        state["result"] = put_call(where, swapped[part], state["result"], part, tile_cols)
 
     order = sorted(
         ((part, s) for part in range(count) for s in range(1, line)),
@@ -380,7 +426,7 @@
     place(count - 1, *handed[:-1])
     for part in range(count):
         exchange(part, *moved[-1][1:])
-        put(part)
+    state["result"] = put_call(where, swapped, state["result"], tile_cols)
     return (state["new_pair"], state["result"])
 
 

time: 269 us -> 269 us (level)
  the two profiles are of different devices: /device:TPU:0 before, /device:TPU:19 now
where the time goes in v6:
time: 269 us; the launch traced here: 268 us
  waiting for transfers between devices  129 us (48%)
  starting transfers between devices  65 us (24%)
  Pallas kernels  56.2 us (21%)
  local copies, waits for them, and re-layouts  15.7 us (6%)
    ppermute x12, waiting for transfers between devices, send(): lax.ppermute(piece, 'row', [(a, a ^ d) for a in range(parts)])  42.5 us
    ppermute x12, starting transfers between devices, shift(): here[-s] = lax.ppermute(after(here[-(s - 1)], *others), 'col', onward)  38.8 us
    ppermute x12, waiting for transfers between devices, shift(): here[-s] = lax.ppermute(after(here[-(s - 1)], *others), 'col', onward)  31.3 us
    pallas_call x4, Pallas kernels, update_call(): pl.pallas_call(functools.partial(update_kernel, parts, part, cols, plan),...  29.1 us
    ppermute x12, waiting for transfers between devices, shift(): here[s] = lax.ppermute(after(here[s - 1], *others), 'col', back)  19.6 us
    pallas_call x4, Pallas kernels, project_call(): pl.pallas_call(functools.partial(project_kernel, line, parts), in_specs=[...  16.6 us
    ppermute x3, waiting for transfers between devices, shards(): held[-s] = lax.ppermute(ahead, 'col', onward)  16 us
    ppermute x12, starting transfers between devices, send(): lax.ppermute(piece, 'row', [(a, a ^ d) for a in range(parts)])  12 us
  transfers between devices with their start and end apart: 51, of which 27 were waited for; matrix products, arithmetic and copies ran while one was open for 4% of the time, Pallas kernels for 15%

profile of v6, /device:TPU:19, one launch (start us, length us, event | category | flops | bytes accessed | tf_op | source)
XLA Modules:
  0.0 268.3 jit_solution(6653586062635315078)
XLA Ops:
  4.8 7.3 %collective-permute-done.refs_2_ = bf16[16,16384]{1,0:T(8,128)(2,1)S(1)} collective-permute-done((bf16[16,16384]{1,0:T(8,128)(2,1)}, bf16[16,16384]{1,0:T(8,128)(2,1)S(1)}, u32[]{:S(2)}, u32[]{:S(2)}) %collective-permute-start) | collective-permute-done | bytes 524320 | tf_op jit(solution)/shard_map/ppermute | solution.py:305
  12.2 1.8 collective-permute-done.2.refs_4_
  15.3 11.4 %collective-permute-done.6.refs_12_ = bf16[128,2048]{1,0:T(8,128)(2,1)S(1)} collective-permute-done((bf16[128,2048]{1,0:T(8,128)(2,1)}, bf16[128,2048]{1,0:T(8,128)(2,1)S(1)}, u32[]{:S(2)}, u32[]{:S(2)}) %collective-permute-start.6) | collective-permute-done | bytes 524320 | tf_op jit(solution)/shard_map/ppermute | solution.py:293
  28.2 8.7 %collective-permute-done.7.refs_0_ = bf16[16,16384]{1,0:T(8,128)(2,1)S(1)} collective-permute-done((bf16[16,16384]{1,0:T(8,128)(2,1)S(1)}, bf16[16,16384]{1,0:T(8,128)(2,1)S(1)}, u32[]{:S(2)}, u32[]{:S(2)}) %collective-permute-start.7) | collective-permute-done | bytes 524320 | tf_op jit(solution)/shard_map/ppermute | solution.py:305
  39.9 1.8 collective-permute-start.10
  44.4 1.6 collective-permute-done.10.refs_8_
  47.1 7.2 %update.4 = (bf16[128,64,128]{2,1,0:T(8,128)(2,1)}, bf16[16,128,128]{2,1,0:T(8,128)(2,1)S(1)}) custom-call(s32[3]{0:T(128)S(1)} %pad_add_fusion.where_ref, bf16[16,16384]{1,0:T(8,128)(2,1)S(1)} %collective-permute-done.7.refs_0_, bf16[16,16384]{1,0:T(8,128)(2,1)S(1)} %collective-permute-done.1.refs_1_, bf16[16,16384]{1,0:T(8,128)(2,1)S(1)} %collective-permute-done.refs_2_, ...), custom_call_target="tpu_custom_call" | custom-call | flops 2684354560 | bytes 8388608 | tf_op jit(solution)/shard_map/update/pallas_call | solution.py:121
  54.3 3.5 %collective-permute-start.11 = (bf16[16,128,128]{2,1,0:T(8,128)(2,1)S(1)}, bf16[16,128,128]{2,1,0:T(8,128)(2,1)}, u32[]{:S(2)}, u32[]{:S(2)}) collective-permute-start(bf16[16,128,128]{2,1,0:T(8,128)(2,1)S(1)} %get-tuple-element.77.refs_3_), channel_id=1, source_target_pairs={{0,2},{2,4},{4,6},{6,7},{7,5},{5,3},{3,1},{1,0},{8,10},{10,12},{12... | collective-permute-start | bytes 1572872 | tf_op jit(solution)/shard_map/ppermute | solution.py:360
  57.9 7.3 %collective-permute-done.11.refs_2_ = bf16[16,128,128]{2,1,0:T(8,128)(2,1)} collective-permute-done((bf16[16,128,128]{2,1,0:T(8,128)(2,1)S(1)}, bf16[16,128,128]{2,1,0:T(8,128)(2,1)}, u32[]{:S(2)}, u32[]{:S(2)}) %collective-permute-start.11) | collective-permute-done | bytes 524320 | tf_op jit(solution)/shard_map/ppermute | solution.py:360
  65.2 2.3 collective-permute-start.15
  67.5 1.8 collective-permute-done.12.refs_4_
  69.6 1.5 constant_dynamic-slice_fusion.1
  74.0 7.4 %update.5 = (bf16[128,64,128]{2,1,0:T(8,128)(2,1)}, bf16[16,128,128]{2,1,0:T(8,128)(2,1)}) custom-call(s32[3]{0:T(128)S(1)} %pad_add_fusion.where_ref, bf16[16,16384]{1,0:T(8,128)(2,1)S(1)} %collective-permute-done.7.refs_0_, bf16[16,16384]{1,0:T(8,128)(2,1)S(1)} %collective-permute-done.1.refs_1_, ...), custom_call_target="tpu_custom_call", output_to_operand_aliasing={{0}: (18, {})} | custom-call | flops 2684354560 | bytes 8388608 | tf_op jit(solution)/shard_map/update/pallas_call | solution.py:121
  81.4 3.0 %collective-permute-start.13 = (bf16[16,128,128]{2,1,0:T(8,128)(2,1)}, bf16[16,128,128]{2,1,0:T(8,128)(2,1)}, u32[]{:S(2)}, u32[]{:S(2)}) collective-permute-start(bf16[16,128,128]{2,1,0:T(8,128)(2,1)} %get-tuple-element.78.refs_3_), channel_id=1, source_target_pairs={{0,2},{2,4},{4,6},{6,7},{7,5},{5,3},{3,1},{1,0},{8,10},{10,12},{12... | collective-permute-start | bytes 1572872 | tf_op jit(solution)/shard_map/ppermute | solution.py:360
  84.4 1.5 collective-permute-start.17
  87.5 5.2 %collective-permute-done.13.refs_2_ = bf16[16,128,128]{2,1,0:T(8,128)(2,1)} collective-permute-done((bf16[16,128,128]{2,1,0:T(8,128)(2,1)}, bf16[16,128,128]{2,1,0:T(8,128)(2,1)}, u32[]{:S(2)}, u32[]{:S(2)}) %collective-permute-start.13) | collective-permute-done | bytes 524320 | tf_op jit(solution)/shard_map/ppermute | solution.py:360
  92.7 3.7 %collective-permute-done.14.refs_4_ = bf16[16,128,128]{2,1,0:T(8,128)(2,1)} collective-permute-done((bf16[16,128,128]{2,1,0:T(8,128)(2,1)}, bf16[16,128,128]{2,1,0:T(8,128)(2,1)}, u32[]{:S(2)}, u32[]{:S(2)}) %collective-permute-start.14) | collective-permute-done | bytes 524320 | tf_op jit(solution)/shard_map/ppermute | solution.py:361
  96.4 1.7 collective-permute-start.21
  98.1 5.8 %collective-permute-done.17.refs_0_ = bf16[16,128,128]{2,1,0:T(8,128)(2,1)} collective-permute-done((bf16[16,128,128]{2,1,0:T(8,128)(2,1)}, bf16[16,128,128]{2,1,0:T(8,128)(2,1)}, u32[]{:S(2)}, u32[]{:S(2)}) %collective-permute-start.17) | collective-permute-done | bytes 524320 | tf_op jit(solution)/shard_map/ppermute | solution.py:360
  103.9 3.7 %collective-permute-done.18.refs_6_ = bf16[16,128,128]{2,1,0:T(8,128)(2,1)} collective-permute-done((bf16[16,128,128]{2,1,0:T(8,128)(2,1)}, bf16[16,128,128]{2,1,0:T(8,128)(2,1)}, u32[]{:S(2)}, u32[]{:S(2)}) %collective-permute-start.18) | collective-permute-done | bytes 524320 | tf_op jit(solution)/shard_map/ppermute | solution.py:361
  107.6 3.8 %project.4 = (bf16[2,16,64,128]{3,2,1,0:T(8,128)(2,1)S(1)}, bf16[2,16,64,128]{3,2,1,0:T(8,128)(2,1)S(1)}, bf16[2,16,64,128]{3,2,1,0:T(8,128)(2,1)S(1)}, bf16[2,16,64,128]{3,2,1,0:T(8,128)(2,1)S(1)}) custom-call(s32[3]{0:T(128)S(1)} %pad_add_fusion.where_ref, bf16[128,128]{1,0:T(8,128)(2,1)S(1)} %pad_maximum_fusion.weight_ref, f32[128,1]{1,0:T(8,128)S(1)} %copy.43.offset_ref, ...), custom_call_target="tpu_custom_call" | custom-call | flops 268435456 | bytes 4194304 | tf_op jit(solution)/shard_map/project/pallas_call | solution.py:182
  114.3 7.2 %update.6 = (bf16[128,64,128]{2,1,0:T(8,128)(2,1)}, bf16[16,128,128]{2,1,0:T(8,128)(2,1)S(1)}) custom-call(s32[3]{0:T(128)S(1)} %pad_add_fusion.where_ref, bf16[16,16384]{1,0:T(8,128)(2,1)S(1)} %collective-permute-done.7.refs_0_, bf16[16,16384]{1,0:T(8,128)(2,1)S(1)} %collective-permute-done.1.refs_1_, ...), custom_call_target="tpu_custom_call", output_to_operand_aliasing={{0}: (18, {})} | custom-call | flops 2684354560 | bytes 8388608 | tf_op jit(solution)/shard_map/update/pallas_call | solution.py:121
  123.0 2.2 collective-permute-start.23
  127.6 2.3 collective-permute-done.19.refs_2_
  129.9 2.4 collective-permute-done.20.refs_4_
  132.3 9.6 %collective-permute-start.24 = (bf16[16,128,128]{2,1,0:T(8,128)(2,1)S(1)}, bf16[16,128,128]{2,1,0:T(8,128)(2,1)S(1)}, u32[]{:S(2)}, u32[]{:S(2)}) collective-permute-start(bf16[16,128,128]{2,1,0:T(8,128)(2,1)S(1)} %collective-permute-done.19.refs_2_), channel_id=1, source_target_pairs={{0,2},{2,4},{4,6},{6,7},{7,5},{5,3},{3,1},{1,0},{8,10},{10,12},{12... | collective-permute-start | bytes 1572872 | tf_op jit(solution)/shard_map/ppermute | solution.py:360
  144.3 4.2 %project.5 = (bf16[2,16,64,128]{3,2,1,0:T(8,128)(2,1)S(1)}, bf16[2,16,64,128]{3,2,1,0:T(8,128)(2,1)S(1)}, bf16[2,16,64,128]{3,2,1,0:T(8,128)(2,1)S(1)}, bf16[2,16,64,128]{3,2,1,0:T(8,128)(2,1)S(1)}) custom-call(s32[3]{0:T(128)S(1)} %pad_add_fusion.where_ref, bf16[128,128]{1,0:T(8,128)(2,1)S(1)} %pad_maximum_fusion.weight_ref, f32[128,1]{1,0:T(8,128)S(1)} %copy.43.offset_ref, ...), custom_call_target="tpu_custom_call" | custom-call | flops 268435456 | bytes 4194304 | tf_op jit(solution)/shard_map/project/pallas_call | solution.py:182
  149.6 7.2 %update.7 = (bf16[128,64,128]{2,1,0:T(8,128)(2,1)}, bf16[16,128,128]{2,1,0:T(8,128)(2,1)S(1)}) custom-call(s32[3]{0:T(128)S(1)} %pad_add_fusion.where_ref, bf16[16,16384]{1,0:T(8,128)(2,1)S(1)} %collective-permute-done.7.refs_0_, bf16[16,16384]{1,0:T(8,128)(2,1)S(1)} %collective-permute-done.1.refs_1_, ...), custom_call_target="tpu_custom_call", output_to_operand_aliasing={{0}: (18, {})} | custom-call | flops 2684354560 | bytes 8388608 | tf_op jit(solution)/shard_map/update/pallas_call | solution.py:121
  156.9 9.7 %collective-permute-start.36 = (bf16[16,128,128]{2,1,0:T(8,128)(2,1)S(1)}, bf16[16,128,128]{2,1,0:T(8,128)(2,1)S(1)}, u32[]{:S(2)}, u32[]{:S(2)}) collective-permute-start(bf16[16,128,128]{2,1,0:T(8,128)(2,1)S(1)} %get-tuple-element.117.refs_3_), channel_id=1, source_target_pairs={{0,2},{2,4},{4,6},{6,7},{7,5},{5,3},{3,1},{1,0},{8,10},{10,12},{12... | collective-permute-start | bytes 1572872 | tf_op jit(solution)/shard_map/ppermute | solution.py:360
  167.1 3.9 %collective-permute-start.31 = (bf16[16,128,128]{2,1,0:T(8,128)(2,1)S(1)}, bf16[16,128,128]{2,1,0:T(8,128)(2,1)S(1)}, u32[]{:S(2)}, u32[]{:S(2)}) collective-permute-start(bf16[16,128,128]{2,1,0:T(8,128)(2,1)S(1)} %collective-permute-done.24.refs_1_), channel_id=1, source_target_pairs={{0,2},{2,4},{4,6},{6,7},{7,5},{5,3},{3,1},{1,0},{8,10},{10,12},{12... | collective-permute-start | bytes 1572872 | tf_op jit(solution)/shard_map/ppermute | solution.py:360
  171.0 1.8 place.4
  172.9 3.7 %collective-permute-done.36.refs_2_ = bf16[16,128,128]{2,1,0:T(8,128)(2,1)S(1)} collective-permute-done((bf16[16,128,128]{2,1,0:T(8,128)(2,1)S(1)}, bf16[16,128,128]{2,1,0:T(8,128)(2,1)S(1)}, u32[]{:S(2)}, u32[]{:S(2)}) %collective-permute-start.36) | collective-permute-done | bytes 524320 | tf_op jit(solution)/shard_map/ppermute | solution.py:360
  176.7 3.8 %collective-permute-done.37.refs_4_ = bf16[16,128,128]{2,1,0:T(8,128)(2,1)S(1)} collective-permute-done((bf16[16,128,128]{2,1,0:T(8,128)(2,1)S(1)}, bf16[16,128,128]{2,1,0:T(8,128)(2,1)S(1)}, u32[]{:S(2)}, u32[]{:S(2)}) %collective-permute-start.37) | collective-permute-done | bytes 524320 | tf_op jit(solution)/shard_map/ppermute | solution.py:361
  181.0 6.9 %collective-permute-done.31.refs_0_ = bf16[16,128,128]{2,1,0:T(8,128)(2,1)S(1)} collective-permute-done((bf16[16,128,128]{2,1,0:T(8,128)(2,1)S(1)}, bf16[16,128,128]{2,1,0:T(8,128)(2,1)S(1)}, u32[]{:S(2)}, u32[]{:S(2)}) %collective-permute-start.31) | collective-permute-done | bytes 524320 | tf_op jit(solution)/shard_map/ppermute | solution.py:360
  187.9 3.8 %collective-permute-done.32.refs_6_ = bf16[16,128,128]{2,1,0:T(8,128)(2,1)S(1)} collective-permute-done((bf16[16,128,128]{2,1,0:T(8,128)(2,1)}, bf16[16,128,128]{2,1,0:T(8,128)(2,1)S(1)}, u32[]{:S(2)}, u32[]{:S(2)}) %collective-permute-start.32) | collective-permute-done | bytes 524320 | tf_op jit(solution)/shard_map/ppermute | solution.py:361
  192.5 4.4 %project.6 = (bf16[2,16,64,128]{3,2,1,0:T(8,128)(2,1)S(1)}, bf16[2,16,64,128]{3,2,1,0:T(8,128)(2,1)S(1)}, bf16[2,16,64,128]{3,2,1,0:T(8,128)(2,1)S(1)}, bf16[2,16,64,128]{3,2,1,0:T(8,128)(2,1)S(1)}) custom-call(s32[3]{0:T(128)S(1)} %pad_add_fusion.where_ref, bf16[128,128]{1,0:T(8,128)(2,1)S(1)} %pad_maximum_fusion.weight_ref, f32[128,1]{1,0:T(8,128)S(1)} %copy.43.offset_ref, ...), custom_call_target="tpu_custom_call" | custom-call | flops 268435456 | bytes 4194304 | tf_op jit(solution)/shard_map/project/pallas_call | solution.py:182
  199.2 11.2 %collective-permute-done.33.refs_1_ = bf16[2,16,64,128]{3,2,1,0:T(8,128)(2,1)S(1)} collective-permute-done((bf16[2,16,64,128]{3,2,1,0:T(8,128)(2,1)S(1)}, bf16[2,16,64,128]{3,2,1,0:T(8,128)(2,1)S(1)}, u32[]{:S(2)}, u32[]{:S(2)}) %collective-permute-start.33) | collective-permute-done | bytes 524320 | tf_op jit(solution)/shard_map/ppermute | solution.py:378
  212.3 11.6 %collective-permute-done.35.refs_3_ = bf16[2,16,64,128]{3,2,1,0:T(8,128)(2,1)S(1)} collective-permute-done((bf16[2,16,64,128]{3,2,1,0:T(8,128)(2,1)S(1)}, bf16[2,16,64,128]{3,2,1,0:T(8,128)(2,1)S(1)}, u32[]{:S(2)}, u32[]{:S(2)}) %collective-permute-start.35) | collective-permute-done | bytes 524320 | tf_op jit(solution)/shard_map/ppermute | solution.py:378
  224.7 4.2 %project.7 = (bf16[2,16,64,128]{3,2,1,0:T(8,128)(2,1)S(1)}, bf16[2,16,64,128]{3,2,1,0:T(8,128)(2,1)S(1)}, bf16[2,16,64,128]{3,2,1,0:T(8,128)(2,1)S(1)}, bf16[2,16,64,128]{3,2,1,0:T(8,128)(2,1)S(1)}) custom-call(s32[3]{0:T(128)S(1)} %pad_add_fusion.where_ref, bf16[128,128]{1,0:T(8,128)(2,1)S(1)} %pad_maximum_fusion.weight_ref, f32[128,1]{1,0:T(8,128)S(1)} %copy.43.offset_ref, ...), custom_call_target="tpu_custom_call" | custom-call | flops 268435456 | bytes 4194304 | tf_op jit(solution)/shard_map/project/pallas_call | solution.py:182
  228.9 2.6 collective-permute-start.44
  232.8 1.8 place.5
  234.6 1.8 place.6
  236.5 7.2 %collective-permute-done.44.refs_1_ = bf16[2,16,64,128]{3,2,1,0:T(8,128)(2,1)S(1)} collective-permute-done((bf16[2,16,64,128]{3,2,1,0:T(8,128)(2,1)S(1)}, bf16[2,16,64,128]{3,2,1,0:T(8,128)(2,1)S(1)}, u32[]{:S(2)}, u32[]{:S(2)}) %collective-permute-start.44) | collective-permute-done | bytes 524320 | tf_op jit(solution)/shard_map/ppermute | solution.py:378
  243.7 12.3 %collective-permute-done.45.refs_2_ = bf16[2,16,64,128]{3,2,1,0:T(8,128)(2,1)S(1)} collective-permute-done((bf16[2,16,64,128]{3,2,1,0:T(8,128)(2,1)S(1)}, bf16[2,16,64,128]{3,2,1,0:T(8,128)(2,1)S(1)}, u32[]{:S(2)}, u32[]{:S(2)}) %collective-permute-start.45) | collective-permute-done | bytes 524320 | tf_op jit(solution)/shard_map/ppermute | solution.py:378
  257.6 1.8 place.7
  260.9 1.5 collective-permute-done.49.refs_2_
  262.4 1.5 collective-permute-done.50.refs_3_
  264.8 3.3 %put.1 = bf16[128,64,512]{2,1,0:T(8,128)(2,1)} custom-call(s32[3]{0:T(128)S(1)} %pad_add_fusion.where_ref, bf16[16,64,512]{2,1,0:T(8,128)(2,1)S(1)} %collective-permute-done.47.refs_0_, bf16[16,64,512]{2,1,0:T(8,128)(2,1)S(1)} %collective-permute-done.48.refs_1_, ...), custom_call_target="tpu_custom_call", output_to_operand_aliasing={{}: (5, {})} | custom-call | bytes 8388608 | tf_op jit(solution)/shard_map/put/pallas_call | solution.py:261
  (133 shorter events, 40.9 us)
Async XLA Ops:
  0.6 11.4 %collective-permute-start = (bf16[16,16384]{1,0:T(8,128)(2,1)}, bf16[16,16384]{1,0:T(8,128)(2,1)S(1)}, u32[]{:S(2)}, u32[]{:S(2)}) collective-permute-start(bf16[16,16384]{1,0:T(8,128)(2,1)} %refs_3_.7), channel_id=1, source_target_pairs={{0,2},{2,4},{4,6},{6,7},{7,5},{5,3},{3,1},{1,0},{8,10},{10,12},{12... | collective-permute-start | bytes 1572872 | tf_op jit(solution)/shard_map/ppermute | solution.py:305
  0.8 13.2 %collective-permute-start.2 = (bf16[16,16384]{1,0:T(8,128)(2,1)}, bf16[16,16384]{1,0:T(8,128)(2,1)S(1)}, u32[]{:S(2)}, u32[]{:S(2)}) collective-permute-start(bf16[16,16384]{1,0:T(8,128)(2,1)} %refs_3_.7), channel_id=1, source_target_pairs={{2,0},{4,2},{6,4},{7,6},{5,7},{3,5},{1,3},{0,1},{10,8},{12,10},{14... | collective-permute-start | bytes 1572872 | tf_op jit(solution)/shard_map/ppermute | solution.py:306
  2.1 13.2 %collective-permute-start.4 = (bf16[128,2048]{1,0:T(8,128)(2,1)}, bf16[128,2048]{1,0:T(8,128)(2,1)S(1)}, u32[]{:S(2)}, u32[]{:S(2)}) collective-permute-start(bf16[128,2048]{1,0:T(8,128)(2,1)} %refs_9_.7), channel_id=1, source_target_pairs={{0,8},{8,0},{16,24},{24,16},{1,9},{9,1},{17,25},{25,17},{2,10},{10... | collective-permute-start | bytes 1572872 | tf_op jit(solution)/shard_map/ppermute | solution.py:293
  2.4 12.9 %collective-permute-start.5 = (bf16[128,2048]{1,0:T(8,128)(2,1)}, bf16[128,2048]{1,0:T(8,128)(2,1)S(1)}, u32[]{:S(2)}, u32[]{:S(2)}) collective-permute-start(bf16[128,2048]{1,0:T(8,128)(2,1)} %refs_9_.7), channel_id=1, source_target_pairs={{0,16},{8,24},{16,0},{24,8},{1,17},{9,25},{17,1},{25,9},{2,18},{10... | collective-permute-start | bytes 1572872 | tf_op jit(solution)/shard_map/ppermute | solution.py:293
  3.6 23.1 %collective-permute-start.6 = (bf16[128,2048]{1,0:T(8,128)(2,1)}, bf16[128,2048]{1,0:T(8,128)(2,1)S(1)}, u32[]{:S(2)}, u32[]{:S(2)}) collective-permute-start(bf16[128,2048]{1,0:T(8,128)(2,1)} %refs_9_.7), channel_id=1, source_target_pairs={{0,24},{8,16},{16,8},{24,0},{1,25},{9,17},{17,9},{25,1},{2,26},{10... | collective-permute-start | bytes 1572872 | tf_op jit(solution)/shard_map/ppermute | solution.py:293
  12.0 14.7 %collective-permute-start.1 = (bf16[16,16384]{1,0:T(8,128)(2,1)S(1)}, bf16[16,16384]{1,0:T(8,128)(2,1)S(1)}, u32[]{:S(2)}, u32[]{:S(2)}) collective-permute-start(bf16[16,16384]{1,0:T(8,128)(2,1)S(1)} %collective-permute-done.refs_2_), channel_id=1, source_target_pairs={{0,2},{2,4},{4,6},{6,7},{7,5},{5,3},{3,1},{1,0},{8,10},{10,12},{12... | collective-permute-start | bytes 1572872 | tf_op jit(solution)/shard_map/ppermute | solution.py:305
  14.0 12.7 %collective-permute-start.3 = (bf16[16,16384]{1,0:T(8,128)(2,1)S(1)}, bf16[16,16384]{1,0:T(8,128)(2,1)S(1)}, u32[]{:S(2)}, u32[]{:S(2)}) collective-permute-start(bf16[16,16384]{1,0:T(8,128)(2,1)S(1)} %collective-permute-done.2.refs_4_), channel_id=1, source_target_pairs={{2,0},{4,2},{6,4},{7,6},{5,7},{3,5},{1,3},{0,1},{10,8},{12,10},{14... | collective-permute-start | bytes 1572872 | tf_op jit(solution)/shard_map/ppermute | solution.py:306
  26.7 10.2 %collective-permute-start.7 = (bf16[16,16384]{1,0:T(8,128)(2,1)S(1)}, bf16[16,16384]{1,0:T(8,128)(2,1)S(1)}, u32[]{:S(2)}, u32[]{:S(2)}) collective-permute-start(bf16[16,16384]{1,0:T(8,128)(2,1)S(1)} %collective-permute-done.1.refs_1_), channel_id=1, source_target_pairs={{0,2},{2,4},{4,6},{6,7},{7,5},{5,3},{3,1},{1,0},{8,10},{10,12},{12... | collective-permute-start | bytes 1572872 | tf_op jit(solution)/shard_map/ppermute | solution.py:305
  26.9 11.4 %collective-permute-start.8 = (bf16[16,16384]{1,0:T(8,128)(2,1)S(1)}, bf16[16,16384]{1,0:T(8,128)(2,1)S(1)}, u32[]{:S(2)}, u32[]{:S(2)}) collective-permute-start(bf16[16,16384]{1,0:T(8,128)(2,1)S(1)} %collective-permute-done.3.refs_5_), channel_id=1, source_target_pairs={{2,0},{4,2},{6,4},{7,6},{5,7},{3,5},{1,3},{0,1},{10,8},{12,10},{14... | collective-permute-start | bytes 1572872 | tf_op jit(solution)/shard_map/ppermute | solution.py:306
  37.7 6.7 %collective-permute-start.9 = (bf16[16,8192]{1,0:T(8,128)(2,1)}, bf16[16,8192]{1,0:T(8,128)(2,1)S(1)}, u32[]{:S(2)}, u32[]{:S(2)}) collective-permute-start(bf16[16,8192]{1,0:T(8,128)(2,1)} %slice.8), channel_id=1, source_target_pairs={{0,2},{2,4},{4,6},{6,7},{7,5},{5,3},{3,1},{1,0},{8,10},{10,12},{12... | collective-permute-start | bytes 786440 | tf_op jit(solution)/shard_map/ppermute | solution.py:310
  39.9 6.2 %collective-permute-start.10 = (bf16[16,8192]{1,0:T(8,128)(2,1)}, bf16[16,8192]{1,0:T(8,128)(2,1)S(1)}, u32[]{:S(2)}, u32[]{:S(2)}) collective-permute-start(bf16[16,8192]{1,0:T(8,128)(2,1)} %slice.9), channel_id=1, source_target_pairs={{2,0},{4,2},{6,4},{7,6},{5,7},{3,5},{1,3},{0,1},{10,8},{12,10},{14... | collective-permute-start | bytes 786440 | tf_op jit(solution)/shard_map/ppermute | solution.py:311
  54.3 10.9 %collective-permute-start.11 = (bf16[16,128,128]{2,1,0:T(8,128)(2,1)S(1)}, bf16[16,128,128]{2,1,0:T(8,128)(2,1)}, u32[]{:S(2)}, u32[]{:S(2)}) collective-permute-start(bf16[16,128,128]{2,1,0:T(8,128)(2,1)S(1)} %get-tuple-element.77.refs_3_), channel_id=1, source_target_pairs={{0,2},{2,4},{4,6},{6,7},{7,5},{5,3},{3,1},{1,0},{8,10},{10,12},{12... | collective-permute-start | bytes 1572872 | tf_op jit(solution)/shard_map/ppermute | solution.py:360
  57.9 11.4 %collective-permute-start.12 = (bf16[16,128,128]{2,1,0:T(8,128)(2,1)S(1)}, bf16[16,128,128]{2,1,0:T(8,128)(2,1)}, u32[]{:S(2)}, u32[]{:S(2)}) collective-permute-start(bf16[16,128,128]{2,1,0:T(8,128)(2,1)S(1)} %get-tuple-element.77.refs_3_), channel_id=1, source_target_pairs={{2,0},{4,2},{6,4},{7,6},{5,7},{3,5},{1,3},{0,1},{10,8},{12,10},{14... | collective-permute-start | bytes 1572872 | tf_op jit(solution)/shard_map/ppermute | solution.py:361
  65.2 19.2 %collective-permute-start.15 = (bf16[16,128,128]{2,1,0:T(8,128)(2,1)}, bf16[16,128,128]{2,1,0:T(8,128)(2,1)}, u32[]{:S(2)}, u32[]{:S(2)}) collective-permute-start(bf16[16,128,128]{2,1,0:T(8,128)(2,1)} %collective-permute-done.11.refs_2_), channel_id=1, source_target_pairs={{0,2},{2,4},{4,6},{6,7},{7,5},{5,3},{3,1},{1,0},{8,10},{10,12},{12... | collective-permute-start | bytes 1572872 | tf_op jit(solution)/shard_map/ppermute | solution.py:360
  69.3 15.1 %collective-permute-start.16 = (bf16[16,128,128]{2,1,0:T(8,128)(2,1)}, bf16[16,128,128]{2,1,0:T(8,128)(2,1)}, u32[]{:S(2)}, u32[]{:S(2)}) collective-permute-start(bf16[16,128,128]{2,1,0:T(8,128)(2,1)} %collective-permute-done.12.refs_4_), channel_id=1, source_target_pairs={{2,0},{4,2},{6,4},{7,6},{5,7},{3,5},{1,3},{0,1},{10,8},{12,10},{14... | collective-permute-start | bytes 1572872 | tf_op jit(solution)/shard_map/ppermute | solution.py:361
  81.4 11.3 %collective-permute-start.13 = (bf16[16,128,128]{2,1,0:T(8,128)(2,1)}, bf16[16,128,128]{2,1,0:T(8,128)(2,1)}, u32[]{:S(2)}, u32[]{:S(2)}) collective-permute-start(bf16[16,128,128]{2,1,0:T(8,128)(2,1)} %get-tuple-element.78.refs_3_), channel_id=1, source_target_pairs={{0,2},{2,4},{4,6},{6,7},{7,5},{5,3},{3,1},{1,0},{8,10},{10,12},{12... | collective-permute-start | bytes 1572872 | tf_op jit(solution)/shard_map/ppermute | solution.py:360
  84.4 12.0 %collective-permute-start.14 = (bf16[16,128,128]{2,1,0:T(8,128)(2,1)}, bf16[16,128,128]{2,1,0:T(8,128)(2,1)}, u32[]{:S(2)}, u32[]{:S(2)}) collective-permute-start(bf16[16,128,128]{2,1,0:T(8,128)(2,1)} %get-tuple-element.78.refs_3_), channel_id=1, source_target_pairs={{2,0},{4,2},{6,4},{7,6},{5,7},{3,5},{1,3},{0,1},{10,8},{12,10},{14... | collective-permute-start | bytes 1572872 | tf_op jit(solution)/shard_map/ppermute | solution.py:361
  84.4 19.5 %collective-permute-start.17 = (bf16[16,128,128]{2,1,0:T(8,128)(2,1)}, bf16[16,128,128]{2,1,0:T(8,128)(2,1)}, u32[]{:S(2)}, u32[]{:S(2)}) collective-permute-start(bf16[16,128,128]{2,1,0:T(8,128)(2,1)} %collective-permute-done.15.refs_1_), channel_id=1, source_target_pairs={{0,2},{2,4},{4,6},{6,7},{7,5},{5,3},{3,1},{1,0},{8,10},{10,12},{12... | collective-permute-start | bytes 1572872 | tf_op jit(solution)/shard_map/ppermute | solution.py:360
  85.9 21.7 %collective-permute-start.18 = (bf16[16,128,128]{2,1,0:T(8,128)(2,1)}, bf16[16,128,128]{2,1,0:T(8,128)(2,1)}, u32[]{:S(2)}, u32[]{:S(2)}) collective-permute-start(bf16[16,128,128]{2,1,0:T(8,128)(2,1)} %collective-permute-done.16.refs_5_), channel_id=1, source_target_pairs={{2,0},{4,2},{6,4},{7,6},{5,7},{3,5},{1,3},{0,1},{10,8},{12,10},{14... | collective-permute-start | bytes 1572872 | tf_op jit(solution)/shard_map/ppermute | solution.py:361
  96.4 26.6 %collective-permute-start.21 = (bf16[16,128,128]{2,1,0:T(8,128)(2,1)}, bf16[16,128,128]{2,1,0:T(8,128)(2,1)S(1)}, u32[]{:S(2)}, u32[]{:S(2)}) collective-permute-start(bf16[16,128,128]{2,1,0:T(8,128)(2,1)} %collective-permute-done.13.refs_2_), channel_id=1, source_target_pairs={{0,2},{2,4},{4,6},{6,7},{7,5},{5,3},{3,1},{1,0},{8,10},{10,12},{12... | collective-permute-start | bytes 1572872 | tf_op jit(solution)/shard_map/ppermute | solution.py:360
  98.1 24.9 %collective-permute-start.22 = (bf16[16,128,128]{2,1,0:T(8,128)(2,1)}, bf16[16,128,128]{2,1,0:T(8,128)(2,1)S(1)}, u32[]{:S(2)}, u32[]{:S(2)}) collective-permute-start(bf16[16,128,128]{2,1,0:T(8,128)(2,1)} %collective-permute-done.14.refs_4_), channel_id=1, source_target_pairs={{2,0},{4,2},{6,4},{7,6},{5,7},{3,5},{1,3},{0,1},{10,8},{12,10},{14... | collective-permute-start | bytes 1572872 | tf_op jit(solution)/shard_map/ppermute | solution.py:361
  111.5 13.8 %collective-permute-start.26 = (bf16[2,16,64,128]{3,2,1,0:T(8,128)(2,1)S(1)}, bf16[2,16,64,128]{3,2,1,0:T(8,128)(2,1)S(1)}, u32[]{:S(2)}, u32[]{:S(2)}) collective-permute-start(bf16[2,16,64,128]{3,2,1,0:T(8,128)(2,1)S(1)} %get-tuple-element.98), channel_id=1, source_target_pairs={{0,8},{8,0},{16,24},{24,16},{1,9},{9,1},{17,25},{25,17},{2,10},{10... | collective-permute-start | bytes 1572872 | tf_op jit(solution)/shard_map/ppermute | solution.py:378
  121.5 8.4 %collective-permute-start.19 = (bf16[16,128,128]{2,1,0:T(8,128)(2,1)S(1)}, bf16[16,128,128]{2,1,0:T(8,128)(2,1)S(1)}, u32[]{:S(2)}, u32[]{:S(2)}) collective-permute-start(bf16[16,128,128]{2,1,0:T(8,128)(2,1)S(1)} %get-tuple-element.84.refs_3_), channel_id=1, source_target_pairs={{0,2},{2,4},{4,6},{6,7},{7,5},{5,3},{3,1},{1,0},{8,10},{10,12},{12... | collective-permute-start | bytes 1572872 | tf_op jit(solution)/shard_map/ppermute | solution.py:360
  122.7 9.6 %collective-permute-start.20 = (bf16[16,128,128]{2,1,0:T(8,128)(2,1)S(1)}, bf16[16,128,128]{2,1,0:T(8,128)(2,1)S(1)}, u32[]{:S(2)}, u32[]{:S(2)}) collective-permute-start(bf16[16,128,128]{2,1,0:T(8,128)(2,1)S(1)} %get-tuple-element.84.refs_3_), channel_id=1, source_target_pairs={{2,0},{4,2},{6,4},{7,6},{5,7},{3,5},{1,3},{0,1},{10,8},{12,10},{14... | collective-permute-start | bytes 1572872 | tf_op jit(solution)/shard_map/ppermute | solution.py:361
  123.0 9.3 %collective-permute-start.23 = (bf16[2,16,64,128]{3,2,1,0:T(8,128)(2,1)S(1)}, bf16[2,16,64,128]{3,2,1,0:T(8,128)(2,1)S(1)}, u32[]{:S(2)}, u32[]{:S(2)}) collective-permute-start(bf16[2,16,64,128]{3,2,1,0:T(8,128)(2,1)S(1)} %get-tuple-element.92), channel_id=1, source_target_pairs={{0,16},{8,24},{16,0},{24,8},{1,17},{9,25},{17,1},{25,9},{2,18},{10... | collective-permute-start | bytes 1572872 | tf_op jit(solution)/shard_map/ppermute | solution.py:378
  125.3 17.9 %collective-permute-start.28 = (bf16[16,128,128]{2,1,0:T(8,128)(2,1)S(1)}, bf16[16,128,128]{2,1,0:T(8,128)(2,1)S(1)}, u32[]{:S(2)}, u32[]{:S(2)}) collective-permute-start(bf16[16,128,128]{2,1,0:T(8,128)(2,1)S(1)} %collective-permute-done.21.refs_1_), channel_id=1, source_target_pairs={{0,2},{2,4},{4,6},{6,7},{7,5},{5,3},{3,1},{1,0},{8,10},{10,12},{12... | collective-permute-start | bytes 1572872 | tf_op jit(solution)/shard_map/ppermute | solution.py:360
  126.4 17.1 %collective-permute-start.29 = (bf16[16,128,128]{2,1,0:T(8,128)(2,1)S(1)}, bf16[16,128,128]{2,1,0:T(8,128)(2,1)S(1)}, u32[]{:S(2)}, u32[]{:S(2)}) collective-permute-start(bf16[16,128,128]{2,1,0:T(8,128)(2,1)S(1)} %collective-permute-done.22.refs_5_), channel_id=1, source_target_pairs={{2,0},{4,2},{6,4},{7,6},{5,7},{3,5},{1,3},{0,1},{10,8},{12,10},{14... | collective-permute-start | bytes 1572872 | tf_op jit(solution)/shard_map/ppermute | solution.py:361
  132.3 34.2 %collective-permute-start.24 = (bf16[16,128,128]{2,1,0:T(8,128)(2,1)S(1)}, bf16[16,128,128]{2,1,0:T(8,128)(2,1)S(1)}, u32[]{:S(2)}, u32[]{:S(2)}) collective-permute-start(bf16[16,128,128]{2,1,0:T(8,128)(2,1)S(1)} %collective-permute-done.19.refs_2_), channel_id=1, source_target_pairs={{0,2},{2,4},{4,6},{6,7},{7,5},{5,3},{3,1},{1,0},{8,10},{10,12},{12... | collective-permute-start | bytes 1572872 | tf_op jit(solution)/shard_map/ppermute | solution.py:360
  142.0 24.6 %collective-permute-start.25 = (bf16[16,128,128]{2,1,0:T(8,128)(2,1)S(1)}, bf16[16,128,128]{2,1,0:T(8,128)(2,1)}, u32[]{:S(2)}, u32[]{:S(2)}) collective-permute-start(bf16[16,128,128]{2,1,0:T(8,128)(2,1)S(1)} %collective-permute-done.20.refs_4_), channel_id=1, source_target_pairs={{2,0},{4,2},{6,4},{7,6},{5,7},{3,5},{1,3},{0,1},{10,8},{12,10},{14... | collective-permute-start | bytes 1572872 | tf_op jit(solution)/shard_map/ppermute | solution.py:361
  142.0 14.9 %collective-permute-start.27 = (bf16[2,16,64,128]{3,2,1,0:T(8,128)(2,1)S(1)}, bf16[2,16,64,128]{3,2,1,0:T(8,128)(2,1)S(1)}, u32[]{:S(2)}, u32[]{:S(2)}) collective-permute-start(bf16[2,16,64,128]{3,2,1,0:T(8,128)(2,1)S(1)} %get-tuple-element.100), channel_id=1, source_target_pairs={{0,24},{8,16},{16,8},{24,0},{1,25},{9,17},{17,9},{25,1},{2,26},{10... | collective-permute-start | bytes 1572872 | tf_op jit(solution)/shard_map/ppermute | solution.py:378
  148.5 18.6 %collective-permute-start.30 = (bf16[2,16,64,128]{3,2,1,0:T(8,128)(2,1)S(1)}, bf16[2,16,64,128]{3,2,1,0:T(8,128)(2,1)S(1)}, u32[]{:S(2)}, u32[]{:S(2)}) collective-permute-start(bf16[2,16,64,128]{3,2,1,0:T(8,128)(2,1)S(1)} %get-tuple-element.107), channel_id=1, source_target_pairs={{0,8},{8,0},{16,24},{24,16},{1,9},{9,1},{17,25},{25,17},{2,10},{10... | collective-permute-start | bytes 1572872 | tf_op jit(solution)/shard_map/ppermute | solution.py:378
  156.9 19.8 %collective-permute-start.36 = (bf16[16,128,128]{2,1,0:T(8,128)(2,1)S(1)}, bf16[16,128,128]{2,1,0:T(8,128)(2,1)S(1)}, u32[]{:S(2)}, u32[]{:S(2)}) collective-permute-start(bf16[16,128,128]{2,1,0:T(8,128)(2,1)S(1)} %get-tuple-element.117.refs_3_), channel_id=1, source_target_pairs={{0,2},{2,4},{4,6},{6,7},{7,5},{5,3},{3,1},{1,0},{8,10},{10,12},{12... | collective-permute-start | bytes 1572872 | tf_op jit(solution)/shard_map/ppermute | solution.py:360
  166.5 13.9 %collective-permute-start.37 = (bf16[16,128,128]{2,1,0:T(8,128)(2,1)S(1)}, bf16[16,128,128]{2,1,0:T(8,128)(2,1)S(1)}, u32[]{:S(2)}, u32[]{:S(2)}) collective-permute-start(bf16[16,128,128]{2,1,0:T(8,128)(2,1)S(1)} %get-tuple-element.117.refs_3_), channel_id=1, source_target_pairs={{2,0},{4,2},{6,4},{7,6},{5,7},{3,5},{1,3},{0,1},{10,8},{12,10},{14... | collective-permute-start | bytes 1572872 | tf_op jit(solution)/shard_map/ppermute | solution.py:361
  166.5 13.9 %collective-permute-start.38 = (bf16[2,16,64,128]{3,2,1,0:T(8,128)(2,1)S(1)}, bf16[2,16,64,128]{3,2,1,0:T(8,128)(2,1)S(1)}, u32[]{:S(2)}, u32[]{:S(2)}) collective-permute-start(bf16[2,16,64,128]{3,2,1,0:T(8,128)(2,1)S(1)} %get-tuple-element.119), channel_id=1, source_target_pairs={{0,16},{8,24},{16,0},{24,8},{1,17},{9,25},{17,1},{25,9},{2,18},{10... | collective-permute-start | bytes 1572872 | tf_op jit(solution)/shard_map/ppermute | solution.py:378
  167.1 20.7 %collective-permute-start.31 = (bf16[16,128,128]{2,1,0:T(8,128)(2,1)S(1)}, bf16[16,128,128]{2,1,0:T(8,128)(2,1)S(1)}, u32[]{:S(2)}, u32[]{:S(2)}) collective-permute-start(bf16[16,128,128]{2,1,0:T(8,128)(2,1)S(1)} %collective-permute-done.24.refs_1_), channel_id=1, source_target_pairs={{0,2},{2,4},{4,6},{6,7},{7,5},{5,3},{3,1},{1,0},{8,10},{10,12},{12... | collective-permute-start | bytes 1572872 | tf_op jit(solution)/shard_map/ppermute | solution.py:360
  171.0 20.7 %collective-permute-start.32 = (bf16[16,128,128]{2,1,0:T(8,128)(2,1)}, bf16[16,128,128]{2,1,0:T(8,128)(2,1)S(1)}, u32[]{:S(2)}, u32[]{:S(2)}) collective-permute-start(bf16[16,128,128]{2,1,0:T(8,128)(2,1)} %collective-permute-done.25.refs_5_), channel_id=1, source_target_pairs={{2,0},{4,2},{6,4},{7,6},{5,7},{3,5},{1,3},{0,1},{10,8},{12,10},{14... | collective-permute-start | bytes 1572872 | tf_op jit(solution)/shard_map/ppermute | solution.py:361
  180.5 17.5 %collective-permute-start.39 = (bf16[16,128,128]{2,1,0:T(8,128)(2,1)S(1)}, bf16[16,128,128]{2,1,0:T(8,128)(2,1)S(1)}, u32[]{:S(2)}, u32[]{:S(2)}) collective-permute-start(bf16[16,128,128]{2,1,0:T(8,128)(2,1)S(1)} %collective-permute-done.36.refs_2_), channel_id=1, source_target_pairs={{0,2},{2,4},{4,6},{6,7},{7,5},{5,3},{3,1},{1,0},{8,10},{10,12},{12... | collective-permute-start | bytes 1572872 | tf_op jit(solution)/shard_map/ppermute | solution.py:360
  180.5 17.5 %collective-permute-start.40 = (bf16[2,16,64,128]{3,2,1,0:T(8,128)(2,1)S(1)}, bf16[2,16,64,128]{3,2,1,0:T(8,128)(2,1)S(1)}, u32[]{:S(2)}, u32[]{:S(2)}) collective-permute-start(bf16[2,16,64,128]{3,2,1,0:T(8,128)(2,1)S(1)} %get-tuple-element.122), channel_id=1, source_target_pairs={{0,24},{8,16},{16,8},{24,0},{1,25},{9,17},{17,9},{25,1},{2,26},{10... | collective-permute-start | bytes 1572872 | tf_op jit(solution)/shard_map/ppermute | solution.py:378
  196.9 13.5 %collective-permute-start.33 = (bf16[2,16,64,128]{3,2,1,0:T(8,128)(2,1)S(1)}, bf16[2,16,64,128]{3,2,1,0:T(8,128)(2,1)S(1)}, u32[]{:S(2)}, u32[]{:S(2)}) collective-permute-start(bf16[2,16,64,128]{3,2,1,0:T(8,128)(2,1)S(1)} %get-tuple-element.111), channel_id=1, source_target_pairs={{0,8},{8,0},{16,24},{24,16},{1,9},{9,1},{17,25},{25,17},{2,10},{10... | collective-permute-start | bytes 1572872 | tf_op jit(solution)/shard_map/ppermute | solution.py:378
  197.1 13.4 %collective-permute-start.34 = (bf16[2,16,64,128]{3,2,1,0:T(8,128)(2,1)S(1)}, bf16[2,16,64,128]{3,2,1,0:T(8,128)(2,1)S(1)}, u32[]{:S(2)}, u32[]{:S(2)}) collective-permute-start(bf16[2,16,64,128]{3,2,1,0:T(8,128)(2,1)S(1)} %get-tuple-element.112), channel_id=1, source_target_pairs={{0,16},{8,24},{16,0},{24,8},{1,17},{9,25},{17,1},{25,9},{2,18},{10... | collective-permute-start | bytes 1572872 | tf_op jit(solution)/shard_map/ppermute | solution.py:378
  197.7 13.4 %collective-permute-start.42 = (bf16[16,128,128]{2,1,0:T(8,128)(2,1)S(1)}, bf16[16,128,128]{2,1,0:T(8,128)(2,1)S(1)}, u32[]{:S(2)}, u32[]{:S(2)}) collective-permute-start(bf16[16,128,128]{2,1,0:T(8,128)(2,1)S(1)} %collective-permute-done.37.refs_4_), channel_id=1, source_target_pairs={{2,0},{4,2},{6,4},{7,6},{5,7},{3,5},{1,3},{0,1},{10,8},{12,10},{14... | collective-permute-start | bytes 1572872 | tf_op jit(solution)/shard_map/ppermute | solution.py:361
  197.9 25.9 %collective-permute-start.41 = (bf16[16,128,128]{2,1,0:T(8,128)(2,1)S(1)}, bf16[16,128,128]{2,1,0:T(8,128)(2,1)S(1)}, u32[]{:S(2)}, u32[]{:S(2)}) collective-permute-start(bf16[16,128,128]{2,1,0:T(8,128)(2,1)S(1)} %collective-permute-done.39.refs_1_), channel_id=1, source_target_pairs={{0,2},{2,4},{4,6},{6,7},{7,5},{5,3},{3,1},{1,0},{8,10},{10,12},{12... | collective-permute-start | bytes 1572872 | tf_op jit(solution)/shard_map/ppermute | solution.py:360
  210.5 13.4 %collective-permute-start.35 = (bf16[2,16,64,128]{3,2,1,0:T(8,128)(2,1)S(1)}, bf16[2,16,64,128]{3,2,1,0:T(8,128)(2,1)S(1)}, u32[]{:S(2)}, u32[]{:S(2)}) collective-permute-start(bf16[2,16,64,128]{3,2,1,0:T(8,128)(2,1)S(1)} %get-tuple-element.114), channel_id=1, source_target_pairs={{0,24},{8,16},{16,8},{24,0},{1,25},{9,17},{17,9},{25,1},{2,26},{10... | collective-permute-start | bytes 1572872 | tf_op jit(solution)/shard_map/ppermute | solution.py:378
  211.1 12.8 %collective-permute-start.43 = (bf16[16,128,128]{2,1,0:T(8,128)(2,1)S(1)}, bf16[16,128,128]{2,1,0:T(8,128)(2,1)S(1)}, u32[]{:S(2)}, u32[]{:S(2)}) collective-permute-start(bf16[16,128,128]{2,1,0:T(8,128)(2,1)S(1)} %collective-permute-done.42.refs_5_), channel_id=1, source_target_pairs={{2,0},{4,2},{6,4},{7,6},{5,7},{3,5},{1,3},{0,1},{10,8},{12,10},{14... | collective-permute-start | bytes 1572872 | tf_op jit(solution)/shard_map/ppermute | solution.py:361
  228.9 14.8 %collective-permute-start.44 = (bf16[2,16,64,128]{3,2,1,0:T(8,128)(2,1)S(1)}, bf16[2,16,64,128]{3,2,1,0:T(8,128)(2,1)S(1)}, u32[]{:S(2)}, u32[]{:S(2)}) collective-permute-start(bf16[2,16,64,128]{3,2,1,0:T(8,128)(2,1)S(1)} %get-tuple-element.127), channel_id=1, source_target_pairs={{0,8},{8,0},{16,24},{24,16},{1,9},{9,1},{17,25},{25,17},{2,10},{10... | collective-permute-start | bytes 1572872 | tf_op jit(solution)/shard_map/ppermute | solution.py:378
  231.5 24.5 %collective-permute-start.45 = (bf16[2,16,64,128]{3,2,1,0:T(8,128)(2,1)S(1)}, bf16[2,16,64,128]{3,2,1,0:T(8,128)(2,1)S(1)}, u32[]{:S(2)}, u32[]{:S(2)}) collective-permute-start(bf16[2,16,64,128]{3,2,1,0:T(8,128)(2,1)S(1)} %get-tuple-element.128), channel_id=1, source_target_pairs={{0,16},{8,24},{16,0},{24,8},{1,17},{9,25},{17,1},{25,9},{2,18},{10... | collective-permute-start | bytes 1572872 | tf_op jit(solution)/shard_map/ppermute | solution.py:378
  231.5 24.5 %collective-permute-start.46 = (bf16[2,16,64,128]{3,2,1,0:T(8,128)(2,1)S(1)}, bf16[2,16,64,128]{3,2,1,0:T(8,128)(2,1)S(1)}, u32[]{:S(2)}, u32[]{:S(2)}) collective-permute-start(bf16[2,16,64,128]{3,2,1,0:T(8,128)(2,1)S(1)} %get-tuple-element.129), channel_id=1, source_target_pairs={{0,24},{8,16},{16,8},{24,0},{1,25},{9,17},{17,9},{25,1},{2,26},{10... | collective-permute-start | bytes 1572872 | tf_op jit(solution)/shard_map/ppermute | solution.py:378
  257.1 5.3 %collective-permute-start.49 = (bf16[16,64,512]{2,1,0:T(8,128)(2,1)S(1)}, bf16[16,64,512]{2,1,0:T(8,128)(2,1)S(1)}, u32[]{:S(2)}, u32[]{:S(2)}) collective-permute-start(bf16[16,64,512]{2,1,0:T(8,128)(2,1)S(1)} %get-tuple-element.137), channel_id=1, source_target_pairs={{0,1},{1,0},{2,3},{3,2},{4,5},{5,4},{6,7},{7,6},{8,9},{9,8},{10,11... | collective-permute-start | bytes 3145736 | tf_op jit(solution)/shard_map/ppermute | solution.py:387
  (28 other events, 608.7 us)

commit v7 on v6

--- a/solution.py
+++ b/solution.py
@@ -396,7 +396,7 @@
     swapped = [None] * count
     done = []
 
-    update(0)
+    update(0, my_weight, my_offsets, my_gates)
     for index, (part, s) in enumerate(order):
         shift(part, s, *gates[index])
         done.append([tiles[part][-s], tiles[part][s]])
@@ -408,7 +408,7 @@
                 gates[index + 2].append(tiles[p][0])
         for p in range(count - 1):
             if index == last[p] + 1:
-                project(p, *before)
+                project(p, *before, *(moved[p - 1][1:] if p else []))
                 gates[min(index + 2, len(order) - 1)].append(moved[p][0])
             for d in range(1, parts):
                 if index == last[p] + d and p < count - 2:

time: 269 us -> 258 us (0.959)
  the two profiles are of different devices: /device:TPU:19 before, /device:TPU:0 now
where the time goes in v7:
time: 258 us; the launch traced here: 256 us
  waiting for transfers between devices  133 us (52%)
  Pallas kernels  56.9 us (22%)
  starting transfers between devices  49.1 us (19%)
  local copies, waits for them, and re-layouts  15 us (6%)
    ppermute x12, waiting for transfers between devices, shift(): here[-s] = lax.ppermute(after(here[-(s - 1)], *others), 'col', onward)  45.2 us
    ppermute x12, waiting for transfers between devices, send(): lax.ppermute(piece, 'row', [(a, a ^ d) for a in range(parts)])  41.5 us
    pallas_call x4, Pallas kernels, update_call(): pl.pallas_call(functools.partial(update_kernel, parts, part, cols, plan),...  29.4 us
    ppermute x12, starting transfers between devices, shift(): here[-s] = lax.ppermute(after(here[-(s - 1)], *others), 'col', onward)  19.4 us
    pallas_call x4, Pallas kernels, project_call(): pl.pallas_call(functools.partial(project_kernel, line, parts), in_specs=[...  16.9 us
    ppermute x3, waiting for transfers between devices, shards(): held[-s] = lax.ppermute(ahead, 'col', onward)  16.3 us
    ppermute x12, starting transfers between devices, send(): lax.ppermute(piece, 'row', [(a, a ^ d) for a in range(parts)])  14.3 us
    ppermute x12, waiting for transfers between devices, shift(): here[s] = lax.ppermute(after(here[s - 1], *others), 'col', back)  13.1 us
  transfers between devices with their start and end apart: 51, of which 29 were waited for; matrix products, arithmetic and copies ran while one was open for 4% of the time, Pallas kernels for 16%

profile of v7, /device:TPU:0, one launch (start us, length us, event | category | flops | bytes accessed | tf_op | source)
XLA Modules:
  0.0 256.5 jit_solution(2486181167936184172)
XLA Ops:
  0.6 3.0 %collective-permute-start = (bf16[16,16384]{1,0:T(8,128)(2,1)}, bf16[16,16384]{1,0:T(8,128)(2,1)S(1)}, u32[]{:S(2)}, u32[]{:S(2)}) collective-permute-start(bf16[16,16384]{1,0:T(8,128)(2,1)} %refs_3_.7), channel_id=1, source_target_pairs={{0,2},{2,4},{4,6},{6,7},{7,5},{5,3},{3,1},{1,0},{8,10},{10,12},{12... | collective-permute-start | bytes 1572872 | tf_op jit(solution)/shard_map/ppermute | solution.py:305
  7.2 8.0 %collective-permute-done.refs_2_ = bf16[16,16384]{1,0:T(8,128)(2,1)S(1)} collective-permute-done((bf16[16,16384]{1,0:T(8,128)(2,1)}, bf16[16,16384]{1,0:T(8,128)(2,1)S(1)}, u32[]{:S(2)}, u32[]{:S(2)}) %collective-permute-start) | collective-permute-done | bytes 524320 | tf_op jit(solution)/shard_map/ppermute | solution.py:305
  15.2 2.4 collective-permute-start.1
  18.7 11.2 %collective-permute-done.5.refs_11_ = bf16[128,2048]{1,0:T(8,128)(2,1)S(1)} collective-permute-done((bf16[128,2048]{1,0:T(8,128)(2,1)}, bf16[128,2048]{1,0:T(8,128)(2,1)S(1)}, u32[]{:S(2)}, u32[]{:S(2)}) %collective-permute-start.5) | collective-permute-done | bytes 524320 | tf_op jit(solution)/shard_map/ppermute | solution.py:293
  34.0 8.3 %collective-permute-done.7.refs_0_ = bf16[16,16384]{1,0:T(8,128)(2,1)S(1)} collective-permute-done((bf16[16,16384]{1,0:T(8,128)(2,1)S(1)}, bf16[16,16384]{1,0:T(8,128)(2,1)S(1)}, u32[]{:S(2)}, u32[]{:S(2)}) %collective-permute-start.7) | collective-permute-done | bytes 524320 | tf_op jit(solution)/shard_map/ppermute | solution.py:305
  43.0 2.5 collective-permute-start.9
  54.4 7.3 %update.4 = (bf16[128,64,128]{2,1,0:T(8,128)(2,1)}, bf16[16,128,128]{2,1,0:T(8,128)(2,1)S(1)}) custom-call(s32[3]{0:T(128)S(1)} %pad_add_fusion.where_ref, bf16[16,16384]{1,0:T(8,128)(2,1)S(1)} %collective-permute-done.7.refs_0_, bf16[16,16384]{1,0:T(8,128)(2,1)S(1)} %collective-permute-done.1.refs_1_, bf16[16,16384]{1,0:T(8,128)(2,1)S(1)} %collective-permute-done.refs_2_, ...), custom_call_target="tpu_custom_call" | custom-call | flops 2684354560 | bytes 8388608 | tf_op jit(solution)/shard_map/update/pallas_call | solution.py:121
  61.7 2.0 collective-permute-start.11
  63.7 10.1 %collective-permute-done.11.refs_2_ = bf16[16,128,128]{2,1,0:T(8,128)(2,1)S(1)} collective-permute-done((bf16[16,128,128]{2,1,0:T(8,128)(2,1)S(1)}, bf16[16,128,128]{2,1,0:T(8,128)(2,1)S(1)}, u32[]{:S(2)}, u32[]{:S(2)}) %collective-permute-start.11) | collective-permute-done | bytes 524320 | tf_op jit(solution)/shard_map/ppermute | solution.py:360
  73.9 2.5 collective-permute-start.15
  76.4 7.6 %update.5 = (bf16[128,64,128]{2,1,0:T(8,128)(2,1)}, bf16[16,128,128]{2,1,0:T(8,128)(2,1)}) custom-call(s32[3]{0:T(128)S(1)} %pad_add_fusion.where_ref, bf16[16,16384]{1,0:T(8,128)(2,1)S(1)} %collective-permute-done.7.refs_0_, bf16[16,16384]{1,0:T(8,128)(2,1)S(1)} %collective-permute-done.1.refs_1_, ...), custom_call_target="tpu_custom_call", output_to_operand_aliasing={{0}: (18, {})} | custom-call | flops 2684354560 | bytes 8388608 | tf_op jit(solution)/shard_map/update/pallas_call | solution.py:121
  84.0 1.8 collective-permute-start.13
  86.8 2.6 %collective-permute-start.17 = (bf16[16,128,128]{2,1,0:T(8,128)(2,1)}, bf16[16,128,128]{2,1,0:T(8,128)(2,1)}, u32[]{:S(2)}, u32[]{:S(2)}) collective-permute-start(bf16[16,128,128]{2,1,0:T(8,128)(2,1)} %collective-permute-done.15.refs_1_), channel_id=1, source_target_pairs={{0,2},{2,4},{4,6},{6,7},{7,5},{5,3},{3,1},{1,0},{8,10},{10,12},{12... | collective-permute-start | bytes 1572872 | tf_op jit(solution)/shard_map/ppermute | solution.py:360
  89.7 8.9 %collective-permute-done.13.refs_2_ = bf16[16,128,128]{2,1,0:T(8,128)(2,1)} collective-permute-done((bf16[16,128,128]{2,1,0:T(8,128)(2,1)}, bf16[16,128,128]{2,1,0:T(8,128)(2,1)}, u32[]{:S(2)}, u32[]{:S(2)}) %collective-permute-start.13) | collective-permute-done | bytes 524320 | tf_op jit(solution)/shard_map/ppermute | solution.py:360
  98.5 2.5 collective-permute-done.14.refs_4_
  103.2 7.3 %update.6 = (bf16[128,64,128]{2,1,0:T(8,128)(2,1)}, bf16[16,128,128]{2,1,0:T(8,128)(2,1)S(1)}) custom-call(s32[3]{0:T(128)S(1)} %pad_add_fusion.where_ref, bf16[16,16384]{1,0:T(8,128)(2,1)S(1)} %collective-permute-done.7.refs_0_, bf16[16,16384]{1,0:T(8,128)(2,1)S(1)} %collective-permute-done.1.refs_1_, ...), custom_call_target="tpu_custom_call", output_to_operand_aliasing={{0}: (18, {})} | custom-call | flops 2684354560 | bytes 8388608 | tf_op jit(solution)/shard_map/update/pallas_call | solution.py:121
  110.5 1.7 collective-permute-done.18.refs_6_
  112.8 4.1 %project.4 = (bf16[2,16,64,128]{3,2,1,0:T(8,128)(2,1)S(1)}, bf16[2,16,64,128]{3,2,1,0:T(8,128)(2,1)S(1)}, bf16[2,16,64,128]{3,2,1,0:T(8,128)(2,1)S(1)}, bf16[2,16,64,128]{3,2,1,0:T(8,128)(2,1)S(1)}) custom-call(s32[3]{0:T(128)S(1)} %pad_add_fusion.where_ref, bf16[128,128]{1,0:T(8,128)(2,1)S(1)} %copy-done.8, f32[128,1]{1,0:T(8,128)S(1)} %copy.43.offset_ref, ...), custom_call_target="tpu_custom_call" | custom-call | flops 268435456 | bytes 4194304 | tf_op jit(solution)/shard_map/project/pallas_call | solution.py:182
  118.2 2.8 %collective-permute-done.21.refs_1_ = bf16[16,128,128]{2,1,0:T(8,128)(2,1)S(1)} collective-permute-done((bf16[16,128,128]{2,1,0:T(8,128)(2,1)}, bf16[16,128,128]{2,1,0:T(8,128)(2,1)S(1)}, u32[]{:S(2)}, u32[]{:S(2)}) %collective-permute-start.21) | collective-permute-done | bytes 524320 | tf_op jit(solution)/shard_map/ppermute | solution.py:360
  121.0 2.4 collective-permute-done.22.refs_5_
  124.9 6.1 %collective-permute-done.19.refs_2_ = bf16[16,128,128]{2,1,0:T(8,128)(2,1)S(1)} collective-permute-done((bf16[16,128,128]{2,1,0:T(8,128)(2,1)S(1)}, bf16[16,128,128]{2,1,0:T(8,128)(2,1)S(1)}, u32[]{:S(2)}, u32[]{:S(2)}) %collective-permute-start.19) | collective-permute-done | bytes 524320 | tf_op jit(solution)/shard_map/ppermute | solution.py:360
  132.5 2.5 collective-permute-start.28
  134.9 2.0 collective-permute-start.24
  137.0 7.6 %collective-permute-done.27.refs_3_ = bf16[2,16,64,128]{3,2,1,0:T(8,128)(2,1)S(1)} collective-permute-done((bf16[2,16,64,128]{3,2,1,0:T(8,128)(2,1)S(1)}, bf16[2,16,64,128]{3,2,1,0:T(8,128)(2,1)S(1)}, u32[]{:S(2)}, u32[]{:S(2)}) %collective-permute-start.27) | collective-permute-done | bytes 524320 | tf_op jit(solution)/shard_map/ppermute | solution.py:378
  144.6 2.7 %collective-permute-done.28.refs_0_ = bf16[16,128,128]{2,1,0:T(8,128)(2,1)S(1)} collective-permute-done((bf16[16,128,128]{2,1,0:T(8,128)(2,1)S(1)}, bf16[16,128,128]{2,1,0:T(8,128)(2,1)S(1)}, u32[]{:S(2)}, u32[]{:S(2)}) %collective-permute-start.28) | collective-permute-done | bytes 524320 | tf_op jit(solution)/shard_map/ppermute | solution.py:360
  147.3 2.5 collective-permute-done.29.refs_6_
  150.6 4.2 %project.5 = (bf16[2,16,64,128]{3,2,1,0:T(8,128)(2,1)S(1)}, bf16[2,16,64,128]{3,2,1,0:T(8,128)(2,1)S(1)}, bf16[2,16,64,128]{3,2,1,0:T(8,128)(2,1)S(1)}, bf16[2,16,64,128]{3,2,1,0:T(8,128)(2,1)S(1)}) custom-call(s32[3]{0:T(128)S(1)} %pad_add_fusion.where_ref, bf16[128,128]{1,0:T(8,128)(2,1)S(1)} %copy-done.8, f32[128,1]{1,0:T(8,128)S(1)} %copy.43.offset_ref, ...), custom_call_target="tpu_custom_call" | custom-call | flops 268435456 | bytes 4194304 | tf_op jit(solution)/shard_map/project/pallas_call | solution.py:182
  156.4 7.2 %update.7 = (bf16[128,64,128]{2,1,0:T(8,128)(2,1)}, bf16[16,128,128]{2,1,0:T(8,128)(2,1)S(1)}) custom-call(s32[3]{0:T(128)S(1)} %pad_add_fusion.where_ref, bf16[16,16384]{1,0:T(8,128)(2,1)S(1)} %collective-permute-done.7.refs_0_, bf16[16,16384]{1,0:T(8,128)(2,1)S(1)} %collective-permute-done.1.refs_1_, ...), custom_call_target="tpu_custom_call", output_to_operand_aliasing={{0}: (18, {})} | custom-call | flops 2684354560 | bytes 8388608 | tf_op jit(solution)/shard_map/update/pallas_call | solution.py:121
  166.3 9.7 %collective-permute-done.34.refs_2_ = bf16[16,128,128]{2,1,0:T(8,128)(2,1)S(1)} collective-permute-done((bf16[16,128,128]{2,1,0:T(8,128)(2,1)S(1)}, bf16[16,128,128]{2,1,0:T(8,128)(2,1)S(1)}, u32[]{:S(2)}, u32[]{:S(2)}) %collective-permute-start.34) | collective-permute-done | bytes 524320 | tf_op jit(solution)/shard_map/ppermute | solution.py:360
  175.9 2.3 collective-permute-done.35.refs_4_
  179.4 1.8 place.4
  181.3 1.7 collective-permute-start.40
  183.0 4.0 %collective-permute-done.31.refs_0_ = bf16[16,128,128]{2,1,0:T(8,128)(2,1)S(1)} collective-permute-done((bf16[16,128,128]{2,1,0:T(8,128)(2,1)S(1)}, bf16[16,128,128]{2,1,0:T(8,128)(2,1)S(1)}, u32[]{:S(2)}, u32[]{:S(2)}) %collective-permute-start.31) | collective-permute-done | bytes 524320 | tf_op jit(solution)/shard_map/ppermute | solution.py:360
  187.0 3.4 %collective-permute-done.36.refs_3_ = bf16[2,16,64,128]{3,2,1,0:T(8,128)(2,1)S(1)} collective-permute-done((bf16[2,16,64,128]{3,2,1,0:T(8,128)(2,1)S(1)}, bf16[2,16,64,128]{3,2,1,0:T(8,128)(2,1)S(1)}, u32[]{:S(2)}, u32[]{:S(2)}) %collective-permute-start.36) | collective-permute-done | bytes 524320 | tf_op jit(solution)/shard_map/ppermute | solution.py:378
  190.4 4.2 %project.6 = (bf16[2,16,64,128]{3,2,1,0:T(8,128)(2,1)S(1)}, bf16[2,16,64,128]{3,2,1,0:T(8,128)(2,1)S(1)}, bf16[2,16,64,128]{3,2,1,0:T(8,128)(2,1)S(1)}, bf16[2,16,64,128]{3,2,1,0:T(8,128)(2,1)S(1)}) custom-call(s32[3]{0:T(128)S(1)} %pad_add_fusion.where_ref, bf16[128,128]{1,0:T(8,128)(2,1)S(1)} %copy-done.8, f32[128,1]{1,0:T(8,128)S(1)} %copy.43.offset_ref, ...), custom_call_target="tpu_custom_call" | custom-call | flops 268435456 | bytes 4194304 | tf_op jit(solution)/shard_map/project/pallas_call | solution.py:182
  196.4 2.4 collective-permute-start.41
  198.8 8.2 %collective-permute-done.37.refs_1_ = bf16[2,16,64,128]{3,2,1,0:T(8,128)(2,1)S(1)} collective-permute-done((bf16[2,16,64,128]{3,2,1,0:T(8,128)(2,1)S(1)}, bf16[2,16,64,128]{3,2,1,0:T(8,128)(2,1)S(1)}, u32[]{:S(2)}, u32[]{:S(2)}) %collective-permute-start.37) | collective-permute-done | bytes 524320 | tf_op jit(solution)/shard_map/ppermute | solution.py:378
  207.0 4.0 %collective-permute-done.38.refs_2_ = bf16[2,16,64,128]{3,2,1,0:T(8,128)(2,1)S(1)} collective-permute-done((bf16[2,16,64,128]{3,2,1,0:T(8,128)(2,1)S(1)}, bf16[2,16,64,128]{3,2,1,0:T(8,128)(2,1)S(1)}, u32[]{:S(2)}, u32[]{:S(2)}) %collective-permute-start.38) | collective-permute-done | bytes 524320 | tf_op jit(solution)/shard_map/ppermute | solution.py:378
  212.4 8.7 %collective-permute-done.39.refs_3_ = bf16[2,16,64,128]{3,2,1,0:T(8,128)(2,1)S(1)} collective-permute-done((bf16[2,16,64,128]{3,2,1,0:T(8,128)(2,1)S(1)}, bf16[2,16,64,128]{3,2,1,0:T(8,128)(2,1)S(1)}, u32[]{:S(2)}, u32[]{:S(2)}) %collective-permute-start.39) | collective-permute-done | bytes 524320 | tf_op jit(solution)/shard_map/ppermute | solution.py:378
  221.1 1.8 collective-permute-done.43.refs_6_
  223.7 4.4 %project.7 = (bf16[2,16,64,128]{3,2,1,0:T(8,128)(2,1)S(1)}, bf16[2,16,64,128]{3,2,1,0:T(8,128)(2,1)S(1)}, bf16[2,16,64,128]{3,2,1,0:T(8,128)(2,1)S(1)}, bf16[2,16,64,128]{3,2,1,0:T(8,128)(2,1)S(1)}) custom-call(s32[3]{0:T(128)S(1)} %pad_add_fusion.where_ref, bf16[128,128]{1,0:T(8,128)(2,1)S(1)} %copy-done.8, f32[128,1]{1,0:T(8,128)S(1)} %copy.43.offset_ref, ...), custom_call_target="tpu_custom_call" | custom-call | flops 268435456 | bytes 4194304 | tf_op jit(solution)/shard_map/project/pallas_call | solution.py:182
  229.0 2.7 %collective-permute-start.46 = (bf16[2,16,64,128]{3,2,1,0:T(8,128)(2,1)S(1)}, bf16[2,16,64,128]{3,2,1,0:T(8,128)(2,1)S(1)}, u32[]{:S(2)}, u32[]{:S(2)}) collective-permute-start(bf16[2,16,64,128]{3,2,1,0:T(8,128)(2,1)S(1)} %get-tuple-element.131), channel_id=1, source_target_pairs={{0,24},{8,16},{16,8},{24,0},{1,25},{9,17},{17,9},{25,1},{2,26},{10... | collective-permute-start | bytes 1572872 | tf_op jit(solution)/shard_map/ppermute | solution.py:378
  231.6 1.8 place.5
  233.5 1.8 place.6
  235.3 3.2 %collective-permute-done.44.refs_1_ = bf16[2,16,64,128]{3,2,1,0:T(8,128)(2,1)S(1)} collective-permute-done((bf16[2,16,64,128]{3,2,1,0:T(8,128)(2,1)S(1)}, bf16[2,16,64,128]{3,2,1,0:T(8,128)(2,1)S(1)}, u32[]{:S(2)}, u32[]{:S(2)}) %collective-permute-start.44) | collective-permute-done | bytes 524320 | tf_op jit(solution)/shard_map/ppermute | solution.py:378
  239.3 5.6 %collective-permute-done.46.refs_3_ = bf16[2,16,64,128]{3,2,1,0:T(8,128)(2,1)S(1)} collective-permute-done((bf16[2,16,64,128]{3,2,1,0:T(8,128)(2,1)S(1)}, bf16[2,16,64,128]{3,2,1,0:T(8,128)(2,1)S(1)}, u32[]{:S(2)}, u32[]{:S(2)}) %collective-permute-start.46) | collective-permute-done | bytes 524320 | tf_op jit(solution)/shard_map/ppermute | solution.py:378
  245.4 1.8 place.7
  253.0 3.3 %put.1 = bf16[128,64,512]{2,1,0:T(8,128)(2,1)} custom-call(s32[3]{0:T(128)S(1)} %pad_add_fusion.where_ref, bf16[16,64,512]{2,1,0:T(8,128)(2,1)S(1)} %collective-permute-done.47.refs_0_, bf16[16,64,512]{2,1,0:T(8,128)(2,1)S(1)} %collective-permute-done.48.refs_1_, ...), custom_call_target="tpu_custom_call", output_to_operand_aliasing={{}: (5, {})} | custom-call | bytes 8388608 | tf_op jit(solution)/shard_map/put/pallas_call | solution.py:261
  (139 shorter events, 44.7 us)
Async XLA Ops:
  0.6 14.6 %collective-permute-start = (bf16[16,16384]{1,0:T(8,128)(2,1)}, bf16[16,16384]{1,0:T(8,128)(2,1)S(1)}, u32[]{:S(2)}, u32[]{:S(2)}) collective-permute-start(bf16[16,16384]{1,0:T(8,128)(2,1)} %refs_3_.7), channel_id=1, source_target_pairs={{0,2},{2,4},{4,6},{6,7},{7,5},{5,3},{3,1},{1,0},{8,10},{10,12},{12... | collective-permute-start | bytes 1572872 | tf_op jit(solution)/shard_map/ppermute | solution.py:305
  3.7 13.9 %collective-permute-start.2 = (bf16[16,16384]{1,0:T(8,128)(2,1)}, bf16[16,16384]{1,0:T(8,128)(2,1)S(1)}, u32[]{:S(2)}, u32[]{:S(2)}) collective-permute-start(bf16[16,16384]{1,0:T(8,128)(2,1)} %refs_3_.7), channel_id=1, source_target_pairs={{2,0},{4,2},{6,4},{7,6},{5,7},{3,5},{1,3},{0,1},{10,8},{12,10},{14... | collective-permute-start | bytes 1572872 | tf_op jit(solution)/shard_map/ppermute | solution.py:306
  3.7 15.1 %collective-permute-start.4 = (bf16[128,2048]{1,0:T(8,128)(2,1)}, bf16[128,2048]{1,0:T(8,128)(2,1)S(1)}, u32[]{:S(2)}, u32[]{:S(2)}) collective-permute-start(bf16[128,2048]{1,0:T(8,128)(2,1)} %refs_9_.7), channel_id=1, source_target_pairs={{0,8},{8,0},{16,24},{24,16},{1,9},{9,1},{17,25},{25,17},{2,10},{10... | collective-permute-start | bytes 1572872 | tf_op jit(solution)/shard_map/ppermute | solution.py:293
  5.2 24.7 %collective-permute-start.5 = (bf16[128,2048]{1,0:T(8,128)(2,1)}, bf16[128,2048]{1,0:T(8,128)(2,1)S(1)}, u32[]{:S(2)}, u32[]{:S(2)}) collective-permute-start(bf16[128,2048]{1,0:T(8,128)(2,1)} %refs_9_.7), channel_id=1, source_target_pairs={{0,16},{8,24},{16,0},{24,8},{1,17},{9,25},{17,1},{25,9},{2,18},{10... | collective-permute-start | bytes 1572872 | tf_op jit(solution)/shard_map/ppermute | solution.py:293
  6.7 23.2 %collective-permute-start.6 = (bf16[128,2048]{1,0:T(8,128)(2,1)}, bf16[128,2048]{1,0:T(8,128)(2,1)S(1)}, u32[]{:S(2)}, u32[]{:S(2)}) collective-permute-start(bf16[128,2048]{1,0:T(8,128)(2,1)} %refs_9_.7), channel_id=1, source_target_pairs={{0,24},{8,16},{16,8},{24,0},{1,25},{9,17},{17,9},{25,1},{2,26},{10... | collective-permute-start | bytes 1572872 | tf_op jit(solution)/shard_map/ppermute | solution.py:293
  15.2 14.7 %collective-permute-start.1 = (bf16[16,16384]{1,0:T(8,128)(2,1)S(1)}, bf16[16,16384]{1,0:T(8,128)(2,1)S(1)}, u32[]{:S(2)}, u32[]{:S(2)}) collective-permute-start(bf16[16,16384]{1,0:T(8,128)(2,1)S(1)} %collective-permute-done.refs_2_), channel_id=1, source_target_pairs={{0,2},{2,4},{4,6},{6,7},{7,5},{5,3},{3,1},{1,0},{8,10},{10,12},{12... | collective-permute-start | bytes 1572872 | tf_op jit(solution)/shard_map/ppermute | solution.py:305
  17.6 12.3 %collective-permute-start.3 = (bf16[16,16384]{1,0:T(8,128)(2,1)S(1)}, bf16[16,16384]{1,0:T(8,128)(2,1)}, u32[]{:S(2)}, u32[]{:S(2)}) collective-permute-start(bf16[16,16384]{1,0:T(8,128)(2,1)S(1)} %collective-permute-done.2.refs_4_), channel_id=1, source_target_pairs={{2,0},{4,2},{6,4},{7,6},{5,7},{3,5},{1,3},{0,1},{10,8},{12,10},{14... | collective-permute-start | bytes 1572872 | tf_op jit(solution)/shard_map/ppermute | solution.py:306
  29.9 12.4 %collective-permute-start.7 = (bf16[16,16384]{1,0:T(8,128)(2,1)S(1)}, bf16[16,16384]{1,0:T(8,128)(2,1)S(1)}, u32[]{:S(2)}, u32[]{:S(2)}) collective-permute-start(bf16[16,16384]{1,0:T(8,128)(2,1)S(1)} %collective-permute-done.1.refs_1_), channel_id=1, source_target_pairs={{0,2},{2,4},{4,6},{6,7},{7,5},{5,3},{3,1},{1,0},{8,10},{10,12},{12... | collective-permute-start | bytes 1572872 | tf_op jit(solution)/shard_map/ppermute | solution.py:305
  31.5 14.0 %collective-permute-start.8 = (bf16[16,16384]{1,0:T(8,128)(2,1)}, bf16[16,16384]{1,0:T(8,128)(2,1)S(1)}, u32[]{:S(2)}, u32[]{:S(2)}) collective-permute-start(bf16[16,16384]{1,0:T(8,128)(2,1)} %collective-permute-done.3.refs_5_), channel_id=1, source_target_pairs={{2,0},{4,2},{6,4},{7,6},{5,7},{3,5},{1,3},{0,1},{10,8},{12,10},{14... | collective-permute-start | bytes 1572872 | tf_op jit(solution)/shard_map/ppermute | solution.py:306
  43.0 10.3 %collective-permute-start.9 = (bf16[16,8192]{1,0:T(8,128)(2,1)}, bf16[16,8192]{1,0:T(8,128)(2,1)S(1)}, u32[]{:S(2)}, u32[]{:S(2)}) collective-permute-start(bf16[16,8192]{1,0:T(8,128)(2,1)} %slice.8), channel_id=1, source_target_pairs={{0,2},{2,4},{4,6},{6,7},{7,5},{5,3},{3,1},{1,0},{8,10},{10,12},{12... | collective-permute-start | bytes 786440 | tf_op jit(solution)/shard_map/ppermute | solution.py:310
  46.3 7.1 %collective-permute-start.10 = (bf16[16,8192]{1,0:T(8,128)(2,1)}, bf16[16,8192]{1,0:T(8,128)(2,1)S(1)}, u32[]{:S(2)}, u32[]{:S(2)}) collective-permute-start(bf16[16,8192]{1,0:T(8,128)(2,1)} %slice.9), channel_id=1, source_target_pairs={{2,0},{4,2},{6,4},{7,6},{5,7},{3,5},{1,3},{0,1},{10,8},{12,10},{14... | collective-permute-start | bytes 786440 | tf_op jit(solution)/shard_map/ppermute | solution.py:311
  61.7 12.2 %collective-permute-start.11 = (bf16[16,128,128]{2,1,0:T(8,128)(2,1)S(1)}, bf16[16,128,128]{2,1,0:T(8,128)(2,1)S(1)}, u32[]{:S(2)}, u32[]{:S(2)}) collective-permute-start(bf16[16,128,128]{2,1,0:T(8,128)(2,1)S(1)} %get-tuple-element.79.refs_3_), channel_id=1, source_target_pairs={{0,2},{2,4},{4,6},{6,7},{7,5},{5,3},{3,1},{1,0},{8,10},{10,12},{12... | collective-permute-start | bytes 1572872 | tf_op jit(solution)/shard_map/ppermute | solution.py:360
  63.7 12.6 %collective-permute-start.12 = (bf16[16,128,128]{2,1,0:T(8,128)(2,1)S(1)}, bf16[16,128,128]{2,1,0:T(8,128)(2,1)S(1)}, u32[]{:S(2)}, u32[]{:S(2)}) collective-permute-start(bf16[16,128,128]{2,1,0:T(8,128)(2,1)S(1)} %get-tuple-element.79.refs_3_), channel_id=1, source_target_pairs={{2,0},{4,2},{6,4},{7,6},{5,7},{3,5},{1,3},{0,1},{10,8},{12,10},{14... | collective-permute-start | bytes 1572872 | tf_op jit(solution)/shard_map/ppermute | solution.py:361
  73.9 13.0 %collective-permute-start.15 = (bf16[16,128,128]{2,1,0:T(8,128)(2,1)S(1)}, bf16[16,128,128]{2,1,0:T(8,128)(2,1)}, u32[]{:S(2)}, u32[]{:S(2)}) collective-permute-start(bf16[16,128,128]{2,1,0:T(8,128)(2,1)S(1)} %collective-permute-done.11.refs_2_), channel_id=1, source_target_pairs={{0,2},{2,4},{4,6},{6,7},{7,5},{5,3},{3,1},{1,0},{8,10},{10,12},{12... | collective-permute-start | bytes 1572872 | tf_op jit(solution)/shard_map/ppermute | solution.py:360
  76.3 10.5 %collective-permute-start.16 = (bf16[16,128,128]{2,1,0:T(8,128)(2,1)S(1)}, bf16[16,128,128]{2,1,0:T(8,128)(2,1)}, u32[]{:S(2)}, u32[]{:S(2)}) collective-permute-start(bf16[16,128,128]{2,1,0:T(8,128)(2,1)S(1)} %collective-permute-done.12.refs_4_), channel_id=1, source_target_pairs={{2,0},{4,2},{6,4},{7,6},{5,7},{3,5},{1,3},{0,1},{10,8},{12,10},{14... | collective-permute-start | bytes 1572872 | tf_op jit(solution)/shard_map/ppermute | solution.py:361
  84.0 14.5 %collective-permute-start.13 = (bf16[16,128,128]{2,1,0:T(8,128)(2,1)}, bf16[16,128,128]{2,1,0:T(8,128)(2,1)}, u32[]{:S(2)}, u32[]{:S(2)}) collective-permute-start(bf16[16,128,128]{2,1,0:T(8,128)(2,1)} %get-tuple-element.80.refs_3_), channel_id=1, source_target_pairs={{0,2},{2,4},{4,6},{6,7},{7,5},{5,3},{3,1},{1,0},{8,10},{10,12},{12... | collective-permute-start | bytes 1572872 | tf_op jit(solution)/shard_map/ppermute | solution.py:360
  85.8 15.2 %collective-permute-start.14 = (bf16[16,128,128]{2,1,0:T(8,128)(2,1)}, bf16[16,128,128]{2,1,0:T(8,128)(2,1)}, u32[]{:S(2)}, u32[]{:S(2)}) collective-permute-start(bf16[16,128,128]{2,1,0:T(8,128)(2,1)} %get-tuple-element.80.refs_3_), channel_id=1, source_target_pairs={{2,0},{4,2},{6,4},{7,6},{5,7},{3,5},{1,3},{0,1},{10,8},{12,10},{14... | collective-permute-start | bytes 1572872 | tf_op jit(solution)/shard_map/ppermute | solution.py:361
  86.8 23.7 %collective-permute-start.17 = (bf16[16,128,128]{2,1,0:T(8,128)(2,1)}, bf16[16,128,128]{2,1,0:T(8,128)(2,1)}, u32[]{:S(2)}, u32[]{:S(2)}) collective-permute-start(bf16[16,128,128]{2,1,0:T(8,128)(2,1)} %collective-permute-done.15.refs_1_), channel_id=1, source_target_pairs={{0,2},{2,4},{4,6},{6,7},{7,5},{5,3},{3,1},{1,0},{8,10},{10,12},{12... | collective-permute-start | bytes 1572872 | tf_op jit(solution)/shard_map/ppermute | solution.py:360
  89.4 22.8 %collective-permute-start.18 = (bf16[16,128,128]{2,1,0:T(8,128)(2,1)}, bf16[16,128,128]{2,1,0:T(8,128)(2,1)}, u32[]{:S(2)}, u32[]{:S(2)}) collective-permute-start(bf16[16,128,128]{2,1,0:T(8,128)(2,1)} %collective-permute-done.16.refs_5_), channel_id=1, source_target_pairs={{2,0},{4,2},{6,4},{7,6},{5,7},{3,5},{1,3},{0,1},{10,8},{12,10},{14... | collective-permute-start | bytes 1572872 | tf_op jit(solution)/shard_map/ppermute | solution.py:361
  101.0 20.0 %collective-permute-start.21 = (bf16[16,128,128]{2,1,0:T(8,128)(2,1)}, bf16[16,128,128]{2,1,0:T(8,128)(2,1)S(1)}, u32[]{:S(2)}, u32[]{:S(2)}) collective-permute-start(bf16[16,128,128]{2,1,0:T(8,128)(2,1)} %collective-permute-done.13.refs_2_), channel_id=1, source_target_pairs={{0,2},{2,4},{4,6},{6,7},{7,5},{5,3},{3,1},{1,0},{8,10},{10,12},{12... | collective-permute-start | bytes 1572872 | tf_op jit(solution)/shard_map/ppermute | solution.py:360
  101.2 22.2 %collective-permute-start.22 = (bf16[16,128,128]{2,1,0:T(8,128)(2,1)}, bf16[16,128,128]{2,1,0:T(8,128)(2,1)S(1)}, u32[]{:S(2)}, u32[]{:S(2)}) collective-permute-start(bf16[16,128,128]{2,1,0:T(8,128)(2,1)} %collective-permute-done.14.refs_4_), channel_id=1, source_target_pairs={{2,0},{4,2},{6,4},{7,6},{5,7},{3,5},{1,3},{0,1},{10,8},{12,10},{14... | collective-permute-start | bytes 1572872 | tf_op jit(solution)/shard_map/ppermute | solution.py:361
  112.2 18.7 %collective-permute-start.19 = (bf16[16,128,128]{2,1,0:T(8,128)(2,1)S(1)}, bf16[16,128,128]{2,1,0:T(8,128)(2,1)S(1)}, u32[]{:S(2)}, u32[]{:S(2)}) collective-permute-start(bf16[16,128,128]{2,1,0:T(8,128)(2,1)S(1)} %get-tuple-element.86.refs_3_), channel_id=1, source_target_pairs={{0,2},{2,4},{4,6},{6,7},{7,5},{5,3},{3,1},{1,0},{8,10},{10,12},{12... | collective-permute-start | bytes 1572872 | tf_op jit(solution)/shard_map/ppermute | solution.py:360
  112.4 18.6 %collective-permute-start.20 = (bf16[16,128,128]{2,1,0:T(8,128)(2,1)S(1)}, bf16[16,128,128]{2,1,0:T(8,128)(2,1)S(1)}, u32[]{:S(2)}, u32[]{:S(2)}) collective-permute-start(bf16[16,128,128]{2,1,0:T(8,128)(2,1)S(1)} %get-tuple-element.86.refs_3_), channel_id=1, source_target_pairs={{2,0},{4,2},{6,4},{7,6},{5,7},{3,5},{1,3},{0,1},{10,8},{12,10},{14... | collective-permute-start | bytes 1572872 | tf_op jit(solution)/shard_map/ppermute | solution.py:361
  116.9 15.5 %collective-permute-start.26 = (bf16[2,16,64,128]{3,2,1,0:T(8,128)(2,1)S(1)}, bf16[2,16,64,128]{3,2,1,0:T(8,128)(2,1)S(1)}, u32[]{:S(2)}, u32[]{:S(2)}) collective-permute-start(bf16[2,16,64,128]{3,2,1,0:T(8,128)(2,1)S(1)} %get-tuple-element.100), channel_id=1, source_target_pairs={{0,8},{8,0},{16,24},{24,16},{1,9},{9,1},{17,25},{25,17},{2,10},{10... | collective-permute-start | bytes 1572872 | tf_op jit(solution)/shard_map/ppermute | solution.py:378
  123.4 11.6 %collective-permute-start.23 = (bf16[2,16,64,128]{3,2,1,0:T(8,128)(2,1)S(1)}, bf16[2,16,64,128]{3,2,1,0:T(8,128)(2,1)S(1)}, u32[]{:S(2)}, u32[]{:S(2)}) collective-permute-start(bf16[2,16,64,128]{3,2,1,0:T(8,128)(2,1)S(1)} %get-tuple-element.94), channel_id=1, source_target_pairs={{0,16},{8,24},{16,0},{24,8},{1,17},{9,25},{17,1},{25,9},{2,18},{10... | collective-permute-start | bytes 1572872 | tf_op jit(solution)/shard_map/ppermute | solution.py:378
  131.0 13.7 %collective-permute-start.27 = (bf16[2,16,64,128]{3,2,1,0:T(8,128)(2,1)S(1)}, bf16[2,16,64,128]{3,2,1,0:T(8,128)(2,1)S(1)}, u32[]{:S(2)}, u32[]{:S(2)}) collective-permute-start(bf16[2,16,64,128]{3,2,1,0:T(8,128)(2,1)S(1)} %get-tuple-element.102), channel_id=1, source_target_pairs={{0,24},{8,16},{16,8},{24,0},{1,25},{9,17},{17,9},{25,1},{2,26},{10... | collective-permute-start | bytes 1572872 | tf_op jit(solution)/shard_map/ppermute | solution.py:378
  132.5 14.9 %collective-permute-start.28 = (bf16[16,128,128]{2,1,0:T(8,128)(2,1)S(1)}, bf16[16,128,128]{2,1,0:T(8,128)(2,1)S(1)}, u32[]{:S(2)}, u32[]{:S(2)}) collective-permute-start(bf16[16,128,128]{2,1,0:T(8,128)(2,1)S(1)} %collective-permute-done.21.refs_1_), channel_id=1, source_target_pairs={{0,2},{2,4},{4,6},{6,7},{7,5},{5,3},{3,1},{1,0},{8,10},{10,12},{12... | collective-permute-start | bytes 1572872 | tf_op jit(solution)/shard_map/ppermute | solution.py:360
  134.9 14.9 %collective-permute-start.29 = (bf16[16,128,128]{2,1,0:T(8,128)(2,1)S(1)}, bf16[16,128,128]{2,1,0:T(8,128)(2,1)S(1)}, u32[]{:S(2)}, u32[]{:S(2)}) collective-permute-start(bf16[16,128,128]{2,1,0:T(8,128)(2,1)S(1)} %collective-permute-done.22.refs_5_), channel_id=1, source_target_pairs={{2,0},{4,2},{6,4},{7,6},{5,7},{3,5},{1,3},{0,1},{10,8},{12,10},{14... | collective-permute-start | bytes 1572872 | tf_op jit(solution)/shard_map/ppermute | solution.py:361
  134.9 29.2 %collective-permute-start.24 = (bf16[16,128,128]{2,1,0:T(8,128)(2,1)S(1)}, bf16[16,128,128]{2,1,0:T(8,128)(2,1)S(1)}, u32[]{:S(2)}, u32[]{:S(2)}) collective-permute-start(bf16[16,128,128]{2,1,0:T(8,128)(2,1)S(1)} %collective-permute-done.19.refs_2_), channel_id=1, source_target_pairs={{0,2},{2,4},{4,6},{6,7},{7,5},{5,3},{3,1},{1,0},{8,10},{10,12},{12... | collective-permute-start | bytes 1572872 | tf_op jit(solution)/shard_map/ppermute | solution.py:360
  137.0 27.2 %collective-permute-start.25 = (bf16[16,128,128]{2,1,0:T(8,128)(2,1)S(1)}, bf16[16,128,128]{2,1,0:T(8,128)(2,1)S(1)}, u32[]{:S(2)}, u32[]{:S(2)}) collective-permute-start(bf16[16,128,128]{2,1,0:T(8,128)(2,1)S(1)} %collective-permute-done.20.refs_4_), channel_id=1, source_target_pairs={{2,0},{4,2},{6,4},{7,6},{5,7},{3,5},{1,3},{0,1},{10,8},{12,10},{14... | collective-permute-start | bytes 1572872 | tf_op jit(solution)/shard_map/ppermute | solution.py:361
  154.8 9.9 %collective-permute-start.30 = (bf16[2,16,64,128]{3,2,1,0:T(8,128)(2,1)S(1)}, bf16[2,16,64,128]{3,2,1,0:T(8,128)(2,1)S(1)}, u32[]{:S(2)}, u32[]{:S(2)}) collective-permute-start(bf16[2,16,64,128]{3,2,1,0:T(8,128)(2,1)S(1)} %get-tuple-element.109), channel_id=1, source_target_pairs={{0,8},{8,0},{16,24},{24,16},{1,9},{9,1},{17,25},{25,17},{2,10},{10... | collective-permute-start | bytes 1572872 | tf_op jit(solution)/shard_map/ppermute | solution.py:378
  163.6 12.3 %collective-permute-start.34 = (bf16[16,128,128]{2,1,0:T(8,128)(2,1)S(1)}, bf16[16,128,128]{2,1,0:T(8,128)(2,1)S(1)}, u32[]{:S(2)}, u32[]{:S(2)}) collective-permute-start(bf16[16,128,128]{2,1,0:T(8,128)(2,1)S(1)} %get-tuple-element.116.refs_3_), channel_id=1, source_target_pairs={{0,2},{2,4},{4,6},{6,7},{7,5},{5,3},{3,1},{1,0},{8,10},{10,12},{12... | collective-permute-start | bytes 1572872 | tf_op jit(solution)/shard_map/ppermute | solution.py:360
  163.6 14.6 %collective-permute-start.35 = (bf16[16,128,128]{2,1,0:T(8,128)(2,1)S(1)}, bf16[16,128,128]{2,1,0:T(8,128)(2,1)S(1)}, u32[]{:S(2)}, u32[]{:S(2)}) collective-permute-start(bf16[16,128,128]{2,1,0:T(8,128)(2,1)S(1)} %get-tuple-element.116.refs_3_), channel_id=1, source_target_pairs={{2,0},{4,2},{6,4},{7,6},{5,7},{3,5},{1,3},{0,1},{10,8},{12,10},{14... | collective-permute-start | bytes 1572872 | tf_op jit(solution)/shard_map/ppermute | solution.py:361
  164.1 17.2 %collective-permute-start.33 = (bf16[2,16,64,128]{3,2,1,0:T(8,128)(2,1)S(1)}, bf16[2,16,64,128]{3,2,1,0:T(8,128)(2,1)S(1)}, u32[]{:S(2)}, u32[]{:S(2)}) collective-permute-start(bf16[2,16,64,128]{3,2,1,0:T(8,128)(2,1)S(1)} %get-tuple-element.113), channel_id=1, source_target_pairs={{0,16},{8,24},{16,0},{24,8},{1,17},{9,25},{17,1},{25,9},{2,18},{10... | collective-permute-start | bytes 1572872 | tf_op jit(solution)/shard_map/ppermute | solution.py:378
  164.7 22.3 %collective-permute-start.31 = (bf16[16,128,128]{2,1,0:T(8,128)(2,1)S(1)}, bf16[16,128,128]{2,1,0:T(8,128)(2,1)S(1)}, u32[]{:S(2)}, u32[]{:S(2)}) collective-permute-start(bf16[16,128,128]{2,1,0:T(8,128)(2,1)S(1)} %collective-permute-done.24.refs_1_), channel_id=1, source_target_pairs={{0,2},{2,4},{4,6},{6,7},{7,5},{5,3},{3,1},{1,0},{8,10},{10,12},{12... | collective-permute-start | bytes 1572872 | tf_op jit(solution)/shard_map/ppermute | solution.py:360
  166.3 20.7 %collective-permute-start.32 = (bf16[16,128,128]{2,1,0:T(8,128)(2,1)S(1)}, bf16[16,128,128]{2,1,0:T(8,128)(2,1)S(1)}, u32[]{:S(2)}, u32[]{:S(2)}) collective-permute-start(bf16[16,128,128]{2,1,0:T(8,128)(2,1)S(1)} %collective-permute-done.25.refs_5_), channel_id=1, source_target_pairs={{2,0},{4,2},{6,4},{7,6},{5,7},{3,5},{1,3},{0,1},{10,8},{12,10},{14... | collective-permute-start | bytes 1572872 | tf_op jit(solution)/shard_map/ppermute | solution.py:361
  178.3 12.1 %collective-permute-start.36 = (bf16[2,16,64,128]{3,2,1,0:T(8,128)(2,1)S(1)}, bf16[2,16,64,128]{3,2,1,0:T(8,128)(2,1)S(1)}, u32[]{:S(2)}, u32[]{:S(2)}) collective-permute-start(bf16[2,16,64,128]{3,2,1,0:T(8,128)(2,1)S(1)} %get-tuple-element.117), channel_id=1, source_target_pairs={{0,24},{8,16},{16,8},{24,0},{1,25},{9,17},{17,9},{25,1},{2,26},{10... | collective-permute-start | bytes 1572872 | tf_op jit(solution)/shard_map/ppermute | solution.py:378
  181.3 15.1 %collective-permute-start.40 = (bf16[16,128,128]{2,1,0:T(8,128)(2,1)S(1)}, bf16[16,128,128]{2,1,0:T(8,128)(2,1)S(1)}, u32[]{:S(2)}, u32[]{:S(2)}) collective-permute-start(bf16[16,128,128]{2,1,0:T(8,128)(2,1)S(1)} %collective-permute-done.34.refs_2_), channel_id=1, source_target_pairs={{0,2},{2,4},{4,6},{6,7},{7,5},{5,3},{3,1},{1,0},{8,10},{10,12},{12... | collective-permute-start | bytes 1572872 | tf_op jit(solution)/shard_map/ppermute | solution.py:360
  194.6 12.4 %collective-permute-start.37 = (bf16[2,16,64,128]{3,2,1,0:T(8,128)(2,1)S(1)}, bf16[2,16,64,128]{3,2,1,0:T(8,128)(2,1)S(1)}, u32[]{:S(2)}, u32[]{:S(2)}) collective-permute-start(bf16[2,16,64,128]{3,2,1,0:T(8,128)(2,1)S(1)} %get-tuple-element.119), channel_id=1, source_target_pairs={{0,8},{8,0},{16,24},{24,16},{1,9},{9,1},{17,25},{25,17},{2,10},{10... | collective-permute-start | bytes 1572872 | tf_op jit(solution)/shard_map/ppermute | solution.py:378
  195.2 15.8 %collective-permute-start.38 = (bf16[2,16,64,128]{3,2,1,0:T(8,128)(2,1)S(1)}, bf16[2,16,64,128]{3,2,1,0:T(8,128)(2,1)S(1)}, u32[]{:S(2)}, u32[]{:S(2)}) collective-permute-start(bf16[2,16,64,128]{3,2,1,0:T(8,128)(2,1)S(1)} %get-tuple-element.120), channel_id=1, source_target_pairs={{0,16},{8,24},{16,0},{24,8},{1,17},{9,25},{17,1},{25,9},{2,18},{10... | collective-permute-start | bytes 1572872 | tf_op jit(solution)/shard_map/ppermute | solution.py:378
  196.4 16.0 %collective-permute-start.42 = (bf16[16,128,128]{2,1,0:T(8,128)(2,1)S(1)}, bf16[16,128,128]{2,1,0:T(8,128)(2,1)S(1)}, u32[]{:S(2)}, u32[]{:S(2)}) collective-permute-start(bf16[16,128,128]{2,1,0:T(8,128)(2,1)S(1)} %collective-permute-done.35.refs_4_), channel_id=1, source_target_pairs={{2,0},{4,2},{6,4},{7,6},{5,7},{3,5},{1,3},{0,1},{10,8},{12,10},{14... | collective-permute-start | bytes 1572872 | tf_op jit(solution)/shard_map/ppermute | solution.py:361
  196.4 24.7 %collective-permute-start.41 = (bf16[16,128,128]{2,1,0:T(8,128)(2,1)S(1)}, bf16[16,128,128]{2,1,0:T(8,128)(2,1)S(1)}, u32[]{:S(2)}, u32[]{:S(2)}) collective-permute-start(bf16[16,128,128]{2,1,0:T(8,128)(2,1)S(1)} %collective-permute-done.40.refs_1_), channel_id=1, source_target_pairs={{0,2},{2,4},{4,6},{6,7},{7,5},{5,3},{3,1},{1,0},{8,10},{10,12},{12... | collective-permute-start | bytes 1572872 | tf_op jit(solution)/shard_map/ppermute | solution.py:360
  211.0 10.1 %collective-permute-start.39 = (bf16[2,16,64,128]{3,2,1,0:T(8,128)(2,1)S(1)}, bf16[2,16,64,128]{3,2,1,0:T(8,128)(2,1)S(1)}, u32[]{:S(2)}, u32[]{:S(2)}) collective-permute-start(bf16[2,16,64,128]{3,2,1,0:T(8,128)(2,1)S(1)} %get-tuple-element.122), channel_id=1, source_target_pairs={{0,24},{8,16},{16,8},{24,0},{1,25},{9,17},{17,9},{25,1},{2,26},{10... | collective-permute-start | bytes 1572872 | tf_op jit(solution)/shard_map/ppermute | solution.py:378
  212.4 10.5 %collective-permute-start.43 = (bf16[16,128,128]{2,1,0:T(8,128)(2,1)S(1)}, bf16[16,128,128]{2,1,0:T(8,128)(2,1)S(1)}, u32[]{:S(2)}, u32[]{:S(2)}) collective-permute-start(bf16[16,128,128]{2,1,0:T(8,128)(2,1)S(1)} %collective-permute-done.42.refs_5_), channel_id=1, source_target_pairs={{2,0},{4,2},{6,4},{7,6},{5,7},{3,5},{1,3},{0,1},{10,8},{12,10},{14... | collective-permute-start | bytes 1572872 | tf_op jit(solution)/shard_map/ppermute | solution.py:361
  228.1 10.4 %collective-permute-start.44 = (bf16[2,16,64,128]{3,2,1,0:T(8,128)(2,1)S(1)}, bf16[2,16,64,128]{3,2,1,0:T(8,128)(2,1)S(1)}, u32[]{:S(2)}, u32[]{:S(2)}) collective-permute-start(bf16[2,16,64,128]{3,2,1,0:T(8,128)(2,1)S(1)} %get-tuple-element.129), channel_id=1, source_target_pairs={{0,8},{8,0},{16,24},{24,16},{1,9},{9,1},{17,25},{25,17},{2,10},{10... | collective-permute-start | bytes 1572872 | tf_op jit(solution)/shard_map/ppermute | solution.py:378
  228.2 11.1 %collective-permute-start.45 = (bf16[2,16,64,128]{3,2,1,0:T(8,128)(2,1)S(1)}, bf16[2,16,64,128]{3,2,1,0:T(8,128)(2,1)S(1)}, u32[]{:S(2)}, u32[]{:S(2)}) collective-permute-start(bf16[2,16,64,128]{3,2,1,0:T(8,128)(2,1)S(1)} %get-tuple-element.130), channel_id=1, source_target_pairs={{0,16},{8,24},{16,0},{24,8},{1,17},{9,25},{17,1},{25,9},{2,18},{10... | collective-permute-start | bytes 1572872 | tf_op jit(solution)/shard_map/ppermute | solution.py:378
  229.0 15.9 %collective-permute-start.46 = (bf16[2,16,64,128]{3,2,1,0:T(8,128)(2,1)S(1)}, bf16[2,16,64,128]{3,2,1,0:T(8,128)(2,1)S(1)}, u32[]{:S(2)}, u32[]{:S(2)}) collective-permute-start(bf16[2,16,64,128]{3,2,1,0:T(8,128)(2,1)S(1)} %get-tuple-element.131), channel_id=1, source_target_pairs={{0,24},{8,16},{16,8},{24,0},{1,25},{9,17},{17,9},{25,1},{2,26},{10... | collective-permute-start | bytes 1572872 | tf_op jit(solution)/shard_map/ppermute | solution.py:378
  245.4 5.1 %collective-permute-start.49 = (bf16[16,64,512]{2,1,0:T(8,128)(2,1)S(1)}, bf16[16,64,512]{2,1,0:T(8,128)(2,1)S(1)}, u32[]{:S(2)}, u32[]{:S(2)}) collective-permute-start(bf16[16,64,512]{2,1,0:T(8,128)(2,1)S(1)} %get-tuple-element.139), channel_id=1, source_target_pairs={{0,1},{1,0},{2,3},{3,2},{4,5},{5,4},{6,7},{7,6},{8,9},{9,8},{10,11... | collective-permute-start | bytes 3145736 | tf_op jit(solution)/shard_map/ppermute | solution.py:387
  (31 other events, 613.0 us)

commit v8 on v7

--- a/solution.py
+++ b/solution.py
@@ -242,24 +242,24 @@
     )(*args)
 
 
-def put_kernel(tile_cols, where_ref, *refs):
+def put_kernel(owners, tile_cols, where_ref, *refs):
     out_ref, sems = refs[-2:]
     copies = []
-    for part, rows_ref in enumerate(refs[:-3]):
+    for n, rows_ref in enumerate(refs[:-3]):
         step = rows_ref.shape[0]
-        row = pl.multiple_of((1 - where_ref[2]) * tile_cols + part * step, step)
-        copy = pltpu.make_async_copy(rows_ref, out_ref.at[pl.ds(row, step)], sems.at[part])
+        row = pl.multiple_of((1 - where_ref[2]) * tile_cols + owners[n] * step, step)
+        copy = pltpu.make_async_copy(rows_ref, out_ref.at[pl.ds(row, step)], sems.at[n])
         copy.start()
         copies.append(copy)
     for copy in copies:
         copy.wait()
 
 
-def put_call(where, rows, earlier, tile_cols):
+def put_call(where, owners, rows, earlier, tile_cols):
     far = pl.BlockSpec(memory_space=pl.ANY)
     whole = pl.BlockSpec(memory_space=pltpu.VMEM)
     return pl.pallas_call(
-        functools.partial(put_kernel, tile_cols),
+        functools.partial(put_kernel, tuple(owners), tile_cols),
         in_specs=[pl.BlockSpec(memory_space=pltpu.SMEM), *[whole] * len(rows), far],
         out_specs=far,
         out_shape=jax.ShapeDtypeStruct(earlier.shape, earlier.dtype),
@@ -418,15 +418,15 @@
                 place(p, *before)
                 gates[min(index + 2, len(order) - 1)].append(handed[p])
     for d in range(1, parts):
-        send(count - 2, d, *(moved[count - 2][1:3] if d > 2 else []))
+        send(count - 2, d, *(done[-2] if d > 2 else []))
     project(count - 1, *moved[count - 2][1:])
     for d in range(1, parts):
         send(count - 1, d)
     place(count - 2)
     place(count - 1, *handed[:-1])
     for part in range(count):
-        exchange(part, *moved[-1][1:])
-    state["result"] = put_call(where, swapped, state["result"], tile_cols)
+        exchange(part, *(moved[-1][1:] if part >= count - 2 else moved[-1][:1]))
+    state["result"] = put_call(where, range(count), swapped, state["result"], tile_cols)
     return (state["new_pair"], state["result"])
 
 

time: 258 us -> 256 us (level)
  waiting for transfers between devices: 133 us -> 129 us
  transfers between devices with their start and end apart: 51 -> 51, of which waited for: 29 -> 26; matrix products, arithmetic and copies ran while one was open for 4% -> 4% of each run, Pallas kernels for 16% -> 17%
where the time goes in v8:
time: 256 us; the launch traced here: 253 us
  waiting for transfers between devices  129 us (50%)
  Pallas kernels  57.6 us (22%)
  starting transfers between devices  49 us (19%)
  local copies, waits for them, and re-layouts  15 us (6%)
    ppermute x12, waiting for transfers between devices, shift(): here[-s] = lax.ppermute(after(here[-(s - 1)], *others), 'col', onward)  47.2 us
    ppermute x12, waiting for transfers between devices, send(): lax.ppermute(piece, 'row', [(a, a ^ d) for a in range(parts)])  39.2 us
    pallas_call x4, Pallas kernels, update_call(): pl.pallas_call(functools.partial(update_kernel, parts, part, cols, plan),...  29.4 us
    ppermute x12, starting transfers between devices, shift(): here[-s] = lax.ppermute(after(here[-(s - 1)], *others), 'col', onward)  19.5 us
    pallas_call x4, Pallas kernels, project_call(): pl.pallas_call(functools.partial(project_kernel, line, parts), in_specs=[...  17.6 us
    ppermute x3, waiting for transfers between devices, shards(): held[-s] = lax.ppermute(ahead, 'col', onward)  16.3 us
    ppermute x12, starting transfers between devices, send(): lax.ppermute(piece, 'row', [(a, a ^ d) for a in range(parts)])  14.1 us
    ppermute x3, waiting for transfers between devices, shards(): lax.ppermute(alignment_right, 'row', [(a, a ^ d) for a in range(parts)])  12.3 us
  transfers between devices with their start and end apart: 51, of which 26 were waited for; matrix products, arithmetic and copies ran while one was open for 4% of the time, Pallas kernels for 17%

profile of v8, /device:TPU:0, one launch (start us, length us, event | category | flops | bytes accessed | tf_op | source)
XLA Modules:
  0.0 253.1 jit_solution(3669670057778761391)
XLA Ops:
  0.6 3.0 %collective-permute-start = (bf16[16,16384]{1,0:T(8,128)(2,1)}, bf16[16,16384]{1,0:T(8,128)(2,1)S(1)}, u32[]{:S(2)}, u32[]{:S(2)}) collective-permute-start(bf16[16,16384]{1,0:T(8,128)(2,1)} %refs_3_.7), channel_id=1, source_target_pairs={{0,2},{2,4},{4,6},{6,7},{7,5},{5,3},{3,1},{1,0},{8,10},{10,12},{12... | collective-permute-start | bytes 1572872 | tf_op jit(solution)/shard_map/ppermute | solution.py:305
  7.2 8.0 %collective-permute-done.refs_2_ = bf16[16,16384]{1,0:T(8,128)(2,1)S(1)} collective-permute-done((bf16[16,16384]{1,0:T(8,128)(2,1)}, bf16[16,16384]{1,0:T(8,128)(2,1)S(1)}, u32[]{:S(2)}, u32[]{:S(2)}) %collective-permute-start) | collective-permute-done | bytes 524320 | tf_op jit(solution)/shard_map/ppermute | solution.py:305
  15.2 2.4 collective-permute-start.1
  18.7 11.2 %collective-permute-done.5.refs_11_ = bf16[128,2048]{1,0:T(8,128)(2,1)S(1)} collective-permute-done((bf16[128,2048]{1,0:T(8,128)(2,1)}, bf16[128,2048]{1,0:T(8,128)(2,1)S(1)}, u32[]{:S(2)}, u32[]{:S(2)}) %collective-permute-start.5) | collective-permute-done | bytes 524320 | tf_op jit(solution)/shard_map/ppermute | solution.py:293
  34.0 8.3 %collective-permute-done.7.refs_0_ = bf16[16,16384]{1,0:T(8,128)(2,1)S(1)} collective-permute-done((bf16[16,16384]{1,0:T(8,128)(2,1)S(1)}, bf16[16,16384]{1,0:T(8,128)(2,1)S(1)}, u32[]{:S(2)}, u32[]{:S(2)}) %collective-permute-start.7) | collective-permute-done | bytes 524320 | tf_op jit(solution)/shard_map/ppermute | solution.py:305
  43.0 2.5 collective-permute-start.9
  54.4 7.3 %update.4 = (bf16[128,64,128]{2,1,0:T(8,128)(2,1)}, bf16[16,128,128]{2,1,0:T(8,128)(2,1)S(1)}) custom-call(s32[3]{0:T(128)S(1)} %pad_add_fusion.where_ref, bf16[16,16384]{1,0:T(8,128)(2,1)S(1)} %collective-permute-done.7.refs_0_, bf16[16,16384]{1,0:T(8,128)(2,1)S(1)} %collective-permute-done.1.refs_1_, bf16[16,16384]{1,0:T(8,128)(2,1)S(1)} %collective-permute-done.refs_2_, ...), custom_call_target="tpu_custom_call" | custom-call | flops 2684354560 | bytes 8388608 | tf_op jit(solution)/shard_map/update/pallas_call | solution.py:121
  61.7 2.0 collective-permute-start.11
  63.7 10.1 %collective-permute-done.11.refs_2_ = bf16[16,128,128]{2,1,0:T(8,128)(2,1)S(1)} collective-permute-done((bf16[16,128,128]{2,1,0:T(8,128)(2,1)S(1)}, bf16[16,128,128]{2,1,0:T(8,128)(2,1)S(1)}, u32[]{:S(2)}, u32[]{:S(2)}) %collective-permute-start.11) | collective-permute-done | bytes 524320 | tf_op jit(solution)/shard_map/ppermute | solution.py:360
  73.9 2.5 collective-permute-start.15
  76.4 7.6 %update.5 = (bf16[128,64,128]{2,1,0:T(8,128)(2,1)}, bf16[16,128,128]{2,1,0:T(8,128)(2,1)}) custom-call(s32[3]{0:T(128)S(1)} %pad_add_fusion.where_ref, bf16[16,16384]{1,0:T(8,128)(2,1)S(1)} %collective-permute-done.7.refs_0_, bf16[16,16384]{1,0:T(8,128)(2,1)S(1)} %collective-permute-done.1.refs_1_, ...), custom_call_target="tpu_custom_call", output_to_operand_aliasing={{0}: (18, {})} | custom-call | flops 2684354560 | bytes 8388608 | tf_op jit(solution)/shard_map/update/pallas_call | solution.py:121
  84.0 1.8 collective-permute-start.13
  86.8 2.6 %collective-permute-start.17 = (bf16[16,128,128]{2,1,0:T(8,128)(2,1)}, bf16[16,128,128]{2,1,0:T(8,128)(2,1)}, u32[]{:S(2)}, u32[]{:S(2)}) collective-permute-start(bf16[16,128,128]{2,1,0:T(8,128)(2,1)} %collective-permute-done.15.refs_1_), channel_id=1, source_target_pairs={{0,2},{2,4},{4,6},{6,7},{7,5},{5,3},{3,1},{1,0},{8,10},{10,12},{12... | collective-permute-start | bytes 1572872 | tf_op jit(solution)/shard_map/ppermute | solution.py:360
  89.7 8.9 %collective-permute-done.13.refs_2_ = bf16[16,128,128]{2,1,0:T(8,128)(2,1)} collective-permute-done((bf16[16,128,128]{2,1,0:T(8,128)(2,1)}, bf16[16,128,128]{2,1,0:T(8,128)(2,1)}, u32[]{:S(2)}, u32[]{:S(2)}) %collective-permute-start.13) | collective-permute-done | bytes 524320 | tf_op jit(solution)/shard_map/ppermute | solution.py:360
  98.5 2.5 collective-permute-done.14.refs_4_
  103.2 7.3 %update.6 = (bf16[128,64,128]{2,1,0:T(8,128)(2,1)}, bf16[16,128,128]{2,1,0:T(8,128)(2,1)S(1)}) custom-call(s32[3]{0:T(128)S(1)} %pad_add_fusion.where_ref, bf16[16,16384]{1,0:T(8,128)(2,1)S(1)} %collective-permute-done.7.refs_0_, bf16[16,16384]{1,0:T(8,128)(2,1)S(1)} %collective-permute-done.1.refs_1_, ...), custom_call_target="tpu_custom_call", output_to_operand_aliasing={{0}: (18, {})} | custom-call | flops 2684354560 | bytes 8388608 | tf_op jit(solution)/shard_map/update/pallas_call | solution.py:121
  110.5 1.7 collective-permute-done.18.refs_6_
  112.8 4.1 %project.4 = (bf16[2,16,64,128]{3,2,1,0:T(8,128)(2,1)S(1)}, bf16[2,16,64,128]{3,2,1,0:T(8,128)(2,1)S(1)}, bf16[2,16,64,128]{3,2,1,0:T(8,128)(2,1)S(1)}, bf16[2,16,64,128]{3,2,1,0:T(8,128)(2,1)S(1)}) custom-call(s32[3]{0:T(128)S(1)} %pad_add_fusion.where_ref, bf16[128,128]{1,0:T(8,128)(2,1)S(1)} %copy-done.8, f32[128,1]{1,0:T(8,128)S(1)} %copy.43.offset_ref, ...), custom_call_target="tpu_custom_call" | custom-call | flops 268435456 | bytes 4194304 | tf_op jit(solution)/shard_map/project/pallas_call | solution.py:182
  118.2 2.8 %collective-permute-done.21.refs_1_ = bf16[16,128,128]{2,1,0:T(8,128)(2,1)S(1)} collective-permute-done((bf16[16,128,128]{2,1,0:T(8,128)(2,1)}, bf16[16,128,128]{2,1,0:T(8,128)(2,1)S(1)}, u32[]{:S(2)}, u32[]{:S(2)}) %collective-permute-start.21) | collective-permute-done | bytes 524320 | tf_op jit(solution)/shard_map/ppermute | solution.py:360
  121.0 2.4 collective-permute-done.22.refs_5_
  124.9 6.1 %collective-permute-done.19.refs_2_ = bf16[16,128,128]{2,1,0:T(8,128)(2,1)S(1)} collective-permute-done((bf16[16,128,128]{2,1,0:T(8,128)(2,1)S(1)}, bf16[16,128,128]{2,1,0:T(8,128)(2,1)S(1)}, u32[]{:S(2)}, u32[]{:S(2)}) %collective-permute-start.19) | collective-permute-done | bytes 524320 | tf_op jit(solution)/shard_map/ppermute | solution.py:360
  132.5 2.5 collective-permute-start.28
  134.9 2.0 collective-permute-start.24
  137.0 7.6 %collective-permute-done.27.refs_3_ = bf16[2,16,64,128]{3,2,1,0:T(8,128)(2,1)S(1)} collective-permute-done((bf16[2,16,64,128]{3,2,1,0:T(8,128)(2,1)S(1)}, bf16[2,16,64,128]{3,2,1,0:T(8,128)(2,1)S(1)}, u32[]{:S(2)}, u32[]{:S(2)}) %collective-permute-start.27) | collective-permute-done | bytes 524320 | tf_op jit(solution)/shard_map/ppermute | solution.py:378
  144.6 2.7 %collective-permute-done.28.refs_0_ = bf16[16,128,128]{2,1,0:T(8,128)(2,1)S(1)} collective-permute-done((bf16[16,128,128]{2,1,0:T(8,128)(2,1)S(1)}, bf16[16,128,128]{2,1,0:T(8,128)(2,1)S(1)}, u32[]{:S(2)}, u32[]{:S(2)}) %collective-permute-start.28) | collective-permute-done | bytes 524320 | tf_op jit(solution)/shard_map/ppermute | solution.py:360
  147.3 2.5 collective-permute-done.29.refs_6_
  150.6 4.2 %project.5 = (bf16[2,16,64,128]{3,2,1,0:T(8,128)(2,1)S(1)}, bf16[2,16,64,128]{3,2,1,0:T(8,128)(2,1)S(1)}, bf16[2,16,64,128]{3,2,1,0:T(8,128)(2,1)S(1)}, bf16[2,16,64,128]{3,2,1,0:T(8,128)(2,1)S(1)}) custom-call(s32[3]{0:T(128)S(1)} %pad_add_fusion.where_ref, bf16[128,128]{1,0:T(8,128)(2,1)S(1)} %copy-done.8, f32[128,1]{1,0:T(8,128)S(1)} %copy.43.offset_ref, ...), custom_call_target="tpu_custom_call" | custom-call | flops 268435456 | bytes 4194304 | tf_op jit(solution)/shard_map/project/pallas_call | solution.py:182
  156.4 7.2 %update.7 = (bf16[128,64,128]{2,1,0:T(8,128)(2,1)}, bf16[16,128,128]{2,1,0:T(8,128)(2,1)S(1)}) custom-call(s32[3]{0:T(128)S(1)} %pad_add_fusion.where_ref, bf16[16,16384]{1,0:T(8,128)(2,1)S(1)} %collective-permute-done.7.refs_0_, bf16[16,16384]{1,0:T(8,128)(2,1)S(1)} %collective-permute-done.1.refs_1_, ...), custom_call_target="tpu_custom_call", output_to_operand_aliasing={{0}: (18, {})} | custom-call | flops 2684354560 | bytes 8388608 | tf_op jit(solution)/shard_map/update/pallas_call | solution.py:121
  166.3 9.7 %collective-permute-done.34.refs_2_ = bf16[16,128,128]{2,1,0:T(8,128)(2,1)S(1)} collective-permute-done((bf16[16,128,128]{2,1,0:T(8,128)(2,1)S(1)}, bf16[16,128,128]{2,1,0:T(8,128)(2,1)S(1)}, u32[]{:S(2)}, u32[]{:S(2)}) %collective-permute-start.34) | collective-permute-done | bytes 524320 | tf_op jit(solution)/shard_map/ppermute | solution.py:360
  175.9 2.3 collective-permute-done.35.refs_4_
  179.4 1.8 place.4
  181.3 1.7 collective-permute-start.39
  183.0 4.2 %collective-permute-done.31.refs_0_ = bf16[16,128,128]{2,1,0:T(8,128)(2,1)S(1)} collective-permute-done((bf16[16,128,128]{2,1,0:T(8,128)(2,1)S(1)}, bf16[16,128,128]{2,1,0:T(8,128)(2,1)S(1)}, u32[]{:S(2)}, u32[]{:S(2)}) %collective-permute-start.31) | collective-permute-done | bytes 524320 | tf_op jit(solution)/shard_map/ppermute | solution.py:360
  187.2 3.2 %collective-permute-done.36.refs_3_ = bf16[2,16,64,128]{3,2,1,0:T(8,128)(2,1)S(1)} collective-permute-done((bf16[2,16,64,128]{3,2,1,0:T(8,128)(2,1)S(1)}, bf16[2,16,64,128]{3,2,1,0:T(8,128)(2,1)S(1)}, u32[]{:S(2)}, u32[]{:S(2)}) %collective-permute-start.36) | collective-permute-done | bytes 524320 | tf_op jit(solution)/shard_map/ppermute | solution.py:378
  190.4 4.2 %project.6 = (bf16[2,16,64,128]{3,2,1,0:T(8,128)(2,1)S(1)}, bf16[2,16,64,128]{3,2,1,0:T(8,128)(2,1)S(1)}, bf16[2,16,64,128]{3,2,1,0:T(8,128)(2,1)S(1)}, bf16[2,16,64,128]{3,2,1,0:T(8,128)(2,1)S(1)}) custom-call(s32[3]{0:T(128)S(1)} %pad_add_fusion.where_ref, bf16[128,128]{1,0:T(8,128)(2,1)S(1)} %copy-done.8, f32[128,1]{1,0:T(8,128)S(1)} %copy.43.offset_ref, ...), custom_call_target="tpu_custom_call" | custom-call | flops 268435456 | bytes 4194304 | tf_op jit(solution)/shard_map/project/pallas_call | solution.py:182
  196.4 1.8 collective-permute-done.39.refs_1_
  199.4 2.5 collective-permute-start.42
  201.9 7.6 %collective-permute-done.37.refs_1_ = bf16[2,16,64,128]{3,2,1,0:T(8,128)(2,1)S(1)} collective-permute-done((bf16[2,16,64,128]{3,2,1,0:T(8,128)(2,1)S(1)}, bf16[2,16,64,128]{3,2,1,0:T(8,128)(2,1)S(1)}, u32[]{:S(2)}, u32[]{:S(2)}) %collective-permute-start.37) | collective-permute-done | bytes 524320 | tf_op jit(solution)/shard_map/ppermute | solution.py:378
  209.5 7.1 %collective-permute-done.38.refs_2_ = bf16[2,16,64,128]{3,2,1,0:T(8,128)(2,1)S(1)} collective-permute-done((bf16[2,16,64,128]{3,2,1,0:T(8,128)(2,1)S(1)}, bf16[2,16,64,128]{3,2,1,0:T(8,128)(2,1)S(1)}, u32[]{:S(2)}, u32[]{:S(2)}) %collective-permute-start.38) | collective-permute-done | bytes 524320 | tf_op jit(solution)/shard_map/ppermute | solution.py:378
  217.5 5.1 %project.7 = (bf16[2,16,64,128]{3,2,1,0:T(8,128)(2,1)S(1)}, bf16[2,16,64,128]{3,2,1,0:T(8,128)(2,1)S(1)}, bf16[2,16,64,128]{3,2,1,0:T(8,128)(2,1)}, bf16[2,16,64,128]{3,2,1,0:T(8,128)(2,1)S(1)}) custom-call(s32[3]{0:T(128)S(1)} %pad_add_fusion.where_ref, bf16[128,128]{1,0:T(8,128)(2,1)S(1)} %copy-done.8, f32[128,1]{1,0:T(8,128)S(1)} %copy.43.offset_ref, ...), custom_call_target="tpu_custom_call" | custom-call | flops 268435456 | bytes 4194304 | tf_op jit(solution)/shard_map/project/pallas_call | solution.py:182
  222.6 1.7 collective-permute-start.46
  226.1 1.8 place.5
  228.5 1.8 place.6
  230.4 7.1 %collective-permute-done.46.refs_1_ = bf16[2,16,64,128]{3,2,1,0:T(8,128)(2,1)S(1)} collective-permute-done((bf16[2,16,64,128]{3,2,1,0:T(8,128)(2,1)S(1)}, bf16[2,16,64,128]{3,2,1,0:T(8,128)(2,1)S(1)}, u32[]{:S(2)}, u32[]{:S(2)}) %collective-permute-start.46) | collective-permute-done | bytes 524320 | tf_op jit(solution)/shard_map/ppermute | solution.py:378
  237.5 6.5 %collective-permute-done.47.refs_2_ = bf16[2,16,64,128]{3,2,1,0:T(8,128)(2,1)S(1)} collective-permute-done((bf16[2,16,64,128]{3,2,1,0:T(8,128)(2,1)}, bf16[2,16,64,128]{3,2,1,0:T(8,128)(2,1)S(1)}, u32[]{:S(2)}, u32[]{:S(2)}) %collective-permute-start.47) | collective-permute-done | bytes 524320 | tf_op jit(solution)/shard_map/ppermute | solution.py:378
  244.0 1.8 place.7
  246.6 2.0 collective-permute-done.50.refs_3_
  249.6 3.3 %put.1 = bf16[128,64,512]{2,1,0:T(8,128)(2,1)} custom-call(s32[3]{0:T(128)S(1)} %pad_add_fusion.where_ref, bf16[16,64,512]{2,1,0:T(8,128)(2,1)S(1)} %collective-permute-done.44.refs_0_, bf16[16,64,512]{2,1,0:T(8,128)(2,1)S(1)} %collective-permute-done.45.refs_1_, ...), custom_call_target="tpu_custom_call", output_to_operand_aliasing={{}: (5, {})} | custom-call | bytes 8388608 | tf_op jit(solution)/shard_map/put/pallas_call | solution.py:261
  (139 shorter events, 40.8 us)
Async XLA Ops:
  0.6 14.6 %collective-permute-start = (bf16[16,16384]{1,0:T(8,128)(2,1)}, bf16[16,16384]{1,0:T(8,128)(2,1)S(1)}, u32[]{:S(2)}, u32[]{:S(2)}) collective-permute-start(bf16[16,16384]{1,0:T(8,128)(2,1)} %refs_3_.7), channel_id=1, source_target_pairs={{0,2},{2,4},{4,6},{6,7},{7,5},{5,3},{3,1},{1,0},{8,10},{10,12},{12... | collective-permute-start | bytes 1572872 | tf_op jit(solution)/shard_map/ppermute | solution.py:305
  3.7 13.9 %collective-permute-start.2 = (bf16[16,16384]{1,0:T(8,128)(2,1)}, bf16[16,16384]{1,0:T(8,128)(2,1)S(1)}, u32[]{:S(2)}, u32[]{:S(2)}) collective-permute-start(bf16[16,16384]{1,0:T(8,128)(2,1)} %refs_3_.7), channel_id=1, source_target_pairs={{2,0},{4,2},{6,4},{7,6},{5,7},{3,5},{1,3},{0,1},{10,8},{12,10},{14... | collective-permute-start | bytes 1572872 | tf_op jit(solution)/shard_map/ppermute | solution.py:306
  3.7 15.1 %collective-permute-start.4 = (bf16[128,2048]{1,0:T(8,128)(2,1)}, bf16[128,2048]{1,0:T(8,128)(2,1)S(1)}, u32[]{:S(2)}, u32[]{:S(2)}) collective-permute-start(bf16[128,2048]{1,0:T(8,128)(2,1)} %refs_9_.7), channel_id=1, source_target_pairs={{0,8},{8,0},{16,24},{24,16},{1,9},{9,1},{17,25},{25,17},{2,10},{10... | collective-permute-start | bytes 1572872 | tf_op jit(solution)/shard_map/ppermute | solution.py:293
  5.2 24.7 %collective-permute-start.5 = (bf16[128,2048]{1,0:T(8,128)(2,1)}, bf16[128,2048]{1,0:T(8,128)(2,1)S(1)}, u32[]{:S(2)}, u32[]{:S(2)}) collective-permute-start(bf16[128,2048]{1,0:T(8,128)(2,1)} %refs_9_.7), channel_id=1, source_target_pairs={{0,16},{8,24},{16,0},{24,8},{1,17},{9,25},{17,1},{25,9},{2,18},{10... | collective-permute-start | bytes 1572872 | tf_op jit(solution)/shard_map/ppermute | solution.py:293
  6.7 23.2 %collective-permute-start.6 = (bf16[128,2048]{1,0:T(8,128)(2,1)}, bf16[128,2048]{1,0:T(8,128)(2,1)S(1)}, u32[]{:S(2)}, u32[]{:S(2)}) collective-permute-start(bf16[128,2048]{1,0:T(8,128)(2,1)} %refs_9_.7), channel_id=1, source_target_pairs={{0,24},{8,16},{16,8},{24,0},{1,25},{9,17},{17,9},{25,1},{2,26},{10... | collective-permute-start | bytes 1572872 | tf_op jit(solution)/shard_map/ppermute | solution.py:293
  15.2 14.7 %collective-permute-start.1 = (bf16[16,16384]{1,0:T(8,128)(2,1)S(1)}, bf16[16,16384]{1,0:T(8,128)(2,1)S(1)}, u32[]{:S(2)}, u32[]{:S(2)}) collective-permute-start(bf16[16,16384]{1,0:T(8,128)(2,1)S(1)} %collective-permute-done.refs_2_), channel_id=1, source_target_pairs={{0,2},{2,4},{4,6},{6,7},{7,5},{5,3},{3,1},{1,0},{8,10},{10,12},{12... | collective-permute-start | bytes 1572872 | tf_op jit(solution)/shard_map/ppermute | solution.py:305
  17.6 12.3 %collective-permute-start.3 = (bf16[16,16384]{1,0:T(8,128)(2,1)S(1)}, bf16[16,16384]{1,0:T(8,128)(2,1)}, u32[]{:S(2)}, u32[]{:S(2)}) collective-permute-start(bf16[16,16384]{1,0:T(8,128)(2,1)S(1)} %collective-permute-done.2.refs_4_), channel_id=1, source_target_pairs={{2,0},{4,2},{6,4},{7,6},{5,7},{3,5},{1,3},{0,1},{10,8},{12,10},{14... | collective-permute-start | bytes 1572872 | tf_op jit(solution)/shard_map/ppermute | solution.py:306
  29.9 12.4 %collective-permute-start.7 = (bf16[16,16384]{1,0:T(8,128)(2,1)S(1)}, bf16[16,16384]{1,0:T(8,128)(2,1)S(1)}, u32[]{:S(2)}, u32[]{:S(2)}) collective-permute-start(bf16[16,16384]{1,0:T(8,128)(2,1)S(1)} %collective-permute-done.1.refs_1_), channel_id=1, source_target_pairs={{0,2},{2,4},{4,6},{6,7},{7,5},{5,3},{3,1},{1,0},{8,10},{10,12},{12... | collective-permute-start | bytes 1572872 | tf_op jit(solution)/shard_map/ppermute | solution.py:305
  31.5 14.0 %collective-permute-start.8 = (bf16[16,16384]{1,0:T(8,128)(2,1)}, bf16[16,16384]{1,0:T(8,128)(2,1)S(1)}, u32[]{:S(2)}, u32[]{:S(2)}) collective-permute-start(bf16[16,16384]{1,0:T(8,128)(2,1)} %collective-permute-done.3.refs_5_), channel_id=1, source_target_pairs={{2,0},{4,2},{6,4},{7,6},{5,7},{3,5},{1,3},{0,1},{10,8},{12,10},{14... | collective-permute-start | bytes 1572872 | tf_op jit(solution)/shard_map/ppermute | solution.py:306
  43.0 10.3 %collective-permute-start.9 = (bf16[16,8192]{1,0:T(8,128)(2,1)}, bf16[16,8192]{1,0:T(8,128)(2,1)S(1)}, u32[]{:S(2)}, u32[]{:S(2)}) collective-permute-start(bf16[16,8192]{1,0:T(8,128)(2,1)} %slice.8), channel_id=1, source_target_pairs={{0,2},{2,4},{4,6},{6,7},{7,5},{5,3},{3,1},{1,0},{8,10},{10,12},{12... | collective-permute-start | bytes 786440 | tf_op jit(solution)/shard_map/ppermute | solution.py:310
  61.7 12.2 %collective-permute-start.11 = (bf16[16,128,128]{2,1,0:T(8,128)(2,1)S(1)}, bf16[16,128,128]{2,1,0:T(8,128)(2,1)S(1)}, u32[]{:S(2)}, u32[]{:S(2)}) collective-permute-start(bf16[16,128,128]{2,1,0:T(8,128)(2,1)S(1)} %get-tuple-element.79.refs_3_), channel_id=1, source_target_pairs={{0,2},{2,4},{4,6},{6,7},{7,5},{5,3},{3,1},{1,0},{8,10},{10,12},{12... | collective-permute-start | bytes 1572872 | tf_op jit(solution)/shard_map/ppermute | solution.py:360
  63.7 12.6 %collective-permute-start.12 = (bf16[16,128,128]{2,1,0:T(8,128)(2,1)S(1)}, bf16[16,128,128]{2,1,0:T(8,128)(2,1)S(1)}, u32[]{:S(2)}, u32[]{:S(2)}) collective-permute-start(bf16[16,128,128]{2,1,0:T(8,128)(2,1)S(1)} %get-tuple-element.79.refs_3_), channel_id=1, source_target_pairs={{2,0},{4,2},{6,4},{7,6},{5,7},{3,5},{1,3},{0,1},{10,8},{12,10},{14... | collective-permute-start | bytes 1572872 | tf_op jit(solution)/shard_map/ppermute | solution.py:361
  73.9 13.0 %collective-permute-start.15 = (bf16[16,128,128]{2,1,0:T(8,128)(2,1)S(1)}, bf16[16,128,128]{2,1,0:T(8,128)(2,1)}, u32[]{:S(2)}, u32[]{:S(2)}) collective-permute-start(bf16[16,128,128]{2,1,0:T(8,128)(2,1)S(1)} %collective-permute-done.11.refs_2_), channel_id=1, source_target_pairs={{0,2},{2,4},{4,6},{6,7},{7,5},{5,3},{3,1},{1,0},{8,10},{10,12},{12... | collective-permute-start | bytes 1572872 | tf_op jit(solution)/shard_map/ppermute | solution.py:360
  76.3 10.5 %collective-permute-start.16 = (bf16[16,128,128]{2,1,0:T(8,128)(2,1)S(1)}, bf16[16,128,128]{2,1,0:T(8,128)(2,1)}, u32[]{:S(2)}, u32[]{:S(2)}) collective-permute-start(bf16[16,128,128]{2,1,0:T(8,128)(2,1)S(1)} %collective-permute-done.12.refs_4_), channel_id=1, source_target_pairs={{2,0},{4,2},{6,4},{7,6},{5,7},{3,5},{1,3},{0,1},{10,8},{12,10},{14... | collective-permute-start | bytes 1572872 | tf_op jit(solution)/shard_map/ppermute | solution.py:361
  84.0 14.5 %collective-permute-start.13 = (bf16[16,128,128]{2,1,0:T(8,128)(2,1)}, bf16[16,128,128]{2,1,0:T(8,128)(2,1)}, u32[]{:S(2)}, u32[]{:S(2)}) collective-permute-start(bf16[16,128,128]{2,1,0:T(8,128)(2,1)} %get-tuple-element.80.refs_3_), channel_id=1, source_target_pairs={{0,2},{2,4},{4,6},{6,7},{7,5},{5,3},{3,1},{1,0},{8,10},{10,12},{12... | collective-permute-start | bytes 1572872 | tf_op jit(solution)/shard_map/ppermute | solution.py:360
  85.8 15.2 %collective-permute-start.14 = (bf16[16,128,128]{2,1,0:T(8,128)(2,1)}, bf16[16,128,128]{2,1,0:T(8,128)(2,1)}, u32[]{:S(2)}, u32[]{:S(2)}) collective-permute-start(bf16[16,128,128]{2,1,0:T(8,128)(2,1)} %get-tuple-element.80.refs_3_), channel_id=1, source_target_pairs={{2,0},{4,2},{6,4},{7,6},{5,7},{3,5},{1,3},{0,1},{10,8},{12,10},{14... | collective-permute-start | bytes 1572872 | tf_op jit(solution)/shard_map/ppermute | solution.py:361
  86.8 23.7 %collective-permute-start.17 = (bf16[16,128,128]{2,1,0:T(8,128)(2,1)}, bf16[16,128,128]{2,1,0:T(8,128)(2,1)}, u32[]{:S(2)}, u32[]{:S(2)}) collective-permute-start(bf16[16,128,128]{2,1,0:T(8,128)(2,1)} %collective-permute-done.15.refs_1_), channel_id=1, source_target_pairs={{0,2},{2,4},{4,6},{6,7},{7,5},{5,3},{3,1},{1,0},{8,10},{10,12},{12... | collective-permute-start | bytes 1572872 | tf_op jit(solution)/shard_map/ppermute | solution.py:360
  89.4 22.8 %collective-permute-start.18 = (bf16[16,128,128]{2,1,0:T(8,128)(2,1)}, bf16[16,128,128]{2,1,0:T(8,128)(2,1)}, u32[]{:S(2)}, u32[]{:S(2)}) collective-permute-start(bf16[16,128,128]{2,1,0:T(8,128)(2,1)} %collective-permute-done.16.refs_5_), channel_id=1, source_target_pairs={{2,0},{4,2},{6,4},{7,6},{5,7},{3,5},{1,3},{0,1},{10,8},{12,10},{14... | collective-permute-start | bytes 1572872 | tf_op jit(solution)/shard_map/ppermute | solution.py:361
  101.0 20.0 %collective-permute-start.21 = (bf16[16,128,128]{2,1,0:T(8,128)(2,1)}, bf16[16,128,128]{2,1,0:T(8,128)(2,1)S(1)}, u32[]{:S(2)}, u32[]{:S(2)}) collective-permute-start(bf16[16,128,128]{2,1,0:T(8,128)(2,1)} %collective-permute-done.13.refs_2_), channel_id=1, source_target_pairs={{0,2},{2,4},{4,6},{6,7},{7,5},{5,3},{3,1},{1,0},{8,10},{10,12},{12... | collective-permute-start | bytes 1572872 | tf_op jit(solution)/shard_map/ppermute | solution.py:360
  101.2 22.2 %collective-permute-start.22 = (bf16[16,128,128]{2,1,0:T(8,128)(2,1)}, bf16[16,128,128]{2,1,0:T(8,128)(2,1)S(1)}, u32[]{:S(2)}, u32[]{:S(2)}) collective-permute-start(bf16[16,128,128]{2,1,0:T(8,128)(2,1)} %collective-permute-done.14.refs_4_), channel_id=1, source_target_pairs={{2,0},{4,2},{6,4},{7,6},{5,7},{3,5},{1,3},{0,1},{10,8},{12,10},{14... | collective-permute-start | bytes 1572872 | tf_op jit(solution)/shard_map/ppermute | solution.py:361
  112.2 18.7 %collective-permute-start.19 = (bf16[16,128,128]{2,1,0:T(8,128)(2,1)S(1)}, bf16[16,128,128]{2,1,0:T(8,128)(2,1)S(1)}, u32[]{:S(2)}, u32[]{:S(2)}) collective-permute-start(bf16[16,128,128]{2,1,0:T(8,128)(2,1)S(1)} %get-tuple-element.86.refs_3_), channel_id=1, source_target_pairs={{0,2},{2,4},{4,6},{6,7},{7,5},{5,3},{3,1},{1,0},{8,10},{10,12},{12... | collective-permute-start | bytes 1572872 | tf_op jit(solution)/shard_map/ppermute | solution.py:360
  112.4 18.6 %collective-permute-start.20 = (bf16[16,128,128]{2,1,0:T(8,128)(2,1)S(1)}, bf16[16,128,128]{2,1,0:T(8,128)(2,1)S(1)}, u32[]{:S(2)}, u32[]{:S(2)}) collective-permute-start(bf16[16,128,128]{2,1,0:T(8,128)(2,1)S(1)} %get-tuple-element.86.refs_3_), channel_id=1, source_target_pairs={{2,0},{4,2},{6,4},{7,6},{5,7},{3,5},{1,3},{0,1},{10,8},{12,10},{14... | collective-permute-start | bytes 1572872 | tf_op jit(solution)/shard_map/ppermute | solution.py:361
  116.9 15.5 %collective-permute-start.26 = (bf16[2,16,64,128]{3,2,1,0:T(8,128)(2,1)S(1)}, bf16[2,16,64,128]{3,2,1,0:T(8,128)(2,1)S(1)}, u32[]{:S(2)}, u32[]{:S(2)}) collective-permute-start(bf16[2,16,64,128]{3,2,1,0:T(8,128)(2,1)S(1)} %get-tuple-element.100), channel_id=1, source_target_pairs={{0,8},{8,0},{16,24},{24,16},{1,9},{9,1},{17,25},{25,17},{2,10},{10... | collective-permute-start | bytes 1572872 | tf_op jit(solution)/shard_map/ppermute | solution.py:378
  123.4 11.6 %collective-permute-start.23 = (bf16[2,16,64,128]{3,2,1,0:T(8,128)(2,1)S(1)}, bf16[2,16,64,128]{3,2,1,0:T(8,128)(2,1)S(1)}, u32[]{:S(2)}, u32[]{:S(2)}) collective-permute-start(bf16[2,16,64,128]{3,2,1,0:T(8,128)(2,1)S(1)} %get-tuple-element.94), channel_id=1, source_target_pairs={{0,16},{8,24},{16,0},{24,8},{1,17},{9,25},{17,1},{25,9},{2,18},{10... | collective-permute-start | bytes 1572872 | tf_op jit(solution)/shard_map/ppermute | solution.py:378
  131.0 13.7 %collective-permute-start.27 = (bf16[2,16,64,128]{3,2,1,0:T(8,128)(2,1)S(1)}, bf16[2,16,64,128]{3,2,1,0:T(8,128)(2,1)S(1)}, u32[]{:S(2)}, u32[]{:S(2)}) collective-permute-start(bf16[2,16,64,128]{3,2,1,0:T(8,128)(2,1)S(1)} %get-tuple-element.102), channel_id=1, source_target_pairs={{0,24},{8,16},{16,8},{24,0},{1,25},{9,17},{17,9},{25,1},{2,26},{10... | collective-permute-start | bytes 1572872 | tf_op jit(solution)/shard_map/ppermute | solution.py:378
  132.5 14.9 %collective-permute-start.28 = (bf16[16,128,128]{2,1,0:T(8,128)(2,1)S(1)}, bf16[16,128,128]{2,1,0:T(8,128)(2,1)S(1)}, u32[]{:S(2)}, u32[]{:S(2)}) collective-permute-start(bf16[16,128,128]{2,1,0:T(8,128)(2,1)S(1)} %collective-permute-done.21.refs_1_), channel_id=1, source_target_pairs={{0,2},{2,4},{4,6},{6,7},{7,5},{5,3},{3,1},{1,0},{8,10},{10,12},{12... | collective-permute-start | bytes 1572872 | tf_op jit(solution)/shard_map/ppermute | solution.py:360
  134.9 14.9 %collective-permute-start.29 = (bf16[16,128,128]{2,1,0:T(8,128)(2,1)S(1)}, bf16[16,128,128]{2,1,0:T(8,128)(2,1)S(1)}, u32[]{:S(2)}, u32[]{:S(2)}) collective-permute-start(bf16[16,128,128]{2,1,0:T(8,128)(2,1)S(1)} %collective-permute-done.22.refs_5_), channel_id=1, source_target_pairs={{2,0},{4,2},{6,4},{7,6},{5,7},{3,5},{1,3},{0,1},{10,8},{12,10},{14... | collective-permute-start | bytes 1572872 | tf_op jit(solution)/shard_map/ppermute | solution.py:361
  134.9 29.2 %collective-permute-start.24 = (bf16[16,128,128]{2,1,0:T(8,128)(2,1)S(1)}, bf16[16,128,128]{2,1,0:T(8,128)(2,1)S(1)}, u32[]{:S(2)}, u32[]{:S(2)}) collective-permute-start(bf16[16,128,128]{2,1,0:T(8,128)(2,1)S(1)} %collective-permute-done.19.refs_2_), channel_id=1, source_target_pairs={{0,2},{2,4},{4,6},{6,7},{7,5},{5,3},{3,1},{1,0},{8,10},{10,12},{12... | collective-permute-start | bytes 1572872 | tf_op jit(solution)/shard_map/ppermute | solution.py:360
  137.0 27.2 %collective-permute-start.25 = (bf16[16,128,128]{2,1,0:T(8,128)(2,1)S(1)}, bf16[16,128,128]{2,1,0:T(8,128)(2,1)S(1)}, u32[]{:S(2)}, u32[]{:S(2)}) collective-permute-start(bf16[16,128,128]{2,1,0:T(8,128)(2,1)S(1)} %collective-permute-done.20.refs_4_), channel_id=1, source_target_pairs={{2,0},{4,2},{6,4},{7,6},{5,7},{3,5},{1,3},{0,1},{10,8},{12,10},{14... | collective-permute-start | bytes 1572872 | tf_op jit(solution)/shard_map/ppermute | solution.py:361
  154.8 9.9 %collective-permute-start.30 = (bf16[2,16,64,128]{3,2,1,0:T(8,128)(2,1)S(1)}, bf16[2,16,64,128]{3,2,1,0:T(8,128)(2,1)S(1)}, u32[]{:S(2)}, u32[]{:S(2)}) collective-permute-start(bf16[2,16,64,128]{3,2,1,0:T(8,128)(2,1)S(1)} %get-tuple-element.109), channel_id=1, source_target_pairs={{0,8},{8,0},{16,24},{24,16},{1,9},{9,1},{17,25},{25,17},{2,10},{10... | collective-permute-start | bytes 1572872 | tf_op jit(solution)/shard_map/ppermute | solution.py:378
  163.6 12.3 %collective-permute-start.34 = (bf16[16,128,128]{2,1,0:T(8,128)(2,1)S(1)}, bf16[16,128,128]{2,1,0:T(8,128)(2,1)S(1)}, u32[]{:S(2)}, u32[]{:S(2)}) collective-permute-start(bf16[16,128,128]{2,1,0:T(8,128)(2,1)S(1)} %get-tuple-element.116.refs_3_), channel_id=1, source_target_pairs={{0,2},{2,4},{4,6},{6,7},{7,5},{5,3},{3,1},{1,0},{8,10},{10,12},{12... | collective-permute-start | bytes 1572872 | tf_op jit(solution)/shard_map/ppermute | solution.py:360
  163.6 14.6 %collective-permute-start.35 = (bf16[16,128,128]{2,1,0:T(8,128)(2,1)S(1)}, bf16[16,128,128]{2,1,0:T(8,128)(2,1)S(1)}, u32[]{:S(2)}, u32[]{:S(2)}) collective-permute-start(bf16[16,128,128]{2,1,0:T(8,128)(2,1)S(1)} %get-tuple-element.116.refs_3_), channel_id=1, source_target_pairs={{2,0},{4,2},{6,4},{7,6},{5,7},{3,5},{1,3},{0,1},{10,8},{12,10},{14... | collective-permute-start | bytes 1572872 | tf_op jit(solution)/shard_map/ppermute | solution.py:361
  164.1 17.2 %collective-permute-start.33 = (bf16[2,16,64,128]{3,2,1,0:T(8,128)(2,1)S(1)}, bf16[2,16,64,128]{3,2,1,0:T(8,128)(2,1)S(1)}, u32[]{:S(2)}, u32[]{:S(2)}) collective-permute-start(bf16[2,16,64,128]{3,2,1,0:T(8,128)(2,1)S(1)} %get-tuple-element.113), channel_id=1, source_target_pairs={{0,16},{8,24},{16,0},{24,8},{1,17},{9,25},{17,1},{25,9},{2,18},{10... | collective-permute-start | bytes 1572872 | tf_op jit(solution)/shard_map/ppermute | solution.py:378
  164.7 22.5 %collective-permute-start.31 = (bf16[16,128,128]{2,1,0:T(8,128)(2,1)S(1)}, bf16[16,128,128]{2,1,0:T(8,128)(2,1)S(1)}, u32[]{:S(2)}, u32[]{:S(2)}) collective-permute-start(bf16[16,128,128]{2,1,0:T(8,128)(2,1)S(1)} %collective-permute-done.24.refs_1_), channel_id=1, source_target_pairs={{0,2},{2,4},{4,6},{6,7},{7,5},{5,3},{3,1},{1,0},{8,10},{10,12},{12... | collective-permute-start | bytes 1572872 | tf_op jit(solution)/shard_map/ppermute | solution.py:360
  166.3 20.9 %collective-permute-start.32 = (bf16[16,128,128]{2,1,0:T(8,128)(2,1)S(1)}, bf16[16,128,128]{2,1,0:T(8,128)(2,1)S(1)}, u32[]{:S(2)}, u32[]{:S(2)}) collective-permute-start(bf16[16,128,128]{2,1,0:T(8,128)(2,1)S(1)} %collective-permute-done.25.refs_5_), channel_id=1, source_target_pairs={{2,0},{4,2},{6,4},{7,6},{5,7},{3,5},{1,3},{0,1},{10,8},{12,10},{14... | collective-permute-start | bytes 1572872 | tf_op jit(solution)/shard_map/ppermute | solution.py:361
  178.3 12.1 %collective-permute-start.36 = (bf16[2,16,64,128]{3,2,1,0:T(8,128)(2,1)S(1)}, bf16[2,16,64,128]{3,2,1,0:T(8,128)(2,1)S(1)}, u32[]{:S(2)}, u32[]{:S(2)}) collective-permute-start(bf16[2,16,64,128]{3,2,1,0:T(8,128)(2,1)S(1)} %get-tuple-element.117), channel_id=1, source_target_pairs={{0,24},{8,16},{16,8},{24,0},{1,25},{9,17},{17,9},{25,1},{2,26},{10... | collective-permute-start | bytes 1572872 | tf_op jit(solution)/shard_map/ppermute | solution.py:378
  181.3 16.9 %collective-permute-start.39 = (bf16[16,128,128]{2,1,0:T(8,128)(2,1)S(1)}, bf16[16,128,128]{2,1,0:T(8,128)(2,1)S(1)}, u32[]{:S(2)}, u32[]{:S(2)}) collective-permute-start(bf16[16,128,128]{2,1,0:T(8,128)(2,1)S(1)} %collective-permute-done.34.refs_2_), channel_id=1, source_target_pairs={{0,2},{2,4},{4,6},{6,7},{7,5},{5,3},{3,1},{1,0},{8,10},{10,12},{12... | collective-permute-start | bytes 1572872 | tf_op jit(solution)/shard_map/ppermute | solution.py:360
  183.0 15.2 %collective-permute-start.40 = (bf16[16,128,128]{2,1,0:T(8,128)(2,1)S(1)}, bf16[16,128,128]{2,1,0:T(8,128)(2,1)S(1)}, u32[]{:S(2)}, u32[]{:S(2)}) collective-permute-start(bf16[16,128,128]{2,1,0:T(8,128)(2,1)S(1)} %collective-permute-done.35.refs_4_), channel_id=1, source_target_pairs={{2,0},{4,2},{6,4},{7,6},{5,7},{3,5},{1,3},{0,1},{10,8},{12,10},{14... | collective-permute-start | bytes 1572872 | tf_op jit(solution)/shard_map/ppermute | solution.py:361
  194.6 14.9 %collective-permute-start.37 = (bf16[2,16,64,128]{3,2,1,0:T(8,128)(2,1)S(1)}, bf16[2,16,64,128]{3,2,1,0:T(8,128)(2,1)S(1)}, u32[]{:S(2)}, u32[]{:S(2)}) collective-permute-start(bf16[2,16,64,128]{3,2,1,0:T(8,128)(2,1)S(1)} %get-tuple-element.119), channel_id=1, source_target_pairs={{0,8},{8,0},{16,24},{24,16},{1,9},{9,1},{17,25},{25,17},{2,10},{10... | collective-permute-start | bytes 1572872 | tf_op jit(solution)/shard_map/ppermute | solution.py:378
  195.2 21.4 %collective-permute-start.38 = (bf16[2,16,64,128]{3,2,1,0:T(8,128)(2,1)S(1)}, bf16[2,16,64,128]{3,2,1,0:T(8,128)(2,1)S(1)}, u32[]{:S(2)}, u32[]{:S(2)}) collective-permute-start(bf16[2,16,64,128]{3,2,1,0:T(8,128)(2,1)S(1)} %get-tuple-element.120), channel_id=1, source_target_pairs={{0,16},{8,24},{16,0},{24,8},{1,17},{9,25},{17,1},{25,9},{2,18},{10... | collective-permute-start | bytes 1572872 | tf_op jit(solution)/shard_map/ppermute | solution.py:378
  198.2 18.4 %collective-permute-start.41 = (bf16[2,16,64,128]{3,2,1,0:T(8,128)(2,1)S(1)}, bf16[2,16,64,128]{3,2,1,0:T(8,128)(2,1)S(1)}, u32[]{:S(2)}, u32[]{:S(2)}) collective-permute-start(bf16[2,16,64,128]{3,2,1,0:T(8,128)(2,1)S(1)} %get-tuple-element.124), channel_id=1, source_target_pairs={{0,24},{8,16},{16,8},{24,0},{1,25},{9,17},{17,9},{25,1},{2,26},{10... | collective-permute-start | bytes 1572872 | tf_op jit(solution)/shard_map/ppermute | solution.py:378
  199.4 17.2 %collective-permute-start.42 = (bf16[16,128,128]{2,1,0:T(8,128)(2,1)S(1)}, bf16[16,128,128]{2,1,0:T(8,128)(2,1)S(1)}, u32[]{:S(2)}, u32[]{:S(2)}) collective-permute-start(bf16[16,128,128]{2,1,0:T(8,128)(2,1)S(1)} %collective-permute-done.39.refs_1_), channel_id=1, source_target_pairs={{0,2},{2,4},{4,6},{6,7},{7,5},{5,3},{3,1},{1,0},{8,10},{10,12},{12... | collective-permute-start | bytes 1572872 | tf_op jit(solution)/shard_map/ppermute | solution.py:360
  201.9 14.7 %collective-permute-start.43 = (bf16[16,128,128]{2,1,0:T(8,128)(2,1)S(1)}, bf16[16,128,128]{2,1,0:T(8,128)(2,1)S(1)}, u32[]{:S(2)}, u32[]{:S(2)}) collective-permute-start(bf16[16,128,128]{2,1,0:T(8,128)(2,1)S(1)} %collective-permute-done.40.refs_5_), channel_id=1, source_target_pairs={{2,0},{4,2},{6,4},{7,6},{5,7},{3,5},{1,3},{0,1},{10,8},{12,10},{14... | collective-permute-start | bytes 1572872 | tf_op jit(solution)/shard_map/ppermute | solution.py:361
  222.6 14.9 %collective-permute-start.46 = (bf16[2,16,64,128]{3,2,1,0:T(8,128)(2,1)S(1)}, bf16[2,16,64,128]{3,2,1,0:T(8,128)(2,1)S(1)}, u32[]{:S(2)}, u32[]{:S(2)}) collective-permute-start(bf16[2,16,64,128]{3,2,1,0:T(8,128)(2,1)S(1)} %get-tuple-element.137), channel_id=1, source_target_pairs={{0,8},{8,0},{16,24},{24,16},{1,9},{9,1},{17,25},{25,17},{2,10},{10... | collective-permute-start | bytes 1572872 | tf_op jit(solution)/shard_map/ppermute | solution.py:378
  224.3 19.7 %collective-permute-start.47 = (bf16[2,16,64,128]{3,2,1,0:T(8,128)(2,1)}, bf16[2,16,64,128]{3,2,1,0:T(8,128)(2,1)S(1)}, u32[]{:S(2)}, u32[]{:S(2)}) collective-permute-start(bf16[2,16,64,128]{3,2,1,0:T(8,128)(2,1)} %get-tuple-element.138), channel_id=1, source_target_pairs={{0,16},{8,24},{16,0},{24,8},{1,17},{9,25},{17,1},{25,9},{2,18},{10... | collective-permute-start | bytes 1572872 | tf_op jit(solution)/shard_map/ppermute | solution.py:378
  224.6 19.4 %collective-permute-start.48 = (bf16[2,16,64,128]{3,2,1,0:T(8,128)(2,1)S(1)}, bf16[2,16,64,128]{3,2,1,0:T(8,128)(2,1)S(1)}, u32[]{:S(2)}, u32[]{:S(2)}) collective-permute-start(bf16[2,16,64,128]{3,2,1,0:T(8,128)(2,1)S(1)} %get-tuple-element.139), channel_id=1, source_target_pairs={{0,24},{8,16},{16,8},{24,0},{1,25},{9,17},{17,9},{25,1},{2,26},{10... | collective-permute-start | bytes 1572872 | tf_op jit(solution)/shard_map/ppermute | solution.py:378
  228.0 18.4 %collective-permute-start.44 = (bf16[16,64,512]{2,1,0:T(8,128)(2,1)S(1)}, bf16[16,64,512]{2,1,0:T(8,128)(2,1)S(1)}, u32[]{:S(2)}, u32[]{:S(2)}) collective-permute-start(bf16[16,64,512]{2,1,0:T(8,128)(2,1)S(1)} %get-tuple-element.130), channel_id=1, source_target_pairs={{0,1},{1,0},{2,3},{3,2},{4,5},{5,4},{6,7},{7,6},{8,9},{9,8},{10,11... | collective-permute-start | bytes 3145736 | tf_op jit(solution)/shard_map/ppermute | solution.py:387
  228.1 18.3 %collective-permute-start.45 = (bf16[16,64,512]{2,1,0:T(8,128)(2,1)S(1)}, bf16[16,64,512]{2,1,0:T(8,128)(2,1)S(1)}, u32[]{:S(2)}, u32[]{:S(2)}) collective-permute-start(bf16[16,64,512]{2,1,0:T(8,128)(2,1)S(1)} %get-tuple-element.134), channel_id=1, source_target_pairs={{0,1},{1,0},{2,3},{3,2},{4,5},{5,4},{6,7},{7,6},{8,9},{9,8},{10,11... | collective-permute-start | bytes 3145736 | tf_op jit(solution)/shard_map/ppermute | solution.py:387
  (31 other events, 609.0 us)

commit v9 on v8

--- a/solution.py
+++ b/solution.py
@@ -408,7 +408,7 @@
                 gates[index + 2].append(tiles[p][0])
         for p in range(count - 1):
             if index == last[p] + 1:
-                project(p, *before, *(moved[p - 1][1:] if p else []))
+                project(p, *before, *(moved[p - 1][1:3] if p else []))
                 gates[min(index + 2, len(order) - 1)].append(moved[p][0])
             for d in range(1, parts):
                 if index == last[p] + d and p < count - 2:

time: 256 us -> 258 us (level)
  waiting for transfers between devices: 129 us -> 132 us
  local copies, waits for them, and re-layouts: 15 us -> 17.6 us
    ppermute x12, waiting for transfers between devices: 47.2 us -> 55.5 us  [shift(): here[-s] = lax.ppermute(after(here[-(s - 1)], *others), 'col', onward)]
    ppermute x12, waiting for transfers between devices: 39.2 us -> 32.9 us  [send(): lax.ppermute(piece, 'row', [(a, a ^ d) for a in range(parts)])]
    unnamed x59 -> x61, local copies, waits for them, and re-layouts: 9.37 us -> 11.9 us
  transfers between devices with their start and end apart: 51 -> 51, of which waited for: 26 -> 26; matrix products, arithmetic and copies ran while one was open for 4% -> 4% of each run, Pallas kernels for 17% -> 16%
where the time goes in v9:
time: 258 us; the launch traced here: 257 us
  waiting for transfers between devices  132 us (51%)
  Pallas kernels  56 us (22%)
  starting transfers between devices  48.7 us (19%)
  local copies, waits for them, and re-layouts  17.6 us (7%)
    ppermute x12, waiting for transfers between devices, shift(): here[-s] = lax.ppermute(after(here[-(s - 1)], *others), 'col', onward)  55.5 us
    ppermute x12, waiting for transfers between devices, send(): lax.ppermute(piece, 'row', [(a, a ^ d) for a in range(parts)])  32.9 us
    pallas_call x4, Pallas kernels, update_call(): pl.pallas_call(functools.partial(update_kernel, parts, part, cols, plan),...  28.8 us
    ppermute x12, starting transfers between devices, shift(): here[-s] = lax.ppermute(after(here[-(s - 1)], *others), 'col', onward)  19.6 us
    pallas_call x4, Pallas kernels, project_call(): pl.pallas_call(functools.partial(project_kernel, line, parts), in_specs=[...  16.6 us
    ppermute x3, waiting for transfers between devices, shards(): held[-s] = lax.ppermute(ahead, 'col', onward)  16.3 us
    ppermute x12, starting transfers between devices, send(): lax.ppermute(piece, 'row', [(a, a ^ d) for a in range(parts)])  14.4 us
    ppermute x12, waiting for transfers between devices, shift(): here[s] = lax.ppermute(after(here[s - 1], *others), 'col', back)  12.5 us
  transfers between devices with their start and end apart: 51, of which 26 were waited for; matrix products, arithmetic and copies ran while one was open for 4% of the time, Pallas kernels for 16%

profile of v9, /device:TPU:0, one launch (start us, length us, event | category | flops | bytes accessed | tf_op | source)
XLA Modules:
  0.0 256.8 jit_solution(13182199202971597805)
XLA Ops:
  0.6 3.0 %collective-permute-start = (bf16[16,16384]{1,0:T(8,128)(2,1)}, bf16[16,16384]{1,0:T(8,128)(2,1)S(1)}, u32[]{:S(2)}, u32[]{:S(2)}) collective-permute-start(bf16[16,16384]{1,0:T(8,128)(2,1)} %refs_3_.7), channel_id=1, source_target_pairs={{0,2},{2,4},{4,6},{6,7},{7,5},{5,3},{3,1},{1,0},{8,10},{10,12},{12... | collective-permute-start | bytes 1572872 | tf_op jit(solution)/shard_map/ppermute | solution.py:305
  7.2 8.0 %collective-permute-done.refs_2_ = bf16[16,16384]{1,0:T(8,128)(2,1)S(1)} collective-permute-done((bf16[16,16384]{1,0:T(8,128)(2,1)}, bf16[16,16384]{1,0:T(8,128)(2,1)S(1)}, u32[]{:S(2)}, u32[]{:S(2)}) %collective-permute-start) | collective-permute-done | bytes 524320 | tf_op jit(solution)/shard_map/ppermute | solution.py:305
  15.2 2.4 collective-permute-start.1
  18.7 11.2 %collective-permute-done.5.refs_11_ = bf16[128,2048]{1,0:T(8,128)(2,1)S(1)} collective-permute-done((bf16[128,2048]{1,0:T(8,128)(2,1)}, bf16[128,2048]{1,0:T(8,128)(2,1)S(1)}, u32[]{:S(2)}, u32[]{:S(2)}) %collective-permute-start.5) | collective-permute-done | bytes 524320 | tf_op jit(solution)/shard_map/ppermute | solution.py:293
  34.0 8.3 %collective-permute-done.7.refs_0_ = bf16[16,16384]{1,0:T(8,128)(2,1)S(1)} collective-permute-done((bf16[16,16384]{1,0:T(8,128)(2,1)S(1)}, bf16[16,16384]{1,0:T(8,128)(2,1)S(1)}, u32[]{:S(2)}, u32[]{:S(2)}) %collective-permute-start.7) | collective-permute-done | bytes 524320 | tf_op jit(solution)/shard_map/ppermute | solution.py:305
  43.0 2.5 collective-permute-start.9
  54.4 7.1 %update.4 = (bf16[128,64,128]{2,1,0:T(8,128)(2,1)}, bf16[16,128,128]{2,1,0:T(8,128)(2,1)S(1)}) custom-call(s32[3]{0:T(128)S(1)} %pad_add_fusion.where_ref, bf16[16,16384]{1,0:T(8,128)(2,1)S(1)} %collective-permute-done.7.refs_0_, bf16[16,16384]{1,0:T(8,128)(2,1)S(1)} %collective-permute-done.1.refs_1_, bf16[16,16384]{1,0:T(8,128)(2,1)S(1)} %collective-permute-done.refs_2_, ...), custom_call_target="tpu_custom_call" | custom-call | flops 2684354560 | bytes 8388608 | tf_op jit(solution)/shard_map/update/pallas_call | solution.py:121
  61.6 2.0 collective-permute-start.11
  63.6 10.1 %collective-permute-done.11.refs_2_ = bf16[16,128,128]{2,1,0:T(8,128)(2,1)S(1)} collective-permute-done((bf16[16,128,128]{2,1,0:T(8,128)(2,1)S(1)}, bf16[16,128,128]{2,1,0:T(8,128)(2,1)S(1)}, u32[]{:S(2)}, u32[]{:S(2)}) %collective-permute-start.11) | collective-permute-done | bytes 524320 | tf_op jit(solution)/shard_map/ppermute | solution.py:360
  73.7 2.5 collective-permute-start.15
  76.2 7.3 %update.5 = (bf16[128,64,128]{2,1,0:T(8,128)(2,1)}, bf16[16,128,128]{2,1,0:T(8,128)(2,1)S(1)}) custom-call(s32[3]{0:T(128)S(1)} %pad_add_fusion.where_ref, bf16[16,16384]{1,0:T(8,128)(2,1)S(1)} %collective-permute-done.7.refs_0_, bf16[16,16384]{1,0:T(8,128)(2,1)S(1)} %collective-permute-done.1.refs_1_, ...), custom_call_target="tpu_custom_call", output_to_operand_aliasing={{0}: (18, {})} | custom-call | flops 2684354560 | bytes 8388608 | tf_op jit(solution)/shard_map/update/pallas_call | solution.py:121
  83.6 1.8 collective-permute-start.13
  85.4 1.7 collective-permute-done.15.refs_1_
  87.1 2.6 %collective-permute-start.17 = (bf16[16,128,128]{2,1,0:T(8,128)(2,1)}, bf16[16,128,128]{2,1,0:T(8,128)(2,1)}, u32[]{:S(2)}, u32[]{:S(2)}) collective-permute-start(bf16[16,128,128]{2,1,0:T(8,128)(2,1)} %collective-permute-done.15.refs_1_), channel_id=1, source_target_pairs={{0,2},{2,4},{4,6},{6,7},{7,5},{5,3},{3,1},{1,0},{8,10},{10,12},{12... | collective-permute-start | bytes 1572872 | tf_op jit(solution)/shard_map/ppermute | solution.py:360
  89.7 8.6 %collective-permute-done.13.refs_2_ = bf16[16,128,128]{2,1,0:T(8,128)(2,1)} collective-permute-done((bf16[16,128,128]{2,1,0:T(8,128)(2,1)S(1)}, bf16[16,128,128]{2,1,0:T(8,128)(2,1)}, u32[]{:S(2)}, u32[]{:S(2)}) %collective-permute-start.13) | collective-permute-done | bytes 524320 | tf_op jit(solution)/shard_map/ppermute | solution.py:360
  98.4 2.0 collective-permute-done.14.refs_4_
  101.2 8.5 %collective-permute-done.17.refs_0_ = bf16[16,128,128]{2,1,0:T(8,128)(2,1)} collective-permute-done((bf16[16,128,128]{2,1,0:T(8,128)(2,1)}, bf16[16,128,128]{2,1,0:T(8,128)(2,1)}, u32[]{:S(2)}, u32[]{:S(2)}) %collective-permute-start.17) | collective-permute-done | bytes 524320 | tf_op jit(solution)/shard_map/ppermute | solution.py:360
  109.7 1.9 collective-permute-done.18.refs_6_
  113.4 4.3 %project.4 = (bf16[2,16,64,128]{3,2,1,0:T(8,128)(2,1)S(1)}, bf16[2,16,64,128]{3,2,1,0:T(8,128)(2,1)S(1)}, bf16[2,16,64,128]{3,2,1,0:T(8,128)(2,1)S(1)}, bf16[2,16,64,128]{3,2,1,0:T(8,128)(2,1)S(1)}) custom-call(s32[3]{0:T(128)S(1)} %pad_add_fusion.where_ref, bf16[128,128]{1,0:T(8,128)(2,1)S(1)} %copy-done.8, f32[128,1]{1,0:T(8,128)S(1)} %copy.43.offset_ref, ...), custom_call_target="tpu_custom_call" | custom-call | flops 268435456 | bytes 4194304 | tf_op jit(solution)/shard_map/project/pallas_call | solution.py:182
  120.7 7.2 %update.6 = (bf16[128,64,128]{2,1,0:T(8,128)(2,1)}, bf16[16,128,128]{2,1,0:T(8,128)(2,1)S(1)}) custom-call(s32[3]{0:T(128)S(1)} %pad_add_fusion.where_ref, bf16[16,16384]{1,0:T(8,128)(2,1)S(1)} %collective-permute-done.7.refs_0_, bf16[16,16384]{1,0:T(8,128)(2,1)S(1)} %collective-permute-done.1.refs_1_, ...), custom_call_target="tpu_custom_call", output_to_operand_aliasing={{0}: (18, {})} | custom-call | flops 2684354560 | bytes 8388608 | tf_op jit(solution)/shard_map/update/pallas_call | solution.py:121
  129.2 1.9 collective-permute-start.28
  131.1 9.6 %collective-permute-done.19.refs_2_ = bf16[16,128,128]{2,1,0:T(8,128)(2,1)S(1)} collective-permute-done((bf16[16,128,128]{2,1,0:T(8,128)(2,1)S(1)}, bf16[16,128,128]{2,1,0:T(8,128)(2,1)S(1)}, u32[]{:S(2)}, u32[]{:S(2)}) %collective-permute-start.19) | collective-permute-done | bytes 524320 | tf_op jit(solution)/shard_map/ppermute | solution.py:360
  140.7 2.3 collective-permute-done.20.refs_4_
  145.3 6.7 %collective-permute-done.28.refs_0_ = bf16[16,128,128]{2,1,0:T(8,128)(2,1)S(1)} collective-permute-done((bf16[16,128,128]{2,1,0:T(8,128)(2,1)}, bf16[16,128,128]{2,1,0:T(8,128)(2,1)S(1)}, u32[]{:S(2)}, u32[]{:S(2)}) %collective-permute-start.28) | collective-permute-done | bytes 524320 | tf_op jit(solution)/shard_map/ppermute | solution.py:360
  154.1 4.1 %project.5 = (bf16[2,16,64,128]{3,2,1,0:T(8,128)(2,1)S(1)}, bf16[2,16,64,128]{3,2,1,0:T(8,128)(2,1)S(1)}, bf16[2,16,64,128]{3,2,1,0:T(8,128)(2,1)S(1)}, bf16[2,16,64,128]{3,2,1,0:T(8,128)(2,1)S(1)}) custom-call(s32[3]{0:T(128)S(1)} %pad_add_fusion.where_ref, bf16[128,128]{1,0:T(8,128)(2,1)S(1)} %copy-done.9, f32[128,1]{1,0:T(8,128)S(1)} %copy.43.offset_ref, ...), custom_call_target="tpu_custom_call" | custom-call | flops 268435456 | bytes 4194304 | tf_op jit(solution)/shard_map/project/pallas_call | solution.py:182
  158.7 7.2 %update.7 = (bf16[128,64,128]{2,1,0:T(8,128)(2,1)}, bf16[16,128,128]{2,1,0:T(8,128)(2,1)S(1)}) custom-call(s32[3]{0:T(128)S(1)} %pad_add_fusion.where_ref, bf16[16,16384]{1,0:T(8,128)(2,1)S(1)} %collective-permute-done.7.refs_0_, bf16[16,16384]{1,0:T(8,128)(2,1)S(1)} %collective-permute-done.1.refs_1_, ...), custom_call_target="tpu_custom_call", output_to_operand_aliasing={{0}: (18, {})} | custom-call | flops 2684354560 | bytes 8388608 | tf_op jit(solution)/shard_map/update/pallas_call | solution.py:121
  166.0 1.7 collective-permute-start.33
  167.7 1.7 collective-permute-start.36
  169.5 2.4 collective-permute-start.31
  171.9 1.8 place.4
  173.8 4.0 %collective-permute-done.33.refs_2_ = bf16[2,16,64,128]{3,2,1,0:T(8,128)(2,1)S(1)} collective-permute-done((bf16[2,16,64,128]{3,2,1,0:T(8,128)(2,1)S(1)}, bf16[2,16,64,128]{3,2,1,0:T(8,128)(2,1)S(1)}, u32[]{:S(2)}, u32[]{:S(2)}) %collective-permute-start.33) | collective-permute-done | bytes 524320 | tf_op jit(solution)/shard_map/ppermute | solution.py:378
  177.7 4.0 %collective-permute-done.36.refs_2_ = bf16[16,128,128]{2,1,0:T(8,128)(2,1)S(1)} collective-permute-done((bf16[16,128,128]{2,1,0:T(8,128)(2,1)S(1)}, bf16[16,128,128]{2,1,0:T(8,128)(2,1)S(1)}, u32[]{:S(2)}, u32[]{:S(2)}) %collective-permute-start.36) | collective-permute-done | bytes 524320 | tf_op jit(solution)/shard_map/ppermute | solution.py:360
  181.8 2.5 collective-permute-done.37.refs_4_
  184.8 2.1 collective-permute-start.41
  186.8 6.2 %collective-permute-done.31.refs_0_ = bf16[16,128,128]{2,1,0:T(8,128)(2,1)S(1)} collective-permute-done((bf16[16,128,128]{2,1,0:T(8,128)(2,1)S(1)}, bf16[16,128,128]{2,1,0:T(8,128)(2,1)S(1)}, u32[]{:S(2)}, u32[]{:S(2)}) %collective-permute-start.31) | collective-permute-done | bytes 524320 | tf_op jit(solution)/shard_map/ppermute | solution.py:360
  193.0 2.5 collective-permute-done.32.refs_6_
  196.3 4.1 %project.6 = (bf16[2,16,64,128]{3,2,1,0:T(8,128)(2,1)S(1)}, bf16[2,16,64,128]{3,2,1,0:T(8,128)(2,1)S(1)}, bf16[2,16,64,128]{3,2,1,0:T(8,128)(2,1)S(1)}, bf16[2,16,64,128]{3,2,1,0:T(8,128)(2,1)S(1)}) custom-call(s32[3]{0:T(128)S(1)} %pad_add_fusion.where_ref, bf16[128,128]{1,0:T(8,128)(2,1)S(1)} %copy-done.9, f32[128,1]{1,0:T(8,128)S(1)} %copy.43.offset_ref, ...), custom_call_target="tpu_custom_call" | custom-call | flops 268435456 | bytes 4194304 | tf_op jit(solution)/shard_map/project/pallas_call | solution.py:182
  204.0 2.1 collective-permute-start.42
  206.2 9.2 %collective-permute-done.34.refs_1_ = bf16[2,16,64,128]{3,2,1,0:T(8,128)(2,1)S(1)} collective-permute-done((bf16[2,16,64,128]{3,2,1,0:T(8,128)(2,1)S(1)}, bf16[2,16,64,128]{3,2,1,0:T(8,128)(2,1)S(1)}, u32[]{:S(2)}, u32[]{:S(2)}) %collective-permute-start.34) | collective-permute-done | bytes 524320 | tf_op jit(solution)/shard_map/ppermute | solution.py:378
  215.3 6.9 %collective-permute-done.35.refs_2_ = bf16[2,16,64,128]{3,2,1,0:T(8,128)(2,1)S(1)} collective-permute-done((bf16[2,16,64,128]{3,2,1,0:T(8,128)(2,1)S(1)}, bf16[2,16,64,128]{3,2,1,0:T(8,128)(2,1)S(1)}, u32[]{:S(2)}, u32[]{:S(2)}) %collective-permute-start.35) | collective-permute-done | bytes 524320 | tf_op jit(solution)/shard_map/ppermute | solution.py:378
  223.1 4.1 %project.7 = (bf16[2,16,64,128]{3,2,1,0:T(8,128)(2,1)S(1)}, bf16[2,16,64,128]{3,2,1,0:T(8,128)(2,1)S(1)}, bf16[2,16,64,128]{3,2,1,0:T(8,128)(2,1)S(1)}, bf16[2,16,64,128]{3,2,1,0:T(8,128)(2,1)S(1)}) custom-call(s32[3]{0:T(128)S(1)} %pad_add_fusion.where_ref, bf16[128,128]{1,0:T(8,128)(2,1)S(1)} %copy-done.9, f32[128,1]{1,0:T(8,128)S(1)} %copy.43.offset_ref, ...), custom_call_target="tpu_custom_call" | custom-call | flops 268435456 | bytes 4194304 | tf_op jit(solution)/shard_map/project/pallas_call | solution.py:182
  230.7 1.8 place.5
  233.2 1.8 place.6
  235.0 5.7 %collective-permute-done.46.refs_1_ = bf16[2,16,64,128]{3,2,1,0:T(8,128)(2,1)S(1)} collective-permute-done((bf16[2,16,64,128]{3,2,1,0:T(8,128)(2,1)S(1)}, bf16[2,16,64,128]{3,2,1,0:T(8,128)(2,1)S(1)}, u32[]{:S(2)}, u32[]{:S(2)}) %collective-permute-start.46) | collective-permute-done | bytes 524320 | tf_op jit(solution)/shard_map/ppermute | solution.py:378
  240.7 7.0 %collective-permute-done.47.refs_2_ = bf16[2,16,64,128]{3,2,1,0:T(8,128)(2,1)S(1)} collective-permute-done((bf16[2,16,64,128]{3,2,1,0:T(8,128)(2,1)S(1)}, bf16[2,16,64,128]{3,2,1,0:T(8,128)(2,1)S(1)}, u32[]{:S(2)}, u32[]{:S(2)}) %collective-permute-start.47) | collective-permute-done | bytes 524320 | tf_op jit(solution)/shard_map/ppermute | solution.py:378
  247.7 1.8 place.7
  250.4 2.0 collective-permute-done.50.refs_3_
  253.4 3.3 %put.1 = bf16[128,64,512]{2,1,0:T(8,128)(2,1)} custom-call(s32[3]{0:T(128)S(1)} %pad_add_fusion.where_ref, bf16[16,64,512]{2,1,0:T(8,128)(2,1)S(1)} %collective-permute-done.44.refs_0_, bf16[16,64,512]{2,1,0:T(8,128)(2,1)S(1)} %collective-permute-done.45.refs_1_, ...), custom_call_target="tpu_custom_call", output_to_operand_aliasing={{}: (5, {})} | custom-call | bytes 8388608 | tf_op jit(solution)/shard_map/put/pallas_call | solution.py:261
  (141 shorter events, 41.9 us)
Async XLA Ops:
  0.6 14.6 %collective-permute-start = (bf16[16,16384]{1,0:T(8,128)(2,1)}, bf16[16,16384]{1,0:T(8,128)(2,1)S(1)}, u32[]{:S(2)}, u32[]{:S(2)}) collective-permute-start(bf16[16,16384]{1,0:T(8,128)(2,1)} %refs_3_.7), channel_id=1, source_target_pairs={{0,2},{2,4},{4,6},{6,7},{7,5},{5,3},{3,1},{1,0},{8,10},{10,12},{12... | collective-permute-start | bytes 1572872 | tf_op jit(solution)/shard_map/ppermute | solution.py:305
  3.7 13.9 %collective-permute-start.2 = (bf16[16,16384]{1,0:T(8,128)(2,1)}, bf16[16,16384]{1,0:T(8,128)(2,1)S(1)}, u32[]{:S(2)}, u32[]{:S(2)}) collective-permute-start(bf16[16,16384]{1,0:T(8,128)(2,1)} %refs_3_.7), channel_id=1, source_target_pairs={{2,0},{4,2},{6,4},{7,6},{5,7},{3,5},{1,3},{0,1},{10,8},{12,10},{14... | collective-permute-start | bytes 1572872 | tf_op jit(solution)/shard_map/ppermute | solution.py:306
  3.7 15.1 %collective-permute-start.4 = (bf16[128,2048]{1,0:T(8,128)(2,1)}, bf16[128,2048]{1,0:T(8,128)(2,1)S(1)}, u32[]{:S(2)}, u32[]{:S(2)}) collective-permute-start(bf16[128,2048]{1,0:T(8,128)(2,1)} %refs_9_.7), channel_id=1, source_target_pairs={{0,8},{8,0},{16,24},{24,16},{1,9},{9,1},{17,25},{25,17},{2,10},{10... | collective-permute-start | bytes 1572872 | tf_op jit(solution)/shard_map/ppermute | solution.py:293
  5.2 24.7 %collective-permute-start.5 = (bf16[128,2048]{1,0:T(8,128)(2,1)}, bf16[128,2048]{1,0:T(8,128)(2,1)S(1)}, u32[]{:S(2)}, u32[]{:S(2)}) collective-permute-start(bf16[128,2048]{1,0:T(8,128)(2,1)} %refs_9_.7), channel_id=1, source_target_pairs={{0,16},{8,24},{16,0},{24,8},{1,17},{9,25},{17,1},{25,9},{2,18},{10... | collective-permute-start | bytes 1572872 | tf_op jit(solution)/shard_map/ppermute | solution.py:293
  6.7 23.2 %collective-permute-start.6 = (bf16[128,2048]{1,0:T(8,128)(2,1)}, bf16[128,2048]{1,0:T(8,128)(2,1)S(1)}, u32[]{:S(2)}, u32[]{:S(2)}) collective-permute-start(bf16[128,2048]{1,0:T(8,128)(2,1)} %refs_9_.7), channel_id=1, source_target_pairs={{0,24},{8,16},{16,8},{24,0},{1,25},{9,17},{17,9},{25,1},{2,26},{10... | collective-permute-start | bytes 1572872 | tf_op jit(solution)/shard_map/ppermute | solution.py:293
  15.2 14.7 %collective-permute-start.1 = (bf16[16,16384]{1,0:T(8,128)(2,1)S(1)}, bf16[16,16384]{1,0:T(8,128)(2,1)S(1)}, u32[]{:S(2)}, u32[]{:S(2)}) collective-permute-start(bf16[16,16384]{1,0:T(8,128)(2,1)S(1)} %collective-permute-done.refs_2_), channel_id=1, source_target_pairs={{0,2},{2,4},{4,6},{6,7},{7,5},{5,3},{3,1},{1,0},{8,10},{10,12},{12... | collective-permute-start | bytes 1572872 | tf_op jit(solution)/shard_map/ppermute | solution.py:305
  17.6 12.3 %collective-permute-start.3 = (bf16[16,16384]{1,0:T(8,128)(2,1)S(1)}, bf16[16,16384]{1,0:T(8,128)(2,1)}, u32[]{:S(2)}, u32[]{:S(2)}) collective-permute-start(bf16[16,16384]{1,0:T(8,128)(2,1)S(1)} %collective-permute-done.2.refs_4_), channel_id=1, source_target_pairs={{2,0},{4,2},{6,4},{7,6},{5,7},{3,5},{1,3},{0,1},{10,8},{12,10},{14... | collective-permute-start | bytes 1572872 | tf_op jit(solution)/shard_map/ppermute | solution.py:306
  29.9 12.4 %collective-permute-start.7 = (bf16[16,16384]{1,0:T(8,128)(2,1)S(1)}, bf16[16,16384]{1,0:T(8,128)(2,1)S(1)}, u32[]{:S(2)}, u32[]{:S(2)}) collective-permute-start(bf16[16,16384]{1,0:T(8,128)(2,1)S(1)} %collective-permute-done.1.refs_1_), channel_id=1, source_target_pairs={{0,2},{2,4},{4,6},{6,7},{7,5},{5,3},{3,1},{1,0},{8,10},{10,12},{12... | collective-permute-start | bytes 1572872 | tf_op jit(solution)/shard_map/ppermute | solution.py:305
  31.5 14.0 %collective-permute-start.8 = (bf16[16,16384]{1,0:T(8,128)(2,1)}, bf16[16,16384]{1,0:T(8,128)(2,1)S(1)}, u32[]{:S(2)}, u32[]{:S(2)}) collective-permute-start(bf16[16,16384]{1,0:T(8,128)(2,1)} %collective-permute-done.3.refs_5_), channel_id=1, source_target_pairs={{2,0},{4,2},{6,4},{7,6},{5,7},{3,5},{1,3},{0,1},{10,8},{12,10},{14... | collective-permute-start | bytes 1572872 | tf_op jit(solution)/shard_map/ppermute | solution.py:306
  43.0 10.3 %collective-permute-start.9 = (bf16[16,8192]{1,0:T(8,128)(2,1)}, bf16[16,8192]{1,0:T(8,128)(2,1)S(1)}, u32[]{:S(2)}, u32[]{:S(2)}) collective-permute-start(bf16[16,8192]{1,0:T(8,128)(2,1)} %slice.8), channel_id=1, source_target_pairs={{0,2},{2,4},{4,6},{6,7},{7,5},{5,3},{3,1},{1,0},{8,10},{10,12},{12... | collective-permute-start | bytes 786440 | tf_op jit(solution)/shard_map/ppermute | solution.py:310
  61.6 12.2 %collective-permute-start.11 = (bf16[16,128,128]{2,1,0:T(8,128)(2,1)S(1)}, bf16[16,128,128]{2,1,0:T(8,128)(2,1)S(1)}, u32[]{:S(2)}, u32[]{:S(2)}) collective-permute-start(bf16[16,128,128]{2,1,0:T(8,128)(2,1)S(1)} %get-tuple-element.79.refs_3_), channel_id=1, source_target_pairs={{0,2},{2,4},{4,6},{6,7},{7,5},{5,3},{3,1},{1,0},{8,10},{10,12},{12... | collective-permute-start | bytes 1572872 | tf_op jit(solution)/shard_map/ppermute | solution.py:360
  63.6 12.6 %collective-permute-start.12 = (bf16[16,128,128]{2,1,0:T(8,128)(2,1)S(1)}, bf16[16,128,128]{2,1,0:T(8,128)(2,1)S(1)}, u32[]{:S(2)}, u32[]{:S(2)}) collective-permute-start(bf16[16,128,128]{2,1,0:T(8,128)(2,1)S(1)} %get-tuple-element.79.refs_3_), channel_id=1, source_target_pairs={{2,0},{4,2},{6,4},{7,6},{5,7},{3,5},{1,3},{0,1},{10,8},{12,10},{14... | collective-permute-start | bytes 1572872 | tf_op jit(solution)/shard_map/ppermute | solution.py:361
  73.7 13.4 %collective-permute-start.15 = (bf16[16,128,128]{2,1,0:T(8,128)(2,1)S(1)}, bf16[16,128,128]{2,1,0:T(8,128)(2,1)}, u32[]{:S(2)}, u32[]{:S(2)}) collective-permute-start(bf16[16,128,128]{2,1,0:T(8,128)(2,1)S(1)} %collective-permute-done.11.refs_2_), channel_id=1, source_target_pairs={{0,2},{2,4},{4,6},{6,7},{7,5},{5,3},{3,1},{1,0},{8,10},{10,12},{12... | collective-permute-start | bytes 1572872 | tf_op jit(solution)/shard_map/ppermute | solution.py:360
  76.2 10.9 %collective-permute-start.16 = (bf16[16,128,128]{2,1,0:T(8,128)(2,1)S(1)}, bf16[16,128,128]{2,1,0:T(8,128)(2,1)}, u32[]{:S(2)}, u32[]{:S(2)}) collective-permute-start(bf16[16,128,128]{2,1,0:T(8,128)(2,1)S(1)} %collective-permute-done.12.refs_4_), channel_id=1, source_target_pairs={{2,0},{4,2},{6,4},{7,6},{5,7},{3,5},{1,3},{0,1},{10,8},{12,10},{14... | collective-permute-start | bytes 1572872 | tf_op jit(solution)/shard_map/ppermute | solution.py:361
  83.6 14.8 %collective-permute-start.13 = (bf16[16,128,128]{2,1,0:T(8,128)(2,1)S(1)}, bf16[16,128,128]{2,1,0:T(8,128)(2,1)}, u32[]{:S(2)}, u32[]{:S(2)}) collective-permute-start(bf16[16,128,128]{2,1,0:T(8,128)(2,1)S(1)} %get-tuple-element.80.refs_3_), channel_id=1, source_target_pairs={{0,2},{2,4},{4,6},{6,7},{7,5},{5,3},{3,1},{1,0},{8,10},{10,12},{12... | collective-permute-start | bytes 1572872 | tf_op jit(solution)/shard_map/ppermute | solution.py:360
  85.4 15.0 %collective-permute-start.14 = (bf16[16,128,128]{2,1,0:T(8,128)(2,1)S(1)}, bf16[16,128,128]{2,1,0:T(8,128)(2,1)}, u32[]{:S(2)}, u32[]{:S(2)}) collective-permute-start(bf16[16,128,128]{2,1,0:T(8,128)(2,1)S(1)} %get-tuple-element.80.refs_3_), channel_id=1, source_target_pairs={{2,0},{4,2},{6,4},{7,6},{5,7},{3,5},{1,3},{0,1},{10,8},{12,10},{14... | collective-permute-start | bytes 1572872 | tf_op jit(solution)/shard_map/ppermute | solution.py:361
  87.1 22.6 %collective-permute-start.17 = (bf16[16,128,128]{2,1,0:T(8,128)(2,1)}, bf16[16,128,128]{2,1,0:T(8,128)(2,1)}, u32[]{:S(2)}, u32[]{:S(2)}) collective-permute-start(bf16[16,128,128]{2,1,0:T(8,128)(2,1)} %collective-permute-done.15.refs_1_), channel_id=1, source_target_pairs={{0,2},{2,4},{4,6},{6,7},{7,5},{5,3},{3,1},{1,0},{8,10},{10,12},{12... | collective-permute-start | bytes 1572872 | tf_op jit(solution)/shard_map/ppermute | solution.py:360
  89.7 21.9 %collective-permute-start.18 = (bf16[16,128,128]{2,1,0:T(8,128)(2,1)}, bf16[16,128,128]{2,1,0:T(8,128)(2,1)}, u32[]{:S(2)}, u32[]{:S(2)}) collective-permute-start(bf16[16,128,128]{2,1,0:T(8,128)(2,1)} %collective-permute-done.16.refs_5_), channel_id=1, source_target_pairs={{2,0},{4,2},{6,4},{7,6},{5,7},{3,5},{1,3},{0,1},{10,8},{12,10},{14... | collective-permute-start | bytes 1572872 | tf_op jit(solution)/shard_map/ppermute | solution.py:361
  100.4 28.1 %collective-permute-start.21 = (bf16[16,128,128]{2,1,0:T(8,128)(2,1)}, bf16[16,128,128]{2,1,0:T(8,128)(2,1)}, u32[]{:S(2)}, u32[]{:S(2)}) collective-permute-start(bf16[16,128,128]{2,1,0:T(8,128)(2,1)} %collective-permute-done.13.refs_2_), channel_id=1, source_target_pairs={{0,2},{2,4},{4,6},{6,7},{7,5},{5,3},{3,1},{1,0},{8,10},{10,12},{12... | collective-permute-start | bytes 1572872 | tf_op jit(solution)/shard_map/ppermute | solution.py:360
  101.0 27.5 %collective-permute-start.22 = (bf16[16,128,128]{2,1,0:T(8,128)(2,1)}, bf16[16,128,128]{2,1,0:T(8,128)(2,1)}, u32[]{:S(2)}, u32[]{:S(2)}) collective-permute-start(bf16[16,128,128]{2,1,0:T(8,128)(2,1)} %collective-permute-done.14.refs_4_), channel_id=1, source_target_pairs={{2,0},{4,2},{6,4},{7,6},{5,7},{3,5},{1,3},{0,1},{10,8},{12,10},{14... | collective-permute-start | bytes 1572872 | tf_op jit(solution)/shard_map/ppermute | solution.py:361
  117.7 11.5 %collective-permute-start.26 = (bf16[2,16,64,128]{3,2,1,0:T(8,128)(2,1)S(1)}, bf16[2,16,64,128]{3,2,1,0:T(8,128)(2,1)S(1)}, u32[]{:S(2)}, u32[]{:S(2)}) collective-permute-start(bf16[2,16,64,128]{3,2,1,0:T(8,128)(2,1)S(1)} %get-tuple-element.100), channel_id=1, source_target_pairs={{0,8},{8,0},{16,24},{24,16},{1,9},{9,1},{17,25},{25,17},{2,10},{10... | collective-permute-start | bytes 1572872 | tf_op jit(solution)/shard_map/ppermute | solution.py:378
  127.9 12.9 %collective-permute-start.19 = (bf16[16,128,128]{2,1,0:T(8,128)(2,1)S(1)}, bf16[16,128,128]{2,1,0:T(8,128)(2,1)S(1)}, u32[]{:S(2)}, u32[]{:S(2)}) collective-permute-start(bf16[16,128,128]{2,1,0:T(8,128)(2,1)S(1)} %get-tuple-element.86.refs_3_), channel_id=1, source_target_pairs={{0,2},{2,4},{4,6},{6,7},{7,5},{5,3},{3,1},{1,0},{8,10},{10,12},{12... | collective-permute-start | bytes 1572872 | tf_op jit(solution)/shard_map/ppermute | solution.py:360
  128.4 14.6 %collective-permute-start.20 = (bf16[16,128,128]{2,1,0:T(8,128)(2,1)S(1)}, bf16[16,128,128]{2,1,0:T(8,128)(2,1)S(1)}, u32[]{:S(2)}, u32[]{:S(2)}) collective-permute-start(bf16[16,128,128]{2,1,0:T(8,128)(2,1)S(1)} %get-tuple-element.86.refs_3_), channel_id=1, source_target_pairs={{2,0},{4,2},{6,4},{7,6},{5,7},{3,5},{1,3},{0,1},{10,8},{12,10},{14... | collective-permute-start | bytes 1572872 | tf_op jit(solution)/shard_map/ppermute | solution.py:361
  128.5 14.6 %collective-permute-start.23 = (bf16[2,16,64,128]{3,2,1,0:T(8,128)(2,1)S(1)}, bf16[2,16,64,128]{3,2,1,0:T(8,128)(2,1)S(1)}, u32[]{:S(2)}, u32[]{:S(2)}) collective-permute-start(bf16[2,16,64,128]{3,2,1,0:T(8,128)(2,1)S(1)} %get-tuple-element.94), channel_id=1, source_target_pairs={{0,16},{8,24},{16,0},{24,8},{1,17},{9,25},{17,1},{25,9},{2,18},{10... | collective-permute-start | bytes 1572872 | tf_op jit(solution)/shard_map/ppermute | solution.py:378
  129.2 22.8 %collective-permute-start.28 = (bf16[16,128,128]{2,1,0:T(8,128)(2,1)}, bf16[16,128,128]{2,1,0:T(8,128)(2,1)S(1)}, u32[]{:S(2)}, u32[]{:S(2)}) collective-permute-start(bf16[16,128,128]{2,1,0:T(8,128)(2,1)} %collective-permute-done.21.refs_1_), channel_id=1, source_target_pairs={{0,2},{2,4},{4,6},{6,7},{7,5},{5,3},{3,1},{1,0},{8,10},{10,12},{12... | collective-permute-start | bytes 1572872 | tf_op jit(solution)/shard_map/ppermute | solution.py:360
  131.1 22.2 %collective-permute-start.29 = (bf16[16,128,128]{2,1,0:T(8,128)(2,1)}, bf16[16,128,128]{2,1,0:T(8,128)(2,1)S(1)}, u32[]{:S(2)}, u32[]{:S(2)}) collective-permute-start(bf16[16,128,128]{2,1,0:T(8,128)(2,1)} %collective-permute-done.22.refs_5_), channel_id=1, source_target_pairs={{2,0},{4,2},{6,4},{7,6},{5,7},{3,5},{1,3},{0,1},{10,8},{12,10},{14... | collective-permute-start | bytes 1572872 | tf_op jit(solution)/shard_map/ppermute | solution.py:361
  143.1 22.9 %collective-permute-start.24 = (bf16[16,128,128]{2,1,0:T(8,128)(2,1)S(1)}, bf16[16,128,128]{2,1,0:T(8,128)(2,1)S(1)}, u32[]{:S(2)}, u32[]{:S(2)}) collective-permute-start(bf16[16,128,128]{2,1,0:T(8,128)(2,1)S(1)} %collective-permute-done.19.refs_2_), channel_id=1, source_target_pairs={{0,2},{2,4},{4,6},{6,7},{7,5},{5,3},{3,1},{1,0},{8,10},{10,12},{12... | collective-permute-start | bytes 1572872 | tf_op jit(solution)/shard_map/ppermute | solution.py:360
  144.5 21.5 %collective-permute-start.25 = (bf16[16,128,128]{2,1,0:T(8,128)(2,1)S(1)}, bf16[16,128,128]{2,1,0:T(8,128)(2,1)S(1)}, u32[]{:S(2)}, u32[]{:S(2)}) collective-permute-start(bf16[16,128,128]{2,1,0:T(8,128)(2,1)S(1)} %collective-permute-done.20.refs_4_), channel_id=1, source_target_pairs={{2,0},{4,2},{6,4},{7,6},{5,7},{3,5},{1,3},{0,1},{10,8},{12,10},{14... | collective-permute-start | bytes 1572872 | tf_op jit(solution)/shard_map/ppermute | solution.py:361
  144.5 23.2 %collective-permute-start.27 = (bf16[2,16,64,128]{3,2,1,0:T(8,128)(2,1)S(1)}, bf16[2,16,64,128]{3,2,1,0:T(8,128)(2,1)S(1)}, u32[]{:S(2)}, u32[]{:S(2)}) collective-permute-start(bf16[2,16,64,128]{3,2,1,0:T(8,128)(2,1)S(1)} %get-tuple-element.102), channel_id=1, source_target_pairs={{0,24},{8,16},{16,8},{24,0},{1,25},{9,17},{17,9},{25,1},{2,26},{10... | collective-permute-start | bytes 1572872 | tf_op jit(solution)/shard_map/ppermute | solution.py:378
  158.2 11.3 %collective-permute-start.30 = (bf16[2,16,64,128]{3,2,1,0:T(8,128)(2,1)S(1)}, bf16[2,16,64,128]{3,2,1,0:T(8,128)(2,1)S(1)}, u32[]{:S(2)}, u32[]{:S(2)}) collective-permute-start(bf16[2,16,64,128]{3,2,1,0:T(8,128)(2,1)S(1)} %get-tuple-element.109), channel_id=1, source_target_pairs={{0,8},{8,0},{16,24},{24,16},{1,9},{9,1},{17,25},{25,17},{2,10},{10... | collective-permute-start | bytes 1572872 | tf_op jit(solution)/shard_map/ppermute | solution.py:378
  166.0 11.8 %collective-permute-start.33 = (bf16[2,16,64,128]{3,2,1,0:T(8,128)(2,1)S(1)}, bf16[2,16,64,128]{3,2,1,0:T(8,128)(2,1)S(1)}, u32[]{:S(2)}, u32[]{:S(2)}) collective-permute-start(bf16[2,16,64,128]{3,2,1,0:T(8,128)(2,1)S(1)} %get-tuple-element.113), channel_id=1, source_target_pairs={{0,16},{8,24},{16,0},{24,8},{1,17},{9,25},{17,1},{25,9},{2,18},{10... | collective-permute-start | bytes 1572872 | tf_op jit(solution)/shard_map/ppermute | solution.py:378
  167.7 14.1 %collective-permute-start.36 = (bf16[16,128,128]{2,1,0:T(8,128)(2,1)S(1)}, bf16[16,128,128]{2,1,0:T(8,128)(2,1)S(1)}, u32[]{:S(2)}, u32[]{:S(2)}) collective-permute-start(bf16[16,128,128]{2,1,0:T(8,128)(2,1)S(1)} %get-tuple-element.119.refs_3_), channel_id=1, source_target_pairs={{0,2},{2,4},{4,6},{6,7},{7,5},{5,3},{3,1},{1,0},{8,10},{10,12},{12... | collective-permute-start | bytes 1572872 | tf_op jit(solution)/shard_map/ppermute | solution.py:360
  169.4 14.9 %collective-permute-start.37 = (bf16[16,128,128]{2,1,0:T(8,128)(2,1)S(1)}, bf16[16,128,128]{2,1,0:T(8,128)(2,1)S(1)}, u32[]{:S(2)}, u32[]{:S(2)}) collective-permute-start(bf16[16,128,128]{2,1,0:T(8,128)(2,1)S(1)} %get-tuple-element.119.refs_3_), channel_id=1, source_target_pairs={{2,0},{4,2},{6,4},{7,6},{5,7},{3,5},{1,3},{0,1},{10,8},{12,10},{14... | collective-permute-start | bytes 1572872 | tf_op jit(solution)/shard_map/ppermute | solution.py:361
  169.5 23.5 %collective-permute-start.31 = (bf16[16,128,128]{2,1,0:T(8,128)(2,1)S(1)}, bf16[16,128,128]{2,1,0:T(8,128)(2,1)S(1)}, u32[]{:S(2)}, u32[]{:S(2)}) collective-permute-start(bf16[16,128,128]{2,1,0:T(8,128)(2,1)S(1)} %collective-permute-done.24.refs_1_), channel_id=1, source_target_pairs={{0,2},{2,4},{4,6},{6,7},{7,5},{5,3},{3,1},{1,0},{8,10},{10,12},{12... | collective-permute-start | bytes 1572872 | tf_op jit(solution)/shard_map/ppermute | solution.py:360
  171.9 23.6 %collective-permute-start.32 = (bf16[16,128,128]{2,1,0:T(8,128)(2,1)S(1)}, bf16[16,128,128]{2,1,0:T(8,128)(2,1)S(1)}, u32[]{:S(2)}, u32[]{:S(2)}) collective-permute-start(bf16[16,128,128]{2,1,0:T(8,128)(2,1)S(1)} %collective-permute-done.25.refs_5_), channel_id=1, source_target_pairs={{2,0},{4,2},{6,4},{7,6},{5,7},{3,5},{1,3},{0,1},{10,8},{12,10},{14... | collective-permute-start | bytes 1572872 | tf_op jit(solution)/shard_map/ppermute | solution.py:361
  184.2 18.5 %collective-permute-start.38 = (bf16[16,128,128]{2,1,0:T(8,128)(2,1)S(1)}, bf16[16,128,128]{2,1,0:T(8,128)(2,1)S(1)}, u32[]{:S(2)}, u32[]{:S(2)}) collective-permute-start(bf16[16,128,128]{2,1,0:T(8,128)(2,1)S(1)} %collective-permute-done.36.refs_2_), channel_id=1, source_target_pairs={{0,2},{2,4},{4,6},{6,7},{7,5},{5,3},{3,1},{1,0},{8,10},{10,12},{12... | collective-permute-start | bytes 1572872 | tf_op jit(solution)/shard_map/ppermute | solution.py:360
  184.3 18.5 %collective-permute-start.39 = (bf16[16,128,128]{2,1,0:T(8,128)(2,1)S(1)}, bf16[16,128,128]{2,1,0:T(8,128)(2,1)S(1)}, u32[]{:S(2)}, u32[]{:S(2)}) collective-permute-start(bf16[16,128,128]{2,1,0:T(8,128)(2,1)S(1)} %collective-permute-done.37.refs_4_), channel_id=1, source_target_pairs={{2,0},{4,2},{6,4},{7,6},{5,7},{3,5},{1,3},{0,1},{10,8},{12,10},{14... | collective-permute-start | bytes 1572872 | tf_op jit(solution)/shard_map/ppermute | solution.py:361
  184.8 19.3 %collective-permute-start.41 = (bf16[2,16,64,128]{3,2,1,0:T(8,128)(2,1)S(1)}, bf16[2,16,64,128]{3,2,1,0:T(8,128)(2,1)S(1)}, u32[]{:S(2)}, u32[]{:S(2)}) collective-permute-start(bf16[2,16,64,128]{3,2,1,0:T(8,128)(2,1)S(1)} %get-tuple-element.125), channel_id=1, source_target_pairs={{0,24},{8,16},{16,8},{24,0},{1,25},{9,17},{17,9},{25,1},{2,26},{10... | collective-permute-start | bytes 1572872 | tf_op jit(solution)/shard_map/ppermute | solution.py:378
  200.4 14.9 %collective-permute-start.34 = (bf16[2,16,64,128]{3,2,1,0:T(8,128)(2,1)S(1)}, bf16[2,16,64,128]{3,2,1,0:T(8,128)(2,1)S(1)}, u32[]{:S(2)}, u32[]{:S(2)}) collective-permute-start(bf16[2,16,64,128]{3,2,1,0:T(8,128)(2,1)S(1)} %get-tuple-element.115), channel_id=1, source_target_pairs={{0,8},{8,0},{16,24},{24,16},{1,9},{9,1},{17,25},{25,17},{2,10},{10... | collective-permute-start | bytes 1572872 | tf_op jit(solution)/shard_map/ppermute | solution.py:378
  201.8 20.4 %collective-permute-start.35 = (bf16[2,16,64,128]{3,2,1,0:T(8,128)(2,1)S(1)}, bf16[2,16,64,128]{3,2,1,0:T(8,128)(2,1)S(1)}, u32[]{:S(2)}, u32[]{:S(2)}) collective-permute-start(bf16[2,16,64,128]{3,2,1,0:T(8,128)(2,1)S(1)} %get-tuple-element.116), channel_id=1, source_target_pairs={{0,16},{8,24},{16,0},{24,8},{1,17},{9,25},{17,1},{25,9},{2,18},{10... | collective-permute-start | bytes 1572872 | tf_op jit(solution)/shard_map/ppermute | solution.py:378
  202.8 19.4 %collective-permute-start.40 = (bf16[2,16,64,128]{3,2,1,0:T(8,128)(2,1)S(1)}, bf16[2,16,64,128]{3,2,1,0:T(8,128)(2,1)S(1)}, u32[]{:S(2)}, u32[]{:S(2)}) collective-permute-start(bf16[2,16,64,128]{3,2,1,0:T(8,128)(2,1)S(1)} %get-tuple-element.122), channel_id=1, source_target_pairs={{0,24},{8,16},{16,8},{24,0},{1,25},{9,17},{17,9},{25,1},{2,26},{10... | collective-permute-start | bytes 1572872 | tf_op jit(solution)/shard_map/ppermute | solution.py:378
  204.0 18.2 %collective-permute-start.42 = (bf16[16,128,128]{2,1,0:T(8,128)(2,1)S(1)}, bf16[16,128,128]{2,1,0:T(8,128)(2,1)S(1)}, u32[]{:S(2)}, u32[]{:S(2)}) collective-permute-start(bf16[16,128,128]{2,1,0:T(8,128)(2,1)S(1)} %collective-permute-done.38.refs_1_), channel_id=1, source_target_pairs={{0,2},{2,4},{4,6},{6,7},{7,5},{5,3},{3,1},{1,0},{8,10},{10,12},{12... | collective-permute-start | bytes 1572872 | tf_op jit(solution)/shard_map/ppermute | solution.py:360
  206.1 16.1 %collective-permute-start.43 = (bf16[16,128,128]{2,1,0:T(8,128)(2,1)S(1)}, bf16[16,128,128]{2,1,0:T(8,128)(2,1)S(1)}, u32[]{:S(2)}, u32[]{:S(2)}) collective-permute-start(bf16[16,128,128]{2,1,0:T(8,128)(2,1)S(1)} %collective-permute-done.39.refs_5_), channel_id=1, source_target_pairs={{2,0},{4,2},{6,4},{7,6},{5,7},{3,5},{1,3},{0,1},{10,8},{12,10},{14... | collective-permute-start | bytes 1572872 | tf_op jit(solution)/shard_map/ppermute | solution.py:361
  227.2 13.5 %collective-permute-start.46 = (bf16[2,16,64,128]{3,2,1,0:T(8,128)(2,1)S(1)}, bf16[2,16,64,128]{3,2,1,0:T(8,128)(2,1)S(1)}, u32[]{:S(2)}, u32[]{:S(2)}) collective-permute-start(bf16[2,16,64,128]{3,2,1,0:T(8,128)(2,1)S(1)} %get-tuple-element.137), channel_id=1, source_target_pairs={{0,8},{8,0},{16,24},{24,16},{1,9},{9,1},{17,25},{25,17},{2,10},{10... | collective-permute-start | bytes 1572872 | tf_op jit(solution)/shard_map/ppermute | solution.py:378
  228.6 19.1 %collective-permute-start.47 = (bf16[2,16,64,128]{3,2,1,0:T(8,128)(2,1)S(1)}, bf16[2,16,64,128]{3,2,1,0:T(8,128)(2,1)S(1)}, u32[]{:S(2)}, u32[]{:S(2)}) collective-permute-start(bf16[2,16,64,128]{3,2,1,0:T(8,128)(2,1)S(1)} %get-tuple-element.138), channel_id=1, source_target_pairs={{0,16},{8,24},{16,0},{24,8},{1,17},{9,25},{17,1},{25,9},{2,18},{10... | collective-permute-start | bytes 1572872 | tf_op jit(solution)/shard_map/ppermute | solution.py:378
  229.6 18.1 %collective-permute-start.48 = (bf16[2,16,64,128]{3,2,1,0:T(8,128)(2,1)S(1)}, bf16[2,16,64,128]{3,2,1,0:T(8,128)(2,1)S(1)}, u32[]{:S(2)}, u32[]{:S(2)}) collective-permute-start(bf16[2,16,64,128]{3,2,1,0:T(8,128)(2,1)S(1)} %get-tuple-element.139), channel_id=1, source_target_pairs={{0,24},{8,16},{16,8},{24,0},{1,25},{9,17},{17,9},{25,1},{2,26},{10... | collective-permute-start | bytes 1572872 | tf_op jit(solution)/shard_map/ppermute | solution.py:378
  232.6 17.5 %collective-permute-start.44 = (bf16[16,64,512]{2,1,0:T(8,128)(2,1)S(1)}, bf16[16,64,512]{2,1,0:T(8,128)(2,1)S(1)}, u32[]{:S(2)}, u32[]{:S(2)}) collective-permute-start(bf16[16,64,512]{2,1,0:T(8,128)(2,1)S(1)} %get-tuple-element.130), channel_id=1, source_target_pairs={{0,1},{1,0},{2,3},{3,2},{4,5},{5,4},{6,7},{7,6},{8,9},{9,8},{10,11... | collective-permute-start | bytes 3145736 | tf_op jit(solution)/shard_map/ppermute | solution.py:387
  232.7 17.5 %collective-permute-start.45 = (bf16[16,64,512]{2,1,0:T(8,128)(2,1)S(1)}, bf16[16,64,512]{2,1,0:T(8,128)(2,1)S(1)}, u32[]{:S(2)}, u32[]{:S(2)}) collective-permute-start(bf16[16,64,512]{2,1,0:T(8,128)(2,1)S(1)} %get-tuple-element.134), channel_id=1, source_target_pairs={{0,1},{1,0},{2,3},{3,2},{4,5},{5,4},{6,7},{7,6},{8,9},{9,8},{10,11... | collective-permute-start | bytes 3145736 | tf_op jit(solution)/shard_map/ppermute | solution.py:387
  (32 other events, 629.9 us)
